TPU v7x, 32 devices: a whole 2x2x4 slice. The times are simulated.
32 devices in a mesh: stream: 2 (over x), dp: 4 (over z), tensor: 4 (over y, core).
Axes of the slice: x: 2, y: 2, z: 4, core: 2. Of those that a mesh axis runs over, the one named last changes fastest.
Arguments:
- text_in: bfloat16 [16384, 768], P(('stream', 'dp', 'tensor')), may hold values from -6 to 6
- image_in: bfloat16 [4736, 1024], P(('stream', 'dp', 'tensor')), may hold values from -6 to 6
- lengths: int32 [128], P(('stream', 'dp')), may hold values from 8 to 128, as said below
- text_cot: bfloat16 [16384, 768], P(('stream', 'dp', 'tensor')), may hold values from -6 to 6
- image_cot: bfloat16 [4736, 1024], P(('stream', 'dp', 'tensor')), may hold values from -6 to 6
- text_cross_q: bfloat16 [1, 768, 1024], P(None, None, 'tensor'), may hold values from -0.21875 to 0.21875
- text_cross_kv: bfloat16 [1, 1024, 2, 1024], P(None, None, None, 'tensor'), may hold values from -0.1875 to 0.1875
- text_cross_out: bfloat16 [1, 1024, 768], P(None, 'tensor'), may hold values from -0.5 to 0.5
- text_up: bfloat16 [1, 768, 3072], P(None, None, 'tensor'), may hold values from -0.21875 to 0.21875
- text_down: bfloat16 [1, 3072, 768], P(None, 'tensor'), may hold values from -0.21875 to 0.21875
- text_self_qkv: bfloat16 [1, 768, 3, 768], P(None, None, None, 'tensor'), may hold values from -0.21875 to 0.21875
- text_self_out: bfloat16 [1, 768, 768], P(None, 'tensor'), may hold values from -0.625 to 0.625
- text_gain: bfloat16 [1, 3, 768], replicated, may hold values from 0.099609375 to 1.8984375
- text_bias: bfloat16 [1, 3, 768], replicated, may hold values from -1.5 to 1.5
- image_cross_q: bfloat16 [1, 1024, 1024], P(None, None, 'tensor'), may hold values from -0.1875 to 0.1875
- image_cross_kv: bfloat16 [1, 768, 2, 1024], P(None, None, None, 'tensor'), may hold values from -0.21875 to 0.21875
- image_cross_out: bfloat16 [1, 1024, 1024], P(None, 'tensor'), may hold values from -0.5 to 0.5
- image_up: bfloat16 [1, 1024, 1024], P(None, None, 'tensor'), may hold values from -0.1875 to 0.1875
- image_down: bfloat16 [1, 1024, 1024], P(None, 'tensor'), may hold values from -0.375 to 0.375
- image_self_qkv: bfloat16 [1, 1024, 3, 1024], P(None, None, None, 'tensor'), may hold values from -0.1875 to 0.1875
- image_self_out: bfloat16 [1, 1024, 1024], P(None, 'tensor'), may hold values from -0.5 to 0.5
- image_gain: bfloat16 [1, 3, 1024], replicated, may hold values from 0.099609375 to 1.8984375
- image_bias: bfloat16 [1, 3, 1024], replicated, may hold values from -1.5 to 1.5
Outputs:
- text_out: float32 [16384, 768], P(('stream', 'dp', 'tensor'))
- image_out: float32 [4736, 1024], P(('stream', 'dp', 'tensor'))
- text_grad: float32 [16384, 768], P(('stream', 'dp', 'tensor'))
- image_grad: float32 [4736, 1024], P(('stream', 'dp', 'tensor'))
- grad_text_cross_q: float32 [1, 768, 1024], P(None, ('stream', 'dp'), 'tensor')
- grad_text_cross_kv: float32 [1, 1024, 2, 1024], P(None, ('stream', 'dp'), None, 'tensor')
- grad_text_cross_out: float32 [1, 1024, 768], P(None, 'tensor', ('stream', 'dp'))
- grad_text_up: float32 [1, 768, 3072], P(None, ('stream', 'dp'), 'tensor')
- grad_text_down: float32 [1, 3072, 768], P(None, 'tensor', ('stream', 'dp'))
- grad_text_self_qkv: float32 [1, 768, 3, 768], P(None, ('stream', 'dp'), None, 'tensor')
- grad_text_self_out: float32 [1, 768, 768], P(None, 'tensor', ('stream', 'dp'))
- grad_text_gain: float32 [1, 3, 768], P(None, None, ('stream', 'dp'))
- grad_text_bias: float32 [1, 3, 768], P(None, None, ('stream', 'dp'))
- grad_image_cross_q: float32 [1, 1024, 1024], P(None, ('stream', 'dp'), 'tensor')
- grad_image_cross_kv: float32 [1, 768, 2, 1024], P(None, ('stream', 'dp'), None, 'tensor')
- grad_image_cross_out: float32 [1, 1024, 1024], P(None, 'tensor', ('stream', 'dp'))
- grad_image_up: float32 [1, 1024, 1024], P(None, ('stream', 'dp'), 'tensor')
- grad_image_down: float32 [1, 1024, 1024], P(None, 'tensor', ('stream', 'dp'))
- grad_image_self_qkv: float32 [1, 1024, 3, 1024], P(None, ('stream', 'dp'), None, 'tensor')
- grad_image_self_out: float32 [1, 1024, 1024], P(None, 'tensor', ('stream', 'dp'))
- grad_image_gain: float32 [1, 3, 1024], P(None, None, ('stream', 'dp'))
- grad_image_bias: float32 [1, 3, 1024], P(None, None, ('stream', 'dp'))
Inputs may be any that keep to these rules, and one draw needn't show every extreme that they name: `lengths`: every caption has at least 8 tokens; some caption has all 128.
All inputs are finite; a program needn't handle non-finite values.
Results may differ from a plain program's by a relative error of at most 0.03.
Values may be sent and summed in bfloat16 or wider, within the bound.
A program may use at most 192 MiB of HBM per device.

v0:
```python
import jax
import jax.numpy as jnp
from jax import lax
from jax.sharding import PartitionSpec as P

DT = 768
DV = 1024
DC = 1024
HC = 8
HT = 12
HV = 8
SLOTS = 128
REGIONS = 37
LAYERS = 1


norm_eps = 1e-05
masked_score = -1e30


def partner(value, axis, apart):
    mask = 2**apart
    pairs = [(source, source ^ mask) for source in range(lax.axis_size(axis))]
    return lax.ppermute(value, axis, pairs)


def matmul(left, right):
    return lax.dot_general(
        left, right, (((left.ndim - 1,), (0,)), ((), ())), preferred_element_type=jnp.float32
    )


def weight_grad(inputs, grads):
    return lax.dot_general(
        inputs, grads, (((0,), (0,)), ((), ())), preferred_element_type=jnp.float32
    )


def input_grad(grads, weight):
    inner = weight.ndim - 1
    weight_axes = tuple(range(1, weight.ndim))
    grad_axes = tuple(range(grads.ndim - inner, grads.ndim))
    return lax.dot_general(
        grads, weight, ((grad_axes, weight_axes), ((), ())), preferred_element_type=jnp.float32
    )


def layer_norm(inputs, gain_row, bias_row):
    centered = inputs - jnp.mean(inputs, axis=-1, keepdims=True)
    variance = jnp.mean(centered * centered, axis=-1, keepdims=True)
    return centered * lax.rsqrt(variance + norm_eps) * gain_row + bias_row


def norm_back(pre_norm, gain_row, bias_row, grad_out):
    unused, pullback = jax.vjp(
        layer_norm, pre_norm, gain_row.astype(jnp.float32), bias_row.astype(jnp.float32)
    )
    return pullback(grad_out)


def smooth_gate(inputs):
    return jax.nn.gelu(inputs, approximate=False)


def to_heads(flat, pair_count, head_size):
    return flat.reshape(
        pair_count, flat.shape[0] // pair_count, flat.shape[-1] // head_size, head_size
    )


def flatten(heads):
    return heads.reshape(heads.shape[0] * heads.shape[1], heads.shape[2] * heads.shape[3])


def attend_forward(queries, keys_in, values, key_mask):
    scaling = queries.shape[-1] ** (-0.5)
    scores = (
        jnp.einsum("gqhd,gkhd->ghqk", queries, keys_in, preferred_element_type=jnp.float32)
        * scaling
    )
    scores = jnp.where(key_mask[:, None, None, :], scores, masked_score)
    row_max = jnp.max(scores, axis=-1, keepdims=True)
    row_sum = jnp.sum(jnp.exp(scores - row_max), axis=-1, keepdims=True)
    logsum = row_max + jnp.log(row_sum)
    attn_probs = jnp.exp(scores - logsum).astype(jnp.bfloat16)
    context = jnp.einsum("ghqk,gkhd->gqhd", attn_probs, values, preferred_element_type=jnp.float32)
    return (context.astype(jnp.bfloat16), logsum)


def attend_backward(queries, keys_in, values, key_mask, logsum, grad_context):
    scaling = queries.shape[-1] ** (-0.5)
    scores = (
        jnp.einsum("gqhd,gkhd->ghqk", queries, keys_in, preferred_element_type=jnp.float32)
        * scaling
    )
    scores = jnp.where(key_mask[:, None, None, :], scores, masked_score)
    attn_probs = jnp.exp(scores - logsum)
    grad_probs = jnp.einsum(
        "gqhd,gkhd->ghqk", grad_context, values, preferred_element_type=jnp.float32
    )
    grad_values = jnp.einsum(
        "ghqk,gqhd->gkhd",
        attn_probs.astype(jnp.bfloat16),
        grad_context,
        preferred_element_type=jnp.float32,
    )
    inner_sum = jnp.sum(attn_probs * grad_probs, axis=-1, keepdims=True)
    grad_scores = (attn_probs * (grad_probs - inner_sum)).astype(jnp.bfloat16)
    grad_queries = (
        jnp.einsum("ghqk,gkhd->gqhd", grad_scores, keys_in, preferred_element_type=jnp.float32)
        * scaling
    )
    grad_keys = (
        jnp.einsum("ghqk,gqhd->gkhd", grad_scores, queries, preferred_element_type=jnp.float32)
        * scaling
    )
    return (
        grad_queries.astype(jnp.bfloat16),
        grad_keys.astype(jnp.bfloat16),
        grad_values.astype(jnp.bfloat16),
    )


def cross_forward(own_low, other_low, query_w, pair_w, other_mask, pair_count):
    head_size = DC // HC
    queries = to_heads(matmul(own_low, query_w).astype(jnp.bfloat16), pair_count, head_size)
    pair_proj = matmul(other_low, pair_w).astype(jnp.bfloat16)
    keys_in = to_heads(pair_proj[:, 0], pair_count, head_size)
    values = to_heads(pair_proj[:, 1], pair_count, head_size)
    context, logsum = attend_forward(queries, keys_in, values, other_mask)
    return (queries, keys_in, values, context, logsum)


def self_forward(own_low, qkv_w, key_mask, pair_count, head_size):
    triple = matmul(own_low, qkv_w).astype(jnp.bfloat16)
    queries = to_heads(triple[:, 0], pair_count, head_size)
    keys_in = to_heads(triple[:, 1], pair_count, head_size)
    values = to_heads(triple[:, 2], pair_count, head_size)
    context, logsum = attend_forward(queries, keys_in, values, key_mask)
    return (queries, keys_in, values, context, logsum)


def self_back(grad_add, inputs_low, saved_self, key_mask, qkv_w, out_w, head_size):
    queries, keys_in, values, context, logsum = saved_self
    pair_count = queries.shape[0]
    grad_out_w = weight_grad(flatten(context), grad_add)
    grad_context = to_heads(input_grad(grad_add, out_w).astype(jnp.bfloat16), pair_count, head_size)
    grad_q, grad_k, grad_v = attend_backward(
        queries, keys_in, values, key_mask, logsum, grad_context
    )
    grad_qkv = jnp.stack([flatten(grad_q), flatten(grad_k), flatten(grad_v)], axis=1)
    grad_qkv_w = weight_grad(inputs_low, grad_qkv)
    return (input_grad(grad_qkv, qkv_w), grad_qkv_w, grad_out_w)


def mlp_back(grad_add, inputs_low, hidden, activ, up_w, down_w):
    grad_down_w = weight_grad(activ, grad_add)
    grad_activ = input_grad(grad_add, down_w)
    unused, gate_back = jax.vjp(smooth_gate, hidden)
    grad_hidden = gate_back(grad_activ)[0].astype(jnp.bfloat16)
    grad_up_w = weight_grad(inputs_low, grad_hidden)
    return (input_grad(grad_hidden, up_w), grad_up_w, grad_down_w)


def cross_back(grad_add, own_low, other_low, saved_cross, key_mask, query_w, pair_w, out_w):
    queries, keys_in, values, context, logsum = saved_cross
    pair_count = queries.shape[0]
    grad_out_w = weight_grad(flatten(context), grad_add)
    grad_context = to_heads(input_grad(grad_add, out_w).astype(jnp.bfloat16), pair_count, DC // HC)
    grad_q, grad_k, grad_v = attend_backward(
        queries, keys_in, values, key_mask, logsum, grad_context
    )
    grad_query = flatten(grad_q)
    grad_pair = jnp.stack([flatten(grad_k), flatten(grad_v)], axis=1)
    grad_query_w = weight_grad(own_low, grad_query)
    grad_pair_w = weight_grad(other_low, grad_pair)
    return (
        input_grad(grad_query, query_w),
        input_grad(grad_pair, pair_w),
        grad_query_w,
        grad_pair_w,
        grad_out_w,
    )


def branch_sums(text_part, image_part):
    return (
        lax.psum_scatter(text_part, "tensor", scatter_dimension=0, tiled=True),
        lax.psum_scatter(image_part, "tensor", scatter_dimension=0, tiled=True),
    )


def row_gather(text_part, image_part):
    return (
        lax.all_gather(text_part, "tensor", axis=0, tiled=True),
        lax.all_gather(image_part, "tensor", axis=0, tiled=True),
    )


def grad_gather(text_part, image_part):
    return (
        lax.all_gather(text_part, "tensor", axis=0, tiled=True),
        lax.all_gather(image_part, "tensor", axis=0, tiled=True),
    )


def grad_rows(text_part, image_part):
    return (
        lax.psum_scatter(text_part, "tensor", scatter_dimension=0, tiled=True),
        lax.psum_scatter(image_part, "tensor", scatter_dimension=0, tiled=True),
    )


def local(
    text_in,
    image_in,
    lengths,
    text_cot,
    image_cot,
    text_cross_q,
    text_cross_kv,
    text_cross_out,
    text_up,
    text_down,
    text_self_qkv,
    text_self_out,
    text_gain,
    text_bias,
    image_cross_q,
    image_cross_kv,
    image_cross_out,
    image_up,
    image_down,
    image_self_qkv,
    image_self_out,
    image_gain,
    image_bias,
):
    pair_count = lengths.shape[0]
    slot_ids = lax.broadcasted_iota(jnp.int32, (pair_count, SLOTS), 1)
    text_mask = slot_ids < lengths[:, None]
    image_mask = jnp.ones((pair_count, REGIONS), dtype=jnp.bool_)
    length_low = lengths.astype(jnp.bfloat16)
    text_run = text_in.astype(jnp.float32)
    image_run = image_in.astype(jnp.float32)
    layer_idx = 0
    text_shard = text_run.astype(jnp.bfloat16)
    image_shard = image_run.astype(jnp.bfloat16)
    text_low = lax.all_gather(text_shard, "tensor", axis=0, tiled=True)
    image_low = lax.all_gather(image_shard, "tensor", axis=0, tiled=True)
    other_image, other_text, other_length = partner((image_low, text_low, length_low), "stream", 0)
    other_mask = slot_ids.astype(jnp.float32) < other_length.astype(jnp.float32)[:, None]
    text_cross = cross_forward(
        text_low,
        other_image,
        text_cross_q[layer_idx],
        text_cross_kv[layer_idx],
        image_mask,
        pair_count,
    )
    image_cross = cross_forward(
        image_low,
        other_text,
        image_cross_q[layer_idx],
        image_cross_kv[layer_idx],
        other_mask,
        pair_count,
    )
    text_add, image_add = branch_sums(
        matmul(flatten(text_cross[3]), text_cross_out[layer_idx]),
        matmul(flatten(image_cross[3]), image_cross_out[layer_idx]),
    )
    text_pre1 = text_run + text_add
    image_pre1 = image_run + image_add
    text_one = layer_norm(text_pre1, text_gain[layer_idx, 0], text_bias[layer_idx, 0])
    image_one = layer_norm(image_pre1, image_gain[layer_idx, 0], image_bias[layer_idx, 0])
    text_one_low, image_one_low = row_gather(
        text_one.astype(jnp.bfloat16), image_one.astype(jnp.bfloat16)
    )
    text_hidden = matmul(text_one_low, text_up[layer_idx])
    image_hidden = matmul(image_one_low, image_up[layer_idx])
    text_activ = smooth_gate(text_hidden).astype(jnp.bfloat16)
    image_activ = smooth_gate(image_hidden).astype(jnp.bfloat16)
    text_add, image_add = branch_sums(
        matmul(text_activ, text_down[layer_idx]), matmul(image_activ, image_down[layer_idx])
    )
    text_pre2 = text_one + text_add
    image_pre2 = image_one + image_add
    text_two = layer_norm(text_pre2, text_gain[layer_idx, 1], text_bias[layer_idx, 1])
    image_two = layer_norm(image_pre2, image_gain[layer_idx, 1], image_bias[layer_idx, 1])
    text_two_low, image_two_low = row_gather(
        text_two.astype(jnp.bfloat16), image_two.astype(jnp.bfloat16)
    )
    text_self = self_forward(
        text_two_low, text_self_qkv[layer_idx], text_mask, pair_count, DT // HT
    )
    image_self = self_forward(
        image_two_low, image_self_qkv[layer_idx], image_mask, pair_count, DV // HV
    )
    text_add, image_add = branch_sums(
        matmul(flatten(text_self[3]), text_self_out[layer_idx]),
        matmul(flatten(image_self[3]), image_self_out[layer_idx]),
    )
    text_pre3 = text_two + text_add
    image_pre3 = image_two + image_add
    records = [
        dict(
            text_low=text_low,
            image_low=image_low,
            other_text=other_text,
            other_image=other_image,
            other_mask=other_mask,
            text_cross=text_cross,
            image_cross=image_cross,
            text_pre1=text_pre1,
            image_pre1=image_pre1,
            text_one_low=text_one_low,
            image_one_low=image_one_low,
            text_hidden=text_hidden,
            image_hidden=image_hidden,
            text_activ=text_activ,
            image_activ=image_activ,
            text_pre2=text_pre2,
            image_pre2=image_pre2,
            text_two_low=text_two_low,
            image_two_low=image_two_low,
            text_self=text_self,
            image_self=image_self,
            text_pre3=text_pre3,
            image_pre3=image_pre3,
        )
    ]
    text_run = layer_norm(text_pre3, text_gain[layer_idx, 2], text_bias[layer_idx, 2])
    image_run = layer_norm(image_pre3, image_gain[layer_idx, 2], image_bias[layer_idx, 2])
    grad_text = text_cot.astype(jnp.float32)
    grad_image = image_cot.astype(jnp.float32)
    collected = []
    for layer_idx in reversed(range(LAYERS)):
        record = records[layer_idx]
        text_n3 = norm_back(
            record["text_pre3"], text_gain[layer_idx, 2], text_bias[layer_idx, 2], grad_text
        )
        image_n3 = norm_back(
            record["image_pre3"], image_gain[layer_idx, 2], image_bias[layer_idx, 2], grad_image
        )
        text_g3, image_g3 = grad_gather(
            text_n3[0].astype(jnp.bfloat16), image_n3[0].astype(jnp.bfloat16)
        )
        text_sb = self_back(
            text_g3,
            record["text_two_low"],
            record["text_self"],
            text_mask,
            text_self_qkv[layer_idx],
            text_self_out[layer_idx],
            DT // HT,
        )
        image_sb = self_back(
            image_g3,
            record["image_two_low"],
            record["image_self"],
            image_mask,
            image_self_qkv[layer_idx],
            image_self_out[layer_idx],
            DV // HV,
        )
        text_part, image_part = grad_rows(text_sb[0], image_sb[0])
        grad_text_two = text_n3[0] + text_part
        grad_image_two = image_n3[0] + image_part
        text_n2 = norm_back(
            record["text_pre2"], text_gain[layer_idx, 1], text_bias[layer_idx, 1], grad_text_two
        )
        image_n2 = norm_back(
            record["image_pre2"], image_gain[layer_idx, 1], image_bias[layer_idx, 1], grad_image_two
        )
        text_g2, image_g2 = grad_gather(
            text_n2[0].astype(jnp.bfloat16), image_n2[0].astype(jnp.bfloat16)
        )
        text_mb = mlp_back(
            text_g2,
            record["text_one_low"],
            record["text_hidden"],
            record["text_activ"],
            text_up[layer_idx],
            text_down[layer_idx],
        )
        image_mb = mlp_back(
            image_g2,
            record["image_one_low"],
            record["image_hidden"],
            record["image_activ"],
            image_up[layer_idx],
            image_down[layer_idx],
        )
        text_part, image_part = grad_rows(text_mb[0], image_mb[0])
        grad_text_one = text_n2[0] + text_part
        grad_image_one = image_n2[0] + image_part
        text_n1 = norm_back(
            record["text_pre1"], text_gain[layer_idx, 0], text_bias[layer_idx, 0], grad_text_one
        )
        image_n1 = norm_back(
            record["image_pre1"], image_gain[layer_idx, 0], image_bias[layer_idx, 0], grad_image_one
        )
        text_g1, image_g1 = grad_gather(
            text_n1[0].astype(jnp.bfloat16), image_n1[0].astype(jnp.bfloat16)
        )
        text_cb = cross_back(
            text_g1,
            record["text_low"],
            record["other_image"],
            record["text_cross"],
            image_mask,
            text_cross_q[layer_idx],
            text_cross_kv[layer_idx],
            text_cross_out[layer_idx],
        )
        image_cb = cross_back(
            image_g1,
            record["image_low"],
            record["other_text"],
            record["image_cross"],
            record["other_mask"],
            image_cross_q[layer_idx],
            image_cross_kv[layer_idx],
            image_cross_out[layer_idx],
        )
        text_own, image_for_partner, image_own, text_for_partner = (
            lax.psum_scatter(text_cb[0], "tensor", scatter_dimension=0, tiled=True),
            lax.psum_scatter(text_cb[1], "tensor", scatter_dimension=0, tiled=True),
            lax.psum_scatter(image_cb[0], "tensor", scatter_dimension=0, tiled=True),
            lax.psum_scatter(image_cb[1], "tensor", scatter_dimension=0, tiled=True),
        )
        image_back, text_back = partner((image_for_partner, text_for_partner), "stream", 0)
        grad_text = text_n1[0] + text_own + text_back
        grad_image = image_n1[0] + image_own + image_back
        collected.append(
            (
                text_cb[2],
                text_cb[3],
                text_cb[4],
                text_mb[1],
                text_mb[2],
                text_sb[1],
                text_sb[2],
                jnp.stack([text_n1[1], text_n2[1], text_n3[1]]),
                jnp.stack([text_n1[2], text_n2[2], text_n3[2]]),
                image_cb[2],
                image_cb[3],
                image_cb[4],
                image_mb[1],
                image_mb[2],
                image_sb[1],
                image_sb[2],
                jnp.stack([image_n1[1], image_n2[1], image_n3[1]]),
                jnp.stack([image_n1[2], image_n2[2], image_n3[2]]),
            )
        )
    collected = collected[::-1]

    def stacked(position):
        return jnp.stack([record[position] for record in collected])

    text_gain_sum, text_bias_sum, image_gain_sum, image_bias_sum = lax.psum(
        (stacked(7), stacked(8), stacked(16), stacked(17)), "tensor"
    )
    part_tq = stacked(0)
    part_tkv = stacked(1)
    part_tout = stacked(2)
    part_tup = stacked(3)
    part_tdown = stacked(4)
    part_tqkv = stacked(5)
    part_tsout = stacked(6)
    part_iq = stacked(9)
    part_ikv = stacked(10)
    part_iout = stacked(11)
    part_iup = stacked(12)
    part_idown = stacked(13)
    part_iqkv = stacked(14)
    part_isout = stacked(15)
    (
        half_tq,
        half_tkv,
        half_tout,
        half_tup,
        half_tdown,
        half_tqkv,
        half_tsout,
        half_tgain,
        half_tbias,
        half_iq,
        half_ikv,
        half_iout,
        half_iup,
        half_idown,
        half_iqkv,
        half_isout,
        half_igain,
        half_ibias,
    ) = (
        lax.psum_scatter(part_tq, "stream", scatter_dimension=1, tiled=True),
        lax.psum_scatter(part_tkv, "stream", scatter_dimension=1, tiled=True),
        lax.psum_scatter(part_tout, "stream", scatter_dimension=2, tiled=True),
        lax.psum_scatter(part_tup, "stream", scatter_dimension=1, tiled=True),
        lax.psum_scatter(part_tdown, "stream", scatter_dimension=2, tiled=True),
        lax.psum_scatter(part_tqkv, "stream", scatter_dimension=1, tiled=True),
        lax.psum_scatter(part_tsout, "stream", scatter_dimension=2, tiled=True),
        lax.psum_scatter(text_gain_sum, "stream", scatter_dimension=2, tiled=True),
        lax.psum_scatter(text_bias_sum, "stream", scatter_dimension=2, tiled=True),
        lax.psum_scatter(part_iq, "stream", scatter_dimension=1, tiled=True),
        lax.psum_scatter(part_ikv, "stream", scatter_dimension=1, tiled=True),
        lax.psum_scatter(part_iout, "stream", scatter_dimension=2, tiled=True),
        lax.psum_scatter(part_iup, "stream", scatter_dimension=1, tiled=True),
        lax.psum_scatter(part_idown, "stream", scatter_dimension=2, tiled=True),
        lax.psum_scatter(part_iqkv, "stream", scatter_dimension=1, tiled=True),
        lax.psum_scatter(part_isout, "stream", scatter_dimension=2, tiled=True),
        lax.psum_scatter(image_gain_sum, "stream", scatter_dimension=2, tiled=True),
        lax.psum_scatter(image_bias_sum, "stream", scatter_dimension=2, tiled=True),
    )
    reduced = (
        lax.psum_scatter(half_tq, "dp", scatter_dimension=1, tiled=True),
        lax.psum_scatter(half_tkv, "dp", scatter_dimension=1, tiled=True),
        lax.psum_scatter(half_tout, "dp", scatter_dimension=2, tiled=True),
        lax.psum_scatter(half_tup, "dp", scatter_dimension=1, tiled=True),
        lax.psum_scatter(half_tdown, "dp", scatter_dimension=2, tiled=True),
        lax.psum_scatter(half_tqkv, "dp", scatter_dimension=1, tiled=True),
        lax.psum_scatter(half_tsout, "dp", scatter_dimension=2, tiled=True),
        lax.psum_scatter(half_tgain, "dp", scatter_dimension=2, tiled=True),
        lax.psum_scatter(half_tbias, "dp", scatter_dimension=2, tiled=True),
        lax.psum_scatter(half_iq, "dp", scatter_dimension=1, tiled=True),
        lax.psum_scatter(half_ikv, "dp", scatter_dimension=1, tiled=True),
        lax.psum_scatter(half_iout, "dp", scatter_dimension=2, tiled=True),
        lax.psum_scatter(half_iup, "dp", scatter_dimension=1, tiled=True),
        lax.psum_scatter(half_idown, "dp", scatter_dimension=2, tiled=True),
        lax.psum_scatter(half_iqkv, "dp", scatter_dimension=1, tiled=True),
        lax.psum_scatter(half_isout, "dp", scatter_dimension=2, tiled=True),
        lax.psum_scatter(half_igain, "dp", scatter_dimension=2, tiled=True),
        lax.psum_scatter(half_ibias, "dp", scatter_dimension=2, tiled=True),
    )
    return (
        text_run,
        image_run,
        grad_text,
        grad_image,
        reduced[0],
        reduced[1],
        reduced[2],
        reduced[3],
        reduced[4],
        reduced[5],
        reduced[6],
        reduced[7],
        reduced[8],
        reduced[9],
        reduced[10],
        reduced[11],
        reduced[12],
        reduced[13],
        reduced[14],
        reduced[15],
        reduced[16],
        reduced[17],
    )


def solution(mesh):
    in_specs = (
        P(("stream", "dp", "tensor"), None),
        P(("stream", "dp", "tensor"), None),
        P(("stream", "dp")),
        P(("stream", "dp", "tensor"), None),
        P(("stream", "dp", "tensor"), None),
        P(None, None, "tensor"),
        P(None, None, None, "tensor"),
        P(None, "tensor", None),
        P(None, None, "tensor"),
        P(None, "tensor", None),
        P(None, None, None, "tensor"),
        P(None, "tensor", None),
        P(),
        P(),
        P(None, None, "tensor"),
        P(None, None, None, "tensor"),
        P(None, "tensor", None),
        P(None, None, "tensor"),
        P(None, "tensor", None),
        P(None, None, None, "tensor"),
        P(None, "tensor", None),
        P(),
        P(),
    )
    out_specs = (
        P(("stream", "dp", "tensor"), None),
        P(("stream", "dp", "tensor"), None),
        P(("stream", "dp", "tensor"), None),
        P(("stream", "dp", "tensor"), None),
        P(None, ("stream", "dp"), "tensor"),
        P(None, ("stream", "dp"), None, "tensor"),
        P(None, "tensor", ("stream", "dp")),
        P(None, ("stream", "dp"), "tensor"),
        P(None, "tensor", ("stream", "dp")),
        P(None, ("stream", "dp"), None, "tensor"),
        P(None, "tensor", ("stream", "dp")),
        P(None, None, ("stream", "dp")),
        P(None, None, ("stream", "dp")),
        P(None, ("stream", "dp"), "tensor"),
        P(None, ("stream", "dp"), None, "tensor"),
        P(None, "tensor", ("stream", "dp")),
        P(None, ("stream", "dp"), "tensor"),
        P(None, "tensor", ("stream", "dp")),
        P(None, ("stream", "dp"), None, "tensor"),
        P(None, "tensor", ("stream", "dp")),
        P(None, None, ("stream", "dp")),
        P(None, None, ("stream", "dp")),
    )
    return jax.shard_map(local, mesh=mesh, in_specs=in_specs, out_specs=out_specs, check_vma=False)
```

profile of v0, /device:TPU:0, one launch (start us, length us, event | category | flops | bytes accessed | tf_op | source)
XLA Modules:
  0.0 1905.5 jit_solution(15623066588815679591)
XLA Ops:
  8.7 21.4 %all-gather.31.cloned.1.call-done = bf16[4,148,1024]{2,1,0:T(8,128)(2,1)} async-done(((bf16[1,148,1024]{2,1,0:T(8,128)(2,1)}), bf16[4,148,1024]{2,1,0:T(8,128)(2,1)}) %all-gather.31.cloned.1.call-update) | async-done | bytes 1212432 | tf_op jit(solution)/shard_map/all_gather | solution.py:250
  33.1 27.3 %collective-permute-done = bf16[592,1024]{1,0:T(8,128)(2,1)S(1)} collective-permute-done((bf16[592,1024]{1,0:T(8,128)(2,1)S(1)}, bf16[592,1024]{1,0:T(8,128)(2,1)S(1)}, u32[]{:S(2)}, u32[]{:S(2)}) %collective-permute-start) | collective-permute-done | bytes 1212448 | tf_op jit(solution)/shard_map/ppermute | solution.py:24
  76.9 57.2 %reduce-scatter.74.cloned.1.call-done = f32[512,768]{1,0:T(8,128)} async-done(((f32[2048,768]{1,0:T(8,128)}), f32[512,768]{1,0:T(8,128)}) %reduce-scatter.74.cloned.1.call-update) | async-done | bytes 1572880 | tf_op jit(solution)/shard_map/reduce_scatter | solution.py:188
  137.5 28.7 %all-gather.21.cloned.1.call-done = bf16[2048,768]{1,0:T(8,128)(2,1)} async-done(((bf16[512,768]{1,0:T(8,128)(2,1)}), bf16[2048,768]{1,0:T(8,128)(2,1)}) %all-gather.21.cloned.1.call-update) | async-done | bytes 3145744 | tf_op jit(solution)/shard_map/all_gather | solution.py:195
  193.9 67.9 %collective-permute-done.2 = bf16[16]{0:T(256)(128)(2,1)S(1)} collective-permute-done((bf16[16]{0:T(256)(128)(2,1)S(1)}, bf16[16]{0:T(256)(128)(2,1)S(1)}, u32[]{:S(2)}, u32[]{:S(2)}) %collective-permute-start.2) | collective-permute-done | bytes 64 | tf_op jit(solution)/shard_map/ppermute | solution.py:24
  281.9 26.5 %fusion = f32[152,1024]{1,0:T(8,128)} fusion(f32[592,1024]{1,0:T(8,128)} %fusion.137), kind=kCustom, calls=%all-reduce-scatter | all-reduce-scatter fusion | flops 622593 | bytes 3047936
  350.5 41.0 %fusion.1 = f32[152,1024]{1,0:T(8,128)} fusion(f32[592,1024]{1,0:T(8,128)} %fusion.128), kind=kCustom, calls=%all-reduce-scatter.1 | all-reduce-scatter fusion | flops 622593 | bytes 3047936
  436.6 47.1 %reduce-scatter.78.cloned.1.call-done = f32[512,768]{1,0:T(8,128)} async-done(((f32[2048,768]{1,0:T(8,128)}), f32[512,768]{1,0:T(8,128)}) %reduce-scatter.78.cloned.1.call-update) | async-done | bytes 1572880 | tf_op jit(solution)/shard_map/reduce_scatter | solution.py:188
  494.9 43.4 %fusion.2 = f32[152,1024]{1,0:T(8,128)} fusion(f32[592,1024]{1,0:T(8,128)} %fusion.124), kind=kCustom, calls=%all-reduce-scatter.2 | all-reduce-scatter fusion | flops 622593 | bytes 3047936
  598.0 50.6 %reduce-scatter.80.cloned.1.call-done = f32[512,768]{1,0:T(8,128)} async-done(((f32[2048,768]{1,0:T(8,128)}), f32[512,768]{1,0:T(8,128)}) %reduce-scatter.80.cloned.1.call-update) | async-done | bytes 1572880 | tf_op jit(solution)/shard_map/reduce_scatter | solution.py:209
  674.4 28.3 %fusion.3 = f32[152,1024]{1,0:T(8,128)} fusion(f32[592,1024]{1,0:T(8,128)} %convolution_bitcast_fusion.4), kind=kCustom, calls=%all-reduce-scatter.3 | all-reduce-scatter fusion | flops 622593 | bytes 3047936
  741.9 40.9 %fusion.4 = f32[152,1024]{1,0:T(8,128)} fusion(f32[592,1024]{1,0:T(8,128)} %fusion.132), kind=kCustom, calls=%all-reduce-scatter.4 | all-reduce-scatter fusion | flops 622593 | bytes 3047936
  990.9 28.3 %reduce-scatter.110.cloned.1.call-done = f32[1,384,2,256]{1,3,2,0:T(8,128)} async-done(((f32[1,768,2,256]{1,3,2,0:T(8,128)}), f32[1,384,2,256]{1,3,2,0:T(8,128)}) %reduce-scatter.110.cloned.1.call-update) | async-done | bytes 786448 | tf_op jit(solution)/shard_map/reduce_scatter | solution.py:510
  1021.3 34.8 %reduce-scatter.100.cloned.1.call-done = f32[1,768,384]{2,1,0:T(8,128)} async-done(((f32[1,768,768]{2,1,0:T(8,128)}), f32[1,768,384]{2,1,0:T(8,128)}) %reduce-scatter.100.cloned.1.call-update) | async-done | bytes 1179664 | tf_op jit(solution)/shard_map/reduce_scatter | solution.py:504
  1097.5 32.1 %reduce-scatter.90.cloned.1.call-done = f32[1,512,2,256]{1,3,2,0:T(8,128)} async-done(((f32[1,1024,2,256]{1,3,2,0:T(8,128)}), f32[1,512,2,256]{1,3,2,0:T(8,128)}) %reduce-scatter.90.cloned.1.call-update) | async-done | bytes 1048592 | tf_op jit(solution)/shard_map/reduce_scatter | solution.py:501
  1152.2 22.5 %reduce-scatter.116.cloned.1.call-done = f32[1,512,256]{2,1,0:T(8,128)} async-done(((f32[1,1024,256]{2,1,0:T(8,128)}), f32[1,512,256]{2,1,0:T(8,128)}) %reduce-scatter.116.cloned.1.call-update) | async-done | bytes 524304 | tf_op jit(solution)/shard_map/reduce_scatter | solution.py:512
  1174.8 22.6 %reduce-scatter.120.cloned.1.call-done = f32[1,256,512]{2,1,0:T(8,128)} async-done(((f32[1,256,1024]{2,1,0:T(8,128)}), f32[1,256,512]{2,1,0:T(8,128)}) %reduce-scatter.120.cloned.1.call-update) | async-done | bytes 524304 | tf_op jit(solution)/shard_map/reduce_scatter | solution.py:513
  1197.5 22.4 %reduce-scatter.112.cloned.1.call-done = f32[1,256,512]{2,1,0:T(8,128)} async-done(((f32[1,256,1024]{2,1,0:T(8,128)}), f32[1,256,512]{2,1,0:T(8,128)}) %reduce-scatter.112.cloned.1.call-update) | async-done | bytes 524304 | tf_op jit(solution)/shard_map/reduce_scatter | solution.py:511
  1219.9 45.6 %reduce-scatter.124.cloned.1.call-done = f32[1,512,3,256]{3,1,2,0:T(8,128)} async-done(((f32[1,1024,3,256]{3,1,2,0:T(8,128)}), f32[1,512,3,256]{3,1,2,0:T(8,128)}) %reduce-scatter.124.cloned.1.call-update) | async-done | bytes 1572880 | tf_op jit(solution)/shard_map/reduce_scatter | solution.py:514
  1268.8 57.8 %reduce-scatter.86.cloned.1.call-done = f32[512,768]{1,0:T(8,128)} async-done(((f32[2048,768]{1,0:T(8,128)}), f32[512,768]{1,0:T(8,128)}) %reduce-scatter.86.cloned.1.call-update) | async-done | bytes 1572880 | tf_op jit(solution)/shard_map/reduce_scatter | solution.py:431
  1328.0 60.7 %reduce-scatter.96.cloned.1.call-done = f32[1,384,768]{2,1,0:T(8,128)} async-done(((f32[1,768,768]{2,1,0:T(8,128)}), f32[1,384,768]{2,1,0:T(8,128)}) %reduce-scatter.96.cloned.1.call-update) | async-done | bytes 1179664 | tf_op jit(solution)/shard_map/reduce_scatter | solution.py:503
  1391.0 46.3 %fusion.207 = (f32[152,1024]{1,0:T(8,128)S(1)}, f32[152,1024]{1,0:T(8,128)S(1)}) fusion(f32[592,1024]{1,0:T(8,128)} %convolution_bitcast_fusion.3, f32[592,1024]{1,0:T(8,128)} %fusion.139), kind=kCustom, calls=%all-reduce-scatter.7 | all-reduce-scatter fusion | flops 1245185 | bytes 6095360
  1475.6 25.1 %reduce-scatter.132.cloned.1.call-done = f32[96,576]{1,0:T(8,128)} async-done(((f32[384,576]{1,0:T(8,128)}), f32[96,576]{1,0:T(8,128)}) %reduce-scatter.132.cloned.1.call-update) | async-done | bytes 221200
  1553.8 97.2 %all-reduce.23.cloned.1.call-done = (f32[1,384,256]{2,0,1:T(1,128)}, f32[1,256,384]{1,0,2:T(1,128)}, f32[1,768,384]{1,0,2:T(1,128)}, f32[1,384,2,256]{3,2,0,1:T(2,128)}) async-done(((f32[1,384,256]{2,0,1:T(1,128)}, f32[1,256,384]{1,0,2:T(1,128)}, f32[1,768,384]{1,0,2:T(1,128)}, f32[1,384,2,256]{3,2,0,1:T(2,128)}), (f32[1,384,256]{2,0,1:T(1,128)}, f32[1,256,384]{1,0,2:T(1,128)}, f32[1,768,384]{1,0,2:T(1,128)}, ...) | async-done | bytes 2752528
  1657.5 21.8 %reduce-scatter.92.cloned.1.call-done = f32[1,128,2,256]{1,3,2,0:T(8,128)} async-done(((f32[1,512,2,256]{1,3,2,0:T(8,128)}), f32[1,128,2,256]{1,3,2,0:T(8,128)}) %reduce-scatter.92.cloned.1.call-update) | async-done | bytes 262160 | tf_op jit(solution)/shard_map/reduce_scatter | solution.py:521
  1681.1 57.8 %reduce-scatter.84.cloned.1.call-done = f32[512,768]{1,0:T(8,128)} async-done(((f32[2048,768]{1,0:T(8,128)}), f32[512,768]{1,0:T(8,128)}) %reduce-scatter.84.cloned.1.call-update) | async-done | bytes 1572880 | tf_op jit(solution)/shard_map/reduce_scatter | solution.py:428
  1742.2 21.1 %reduce-scatter.130.cloned.1.call-done = f32[1,256,128]{2,1,0:T(8,128)} async-done(((f32[1,256,512]{2,1,0:T(8,128)}), f32[1,256,128]{2,1,0:T(8,128)}) %reduce-scatter.130.cloned.1.call-update) | async-done | bytes 131088 | tf_op jit(solution)/shard_map/reduce_scatter | solution.py:535
  1763.3 22.6 %reduce-scatter.118.cloned.1.call-done = f32[1,128,256]{2,1,0:T(8,128)} async-done(((f32[1,512,256]{2,1,0:T(8,128)}), f32[1,128,256]{2,1,0:T(8,128)}) %reduce-scatter.118.cloned.1.call-update) | async-done | bytes 131088 | tf_op jit(solution)/shard_map/reduce_scatter | solution.py:532
  1785.9 22.7 %reduce-scatter.122.cloned.1.call-done = f32[1,256,128]{2,1,0:T(8,128)} async-done(((f32[1,256,512]{2,1,0:T(8,128)}), f32[1,256,128]{2,1,0:T(8,128)}) %reduce-scatter.122.cloned.1.call-update) | async-done | bytes 131088 | tf_op jit(solution)/shard_map/reduce_scatter | solution.py:533
  1808.6 22.8 %reduce-scatter.114.cloned.1.call-done = f32[1,256,128]{2,1,0:T(8,128)} async-done(((f32[1,256,512]{2,1,0:T(8,128)}), f32[1,256,128]{2,1,0:T(8,128)}) %reduce-scatter.114.cloned.1.call-update) | async-done | bytes 131088 | tf_op jit(solution)/shard_map/reduce_scatter | solution.py:531
  1831.4 36.4 %reduce-scatter.126.cloned.1.call-done = f32[1,128,3,256]{3,1,2,0:T(8,128)} async-done(((f32[1,512,3,256]{3,1,2,0:T(8,128)}), f32[1,128,3,256]{3,1,2,0:T(8,128)}) %reduce-scatter.126.cloned.1.call-update) | async-done | bytes 393232 | tf_op jit(solution)/shard_map/reduce_scatter | solution.py:534
  1867.7 31.1 %reduce-scatter.98.cloned.1.call-done = f32[1,96,768]{2,1,0:T(8,128)} async-done(((f32[1,384,768]{2,1,0:T(8,128)}), f32[1,96,768]{2,1,0:T(8,128)}) %reduce-scatter.98.cloned.1.call-update) | async-done | bytes 294928 | tf_op jit(solution)/shard_map/reduce_scatter | solution.py:523
  (720 shorter events, 675.3 us)
Async XLA Ops:
  137.5 183.5 %reduce-scatter.76.cloned.1.call-start = ((), (), s32[]{:S(2)}) async-start(), calls=%async_computation.42 | async-start | bytes 7864320 | tf_op jit(solution)/shard_map/reduce_scatter | solution.py:188
  190.9 150.6 %all-gather.33.cloned.1.call-start = ((), (), s32[]{:S(2)}) async-start(), calls=%async_computation.75 | async-start | bytes 1556480 | tf_op jit(solution)/shard_map/all_gather | solution.py:196
  416.2 135.2 %all-gather.25.cloned.1.call-start = ((), (), s32[]{:S(2)}) async-start(), calls=%async_computation.45 | async-start | bytes 3932160 | tf_op jit(solution)/shard_map/all_gather | solution.py:202
  870.9 148.3 %reduce-scatter.110.cloned.1.call-start = ((), (), s32[]{:S(2)}) async-start(), calls=%async_computation.63 | async-start | bytes 2359296 | tf_op jit(solution)/shard_map/reduce_scatter | solution.py:510
  876.5 179.6 %reduce-scatter.100.cloned.1.call-start = ((), (), s32[]{:S(2)}) async-start(), calls=%async_computation.58 | async-start | bytes 3538944 | tf_op jit(solution)/shard_map/reduce_scatter | solution.py:504
  883.8 191.9 %reduce-scatter.94.cloned.1.call-start = ((), (), s32[]{:S(2)}) async-start(), calls=%async_computation.55 | async-start | bytes 1179648 | tf_op jit(solution)/shard_map/reduce_scatter | solution.py:502
  888.7 206.8 %reduce-scatter.88.cloned.1.call-start = ((), (), s32[]{:S(2)}) async-start(), calls=%async_computation.52 | async-start | bytes 1179648 | tf_op jit(solution)/shard_map/reduce_scatter | solution.py:500
  900.4 229.2 %reduce-scatter.90.cloned.1.call-start = ((), (), s32[]{:S(2)}) async-start(), calls=%async_computation.53 | async-start | bytes 3145728 | tf_op jit(solution)/shard_map/reduce_scatter | solution.py:501
  908.1 244.1 %reduce-scatter.128.cloned.1.call-start = ((), (), s32[]{:S(2)}) async-start(), calls=%async_computation.72 | async-start | bytes 1572864 | tf_op jit(solution)/shard_map/reduce_scatter | solution.py:515
  909.8 265.0 %reduce-scatter.116.cloned.1.call-start = ((), (), s32[]{:S(2)}) async-start(), calls=%async_computation.66 | async-start | bytes 1572864 | tf_op jit(solution)/shard_map/reduce_scatter | solution.py:512
  912.9 284.5 %reduce-scatter.120.cloned.1.call-start = ((), (), s32[]{:S(2)}) async-start(), calls=%async_computation.68 | async-start | bytes 1572864 | tf_op jit(solution)/shard_map/reduce_scatter | solution.py:513
  914.6 305.3 %reduce-scatter.112.cloned.1.call-start = ((), (), s32[]{:S(2)}) async-start(), calls=%async_computation.64 | async-start | bytes 1572864 | tf_op jit(solution)/shard_map/reduce_scatter | solution.py:511
  917.6 348.0 %reduce-scatter.124.cloned.1.call-start = ((), (), s32[]{:S(2)}) async-start(), calls=%async_computation.70 | async-start | bytes 4718592 | tf_op jit(solution)/shard_map/reduce_scatter | solution.py:514
  922.3 404.2 %reduce-scatter.86.cloned.1.call-start = ((), (), s32[]{:S(2)}) async-start(), calls=%async_computation.51 | async-start | bytes 7864320 | tf_op jit(solution)/shard_map/reduce_scatter | solution.py:431
  929.6 459.1 %reduce-scatter.96.cloned.1.call-start = ((), (), s32[]{:S(2)}) async-start(), calls=%async_computation.56 | async-start | bytes 3538944 | tf_op jit(solution)/shard_map/reduce_scatter | solution.py:503
  936.5 507.0 %reduce-scatter.150.cloned.1.call-start = ((), (), s32[]{:S(2)}) async-start(), calls=%async_computation.89 | async-start | bytes 327680
  937.1 507.6 %reduce-scatter.148.cloned.1.call-start = ((), (), s32[]{:S(2)}) async-start(), calls=%async_computation.88 | async-start | bytes 327680
  937.9 514.9 %reduce-scatter.108.cloned.1.call-start = ((), (), s32[]{:S(2)}) async-start(), calls=%async_computation.62 | async-start | bytes 655360 | tf_op jit(solution)/shard_map/reduce_scatter | solution.py:529
  938.4 535.5 %reduce-scatter.134.cloned.1.call-start = ((), (), s32[]{:S(2)}) async-start(), calls=%async_computation.81 | async-start | bytes 491520
  940.7 560.0 %reduce-scatter.132.cloned.1.call-start = ((), (), s32[]{:S(2)}) async-start(), calls=%async_computation.80 | async-start | bytes 1228800
  963.1 557.9 %reduce-scatter.146.cloned.1.call-start = ((), (), s32[]{:S(2)}) async-start(), calls=%async_computation.87 | async-start | bytes 245760
  974.9 565.9 %reduce-scatter.144.cloned.1.call-start = ((), (), s32[]{:S(2)}) async-start(), calls=%async_computation.86 | async-start | bytes 245760
  990.8 660.2 %all-reduce.23.cloned.1.call-start = ((), (), s32[]{:S(2)}) async-start(), calls=%async_computation.90 | async-start | bytes 5505024
  1097.5 581.9 %reduce-scatter.92.cloned.1.call-start = ((), (), s32[]{:S(2)}) async-start(), calls=%async_computation.54 | async-start | bytes 1310720 | tf_op jit(solution)/shard_map/reduce_scatter | solution.py:521
  1129.7 609.3 %reduce-scatter.84.cloned.1.call-start = ((), (), s32[]{:S(2)}) async-start(), calls=%async_computation.50 | async-start | bytes 7864320 | tf_op jit(solution)/shard_map/reduce_scatter | solution.py:428
  1133.5 629.8 %reduce-scatter.130.cloned.1.call-start = ((), (), s32[]{:S(2)}) async-start(), calls=%async_computation.73 | async-start | bytes 655360 | tf_op jit(solution)/shard_map/reduce_scatter | solution.py:535
  1152.2 633.7 %reduce-scatter.118.cloned.1.call-start = ((), (), s32[]{:S(2)}) async-start(), calls=%async_computation.67 | async-start | bytes 655360 | tf_op jit(solution)/shard_map/reduce_scatter | solution.py:532
  1174.8 633.8 %reduce-scatter.122.cloned.1.call-start = ((), (), s32[]{:S(2)}) async-start(), calls=%async_computation.69 | async-start | bytes 655360 | tf_op jit(solution)/shard_map/reduce_scatter | solution.py:533
  1197.4 633.9 %reduce-scatter.114.cloned.1.call-start = ((), (), s32[]{:S(2)}) async-start(), calls=%async_computation.65 | async-start | bytes 655360 | tf_op jit(solution)/shard_map/reduce_scatter | solution.py:531
  1219.9 647.9 %reduce-scatter.126.cloned.1.call-start = ((), (), s32[]{:S(2)}) async-start(), calls=%async_computation.71 | async-start | bytes 1966080 | tf_op jit(solution)/shard_map/reduce_scatter | solution.py:534
  1265.6 633.2 %reduce-scatter.98.cloned.1.call-start = ((), (), s32[]{:S(2)}) async-start(), calls=%async_computation.57 | async-start | bytes 1474560 | tf_op jit(solution)/shard_map/reduce_scatter | solution.py:523
  1326.5 354.6 %collective-permute-start.3 = (f32[512,768]{1,0:T(8,128)}, f32[512,768]{1,0:T(8,128)}, u32[]{:S(2)}, u32[]{:S(2)}) collective-permute-start(f32[512,768]{1,0:T(8,128)} %reduce-scatter.86.cloned.1.call-done), channel_id=1, source_target_pairs={{0,16},{16,0},{1,17},{17,1},{2,18},{18,2},{3,19},{19,3},{4,20},{20... | collective-permute-start | bytes 4718600 | tf_op jit(solution)/shard_map/ppermute | solution.py:24
  (176 other events, 6633.7 us)
Sparse Core Ops, SparseCore 0:
  9.6 20.5 all-gather.30
  31.7 28.5 all-gather.18
  75.7 58.3 reduce-scatter.73
  137.6 28.5 all-gather.20
  191.0 58.3 reduce-scatter.75
  321.1 20.4 all-gather.32
  343.7 42.4 all-gather.22
  401.5 21.2 all-gather.34
  425.3 58.3 reduce-scatter.77
  492.0 43.1 all-gather.24
  551.5 22.1 all-gather.36
  586.0 62.5 reduce-scatter.79
  654.9 30.3 all-gather.26
  713.3 21.2 all-gather.38
  737.0 66.1 reduce-scatter.81
  826.6 28.5 all-gather.28
  931.2 28.2 reduce-scatter.101
  993.1 26.0 reduce-scatter.109
  1021.4 34.6 reduce-scatter.99
  1097.7 31.8 reduce-scatter.89
  1131.8 20.3 reduce-scatter.127
  1199.5 20.3 reduce-scatter.111
  1222.2 43.3 reduce-scatter.123
  1268.1 58.3 reduce-scatter.85
  1328.7 59.8 reduce-scatter.95
  1476.3 24.3 reduce-scatter.131
  1543.5 107.5 all-reduce.22
  1653.2 26.0 reduce-scatter.91
  1681.9 57.0 reduce-scatter.83
  1741.6 21.6 reduce-scatter.129
  1834.1 33.5 reduce-scatter.125
  1870.6 28.1 reduce-scatter.97
  (20 shorter events, 356.5 us)
where the time goes:
time: 1920 us; the launch traced here: 1910 us
  waiting for transfers between devices  1190 us (62%)
  blocking collectives  233 us (12%)
  matrix products  203 us (11%)
  local copies, waits for them, and re-layouts  182 us (9%)
  other arithmetic  54.1 us (3%)
  starting transfers between devices  22.9 us (1%)
    unnamed x6, blocking collectives  226 us
    unnamed x70, waiting for transfers between devices  212 us
    unnamed x355, local copies, waits for them, and re-layouts  116 us
    reduce_scatter x3, waiting for transfers between devices, branch_sums(): lax.psum_scatter(text_part, 'tensor', scatter_dimension=0, tiled=True)  104 us
    ppermute x5, waiting for transfers between devices, partner(): return lax.ppermute(value, axis, pairs)  95.3 us
    reduce_scatter x1, waiting for transfers between devices, local(): lax.psum_scatter(part_tup, 'stream', scatter_dimension=1, tiled=True)  60.7 us
    reduce_scatter x2, waiting for transfers between devices, grad_rows(): lax.psum_scatter(text_part, 'tensor', scatter_dimension=0, tiled=True)  58.7 us
    reduce_scatter x1, waiting for transfers between devices, local(): lax.psum_scatter(text_cb[0], 'tensor', scatter_dimension=0, tiled=True)  57.8 us
  transfers between devices with their start and end apart: 64, of which 46 were waited for; matrix products, arithmetic and copies ran while one was open for 31% of the time, Pallas kernels for 0%

commit v1 on v0

v1 whole, which is shorter than its diff:
```python
import functools

import jax
import jax.numpy as jnp
from jax import lax
from jax.experimental import pallas as pl
from jax.experimental.pallas import tpu as pltpu
from jax.sharding import PartitionSpec as P

DT = 768
DV = 1024
HEAD = 128
SELF_HEAD = 64
SLOTS = 128
REGIONS = 37
PADDED = 48
QUARTERS = 4
BLOCK = 256

norm_eps = 1e-05
masked_score = -1e30

BF = jnp.bfloat16
F32 = jnp.float32
FORWARD = (0, 1, 2, 3)
BACKWARD = (1, 3, 0, 2)


def nn(left, right):
    return lax.dot_general(left, right, (((1,), (0,)), ((), ())), preferred_element_type=F32)


def nt(left, right):
    return lax.dot_general(left, right, (((1,), (1,)), ((), ())), preferred_element_type=F32)


def tn(left, right):
    return lax.dot_general(left, right, (((0,), (0,)), ((), ())), preferred_element_type=F32)


def low(value):
    return value.astype(BF)


def normed(inputs):
    centered = inputs - jnp.mean(inputs, axis=-1, keepdims=True)
    scale = lax.rsqrt(jnp.mean(centered * centered, axis=-1, keepdims=True) + norm_eps)
    return centered * scale, scale


def layer_norm(inputs, affine):
    return normed(inputs)[0] * affine[0:1] + affine[1:2]


def norm_back(inputs, affine, grad):
    unit, scale = normed(inputs)
    gain_grad = jnp.sum(grad * unit, axis=0, keepdims=True)
    bias_grad = jnp.sum(grad, axis=0, keepdims=True)
    inner = grad * affine[0:1]
    shift = jnp.mean(inner, axis=-1, keepdims=True)
    slope = jnp.mean(inner * unit, axis=-1, keepdims=True)
    return scale * (inner - shift - unit * slope), gain_grad, bias_grad


def softmax_all(scores):
    tops = [jnp.max(s, axis=-1, keepdims=True) for s in scores]
    powers = [jnp.exp(s - t) for s, t in zip(scores, tops)]
    sums = [jnp.sum(e, axis=-1, keepdims=True) for e in powers]
    return [low(e / total) for e, total in zip(powers, sums)]


def attend(queries, keys, values, scale, masks):
    scores = [nt(q, k) * scale for q, k in zip(queries, keys)]
    scores = [s if m is None else jnp.where(m, s, masked_score) for s, m in zip(scores, masks)]
    probs = softmax_all(scores)
    return probs, [nn(p, v) for p, v in zip(probs, values)]


def attend_back(queries, keys, values, probs, grads, scale):
    grad_probs = [nt(g, v) for g, v in zip(grads, values)]
    grad_values = [low(tn(p, g)) for p, g in zip(probs, grads)]
    wide = [p.astype(F32) for p in probs]
    inner = [jnp.sum(p * g, axis=-1, keepdims=True) for p, g in zip(wide, grad_probs)]
    grad_scores = [low(p * (g - i)) for p, g, i in zip(wide, grad_probs, inner)]
    grad_queries = [low(nn(g, k) * scale) for g, k in zip(grad_scores, keys)]
    grad_keys = [low(tn(g, q) * scale) for g, q in zip(grad_scores, queries)]
    return grad_queries, grad_keys, grad_values


def side(ref, row, width, count):
    return jnp.concatenate([ref[row + b * width : row + (b + 1) * width, :] for b in range(count)], axis=1)


def fetch(step, order, parts, buffer, sems):
    copies = [
        (order.index(quarter), pltpu.make_async_copy(ref, buffer.at[order.index(quarter), pl.ds(row, ref.shape[0])], sems.at[i]))
        for i, (quarter, row, ref) in enumerate(parts)
    ]
    copies.sort(key=lambda entry: entry[0])

    @pl.when(step == 0)
    def begin():
        for unused, copy in copies:
            copy.start()

    for at in range(QUARTERS):

        @pl.when(step == at)
        def arrive():
            for slot, copy in copies:
                if slot == at:
                    copy.wait()


def store_grad(step, buffer, send, keep, sems):
    copies = [
        pltpu.make_async_copy(buffer.at[at], (send if at < 2 else keep).at[at % 2], sems.at[at]) for at in range(QUARTERS)
    ]
    for at in range(QUARTERS):

        @pl.when(step == at)
        def leave():
            copies[at].start()

    @pl.when(step == QUARTERS - 1)
    def finish():
        for copy in copies:
            copy.wait()


def put(buffer, step, x_at, first, value, depth, padded):
    dp = buffer.shape[2]
    for half in range(2):
        place = lax.bitwise_xor(x_at, half)
        for z in range(dp):
            start = (half * dp + z) * depth
            for b in range(value.shape[1] // BLOCK):
                buffer[step, place, z, pl.ds(first + b * padded, depth), :] = low(
                    value[start : start + depth, b * BLOCK : (b + 1) * BLOCK]
                )


def flip(ref, scratch):
    scratch[...] = ref.T


CROSS_ROWS = 7168
MLP_ROWS = 6656
SELF_ROWS = 6400


def rows_of(pair, size):
    return slice(pair * size, (pair + 1) * size)


def cross_forward(pairs, lens, text, image, text_affine, image_affine, *refs):
    parts, (text_pre, text_one, image_pre, image_one, text_kept, image_kept, text_probs, image_probs), scratch = (
        refs[:6],
        refs[6:14],
        refs[14:],
    )
    weights, text_sum, image_sum, sems = scratch
    step = pl.program_id(0)
    fetch(step, FORWARD, gathered(parts), weights, sems)

    @pl.when(step == 0)
    def begin():
        text_sum[...] = text[...].astype(F32)
        image_sum[...] = image[...].astype(F32)

    w = weights.at[step]
    text_low = text[...]
    image_low = image[...]
    text_kept[0, :, 0:256] = low(nn(text_low, w[0:768, :]))
    text_kept[0, :, 256:512] = low(nn(text_low, w[768:1536, :]))
    text_kept[0, :, 512:768] = low(nn(text_low, w[1536:2304, :]))
    image_kept[0, :, 0:256] = low(nn(image_low, w[2304:3328, :]))
    image_kept[0, :, 256:512] = low(nn(image_low, w[3328:4352, :]))
    image_kept[0, :, 512:768] = low(nn(image_low, w[4352:5376, :]))

    image_mask = lax.broadcasted_iota(jnp.int32, (SLOTS, PADDED), 1) < REGIONS
    slots = lax.broadcasted_iota(jnp.int32, (PADDED, SLOTS), 1)
    units = [(p, h) for p in range(pairs) for h in range(2)]

    def text_part(at):
        return [text_kept[0, rows_of(p, SLOTS), at + h * HEAD : at + (h + 1) * HEAD] for p, h in units]

    def image_part(at):
        return [image_kept[0, rows_of(p, PADDED), at + h * HEAD : at + (h + 1) * HEAD] for p, h in units]

    scale = HEAD**-0.5
    probs, context = attend(text_part(0), image_part(0), image_part(256), scale, [image_mask] * len(units))
    for i, (p, h) in enumerate(units):
        text_probs[0, i] = probs[i]
        text_kept[0, rows_of(p, SLOTS), 768 + h * HEAD : 768 + (h + 1) * HEAD] = low(context[i])
    masks = [slots < lens[p] for p, h in units]
    probs, context = attend(image_part(512), text_part(256), text_part(512), scale, masks)
    for i, (p, h) in enumerate(units):
        image_probs[0, i] = probs[i]
        image_kept[0, rows_of(p, PADDED), 768 + h * HEAD : 768 + (h + 1) * HEAD] = low(context[i])

    text_sum[...] += nn(text_kept[0, :, 768:1024], side(w, 5376, 256, 3))
    image_sum[...] += nn(image_kept[0, :, 768:1024], side(w, 6144, 256, 4))

    @pl.when(step == QUARTERS - 1)
    def finish():
        text_pre[...] = text_sum[...]
        text_one[...] = layer_norm(text_sum[...], text_affine)
        image_pre[...] = image_sum[...]
        image_one[...] = layer_norm(image_sum[...], image_affine)


def gate(hidden):
    half = 0.5 * (1.0 + lax.erf(hidden * (2.0**-0.5)))
    density = jnp.exp(-0.5 * hidden * hidden) * 0.3989422804014327
    return hidden * half, half + hidden * density


def mlp_forward(pairs, text, image, text_affine, image_affine, *refs):
    parts, (text_pre, text_two, image_pre, image_two, text_activ, text_slope, image_activ, image_slope), scratch = (
        refs[:6],
        refs[6:14],
        refs[14:],
    )
    weights, text_sum, image_sum, text_low, image_low, sems = scratch
    step = pl.program_id(0)
    fetch(step, FORWARD, gathered(parts), weights, sems)

    @pl.when(step == 0)
    def begin():
        text_sum[...] = text[...]
        image_sum[...] = image[...]
        text_low[...] = low(text[...])
        image_low[...] = low(image[...])

    w = weights.at[step]
    for b in range(3):
        activ, slope = gate(nn(text_low[...], w[b * 768 : (b + 1) * 768, :]))
        text_activ[0, :, b * 256 : (b + 1) * 256] = low(activ)
        text_slope[0, :, b * 256 : (b + 1) * 256] = low(slope)
    activ, slope = gate(nn(image_low[...], w[4608:5632, :]))
    image_activ[0] = low(activ)
    image_slope[0] = low(slope)
    text_sum[...] += nn(text_activ[0], side(w, 2304, 768, 3))
    image_sum[...] += nn(image_activ[0], side(w, 5632, 256, 4))

    @pl.when(step == QUARTERS - 1)
    def finish():
        text_pre[...] = text_sum[...]
        text_two[...] = layer_norm(text_sum[...], text_affine)
        image_pre[...] = image_sum[...]
        image_two[...] = layer_norm(image_sum[...], image_affine)


def lane_masks():
    lane = lax.broadcasted_iota(jnp.int32, (1, 2 * SELF_HEAD), 1)
    left = (lane < SELF_HEAD).astype(F32)
    return low(left), low(1.0 - left), lane < SELF_HEAD


def both_heads(tile, masks):
    return jnp.concatenate([tile * masks[0], tile * masks[1]], axis=0)


def one_tile(stacked, masks):
    return jnp.where(masks[2], stacked[:SLOTS], stacked[SLOTS:])


def self_forward(pairs, lens, text, image, text_affine, image_affine, text_cot, image_cot, *refs):
    parts = refs[:6]
    (
        text_out,
        image_out,
        text_grad,
        image_grad,
        text_vec,
        image_vec,
        text_q,
        text_k,
        text_v,
        text_c,
        text_probs,
        image_kept,
        image_probs,
    ) = refs[6:19]
    weights, text_sum, image_sum, text_low, image_low, sems = refs[19:]
    step = pl.program_id(0)
    fetch(step, FORWARD, gathered(parts), weights, sems)

    @pl.when(step == 0)
    def begin():
        text_sum[...] = text[...]
        image_sum[...] = image[...]
        text_low[...] = low(text[...])
        image_low[...] = low(image[...])

    w = weights.at[step]
    for n, out in enumerate((text_q, text_k, text_v)):
        wide = jnp.concatenate([w[b * 576 + n * 192 : b * 576 + (n + 1) * 192, :] for b in range(3)], axis=1)
        out[0] = low(nt(text_low[...], wide))
    for n in range(3):
        image_kept[0, :, n * 256 : (n + 1) * 256] = low(nn(image_low[...], w[2304 + n * 1024 : 3328 + n * 1024, :]))

    masks = lane_masks()
    slots = lax.broadcasted_iota(jnp.int32, (1, SLOTS), 1)
    valid = [slots < lens[p] for p in range(pairs)]
    first, last = slice(0, 128), slice(128, 192)
    queries, keys, values, limits = [], [], [], []
    for p in range(pairs):
        rows = rows_of(p, SLOTS)
        queries += [both_heads(text_q[0, rows, first], masks), text_q[0, rows, last]]
        keys += [text_k[0, rows, first], text_k[0, rows, last]]
        values += [text_v[0, rows, first], text_v[0, rows, last]]
        limits += [valid[p], valid[p]]
    probs, context = attend(queries, keys, values, SELF_HEAD**-0.5, limits)
    for p in range(pairs):
        rows = rows_of(p, SLOTS)
        text_probs[0, p, 0:256, :] = probs[2 * p]
        text_probs[0, p, 256:384, :] = probs[2 * p + 1]
        text_c[0, rows, first] = low(one_tile(context[2 * p], masks))
        text_c[0, rows, last] = low(context[2 * p + 1])

    image_mask = lax.broadcasted_iota(jnp.int32, (PADDED, PADDED), 1) < REGIONS
    units = [(p, h) for p in range(pairs) for h in range(2)]

    def image_part(at):
        return [image_kept[0, rows_of(p, PADDED), at + h * HEAD : at + (h + 1) * HEAD] for p, h in units]

    probs, context = attend(image_part(0), image_part(256), image_part(512), HEAD**-0.5, [image_mask] * len(units))
    for i, (p, h) in enumerate(units):
        image_probs[0, i] = probs[i]
        image_kept[0, rows_of(p, PADDED), 768 + h * HEAD : 768 + (h + 1) * HEAD] = low(context[i])

    text_sum[...] += nn(text_c[0], side(w, 1728, 192, 3))
    image_sum[...] += nn(image_kept[0, :, 768:1024], side(w, 5376, 256, 4))

    @pl.when(step == QUARTERS - 1)
    def finish():
        for total, affine, cot, out, grad, vec in (
            (text_sum, text_affine, text_cot, text_out, text_grad, text_vec),
            (image_sum, image_affine, image_cot, image_out, image_grad, image_vec),
        ):
            out[...] = layer_norm(total[...], affine).astype(out.dtype)
            back, gain_grad, bias_grad = norm_back(total[...], affine, cot[...].astype(F32))
            grad[...] = back
            vec[0:1] = gain_grad
            vec[1:2] = bias_grad


def self_back(pairs, x_at, text_g, image_g, text_two, image_two, text_pre, image_pre, text_affine, image_affine, *refs):
    text_q, text_k, text_v, text_c, text_probs, image_kept, image_probs = refs[:7]
    parts = refs[7:13]
    text_n, image_n, text_vec, image_vec, send, keep = refs[13:19]
    (
        weights,
        grads,
        text_sum,
        image_sum,
        text_g_low,
        image_g_low,
        text_g_flip,
        image_g_flip,
        text_flip,
        image_flip,
        text_d,
        image_d,
        sems,
        out_sems,
    ) = refs[19:]
    step = pl.program_id(0)
    fetch(step, BACKWARD, gathered(parts), weights, sems)

    @pl.when(step == 0)
    def begin():
        text_sum[...] = text_g[...]
        image_sum[...] = image_g[...]
        text_g_low[...] = low(text_g[...])
        image_g_low[...] = low(image_g[...])
        text_g_flip[...] = text_g_low[...].T
        image_g_flip[...] = image_g_low[...].T
        text_flip[...] = low(text_two[...]).T
        image_flip[...] = low(image_two[...]).T

    w = weights.at[step]
    x = x_at[0]
    masks = lane_masks()
    first, last = slice(0, 128), slice(128, 192)
    text_dc = low(nt(text_g_low[...], side(w, 1728, 192, 3)))
    queries, keys, values, probs, outer = [], [], [], [], []
    for p in range(pairs):
        rows = rows_of(p, SLOTS)
        queries += [both_heads(text_q[0, rows, first], masks), text_q[0, rows, last]]
        keys += [text_k[0, rows, first], text_k[0, rows, last]]
        values += [text_v[0, rows, first], text_v[0, rows, last]]
        probs += [text_probs[0, p, 0:256, :], text_probs[0, p, 256:384, :]]
        outer += [both_heads(text_dc[rows, first], masks), text_dc[rows, last]]
    grad_q, grad_k, grad_v = attend_back(queries, keys, values, probs, outer, SELF_HEAD**-0.5)
    for p in range(pairs):
        rows = rows_of(p, SLOTS)
        text_d[0, rows, first] = one_tile(grad_q[2 * p], masks)
        text_d[0, rows, last] = grad_q[2 * p + 1]
        for n, grad in ((1, grad_k), (2, grad_v)):
            text_d[n, rows, first] = grad[2 * p]
            text_d[n, rows, last] = grad[2 * p + 1]

    image_dc = low(nt(image_g_low[...], side(w, 5376, 256, 4)))
    units = [(p, h) for p in range(pairs) for h in range(2)]

    def image_part(at):
        return [image_kept[0, rows_of(p, PADDED), at + h * HEAD : at + (h + 1) * HEAD] for p, h in units]

    outer = [image_dc[rows_of(p, PADDED), h * HEAD : (h + 1) * HEAD] for p, h in units]
    found = attend_back(
        image_part(0), image_part(256), image_part(512), [image_probs[0, i] for i in range(len(units))], outer, HEAD**-0.5
    )
    for n in range(3):
        for i, (p, h) in enumerate(units):
            image_d[rows_of(p, PADDED), n * 256 + h * HEAD : n * 256 + (h + 1) * HEAD] = found[n][i]

    gained = text_sum[...]
    for n in range(3):
        wide = jnp.concatenate([w[b * 576 + n * 192 : b * 576 + (n + 1) * 192, :] for b in range(3)], axis=1)
        gained = gained + nn(text_d[n], wide)
    text_sum[...] = gained
    image_sum[...] += nt(image_d[...], side(w, 2304, 1024, 3))

    text_depth, image_depth, text_padded = depths(grads)
    text_w = jnp.concatenate(
        [nn(text_flip[...], text_d[n]) for n in range(3)] + [nn(text_g_flip[...], text_c[0])], axis=1
    )
    put(grads, step, x, 0, text_w, text_depth, text_padded)
    put(grads, step, x, 3 * text_padded, nn(image_flip[...], image_d[...]), image_depth, image_depth)
    put(
        grads,
        step,
        x,
        3 * text_padded + 3 * image_depth,
        nn(image_g_flip[...], image_kept[0, :, 768:1024]),
        image_depth,
        image_depth,
    )
    store_grad(step, grads, send, keep, out_sems)
    leave_norm(step, text_sum, image_sum, text_pre, image_pre, text_affine, image_affine, text_n, image_n, text_vec, image_vec)


def leave_norm(step, text_sum, image_sum, text_pre, image_pre, text_affine, image_affine, text_n, image_n, text_vec, image_vec):
    @pl.when(step == QUARTERS - 1)
    def finish():
        for total, pre, affine, out, vec in (
            (text_sum, text_pre, text_affine, text_n, text_vec),
            (image_sum, image_pre, image_affine, image_n, image_vec),
        ):
            back, gain_grad, bias_grad = norm_back(pre[...], affine, total[...])
            out[...] = back
            vec[0:1] = gain_grad
            vec[1:2] = bias_grad


def depths(grads):
    places = 2 * grads.shape[2]
    text_depth = DT // places
    return text_depth, DV // places, -(-text_depth // 16) * 16


def mlp_back(pairs, x_at, text_g, image_g, text_one, image_one, text_pre, image_pre, text_affine, image_affine, *refs):
    text_activ, text_slope, image_activ, image_slope = refs[:4]
    parts = refs[4:10]
    text_n, image_n, text_vec, image_vec, send, keep = refs[10:16]
    (
        weights,
        grads,
        text_sum,
        image_sum,
        text_g_low,
        image_g_low,
        text_g_flip,
        image_g_flip,
        text_flip,
        image_flip,
        text_d,
        sems,
        out_sems,
    ) = refs[16:]
    step = pl.program_id(0)
    fetch(step, BACKWARD, gathered(parts), weights, sems)

    @pl.when(step == 0)
    def begin():
        text_sum[...] = text_g[...]
        image_sum[...] = image_g[...]
        text_g_low[...] = low(text_g[...])
        image_g_low[...] = low(image_g[...])
        text_g_flip[...] = text_g_low[...].T
        image_g_flip[...] = image_g_low[...].T
        text_flip[...] = low(text_one[...]).T
        image_flip[...] = low(image_one[...]).T

    w = weights.at[step]
    x = x_at[0]
    text_depth, image_depth, text_padded = depths(grads)
    wide = side(w, 2304, 768, 3)
    for b in range(3):
        columns = slice(b * 256, (b + 1) * 256)
        back = nt(text_g_low[...], wide[columns])
        text_d[:, columns] = low(back * text_slope[0, :, columns].astype(F32))
    text_sum[...] += nt(text_d[...], side(w, 0, 768, 3))
    put(grads, step, x, 0, nn(text_flip[...], text_d[...]), text_depth, text_padded)
    put(grads, step, x, 3 * text_padded, nn(text_g_flip[...], text_activ[0]), text_depth, text_padded)
    image_d = low(nt(image_g_low[...], side(w, 5632, 256, 4)) * image_slope[0].astype(F32))
    image_sum[...] += nt(image_d, w[4608:5632, :])
    put(grads, step, x, 6 * text_padded, nn(image_flip[...], image_d), image_depth, image_depth)
    put(grads, step, x, 6 * text_padded + image_depth, nn(image_g_flip[...], image_activ[0]), image_depth, image_depth)
    store_grad(step, grads, send, keep, out_sems)
    leave_norm(step, text_sum, image_sum, text_pre, image_pre, text_affine, image_affine, text_n, image_n, text_vec, image_vec)


def cross_back(pairs, x_at, text_g, image_g, text, image, *refs):
    text_kept, image_kept, text_probs, image_probs = refs[:4]
    parts = refs[4:10]
    text_grad, image_grad, send, keep = refs[10:14]
    (
        weights,
        grads,
        text_sum,
        image_sum,
        text_g_low,
        image_g_low,
        text_g_flip,
        image_g_flip,
        text_flip,
        image_flip,
        text_d,
        image_d,
        sems,
        out_sems,
    ) = refs[14:]
    step = pl.program_id(0)
    fetch(step, BACKWARD, gathered(parts), weights, sems)

    @pl.when(step == 0)
    def begin():
        text_sum[...] = text_g[...]
        image_sum[...] = image_g[...]
        text_g_low[...] = low(text_g[...])
        image_g_low[...] = low(image_g[...])
        text_g_flip[...] = text_g_low[...].T
        image_g_flip[...] = image_g_low[...].T
        text_flip[...] = text[...].T
        image_flip[...] = image[...].T

    w = weights.at[step]
    x = x_at[0]
    text_depth, image_depth, text_padded = depths(grads)
    text_dc = low(nt(text_g_low[...], side(w, 5376, 256, 3)))
    image_dc = low(nt(image_g_low[...], side(w, 6144, 256, 4)))
    units = [(p, h) for p in range(pairs) for h in range(2)]

    def text_part(at):
        return [text_kept[0, rows_of(p, SLOTS), at + h * HEAD : at + (h + 1) * HEAD] for p, h in units]

    def image_part(at):
        return [image_kept[0, rows_of(p, PADDED), at + h * HEAD : at + (h + 1) * HEAD] for p, h in units]

    scale = HEAD**-0.5
    outer = [text_dc[rows_of(p, SLOTS), h * HEAD : (h + 1) * HEAD] for p, h in units]
    probs = [text_probs[0, i] for i in range(len(units))]
    found = attend_back(text_part(0), image_part(0), image_part(256), probs, outer, scale)
    for i, (p, h) in enumerate(units):
        text_d[rows_of(p, SLOTS), h * HEAD : (h + 1) * HEAD] = found[0][i]
        image_d[rows_of(p, PADDED), h * HEAD : (h + 1) * HEAD] = found[1][i]
        image_d[rows_of(p, PADDED), 256 + h * HEAD : 256 + (h + 1) * HEAD] = found[2][i]
    outer = [image_dc[rows_of(p, PADDED), h * HEAD : (h + 1) * HEAD] for p, h in units]
    probs = [image_probs[0, i] for i in range(len(units))]
    found = attend_back(image_part(512), text_part(256), text_part(512), probs, outer, scale)
    for i, (p, h) in enumerate(units):
        image_d[rows_of(p, PADDED), 512 + h * HEAD : 512 + (h + 1) * HEAD] = found[0][i]
        text_d[rows_of(p, SLOTS), 256 + h * HEAD : 256 + (h + 1) * HEAD] = found[1][i]
        text_d[rows_of(p, SLOTS), 512 + h * HEAD : 512 + (h + 1) * HEAD] = found[2][i]

    text_sum[...] += nt(text_d[...], side(w, 0, 768, 3))
    image_sum[...] += nt(image_d[...], side(w, 2304, 1024, 3))
    put(grads, step, x, 0, nn(text_flip[...], text_d[...]), text_depth, text_padded)
    put(grads, step, x, 3 * text_padded, nn(text_g_flip[...], text_kept[0, :, 768:1024]), text_depth, text_padded)
    put(grads, step, x, 4 * text_padded, nn(image_flip[...], image_d[...]), image_depth, image_depth)
    put(
        grads,
        step,
        x,
        4 * text_padded + 3 * image_depth,
        nn(image_g_flip[...], image_kept[0, :, 768:1024]),
        image_depth,
        image_depth,
    )
    store_grad(step, grads, send, keep, out_sems)

    @pl.when(step == QUARTERS - 1)
    def finish():
        text_grad[...] = text_sum[...]
        image_grad[...] = image_sum[...].astype(image_grad.dtype)


def gathered(parts):
    own, near, far, far_rest, corner, corner_rest = parts
    cut = far.shape[0]
    return ((0, 0, own), (1, 0, near), (2, 0, far), (2, cut, far_rest), (3, 0, corner), (3, cut, corner_rest))


ANY = pl.BlockSpec(memory_space=pl.ANY)
SCALARS = pl.BlockSpec(memory_space=pltpu.SMEM)


def whole(array):
    zeros = (0,) * len(array.shape)
    return pl.BlockSpec(array.shape, lambda s: zeros)


def quarter(array, order):
    tail = (0,) * (len(array.shape) - 1)
    if order is FORWARD:
        return pl.BlockSpec((1,) + array.shape[1:], lambda s: (s,) + tail)
    return pl.BlockSpec((1,) + array.shape[1:], lambda s: (lax.rem(2 * s + 1 - lax.div(s, 2), 4),) + tail)


def shape(*dims, of=BF):
    return jax.ShapeDtypeStruct(dims, of)


def run(kernel, pairs, order, operands, outs, scratch, flops):
    def spec(kind, array):
        return {"s": lambda: SCALARS, "w": lambda: whole(array), "q": lambda: quarter(array, order), "a": lambda: ANY}[kind]()

    moved = sum(a.size * a.dtype.itemsize for k, a in operands + outs)
    return pl.pallas_call(
        functools.partial(kernel, pairs),
        grid=(QUARTERS,),
        in_specs=[spec(*entry) for entry in operands],
        out_specs=[spec(*entry) for entry in outs],
        out_shape=[array for unused, array in outs],
        scratch_shapes=scratch,
        compiler_params=pltpu.CompilerParams(dimension_semantics=("arbitrary",), vmem_limit_bytes=60 * 2**20),
        cost_estimate=pl.CostEstimate(flops=flops, bytes_accessed=moved, transcendentals=0),
    )(*[array for unused, array in operands])


def swap(value, axis, apart):
    return lax.ppermute(value, axis, [(i, i ^ apart) for i in range(lax.axis_size(axis))])


def spread(own, place, places, rest):
    cut = own.shape[0] - rest
    near = swap(own, "tensor", 1)
    far = swap(own[:cut], "tensor", 2)
    share = rest // places
    mine = lax.dynamic_slice_in_dim(own, cut + place * share, share, 0)
    far_rest = lax.all_gather(swap(mine, "tensor", 2), ("stream", "dp"), axis=0, tiled=True)
    return own, near, far, far_rest, swap(far, "tensor", 1), swap(far_rest, "tensor", 1)


def fold(send, keep):
    got = swap(send, "tensor", 1)
    depth = send.shape[3]
    half = depth // 32 * 16

    def both(*index):
        return low(keep[index].astype(F32) + got[index].astype(F32))

    def add(left, right):
        return low(left.astype(F32) + right.astype(F32))

    every = slice(None)
    top, bottom = slice(0, half), slice(half, depth)
    by_y = swap(both(1, every, every, top), "tensor", 2)
    by_x = swap(both(every, 1, every, bottom), "stream", 1)
    own_top = both(0, every, every, top)
    own_bottom = both(every, 0, every, bottom)
    then_x = swap(add(own_top[1], by_y[1]), "stream", 1)
    then_y = swap(add(own_bottom[1], by_x[1]), "tensor", 2)

    def three(own, first, second):
        return low(own.astype(F32) + first.astype(F32) + second.astype(F32))

    total = jnp.concatenate([three(own_top[0], by_y[0], then_x), three(own_bottom[0], by_x[0], then_y)], axis=1)
    return lax.psum_scatter(total, "dp", scatter_dimension=0, tiled=True)[0]


def stacked(*pieces):
    return jnp.concatenate(pieces, axis=0)


def column_blocks(matrix):
    return [matrix[:, b * BLOCK : (b + 1) * BLOCK] for b in range(matrix.shape[1] // BLOCK)]


def local(
    text_in,
    image_in,
    lengths,
    text_cot,
    image_cot,
    text_cross_q,
    text_cross_kv,
    text_cross_out,
    text_up,
    text_down,
    text_self_qkv,
    text_self_out,
    text_gain,
    text_bias,
    image_cross_q,
    image_cross_kv,
    image_cross_out,
    image_up,
    image_down,
    image_self_qkv,
    image_self_out,
    image_gain,
    image_bias,
):
    dp = lax.axis_size("dp")
    places = 2 * dp
    x_at = lax.axis_index("stream")
    t_at = lax.axis_index("tensor")
    place = x_at * dp + lax.axis_index("dp")
    text_rows = text_in.shape[0]
    pairs = text_rows // SLOTS
    image_rows = pairs * PADDED
    lens = lax.dynamic_slice_in_dim(lengths, t_at * pairs, pairs, 0)
    x_ref = x_at.astype(jnp.int32).reshape(1)

    def arrive(rows):
        moved = swap(rows, "stream", 1).reshape(pairs, REGIONS, DV)
        return jnp.pad(moved, ((0, 0), (0, PADDED - REGIONS), (0, 0))).reshape(image_rows, DV)

    def leave(rows):
        return swap(rows.reshape(pairs, PADDED, DV)[:, :REGIONS].reshape(pairs * REGIONS, DV), "stream", 1)

    cross_own = stacked(
        text_cross_q[0],
        image_cross_kv[0, :, 0],
        image_cross_kv[0, :, 1],
        text_cross_kv[0, :, 0],
        text_cross_kv[0, :, 1],
        image_cross_q[0],
        *column_blocks(text_cross_out[0]),
        *column_blocks(image_cross_out[0]),
    )
    mlp_own = stacked(
        *column_blocks(text_up[0]), *column_blocks(text_down[0]), image_up[0], *column_blocks(image_down[0])
    )
    self_own = stacked(
        *column_blocks(text_self_qkv[0].transpose(1, 2, 0).reshape(-1, DT)),
        *column_blocks(text_self_out[0]),
        *[image_self_qkv[0, :, n] for n in range(3)],
        *column_blocks(image_self_out[0]),
    )
    image = arrive(image_in)
    cross_w = spread(cross_own, place, places, 3584)
    mlp_w = spread(mlp_own, place, places, 3584)
    self_w = spread(self_own, place, places, 3584)
    image_cot_here = arrive(image_cot)

    def affine(gain, bias, norm):
        return jnp.stack([gain[0, norm], bias[0, norm]]).astype(F32)

    text_affine = [affine(text_gain, text_bias, n) for n in range(3)]
    image_affine = [affine(image_gain, image_bias, n) for n in range(3)]

    def parts(weights):
        return [("a", w) for w in weights]

    def s(value):
        return ("s", value)

    def w(value):
        return ("w", value)

    def q(value):
        return ("q", value)

    def buffer(weights):
        return pltpu.VMEM((QUARTERS, weights[0].shape[0], BLOCK), BF)

    text_wide, image_wide = shape(text_rows, DT, of=F32), shape(image_rows, DV, of=F32)
    text_f32, image_f32 = pltpu.VMEM((text_rows, DT), F32), pltpu.VMEM((image_rows, DV), F32)
    text_bf, image_bf = pltpu.VMEM((text_rows, DT), BF), pltpu.VMEM((image_rows, DV), BF)
    text_tr, image_tr = pltpu.VMEM((DT, text_rows), BF), pltpu.VMEM((DV, image_rows), BF)
    in_sems, out_sems = pltpu.SemaphoreType.DMA((6,)), pltpu.SemaphoreType.DMA((QUARTERS,))
    units = 2 * pairs

    def flops(weights):
        return 2 * QUARTERS * weights[0].size * (text_rows + image_rows) // 2

    text_pre1, text_one, image_pre1, image_one, text_kept, image_kept, text_probs, image_probs = run(
        cross_forward,
        pairs,
        FORWARD,
        [s(lens), w(text_in), w(image), w(text_affine[0]), w(image_affine[0])] + parts(cross_w),
        [
            w(text_wide),
            w(text_wide),
            w(image_wide),
            w(image_wide),
            q(shape(QUARTERS, text_rows, 1024)),
            q(shape(QUARTERS, image_rows, 1024)),
            q(shape(QUARTERS, units, SLOTS, PADDED)),
            q(shape(QUARTERS, units, PADDED, SLOTS)),
        ],
        [buffer(cross_w), text_f32, image_f32, in_sems],
        flops(cross_w),
    )
    text_pre2, text_two, image_pre2, image_two, text_activ, text_slope, image_activ, image_slope = run(
        mlp_forward,
        pairs,
        FORWARD,
        [w(text_one), w(image_one), w(text_affine[1]), w(image_affine[1])] + parts(mlp_w),
        [
            w(text_wide),
            w(text_wide),
            w(image_wide),
            w(image_wide),
            q(shape(QUARTERS, text_rows, 768)),
            q(shape(QUARTERS, text_rows, 768)),
            q(shape(QUARTERS, image_rows, 256)),
            q(shape(QUARTERS, image_rows, 256)),
        ],
        [buffer(mlp_w), text_f32, image_f32, text_bf, image_bf, in_sems],
        flops(mlp_w),
    )
    (
        text_out,
        image_out,
        text_n3,
        image_n3,
        text_vec3,
        image_vec3,
        self_q,
        self_k,
        self_v,
        self_c,
        self_probs,
        self_kept,
        self_image_probs,
    ) = run(
        self_forward,
        pairs,
        FORWARD,
        [
            s(lens),
            w(text_two),
            w(image_two),
            w(text_affine[2]),
            w(image_affine[2]),
            w(text_cot),
            w(image_cot_here),
        ]
        + parts(self_w),
        [
            w(text_wide),
            w(shape(image_rows, DV)),
            w(text_wide),
            w(image_wide),
            w(shape(2, DT, of=F32)),
            w(shape(2, DV, of=F32)),
            q(shape(QUARTERS, text_rows, 192)),
            q(shape(QUARTERS, text_rows, 192)),
            q(shape(QUARTERS, text_rows, 192)),
            q(shape(QUARTERS, text_rows, 192)),
            q(shape(QUARTERS, pairs, 384, SLOTS)),
            q(shape(QUARTERS, image_rows, 1024)),
            q(shape(QUARTERS, units, PADDED, PADDED)),
        ],
        [buffer(self_w), text_f32, image_f32, text_bf, image_bf, in_sems],
        flops(self_w),
    )

    text_depth, image_depth = DT // places, DV // places
    text_padded = -(-text_depth // 16) * 16

    def grad_outs(depth):
        return [("a", shape(2, 2, dp, depth, BLOCK))] * 2

    def back_scratch(weights, depth):
        return [
            buffer(weights),
            pltpu.VMEM((QUARTERS, 2, dp, depth, BLOCK), BF),
            text_f32,
            image_f32,
            text_bf,
            image_bf,
            text_tr,
            image_tr,
            text_tr,
            image_tr,
        ]

    image_out = leave(image_out).astype(F32)
    self_depth = 3 * text_padded + 4 * image_depth
    text_n2, image_n2, text_vec2, image_vec2, send, keep = run(
        self_back,
        pairs,
        BACKWARD,
        [
            s(x_ref),
            w(text_n3),
            w(image_n3),
            w(text_two),
            w(image_two),
            w(text_pre2),
            w(image_pre2),
            w(text_affine[1]),
            w(image_affine[1]),
            q(self_q),
            q(self_k),
            q(self_v),
            q(self_c),
            q(self_probs),
            q(self_kept),
            q(self_image_probs),
        ]
        + parts(self_w),
        [w(text_wide), w(image_wide), w(shape(2, DT, of=F32)), w(shape(2, DV, of=F32))] + grad_outs(self_depth),
        back_scratch(self_w, self_depth)
        + [pltpu.VMEM((3, text_rows, 192), BF), pltpu.VMEM((image_rows, 768), BF), in_sems, out_sems],
        2 * flops(self_w),
    )
    self_grads = fold(send, keep)
    mlp_depth = 6 * text_padded + 2 * image_depth
    text_n1, image_n1, text_vec1, image_vec1, send, keep = run(
        mlp_back,
        pairs,
        BACKWARD,
        [
            s(x_ref),
            w(text_n2),
            w(image_n2),
            w(text_one),
            w(image_one),
            w(text_pre1),
            w(image_pre1),
            w(text_affine[0]),
            w(image_affine[0]),
            q(text_activ),
            q(text_slope),
            q(image_activ),
            q(image_slope),
        ]
        + parts(mlp_w),
        [w(text_wide), w(image_wide), w(shape(2, DT, of=F32)), w(shape(2, DV, of=F32))] + grad_outs(mlp_depth),
        back_scratch(mlp_w, mlp_depth) + [text_bf, in_sems, out_sems],
        2 * flops(mlp_w),
    )
    mlp_grads = fold(send, keep)
    cross_depth = 4 * text_padded + 4 * image_depth
    text_grad, image_grad, send, keep = run(
        cross_back,
        pairs,
        BACKWARD,
        [
            s(x_ref),
            w(text_n1),
            w(image_n1),
            w(text_in),
            w(image),
            q(text_kept),
            q(image_kept),
            q(text_probs),
            q(image_probs),
        ]
        + parts(cross_w),
        [w(text_wide), w(shape(image_rows, DV))] + grad_outs(cross_depth),
        back_scratch(cross_w, cross_depth)
        + [pltpu.VMEM((text_rows, 768), BF), pltpu.VMEM((image_rows, 768), BF), in_sems, out_sems],
        2 * flops(cross_w),
    )
    image_grad = leave(image_grad).astype(F32)
    cross_grads = fold(send, keep)

    def pick(packed, first, count, depth, padded):
        rows = [packed[first + b * padded : first + b * padded + depth] for b in range(count)]
        return jnp.concatenate(rows, axis=1).astype(F32)

    def text_pick(packed, at, count):
        return pick(packed, at * text_padded, count, text_depth, text_padded)

    def image_pick(packed, text_blocks, at, count):
        return pick(packed, text_blocks * text_padded + at * image_depth, count, image_depth, image_depth)

    vec_rows = jnp.concatenate([text_vec1, text_vec2, text_vec3], axis=0).reshape(6, places, text_depth)
    vec_rows = jnp.pad(vec_rows, ((0, 0), (0, 0), (0, image_depth - text_depth)))
    vec_image = jnp.concatenate([image_vec1, image_vec2, image_vec3], axis=0).reshape(6, places, image_depth)
    vectors = lax.psum(jnp.concatenate([vec_rows, vec_image], axis=0).transpose(1, 0, 2), "tensor")
    vectors = lax.psum_scatter(vectors, ("stream", "dp"), scatter_dimension=0, tiled=True)[0]
    text_vectors, image_vectors = vectors[:6, :text_depth], vectors[6:]

    self_text = text_pick(self_grads, 0, 3)
    return (
        text_out,
        image_out,
        text_grad,
        image_grad,
        text_pick(cross_grads, 0, 1)[None],
        image_pick(cross_grads, 4, 0, 2).reshape(1, image_depth, 2, 256),
        text_pick(cross_grads, 3, 1).T[None],
        text_pick(mlp_grads, 0, 3)[None],
        text_pick(mlp_grads, 3, 3).T[None],
        self_text[:, :576].reshape(1, text_depth, 3, 192),
        self_text[:, 576:].T[None],
        text_vectors[0::2][None],
        text_vectors[1::2][None],
        image_pick(cross_grads, 4, 2, 1)[None],
        text_pick(cross_grads, 1, 2).reshape(1, text_depth, 2, 256),
        image_pick(cross_grads, 4, 3, 1).T[None],
        image_pick(mlp_grads, 6, 0, 1)[None],
        image_pick(mlp_grads, 6, 1, 1).T[None],
        image_pick(self_grads, 3, 0, 3).reshape(1, image_depth, 3, 256),
        image_pick(self_grads, 3, 3, 1).T[None],
        image_vectors[0::2][None],
        image_vectors[1::2][None],
    )


def solution(mesh):
    rows = P(("stream", "dp", "tensor"), None)
    wide_in = P(None, None, "tensor")
    group_in = P(None, None, None, "tensor")
    wide_out = P(None, "tensor", None)
    grad_in = P(None, ("stream", "dp"), "tensor")
    grad_group = P(None, ("stream", "dp"), None, "tensor")
    grad_out = P(None, "tensor", ("stream", "dp"))
    vector = P(None, None, ("stream", "dp"))
    weights = (wide_in, group_in, wide_out, wide_in, wide_out, group_in, wide_out, P(), P())
    grads = (grad_in, grad_group, grad_out, grad_in, grad_out, grad_group, grad_out, vector, vector)
    return jax.shard_map(
        local,
        mesh=mesh,
        in_specs=(rows, rows, P(("stream", "dp")), rows, rows) + weights + weights,
        out_specs=(rows, rows, rows, rows) + grads + grads,
        check_vma=False,
    )
```

time: 1920 us -> 571 us (0.30)
  waiting for transfers between devices: 1190 us -> 255 us
  blocking collectives: 233 us -> 6.16 us
  matrix products: 203 us -> 0 us
  Pallas kernels: 0 us -> 134 us
  local copies, waits for them, and re-layouts: 182 us -> 57.4 us
    reduce_scatter x29 -> x4, waiting for transfers between devices: 803 us -> 15.5 us  [the longest x3 15.5 us: fold(): return lax.psum_scatter(total, 'dp', scatter_dimension=0, tiled=True)[0]]
    unnamed x6 -> x0, blocking collectives: 226 us -> none
    unnamed x70 -> x7, waiting for transfers between devices: 212 us -> 0.12 us
    dot_general x64 -> x0, matrix products: 193 us -> none  [the longest x13 56.8 us: matmul(): lax.dot_general(left, right, (((left.ndim - 1,), (0,)), ((), ())), prefer...]
    pallas_call x0 -> x6, Pallas kernels: none -> 134 us  [run(): pl.pallas_call(functools.partial(kernel, pairs), grid=(QUARTERS,), in_spe...]
    ppermute x5 -> x34, waiting for transfers between devices: 95.3 us -> 220 us  [swap(): lax.ppermute(value, axis, [(i, i ^ apart) for i in range(lax.axis_size(ax...]
    unnamed x355 -> x111, local copies, waits for them, and re-layouts: 116 us -> 35.2 us
    all_gather x12 -> x3, waiting for transfers between devices: 82.4 us -> 19.6 us  [spread(): lax.all_gather(swap(mine, 'tensor', 2), ('stream', 'dp'), axis=0, tiled=T...]
  transfers between devices with their start and end apart: 64 -> 41, of which waited for: 46 -> 19; matrix products, arithmetic and copies ran while one was open for 31% -> 18% of each run, Pallas kernels for 0% -> 15%
where the time goes in v1:
time: 571 us; the launch traced here: 565 us
  waiting for transfers between devices  255 us (45%)
  Pallas kernels  134 us (23%)
  other arithmetic  67.4 us (12%)
  local copies, waits for them, and re-layouts  57.4 us (10%)
  starting transfers between devices  30 us (5%)
  between operations  15 us (3%)
  blocking collectives  6.16 us (1%)
    ppermute x34, waiting for transfers between devices, swap(): lax.ppermute(value, axis, [(i, i ^ apart) for i in range(lax.axis_size(ax...  220 us
    pallas_call x6, Pallas kernels, run(): pl.pallas_call(functools.partial(kernel, pairs), grid=(QUARTERS,), in_spe...  134 us
    convert_element_type x18, other arithmetic, low(): return value.astype(BF)  48.1 us
    unnamed x111, local copies, waits for them, and re-layouts  35.2 us
    ppermute x34, starting transfers between devices, swap(): lax.ppermute(value, axis, [(i, i ^ apart) for i in range(lax.axis_size(ax...  29.5 us
    all_gather x3, waiting for transfers between devices, spread(): lax.all_gather(swap(mine, 'tensor', 2), ('stream', 'dp'), axis=0, tiled=T...  19.6 us
    reduce_scatter x3, waiting for transfers between devices, fold(): return lax.psum_scatter(total, 'dp', scatter_dimension=0, tiled=True)[0]  15.5 us
  transfers between devices with their start and end apart: 41, of which 19 were waited for; matrix products, arithmetic and copies ran while one was open for 18% of the time, Pallas kernels for 15%

profile of v1, /device:TPU:0, one launch (start us, length us, event | category | flops | bytes accessed | tf_op | source)
XLA Modules:
  0.0 564.9 jit_solution(14003009069187149964)
XLA Ops:
  7.3 2.8 fusion.48
  22.3 3.0 collective-permute-start.3
  25.4 5.7 %collective-permute-done.3 = bf16[448,256]{1,0:T(8,128)(2,1)} collective-permute-done((bf16[448,256]{1,0:T(8,128)(2,1)S(1)}, bf16[448,256]{1,0:T(8,128)(2,1)}, u32[]{:S(2)}, u32[]{:S(2)}) %collective-permute-start.3) | collective-permute-done | bytes 229408 | tf_op jit(solution)/shard_map/ppermute | solution.py:646
  33.6 1.9 fusion.46
  40.0 1.9 bitcast_dynamic-update-slice_fusion.4
  50.8 28.5 %collective-permute-done.8 = bf16[448,256]{1,0:T(8,128)(2,1)} collective-permute-done((bf16[448,256]{1,0:T(8,128)(2,1)S(1)}, bf16[448,256]{1,0:T(8,128)(2,1)}, u32[]{:S(2)}, u32[]{:S(2)}) %collective-permute-start.8) | collective-permute-done | bytes 229408 | tf_op jit(solution)/shard_map/ppermute | solution.py:646
  95.5 26.2 %collective-permute-done.14 = bf16[448,256]{1,0:T(8,128)(2,1)S(1)} collective-permute-done((bf16[448,256]{1,0:T(8,128)(2,1)S(1)}, bf16[448,256]{1,0:T(8,128)(2,1)S(1)}, u32[]{:S(2)}, u32[]{:S(2)}) %collective-permute-start.14) | collective-permute-done | bytes 229408 | tf_op jit(solution)/shard_map/ppermute | solution.py:646
  125.6 8.2 %collective-permute-done = bf16[148,1024]{1,0:T(8,128)(2,1)S(1)} collective-permute-done((bf16[148,1024]{1,0:T(8,128)(2,1)}, bf16[148,1024]{1,0:T(8,128)(2,1)S(1)}, u32[]{:S(2)}, u32[]{:S(2)}) %collective-permute-start) | collective-permute-done | bytes 303136 | tf_op jit(solution)/shard_map/ppermute | solution.py:646
  135.3 9.9 %collective-permute-done.11 = bf16[148,1024]{1,0:T(8,128)(2,1)S(1)} collective-permute-done((bf16[148,1024]{1,0:T(8,128)(2,1)}, bf16[148,1024]{1,0:T(8,128)(2,1)S(1)}, u32[]{:S(2)}, u32[]{:S(2)}) %collective-permute-start.11) | collective-permute-done | bytes 303136 | tf_op jit(solution)/shard_map/ppermute | solution.py:646
  145.2 11.5 %collective-permute-done.13.refs_2_.refs_9_ = bf16[2816,256]{1,0:T(8,128)(2,1)} collective-permute-done((bf16[2816,256]{1,0:T(8,128)(2,1)S(1)}, bf16[2816,256]{1,0:T(8,128)(2,1)}, u32[]{:S(2)}, u32[]{:S(2)}) %collective-permute-start.13) | collective-permute-done | bytes 1441824 | tf_op jit(solution)/shard_map/ppermute | solution.py:646
  157.4 19.6 %all-gather.8.cloned.1.call-done.refs_3_.refs_10_ = bf16[3584,256]{1,0:T(8,128)(2,1)} async-done(((bf16[448,256]{1,0:T(8,128)(2,1)}), bf16[3584,256]{1,0:T(8,128)(2,1)}) %all-gather.8.cloned.1.call-update) | async-done | bytes 1835024 | tf_op jit(solution)/shard_map/all_gather | solution.py:655
  183.6 16.5 %shard_map.390 = (f32[512,768]{1,0:T(8,128)}, f32[512,768]{1,0:T(8,128)}, f32[192,1024]{1,0:T(8,128)}, f32[192,1024]{1,0:T(8,128)}, bf16[4,512,1024]{2,1,0:T(8,1...) custom-call(s32[4]{0:T(128)} %dynamic_slice.12.lens, ...), custom_call_target="tpu_custom_call" | custom-call | flops 5167382528 | bytes 27146256 | tf_op jit(solution)/shard_map/pallas_call | solution.py:633
  200.1 15.4 %shard_map.391 = (f32[512,768]{1,0:T(8,128)}, f32[512,768]{1,0:T(8,128)}, f32[192,1024]{1,0:T(8,128)}, f32[192,1024]{1,0:T(8,128)}, bf16[4,512,768]{2,1,0:T(8,12...) custom-call(f32[512,768]{1,0:T(8,128)} %get-tuple-element.67.text.text_one, ...), custom_call_target="tpu_custom_call" | custom-call | flops 4798283776 | bytes 27801600 | tf_op jit(solution)/shard_map/pallas_call | solution.py:633
  215.5 19.0 %shard_map.392 = (f32[512,768]{1,0:T(8,128)}, bf16[192,1024]{1,0:T(8,128)(2,1)}, f32[512,768]{1,0:T(8,128)}, f32[192,1024]{1,0:T(8,128)}, f32[2,768]{1,0:T(2,128...) custom-call(s32[4]{0:T(128)} %dynamic_slice.12.lens, ...), custom_call_target="tpu_custom_call" | custom-call | flops 4613734400 | bytes 27439120 | tf_op jit(solution)/shard_map/pallas_call | solution.py:633
  234.5 30.6 %shard_map.393 = (f32[512,768]{1,0:T(8,128)}, f32[192,1024]{1,0:T(8,128)}, f32[2,768]{1,0:T(2,128)}, f32[2,1024]{1,0:T(2,128)}, bf16[2,2,4,800,256]{4,3,2,1,0:T(...) custom-call(s32[1]{0:T(128)} %bitcast.37.x_at, f32[512,768]{1,0:T(8,128)} %get-tuple-element.73.text_g, ...), custom_call_target="tpu_custom_call" | custom-call | flops 9227468800 | bytes 42119172 | tf_op jit(solution)/shard_map/pallas_call | solution.py:633
  265.2 26.3 %shard_map.394 = (f32[512,768]{1,0:T(8,128)}, f32[192,1024]{1,0:T(8,128)}, f32[2,768]{1,0:T(2,128)}, f32[2,1024]{1,0:T(2,128)}, bf16[2,2,4,832,256]{4,3,2,1,0:T(...) custom-call(s32[1]{0:T(128)} %bitcast.37.x_at, f32[512,768]{1,0:T(8,128)} %get-tuple-element.84.text_g, ...), custom_call_target="tpu_custom_call" | custom-call | flops 9596567552 | bytes 43806724 | tf_op jit(solution)/shard_map/pallas_call | solution.py:633
  292.0 26.2 %shard_map.395 = (f32[512,768]{1,0:T(8,128)}, bf16[192,1024]{1,0:T(8,128)(2,1)}, bf16[2,2,4,896,256]{4,3,2,1,0:T(8,128)(2,1)}, bf16[2,2,4,896,256]{4,3,2,1,0:T(8,128)(2,1)}) custom-call(s32[1]{0:T(128)} %bitcast.37.x_at, f32[512,768]{1,0:T(8,128)} %get-tuple-element.92.text_g, f32[192,1024]{1,0:T(8,128)} %get-tuple-element.93.image_g, ...), custom_call_target="tpu_custom_call" | custom-call | flops 10334765056 | bytes 41418756 | tf_op jit(solution)/shard_map/pallas_call | solution.py:633
  318.4 5.0 add_convert_fusion.9
  324.1 4.1 add_convert_fusion.11
  330.5 31.8 %collective-permute-done.32 = bf16[2,4,400,256]{3,2,1,0:T(8,128)(2,1)} collective-permute-done((bf16[2,4,400,256]{3,2,1,0:T(8,128)(2,1)}, bf16[2,4,400,256]{3,2,1,0:T(8,128)(2,1)}, u32[]{:S(2)}, u32[]{:S(2)}) %collective-permute-start.32) | collective-permute-done | bytes 1638432 | tf_op jit(solution)/shard_map/ppermute | solution.py:646
  370.1 5.4 add_convert_fusion.5
  376.1 4.9 add_convert_fusion.7
  382.5 2.4 collective-permute-done.33
  386.3 3.6 collective-permute-done.31
  393.0 31.7 %collective-permute-done.27 = bf16[2,4,416,256]{3,2,1,0:T(8,128)(2,1)} collective-permute-done((bf16[2,4,416,256]{3,2,1,0:T(8,128)(2,1)}, bf16[2,4,416,256]{3,2,1,0:T(8,128)(2,1)}, u32[]{:S(2)}, u32[]{:S(2)}) %collective-permute-start.27) | collective-permute-done | bytes 1703968 | tf_op jit(solution)/shard_map/ppermute | solution.py:646
  430.1 6.3 %add_convert_fusion.1 = (bf16[2,1,4,448,256]{4,3,2,1,0:T(8,128)(2,1)}, bf16[2,4,448,256]{3,2,1,0:T(8,128)(2,1)}) fusion(bf16[2,2,4,896,256]{4,3,2,1,0:T(8,128)(2,1)} %collective-permute-done.19, bf16[2,2,4,896,256]{4,3,2,1,0:T(8,128)(2,1)} %get-tuple-element.100), kind=kLoop, calls=%fused_computation.1 | loop fusion | flops 7340032 | bytes 11010048 | tf_op jit(solution)/shard_map/convert_element_type | solution.py:42
  437.5 4.5 add_convert_fusion.3
  442.5 5.5 collective-permute-done.28
  454.0 33.6 %collective-permute-done.22 = bf16[2,4,448,256]{3,2,1,0:T(8,128)(2,1)} collective-permute-done((bf16[2,4,448,256]{3,2,1,0:T(8,128)(2,1)}, bf16[2,4,448,256]{3,2,1,0:T(8,128)(2,1)}, u32[]{:S(2)}, u32[]{:S(2)}) %collective-permute-start.22) | collective-permute-done | bytes 1835040 | tf_op jit(solution)/shard_map/ppermute | solution.py:646
  491.7 17.1 %collective-permute-done.23 = bf16[4,448,256]{2,1,0:T(8,128)(2,1)S(1)} collective-permute-done((bf16[4,448,256]{2,1,0:T(8,128)(2,1)S(1)}, bf16[4,448,256]{2,1,0:T(8,128)(2,1)S(1)}, u32[]{:S(2)}, u32[]{:S(2)}) %collective-permute-start.23) | collective-permute-done | bytes 917536 | tf_op jit(solution)/shard_map/ppermute | solution.py:646
  515.9 6.2 %psum.8 = f32[1,12,128]{2,1,0:T(8,128)S(1)} all-reduce(f32[1,12,128]{2,1,0:T(8,128)} %reduce-scatter.11.cloned.1.call-done), channel_id=1, replica_groups=mesh['stream'=2,'dp'=4,'tensor'=4] {'tensor'}, use_global_device_ids=true, to_apply=%region_3.4 | all-reduce | flops 1536 | bytes 12288 | tf_op jit(solution)/shard_map/psum | solution.py:991
  536.6 15.5 %reduce-scatter.5.cloned.1.call-done = bf16[1,896,256]{2,1,0:T(8,128)(2,1)} async-done(((bf16[4,896,256]{2,1,0:T(8,128)(2,1)}), bf16[1,896,256]{2,1,0:T(8,128)(2,1)}) %reduce-scatter.5.cloned.1.call-update) | async-done | bytes 458768 | tf_op jit(solution)/shard_map/reduce_scatter | solution.py:683
  (262 shorter events, 119.3 us)
Async XLA Ops:
  7.2 149.6 %all-gather.4.cloned.1.call-start = ((), (), s32[]{:S(2)}) async-start(), calls=%async_computation.4 | async-start | bytes 2064384 | tf_op jit(solution)/shard_map/all_gather | solution.py:655
  25.4 151.6 %collective-permute-start.1 = (bf16[7168,256]{1,0:T(8,128)(2,1)}, bf16[7168,256]{1,0:T(8,128)(2,1)}, u32[]{:S(2)}, u32[]{:S(2)}) collective-permute-start(bf16[7168,256]{1,0:T(8,128)(2,1)} %slice_dynamic-update-slice_fusion.16.refs_0_.refs_4_), channel_id=1, source_target_pairs={{0,1},{1,0},{2,3},{3,2},{4,5},{5,4},{6,7},{7,6},{8,9},{9,8},{10,11... | collective-permute-start | bytes 11010056 | tf_op jit(solution)/shard_map/ppermute | solution.py:646
  31.1 126.2 %all-gather.6.cloned.1.call-start = ((), (), s32[]{:S(2)}) async-start(), calls=%async_computation.5 | async-start | bytes 2064384 | tf_op jit(solution)/shard_map/all_gather | solution.py:655
  36.7 85.7 %collective-permute-start.7 = (bf16[3072,256]{1,0:T(8,128)(2,1)}, bf16[3072,256]{1,0:T(8,128)(2,1)}, u32[]{:S(2)}, u32[]{:S(2)}) collective-permute-start(bf16[3072,256]{1,0:T(8,128)(2,1)} %pad_maximum_fusion.3), channel_id=1, source_target_pairs={{0,2},{1,3},{2,0},{3,1},{4,6},{5,7},{6,4},{7,5},{8,10},{9,11},{10,... | collective-permute-start | bytes 4718600 | tf_op jit(solution)/shard_map/ppermute | solution.py:646
  45.6 33.7 %collective-permute-start.8 = (bf16[448,256]{1,0:T(8,128)(2,1)S(1)}, bf16[448,256]{1,0:T(8,128)(2,1)}, u32[]{:S(2)}, u32[]{:S(2)}) collective-permute-start(bf16[448,256]{1,0:T(8,128)(2,1)S(1)} %constant_dynamic-slice_fusion.1), channel_id=1, source_target_pairs={{0,2},{1,3},{2,0},{3,1},{4,6},{5,7},{6,4},{7,5},{8,10},{9,11},{10,... | collective-permute-start | bytes 688136 | tf_op jit(solution)/shard_map/ppermute | solution.py:646
  47.3 88.0 %collective-permute-start.2 = (bf16[3584,256]{1,0:T(8,128)(2,1)}, bf16[3584,256]{1,0:T(8,128)(2,1)}, u32[]{:S(2)}, u32[]{:S(2)}) collective-permute-start(bf16[3584,256]{1,0:T(8,128)(2,1)} %slice.584), channel_id=1, source_target_pairs={{0,2},{1,3},{2,0},{3,1},{4,6},{5,7},{6,4},{7,5},{8,10},{9,11},{10,... | collective-permute-start | bytes 5505032 | tf_op jit(solution)/shard_map/ppermute | solution.py:646
  79.3 97.7 %all-gather.8.cloned.1.call-start = ((), (), s32[]{:S(2)}) async-start(), calls=%async_computation.6 | async-start | bytes 2064384 | tf_op jit(solution)/shard_map/all_gather | solution.py:655
  93.7 28.0 %collective-permute-start.14 = (bf16[448,256]{1,0:T(8,128)(2,1)S(1)}, bf16[448,256]{1,0:T(8,128)(2,1)S(1)}, u32[]{:S(2)}, u32[]{:S(2)}) collective-permute-start(bf16[448,256]{1,0:T(8,128)(2,1)S(1)} %constant_dynamic-slice_fusion), channel_id=1, source_target_pairs={{0,2},{1,3},{2,0},{3,1},{4,6},{5,7},{6,4},{7,5},{8,10},{9,11},{10,... | collective-permute-start | bytes 688136 | tf_op jit(solution)/shard_map/ppermute | solution.py:646
  122.4 393.5 %reduce-scatter.11.cloned.1.call-start = ((), (), s32[]{:S(2)}) async-start(), calls=%async_computation.10 | async-start | bytes 73728 | tf_op jit(solution)/shard_map/reduce_scatter | solution.py:992
  122.5 34.3 %collective-permute-start.9 = (bf16[3072,256]{1,0:T(8,128)(2,1)}, bf16[3072,256]{1,0:T(8,128)(2,1)S(1)}, u32[]{:S(2)}, u32[]{:S(2)}) collective-permute-start(bf16[3072,256]{1,0:T(8,128)(2,1)} %collective-permute-done.7.refs_2_.refs_6_), channel_id=1, source_target_pairs={{0,1},{1,0},{2,3},{3,2},{4,5},{5,4},{6,7},{7,6},{8,9},{9,8},{10,11... | collective-permute-start | bytes 4718600 | tf_op jit(solution)/shard_map/ppermute | solution.py:646
  122.6 34.2 %collective-permute-start.13 = (bf16[2816,256]{1,0:T(8,128)(2,1)S(1)}, bf16[2816,256]{1,0:T(8,128)(2,1)}, u32[]{:S(2)}, u32[]{:S(2)}) collective-permute-start(bf16[2816,256]{1,0:T(8,128)(2,1)S(1)} %slice.605), channel_id=1, source_target_pairs={{0,2},{1,3},{2,0},{3,1},{4,6},{5,7},{6,4},{7,5},{8,10},{9,11},{10,... | collective-permute-start | bytes 4325384 | tf_op jit(solution)/shard_map/ppermute | solution.py:646
  135.3 22.0 %collective-permute-start.4 = (bf16[3584,256]{1,0:T(8,128)(2,1)}, bf16[3584,256]{1,0:T(8,128)(2,1)}, u32[]{:S(2)}, u32[]{:S(2)}) collective-permute-start(bf16[3584,256]{1,0:T(8,128)(2,1)} %collective-permute-done.2.refs_2_.refs_6_), channel_id=1, source_target_pairs={{0,1},{1,0},{2,3},{3,2},{4,5},{5,4},{6,7},{7,6},{8,9},{9,8},{10,11... | collective-permute-start | bytes 5505032 | tf_op jit(solution)/shard_map/ppermute | solution.py:646
  145.2 54.9 %collective-permute-start.6 = (bf16[6656,256]{1,0:T(8,128)(2,1)}, bf16[6656,256]{1,0:T(8,128)(2,1)}, u32[]{:S(2)}, u32[]{:S(2)}) collective-permute-start(bf16[6656,256]{1,0:T(8,128)(2,1)} %slice_dynamic-update-slice_fusion.12.refs_0_.refs_4_), channel_id=1, source_target_pairs={{0,1},{1,0},{2,3},{3,2},{4,5},{5,4},{6,7},{7,6},{8,9},{9,8},{10,11... | collective-permute-start | bytes 10223624 | tf_op jit(solution)/shard_map/ppermute | solution.py:646
  156.8 22.7 %collective-permute-start.5 = (bf16[3584,256]{1,0:T(8,128)(2,1)}, bf16[3584,256]{1,0:T(8,128)(2,1)}, u32[]{:S(2)}, u32[]{:S(2)}) collective-permute-start(bf16[3584,256]{1,0:T(8,128)(2,1)} %all-gather.4.cloned.1.call-done.refs_3_.refs_7_), channel_id=1, source_target_pairs={{0,1},{1,0},{2,3},{3,2},{4,5},{5,4},{6,7},{7,6},{8,9},{9,8},{10,11... | collective-permute-start | bytes 5505032 | tf_op jit(solution)/shard_map/ppermute | solution.py:646
  156.8 58.7 %collective-permute-start.12 = (bf16[6400,256]{1,0:T(8,128)(2,1)}, bf16[6400,256]{1,0:T(8,128)(2,1)}, u32[]{:S(2)}, u32[]{:S(2)}) collective-permute-start(bf16[6400,256]{1,0:T(8,128)(2,1)} %slice_dynamic-update-slice_fusion.8.refs_0_.refs_7_), channel_id=1, source_target_pairs={{0,1},{1,0},{2,3},{3,2},{4,5},{5,4},{6,7},{7,6},{8,9},{9,8},{10,11... | collective-permute-start | bytes 9830408 | tf_op jit(solution)/shard_map/ppermute | solution.py:646
  157.3 42.8 %collective-permute-start.10 = (bf16[3584,256]{1,0:T(8,128)(2,1)}, bf16[3584,256]{1,0:T(8,128)(2,1)}, u32[]{:S(2)}, u32[]{:S(2)}) collective-permute-start(bf16[3584,256]{1,0:T(8,128)(2,1)} %all-gather.6.cloned.1.call-done.refs_3_.refs_7_), channel_id=1, source_target_pairs={{0,1},{1,0},{2,3},{3,2},{4,5},{5,4},{6,7},{7,6},{8,9},{9,8},{10,11... | collective-permute-start | bytes 5505032 | tf_op jit(solution)/shard_map/ppermute | solution.py:646
  177.0 38.5 %collective-permute-start.16 = (bf16[3584,256]{1,0:T(8,128)(2,1)}, bf16[3584,256]{1,0:T(8,128)(2,1)}, u32[]{:S(2)}, u32[]{:S(2)}) collective-permute-start(bf16[3584,256]{1,0:T(8,128)(2,1)} %all-gather.8.cloned.1.call-done.refs_3_.refs_10_), channel_id=1, source_target_pairs={{0,1},{1,0},{2,3},{3,2},{4,5},{5,4},{6,7},{7,6},{8,9},{9,8},{10,11... | collective-permute-start | bytes 5505032 | tf_op jit(solution)/shard_map/ppermute | solution.py:646
  179.5 36.0 %collective-permute-start.15 = (bf16[2816,256]{1,0:T(8,128)(2,1)}, bf16[2816,256]{1,0:T(8,128)(2,1)}, u32[]{:S(2)}, u32[]{:S(2)}) collective-permute-start(bf16[2816,256]{1,0:T(8,128)(2,1)} %collective-permute-done.13.refs_2_.refs_9_), channel_id=1, source_target_pairs={{0,1},{1,0},{2,3},{3,2},{4,5},{5,4},{6,7},{7,6},{8,9},{9,8},{10,11... | collective-permute-start | bytes 4325384 | tf_op jit(solution)/shard_map/ppermute | solution.py:646
  265.1 53.3 %collective-permute-start.29 = (bf16[2,2,4,800,256]{4,3,2,1,0:T(8,128)(2,1)}, bf16[2,2,4,800,256]{4,3,2,1,0:T(8,128)(2,1)}, u32[]{:S(2)}, u32[]{:S(2)}) collective-permute-start(bf16[2,2,4,800,256]{4,3,2,1,0:T(8,128)(2,1)} %get-tuple-element.105), channel_id=1, source_target_pairs={{0,1},{1,0},{2,3},{3,2},{4,5},{5,4},{6,7},{7,6},{8,9},{9,8},{10,11... | collective-permute-start | bytes 19660808 | tf_op jit(solution)/shard_map/ppermute | solution.py:646
  291.5 78.6 %collective-permute-start.24 = (bf16[2,2,4,832,256]{4,3,2,1,0:T(8,128)(2,1)}, bf16[2,2,4,832,256]{4,3,2,1,0:T(8,128)(2,1)}, u32[]{:S(2)}, u32[]{:S(2)}) collective-permute-start(bf16[2,2,4,832,256]{4,3,2,1,0:T(8,128)(2,1)} %get-tuple-element.103), channel_id=1, source_target_pairs={{0,1},{1,0},{2,3},{3,2},{4,5},{5,4},{6,7},{7,6},{8,9},{9,8},{10,11... | collective-permute-start | bytes 20447240 | tf_op jit(solution)/shard_map/ppermute | solution.py:646
  318.3 111.8 %collective-permute-start.19 = (bf16[2,2,4,896,256]{4,3,2,1,0:T(8,128)(2,1)}, bf16[2,2,4,896,256]{4,3,2,1,0:T(8,128)(2,1)}, u32[]{:S(2)}, u32[]{:S(2)}) collective-permute-start(bf16[2,2,4,896,256]{4,3,2,1,0:T(8,128)(2,1)} %get-tuple-element.101), channel_id=1, source_target_pairs={{0,1},{1,0},{2,3},{3,2},{4,5},{5,4},{6,7},{7,6},{8,9},{9,8},{10,11... | collective-permute-start | bytes 22020104 | tf_op jit(solution)/shard_map/ppermute | solution.py:646
  323.5 38.8 %collective-permute-start.32 = (bf16[2,4,400,256]{3,2,1,0:T(8,128)(2,1)}, bf16[2,4,400,256]{3,2,1,0:T(8,128)(2,1)}, u32[]{:S(2)}, u32[]{:S(2)}) collective-permute-start(bf16[2,4,400,256]{3,2,1,0:T(8,128)(2,1)} %get-tuple-element.167), channel_id=1, source_target_pairs={{0,16},{16,0},{1,17},{17,1},{2,18},{18,2},{3,19},{19,3},{4,20},{20... | collective-permute-start | bytes 4915208 | tf_op jit(solution)/shard_map/ppermute | solution.py:646
  328.1 38.9 %collective-permute-start.30 = (bf16[2,4,400,256]{3,2,1,0:T(8,128)(2,1)}, bf16[2,4,400,256]{3,2,1,0:T(8,128)(2,1)}, u32[]{:S(2)}, u32[]{:S(2)}) collective-permute-start(bf16[2,4,400,256]{3,2,1,0:T(8,128)(2,1)} %get-tuple-element.165), channel_id=1, source_target_pairs={{0,2},{1,3},{2,0},{3,1},{4,6},{5,7},{6,4},{7,5},{8,10},{9,11},{10,... | collective-permute-start | bytes 4915208 | tf_op jit(solution)/shard_map/ppermute | solution.py:646
  330.5 196.2 %reduce-scatter.9.cloned.1.call-start = ((), (), s32[]{:S(2)}) async-start(), calls=%async_computation.9 | async-start | bytes 2048000 | tf_op jit(solution)/shard_map/reduce_scatter | solution.py:683
  375.6 49.2 %collective-permute-start.27 = (bf16[2,4,416,256]{3,2,1,0:T(8,128)(2,1)}, bf16[2,4,416,256]{3,2,1,0:T(8,128)(2,1)}, u32[]{:S(2)}, u32[]{:S(2)}) collective-permute-start(bf16[2,4,416,256]{3,2,1,0:T(8,128)(2,1)} %get-tuple-element.163), channel_id=1, source_target_pairs={{0,16},{16,0},{1,17},{17,1},{2,18},{18,2},{3,19},{19,3},{4,20},{20... | collective-permute-start | bytes 5111816 | tf_op jit(solution)/shard_map/ppermute | solution.py:646
  381.0 46.7 %collective-permute-start.25 = (bf16[2,4,416,256]{3,2,1,0:T(8,128)(2,1)}, bf16[2,4,416,256]{3,2,1,0:T(8,128)(2,1)}, u32[]{:S(2)}, u32[]{:S(2)}) collective-permute-start(bf16[2,4,416,256]{3,2,1,0:T(8,128)(2,1)} %get-tuple-element.161), channel_id=1, source_target_pairs={{0,2},{1,3},{2,0},{3,1},{4,6},{5,7},{6,4},{7,5},{8,10},{9,11},{10,... | collective-permute-start | bytes 5111816 | tf_op jit(solution)/shard_map/ppermute | solution.py:646
  392.8 139.1 %reduce-scatter.7.cloned.1.call-start = ((), (), s32[]{:S(2)}) async-start(), calls=%async_computation.8 | async-start | bytes 2129920 | tf_op jit(solution)/shard_map/reduce_scatter | solution.py:683
  426.1 21.9 %collective-permute-start.28 = (bf16[4,416,256]{2,1,0:T(8,128)(2,1)S(1)}, bf16[4,416,256]{2,1,0:T(8,128)(2,1)S(1)}, u32[]{:S(2)}, u32[]{:S(2)}) collective-permute-start(bf16[4,416,256]{2,1,0:T(8,128)(2,1)S(1)} %fusion.33), channel_id=1, source_target_pairs={{0,2},{1,3},{2,0},{3,1},{4,6},{5,7},{6,4},{7,5},{8,10},{9,11},{10,... | collective-permute-start | bytes 2555912 | tf_op jit(solution)/shard_map/ppermute | solution.py:646
  429.1 22.0 %collective-permute-start.26 = (bf16[4,416,256]{2,1,0:T(8,128)(2,1)S(1)}, bf16[4,416,256]{2,1,0:T(8,128)(2,1)S(1)}, u32[]{:S(2)}, u32[]{:S(2)}) collective-permute-start(bf16[4,416,256]{2,1,0:T(8,128)(2,1)S(1)} %fusion.32), channel_id=1, source_target_pairs={{0,16},{16,0},{1,17},{17,1},{2,18},{18,2},{3,19},{19,3},{4,20},{20... | collective-permute-start | bytes 2555912 | tf_op jit(solution)/shard_map/ppermute | solution.py:646
  436.4 51.2 %collective-permute-start.22 = (bf16[2,4,448,256]{3,2,1,0:T(8,128)(2,1)}, bf16[2,4,448,256]{3,2,1,0:T(8,128)(2,1)}, u32[]{:S(2)}, u32[]{:S(2)}) collective-permute-start(bf16[2,4,448,256]{3,2,1,0:T(8,128)(2,1)} %get-tuple-element.159), channel_id=1, source_target_pairs={{0,16},{16,0},{1,17},{17,1},{2,18},{18,2},{3,19},{19,3},{4,20},{20... | collective-permute-start | bytes 5505032 | tf_op jit(solution)/shard_map/ppermute | solution.py:646
  442.0 48.0 %collective-permute-start.20 = (bf16[2,4,448,256]{3,2,1,0:T(8,128)(2,1)}, bf16[2,4,448,256]{3,2,1,0:T(8,128)(2,1)}, u32[]{:S(2)}, u32[]{:S(2)}) collective-permute-start(bf16[2,4,448,256]{3,2,1,0:T(8,128)(2,1)} %get-tuple-element.157), channel_id=1, source_target_pairs={{0,2},{1,3},{2,0},{3,1},{4,6},{5,7},{6,4},{7,5},{8,10},{9,11},{10,... | collective-permute-start | bytes 5505032 | tf_op jit(solution)/shard_map/ppermute | solution.py:646
  453.9 98.2 %reduce-scatter.5.cloned.1.call-start = ((), (), s32[]{:S(2)}) async-start(), calls=%async_computation.7 | async-start | bytes 2293760 | tf_op jit(solution)/shard_map/reduce_scatter | solution.py:683
  (46 other events, 956.5 us)
Sparse Core Ops, SparseCore 0:
  31.2 47.7 all-gather.3
  81.1 46.0 all-gather.5
  129.9 47.0 all-gather.7
  330.6 60.4 reduce-scatter.10
  393.3 35.9 reduce-scatter.8
  454.1 35.7 reduce-scatter.6
  513.6 38.5 reduce-scatter.4

commit v2 on v1

v2 whole, which is shorter than its diff:
```python
import functools

import jax
import jax.numpy as jnp
from jax import lax
from jax.experimental import pallas as pl
from jax.experimental.pallas import tpu as pltpu
from jax.sharding import PartitionSpec as P

DT = 768
DV = 1024
HEAD = 128
SELF_HEAD = 64
SLOTS = 128
REGIONS = 37
PADDED = 48
QUARTERS = 4
BLOCK = 256

norm_eps = 1e-05
masked_score = -1e30

BF = jnp.bfloat16
F32 = jnp.float32
FORWARD = (0, 1, 2, 3)
BACKWARD = (1, 3, 0, 2)


def nn(left, right):
    return lax.dot_general(left, right, (((1,), (0,)), ((), ())), preferred_element_type=F32)


def nt(left, right):
    return lax.dot_general(left, right, (((1,), (1,)), ((), ())), preferred_element_type=F32)


def tn(left, right):
    return lax.dot_general(left, right, (((0,), (0,)), ((), ())), preferred_element_type=F32)


def low(value):
    return value.astype(BF)


def normed(inputs):
    centered = inputs - jnp.mean(inputs, axis=-1, keepdims=True)
    scale = lax.rsqrt(jnp.mean(centered * centered, axis=-1, keepdims=True) + norm_eps)
    return centered * scale, scale


def norm_back(unit, scale, gain, grad, vec):
    vec[0:1] = jnp.sum(grad * unit, axis=0, keepdims=True)
    vec[1:2] = jnp.sum(grad, axis=0, keepdims=True)
    inner = grad * gain
    shift = jnp.mean(inner, axis=-1, keepdims=True)
    slope = jnp.mean(inner * unit, axis=-1, keepdims=True)
    return scale * (inner - shift - unit * slope)


def softmax_all(scores):
    tops = [jnp.max(s, axis=-1, keepdims=True) for s in scores]
    powers = [jnp.exp(s - t) for s, t in zip(scores, tops)]
    sums = [jnp.sum(e, axis=-1, keepdims=True) for e in powers]
    return [low(e / total) for e, total in zip(powers, sums)]


def attend(queries, keys, values, scale, masks):
    scores = [nt(q, k) * scale for q, k in zip(queries, keys)]
    scores = [s if m is None else jnp.where(m, s, masked_score) for s, m in zip(scores, masks)]
    probs = softmax_all(scores)
    return probs, [nn(p, v) for p, v in zip(probs, values)]


def attend_back(queries, keys, values, probs, grads, scale):
    grad_probs = [nt(g, v) for g, v in zip(grads, values)]
    grad_values = [low(tn(p, g)) for p, g in zip(probs, grads)]
    wide = [p.astype(F32) for p in probs]
    inner = [jnp.sum(p * g, axis=-1, keepdims=True) for p, g in zip(wide, grad_probs)]
    grad_scores = [low(p * (g - i)) for p, g, i in zip(wide, grad_probs, inner)]
    grad_queries = [low(nn(g, k) * scale) for g, k in zip(grad_scores, keys)]
    grad_keys = [low(tn(g, q) * scale) for g, q in zip(grad_scores, queries)]
    return grad_queries, grad_keys, grad_values


def side(ref, row, width, count):
    return jnp.concatenate([ref[row + b * width : row + (b + 1) * width, :] for b in range(count)], axis=1)


def rows_of(pair, size):
    return slice(pair * size, (pair + 1) * size)


def fetch(step, order, parts, buffer, sems):
    copies = [
        (order.index(quarter), pltpu.make_async_copy(ref, buffer.at[order.index(quarter), pl.ds(row, ref.shape[0])], sems.at[i]))
        for i, (quarter, row, ref) in enumerate(parts)
    ]
    copies.sort(key=lambda entry: entry[0])

    @pl.when(step == 0)
    def begin():
        for unused, copy in copies:
            copy.start()

    for at in range(QUARTERS):

        @pl.when(step == at)
        def arrive():
            for slot, copy in copies:
                if slot == at:
                    copy.wait()


def leave_quarter(step, buffer, near, keep, sems, copies):
    kept = [pltpu.make_async_copy(buffer.at[at], keep.at[at - 2], sems.at[at - 2]) for at in (2, 3)]
    for at in range(QUARTERS):

        @pl.when(step == at)
        def leave():
            (copies[at] if at < 2 else kept[at - 2]).start()

    @pl.when(step == QUARTERS - 1)
    def finish():
        for copy in list(copies) + kept:
            copy.wait()


def affine_row(gain, bias, norm):
    return gain[0, norm : norm + 1, :].astype(F32), bias[0, norm : norm + 1, :].astype(F32)


def leave_blocks(ref, row, value):
    size = value.shape[0]
    for b in range(value.shape[1] // BLOCK):
        ref[row + b * size : row + (b + 1) * size, :] = value[:, b * BLOCK : (b + 1) * BLOCK]


MESH = pl.DeviceIdType.MESH


def partners():
    t = lax.axis_index("tensor")
    return {"tensor": lax.bitwise_xor(t, 1)}, {"tensor": lax.bitwise_xor(t, 2)}, {"stream": lax.bitwise_xor(lax.axis_index("stream"), 1)}


def greet(*others):
    barrier = pltpu.get_barrier_semaphore()
    for other in others:
        pl.semaphore_signal(barrier, inc=1, device_id=other, device_id_type=MESH)
    pl.semaphore_wait(barrier, len(others))


def sender(send_sems, recv_sems):
    def copy(number, source, target, to):
        return pltpu.make_async_remote_copy(
            src_ref=source,
            dst_ref=target,
            send_sem=send_sems.at[number],
            recv_sem=recv_sems.at[number],
            device_id=to,
            device_id_type=MESH,
        )

    return copy


def pack(pieces, places, rest, ids):
    total = sum(m.size for m in pieces) // BLOCK
    cut, share = total - rest, rest // places

    def kernel(ids, *refs):
        sources, (own, first, mine) = refs[: len(pieces)], refs[len(pieces) :]
        row = 0
        for ref in sources:
            leave_blocks(own, row, ref[...])
            row += ref.size // BLOCK
        first[...] = own[0:cut, :]
        mine[...] = own[pl.ds(pl.multiple_of(cut + ids[1] * share, 16), share), :]

    return run(
        kernel,
        None,
        [s(ids)] + [w(m) for m in pieces],
        [w(shape(total, BLOCK)), w(shape(cut, BLOCK)), w(shape(share, BLOCK))],
        [],
        3,
    )


def cross_block(pairs, first, lengths, text, image, matrices, text_kept, image_kept, text_probs, image_probs, part):
    wq, wkv_text, wkv_image, wq_image, w_out, w_out_image = matrices
    text_low = text[...]
    image_low = image[...]
    text_kept[:, 0:256] = low(nn(text_low, wq[...]))
    text_kept[:, 256:768] = low(nn(text_low, wkv_text[...]))
    image_kept[:, 0:512] = low(nn(image_low, wkv_image[...]))
    image_kept[:, 512:768] = low(nn(image_low, wq_image[...]))

    image_mask = lax.broadcasted_iota(jnp.int32, (SLOTS, PADDED), 1) < REGIONS
    slots = lax.broadcasted_iota(jnp.int32, (PADDED, SLOTS), 1)
    units = [(p, h) for p in range(pairs) for h in range(2)]

    def text_part(at):
        return [text_kept[rows_of(p, SLOTS), at + h * HEAD : at + (h + 1) * HEAD] for p, h in units]

    def image_part(at):
        return [image_kept[rows_of(p, PADDED), at + h * HEAD : at + (h + 1) * HEAD] for p, h in units]

    scale = HEAD**-0.5
    probs, context = attend(text_part(0), image_part(0), image_part(256), scale, [image_mask] * len(units))
    for i, (p, h) in enumerate(units):
        text_probs[i] = probs[i]
        text_kept[rows_of(p, SLOTS), 768 + h * HEAD : 768 + (h + 1) * HEAD] = low(context[i])
    limits = [lengths[first + p] for p in range(pairs)]
    masks = [slots < limits[p] for p, h in units]
    probs, context = attend(image_part(512), text_part(256), text_part(512), scale, masks)
    for i, (p, h) in enumerate(units):
        image_probs[i] = probs[i]
        image_kept[rows_of(p, PADDED), 768 + h * HEAD : 768 + (h + 1) * HEAD] = low(context[i])
    leave_blocks(part, 0, low(nn(text_kept[:, 768:1024], w_out[...])))
    leave_blocks(part, 3 * text.shape[0], low(nn(image_kept[:, 768:1024], w_out_image[...])))


def cross_forward(pairs, lengths, text, image, *refs):
    matrices = refs[:6]
    text_pre, image_pre, image_own = refs[6:9]
    outs = refs[9:15]
    texts, images, text_kept, image_kept, text_probs, image_probs, parts, total, got, send_sems, recv_sems, out_sems = refs[15:]
    core, y, x = partners()
    copy = sender(send_sems, recv_sems)
    text_core = copy(0, text, texts.at[1], core)
    text_y = copy(1, text, texts.at[2], y)
    image_x = copy(2, image, images.at[0], x)
    image_core = copy(3, images.at[0], images.at[1], core)
    image_y = copy(4, images.at[0], images.at[2], y)
    text_corner = copy(5, texts.at[2], texts.at[3], core)
    image_corner = copy(6, images.at[2], images.at[3], core)
    near_part = copy(7, parts.at[1], got.at[0], core)
    corner_part = copy(8, parts.at[3], got.at[1], core)
    far_part = copy(9, total, got.at[2], y)

    greet(core, y, x)
    image_x.start()
    text_y.start()
    text_core.start()
    texts[0] = text[...]
    image_x.wait()
    image_y.start()
    image_core.start()

    def block(j, unused):
        @pl.when(j == 1)
        def near():
            text_core.wait()
            image_core.wait()

        @pl.when(j == 2)
        def far():
            text_y.wait()
            text_corner.start()
            image_y.wait()
            image_corner.start()

        @pl.when(j == 3)
        def corner():
            text_corner.wait()
            image_corner.wait()

        cross_block(
            pairs,
            lax.bitwise_xor(lax.axis_index("tensor"), j) * pairs,
            lengths,
            texts.at[j],
            images.at[j],
            matrices,
            text_kept.at[j],
            image_kept.at[j],
            text_probs.at[j],
            image_probs.at[j],
            parts.at[j],
        )

        @pl.when(j == 1)
        def near_done():
            near_part.start()

        return unused

    lax.fori_loop(0, QUARTERS, block, 0)
    corner_part.start()
    leaving = [
        pltpu.make_async_copy(source, out, out_sems.at[i])
        for i, (source, out) in enumerate(
            zip((texts, images, text_kept, image_kept, text_probs, image_probs), outs)
        )
    ]
    for leave in leaving:
        leave.start()
    corner_part.wait()
    total[...] = add(parts[2], got[1])
    far_part.start()
    near_part.wait()
    size, image_size = text.shape[0], image.shape[0]
    below = 3 * size
    image_own[...] = images[0]

    def summed(row, depth, count, start):
        for ref in (parts.at[0], got.at[0]):
            start = start + side(ref, row, depth, count).astype(F32)
        return start

    text_pre[...] = summed(0, size, 3, text[...].astype(F32))
    image_pre[...] = summed(below, image_size, 4, images[0].astype(F32))
    far_part.wait()
    text_pre[...] += side(got.at[2], 0, size, 3).astype(F32)
    image_pre[...] += side(got.at[2], below, image_size, 4).astype(F32)
    for leave in leaving:
        leave.wait()


def cross_block_back(pairs, grad, matrices, text_kept, image_kept, text_probs, image_probs, text_d, image_d, part):
    wq, wkv_text, wkv_image, wq_image, w_out, w_out_image = matrices
    text_rows, image_rows = text_kept.shape[0], image_kept.shape[0]
    text_dc = low(nt(side(grad, 0, text_rows, 3), w_out[...]))
    image_dc = low(nt(side(grad, 3 * text_rows, image_rows, 4), w_out_image[...]))
    units = [(p, h) for p in range(pairs) for h in range(2)]

    def text_part(at):
        return [text_kept[rows_of(p, SLOTS), at + h * HEAD : at + (h + 1) * HEAD] for p, h in units]

    def image_part(at):
        return [image_kept[rows_of(p, PADDED), at + h * HEAD : at + (h + 1) * HEAD] for p, h in units]

    scale = HEAD**-0.5
    outer = [text_dc[rows_of(p, SLOTS), h * HEAD : (h + 1) * HEAD] for p, h in units]
    probs = [text_probs[i] for i in range(len(units))]
    found = attend_back(text_part(0), image_part(0), image_part(256), probs, outer, scale)
    for i, (p, h) in enumerate(units):
        text_d[rows_of(p, SLOTS), h * HEAD : (h + 1) * HEAD] = found[0][i]
        image_d[rows_of(p, PADDED), h * HEAD : (h + 1) * HEAD] = found[1][i]
        image_d[rows_of(p, PADDED), 256 + h * HEAD : 256 + (h + 1) * HEAD] = found[2][i]
    outer = [image_dc[rows_of(p, PADDED), h * HEAD : (h + 1) * HEAD] for p, h in units]
    probs = [image_probs[i] for i in range(len(units))]
    found = attend_back(image_part(512), text_part(256), text_part(512), probs, outer, scale)
    for i, (p, h) in enumerate(units):
        image_d[rows_of(p, PADDED), 512 + h * HEAD : 512 + (h + 1) * HEAD] = found[0][i]
        text_d[rows_of(p, SLOTS), 256 + h * HEAD : 256 + (h + 1) * HEAD] = found[1][i]
        text_d[rows_of(p, SLOTS), 512 + h * HEAD : 512 + (h + 1) * HEAD] = found[2][i]
    text_dx = nt(text_d[:, 0:256], wq[...]) + nt(text_d[:, 256:768], wkv_text[...])
    image_dx = nt(image_d[:, 0:512], wkv_image[...]) + nt(image_d[:, 512:768], wq_image[...])
    leave_blocks(part, 0, low(text_dx))
    leave_blocks(part, 3 * text_rows, low(image_dx))


def cross_back(pairs, grad, vectors, text_kept, image_kept, text_probs, image_probs, *refs):
    matrices = refs[:6]
    grads_out, text_d_out, image_d_out, own_sum, total, vector_sum = refs[6:12]
    grads, text_d, image_d, parts, got, got_vectors, send_sems, recv_sems, out_sems = refs[12:]
    core, y, unused_x = partners()
    copy = sender(send_sems, recv_sems)
    to_core = copy(0, grad, grads.at[1], core)
    to_y = copy(1, grad, grads.at[2], y)
    corner = copy(2, grads.at[2], grads.at[3], core)
    near_part = copy(3, parts.at[1], got.at[0], core)
    corner_part = copy(4, parts.at[3], got.at[1], core)
    vectors_core = copy(5, vectors, got_vectors.at[0], core)
    vectors_y = copy(6, vector_sum, got_vectors.at[1], y)
    greet(core, y)
    vectors_core.start()
    to_y.start()
    to_core.start()
    grads[0] = grad[...]
    vectors_core.wait()
    vector_sum[...] = vectors[...] + got_vectors[0]
    vectors_y.start()

    def block(j, unused):
        @pl.when(j == 1)
        def near():
            to_core.wait()

        @pl.when(j == 2)
        def far():
            to_y.wait()
            corner.start()

        @pl.when(j == 3)
        def last():
            corner.wait()

        cross_block_back(
            pairs,
            grads.at[j],
            matrices,
            text_kept.at[j],
            image_kept.at[j],
            text_probs.at[j],
            image_probs.at[j],
            text_d.at[j],
            image_d.at[j],
            parts.at[j],
        )

        @pl.when(j == 1)
        def near_done():
            near_part.start()

        return unused

    lax.fori_loop(0, QUARTERS, block, 0)
    corner_part.start()
    leaving = [
        pltpu.make_async_copy(source, out, out_sems.at[i])
        for i, (source, out) in enumerate(((grads, grads_out), (text_d, text_d_out), (image_d, image_d_out)))
    ]
    for leave in leaving:
        leave.start()
    near_part.wait()
    own_sum[...] = parts[0].astype(F32) + got[0].astype(F32)
    vectors_y.wait()
    vector_sum[...] += got_vectors[1]
    corner_part.wait()
    total[...] = add(parts[2], got[1])
    for leave in leaving:
        leave.wait()


def cross_last(total, own_sum, vector_keep, vector_send, text_n, image_n, texts, images, grads, text_kept, image_kept, text_d, image_d, *refs):
    text_grad, image_grad, text_keep, text_send, image_keep, image_send = refs[:6]
    got, text_flip, text_g_flip, image_flip, image_g_flip, send_sems, recv_sems = refs[6:]
    unused_core, y, unused_x = partners()
    copy = sender(send_sems, recv_sems)
    far = copy(0, total, got, y)
    greet(y)
    far.start()
    size, image_size = texts.shape[1], images.shape[1]
    below = 3 * size
    for j in range(QUARTERS):
        text_flip[:, rows_of(j, size)] = texts[j].T
        image_flip[:, rows_of(j, image_size)] = images[j].T
        for b in range(3):
            text_g_flip[rows_of(b, BLOCK), rows_of(j, size)] = grads[j, rows_of(b, size), :].T
        for b in range(4):
            start = below + b * image_size
            image_g_flip[rows_of(b, BLOCK), rows_of(j, image_size)] = grads[j, start : start + image_size, :].T
    at = lax.axis_index("stream")
    for flip, g_flip, d, kept, keep, send in (
        (text_flip, text_g_flip, text_d, text_kept, text_keep, text_send),
        (image_flip, image_g_flip, image_d, image_kept, image_keep, image_send),
    ):
        dp = keep.shape[0]
        half = flip.shape[0] // 2
        depth = half // dp
        padded = -(-depth // 16) * 16
        rows = flip.shape[1]
        outer = d[...].reshape(rows, 768)
        context = kept[:, :, 768:1024].reshape(rows, 256)
        for out, apart in ((send, 1), (keep, 0)):
            start = pl.multiple_of(lax.bitwise_xor(at, apart) * half, 128)
            found = nn(flip[pl.ds(start, half), :], outer)
            last = nn(g_flip[pl.ds(start, half), :], context)
            for z in range(dp):
                taken = slice(z * depth, (z + 1) * depth)
                for b in range(3):
                    out[z, b * padded : b * padded + depth, :] = low(found[taken, b * BLOCK : (b + 1) * BLOCK])
                out[z, 3 * padded : 3 * padded + depth, :] = low(last[taken])
    for out, vector in ((text_keep, vector_keep), (text_send, vector_send)):
        below_all = out.shape[1] - vector.shape[1]
        for z in range(out.shape[0]):
            out[z, below_all:, :] = vector[z]
    far.wait()
    text_grad[...] = text_n[...] + side(own_sum, 0, size, 3) + side(got, 0, size, 3).astype(F32)
    image_grad[...] = low(image_n[...] + side(own_sum, below, image_size, 4) + side(got, below, image_size, 4).astype(F32))


def gate(hidden):
    half = 0.5 * (1.0 + lax.erf(hidden * (2.0**-0.5)))
    density = jnp.exp(-0.5 * hidden * hidden) * 0.3989422804014327
    return hidden * half, half + hidden * density


def mlp_forward(pairs, text_pre, image_pre, text_gain, text_bias, image_gain, image_bias, *refs):
    parts = refs[:6]
    text_low, image_low, text_next, image_next = refs[6:10]
    text_activ, text_slope, image_activ, image_slope = refs[10:14]
    weights, sems = refs[14:]
    step = pl.program_id(0)
    fetch(step, FORWARD, gathered(parts), weights, sems)

    @pl.when(step == 0)
    def begin():
        for pre, gain, bias, rounded, total in (
            (text_pre, text_gain, text_bias, text_low, text_next),
            (image_pre, image_gain, image_bias, image_low, image_next),
        ):
            g, b = affine_row(gain, bias, 0)
            one = normed(pre[...])[0] * g + b
            total[...] = one
            rounded[...] = low(one)

    w = weights.at[step]
    for b in range(3):
        activ, slope = gate(nn(text_low[...], w[b * 768 : (b + 1) * 768, :]))
        text_activ[0, :, b * 256 : (b + 1) * 256] = low(activ)
        text_slope[0, :, b * 256 : (b + 1) * 256] = low(slope)
    activ, slope = gate(nn(image_low[...], w[4608:5632, :]))
    image_activ[0] = low(activ)
    image_slope[0] = low(slope)
    text_next[...] += nn(text_activ[0], side(w, 2304, 768, 3))
    image_next[...] += nn(image_activ[0], side(w, 5632, 256, 4))


def lane_masks():
    lane = lax.broadcasted_iota(jnp.int32, (1, 2 * SELF_HEAD), 1)
    left = (lane < SELF_HEAD).astype(F32)
    return low(left), low(1.0 - left), lane < SELF_HEAD


def both_heads(tile, masks):
    return jnp.concatenate([tile * masks[0], tile * masks[1]], axis=0)


def one_tile(stacked, masks):
    return jnp.where(masks[2], stacked[:SLOTS], stacked[SLOTS:])


def self_forward(pairs, ids, lengths, text_pre, image_pre, text_gain, text_bias, image_gain, image_bias, text_cot, image_cot, *refs):
    parts = refs[:6]
    (
        text_out,
        image_out,
        text_grad,
        image_grad,
        text_vec,
        image_vec,
        rounded,
        text_q,
        text_k,
        text_v,
        text_c,
        text_probs,
        image_kept,
        image_probs,
    ) = refs[6:20]
    weights, text_sum, image_sum, text_low, image_low, sems = refs[20:]
    step = pl.program_id(0)
    fetch(step, FORWARD, gathered(parts), weights, sems)
    text_rows, image_rows = text_pre.shape[0], image_pre.shape[0]

    @pl.when(step == 0)
    def begin():
        for pre, gain, bias, total, lower, at in (
            (text_pre, text_gain, text_bias, text_sum, text_low, 0),
            (image_pre, image_gain, image_bias, image_sum, image_low, 6 * text_rows),
        ):
            g, b = affine_row(gain, bias, 1)
            two = normed(pre[...])[0] * g + b
            total[...] = two
            lower[...] = low(two)
            leave_blocks(rounded, at, low(two))

    w = weights.at[step]
    for n, out in enumerate((text_q, text_k, text_v)):
        wide = jnp.concatenate([w[b * 576 + n * 192 : b * 576 + (n + 1) * 192, :] for b in range(3)], axis=1)
        out[0] = low(nt(text_low[...], wide))
    for n in range(3):
        image_kept[0, :, n * 256 : (n + 1) * 256] = low(nn(image_low[...], w[2304 + n * 1024 : 3328 + n * 1024, :]))

    masks = lane_masks()
    slots = lax.broadcasted_iota(jnp.int32, (1, SLOTS), 1)
    base = ids[2]
    valid = [slots < lengths[base + p] for p in range(pairs)]
    first, last = slice(0, 128), slice(128, 192)
    queries, keys, values, limits = [], [], [], []
    for p in range(pairs):
        rows = rows_of(p, SLOTS)
        queries += [both_heads(text_q[0, rows, first], masks), text_q[0, rows, last]]
        keys += [text_k[0, rows, first], text_k[0, rows, last]]
        values += [text_v[0, rows, first], text_v[0, rows, last]]
        limits += [valid[p], valid[p]]
    probs, context = attend(queries, keys, values, SELF_HEAD**-0.5, limits)
    for p in range(pairs):
        rows = rows_of(p, SLOTS)
        text_probs[0, p, 0:256, :] = probs[2 * p]
        text_probs[0, p, 256:384, :] = probs[2 * p + 1]
        text_c[0, rows, first] = low(one_tile(context[2 * p], masks))
        text_c[0, rows, last] = low(context[2 * p + 1])

    image_mask = lax.broadcasted_iota(jnp.int32, (PADDED, PADDED), 1) < REGIONS
    units = [(p, h) for p in range(pairs) for h in range(2)]

    def image_part(at):
        return [image_kept[0, rows_of(p, PADDED), at + h * HEAD : at + (h + 1) * HEAD] for p, h in units]

    probs, context = attend(image_part(0), image_part(256), image_part(512), HEAD**-0.5, [image_mask] * len(units))
    for i, (p, h) in enumerate(units):
        image_probs[0, i] = probs[i]
        image_kept[0, rows_of(p, PADDED), 768 + h * HEAD : 768 + (h + 1) * HEAD] = low(context[i])

    text_sum[...] += nn(text_c[0], side(w, 1728, 192, 3))
    image_sum[...] += nn(image_kept[0, :, 768:1024], side(w, 5376, 256, 4))

    @pl.when(step == QUARTERS - 1)
    def finish():
        for total, gain, bias, cot, out, grad, vec, at in (
            (text_sum, text_gain, text_bias, text_cot, text_out, text_grad, text_vec, 3 * text_rows),
            (image_sum, image_gain, image_bias, image_cot, image_out, image_grad, image_vec, 6 * text_rows + 4 * image_rows),
        ):
            g, b = affine_row(gain, bias, 2)
            unit, scale = normed(total[...])
            out[...] = (unit * g + b).astype(out.dtype)
            back = norm_back(unit, scale, g, cot[...].astype(F32), vec)
            grad[...] = back
            leave_blocks(rounded, at, low(back))


def self_back(pairs, text_g, image_g, text_pre, image_pre, text_gain, image_gain, *refs):
    text_q, text_k, text_v, text_c, text_probs, image_kept, image_probs = refs[:7]
    parts = refs[7:13]
    text_n, image_n, text_vec, image_vec, near, keep = refs[13:19]
    weights, found, text_sum, image_sum, text_g_low, image_g_low, text_d, image_d, sems, out_sems, send_sems, recv_sems = refs[19:]
    step = pl.program_id(0)
    fetch(step, BACKWARD, gathered(parts), weights, sems)
    core = partners()[0]
    copy = sender(send_sems, recv_sems)

    @pl.when(step == 0)
    def begin():
        greet(core)
        text_sum[...] = text_g[...]
        image_sum[...] = image_g[...]
        text_g_low[...] = low(text_g[...])
        image_g_low[...] = low(image_g[...])

    w = weights.at[step]
    masks = lane_masks()
    first, last = slice(0, 128), slice(128, 192)
    text_dc = low(nt(text_g_low[...], side(w, 1728, 192, 3)))
    queries, keys, values, probs, outer = [], [], [], [], []
    for p in range(pairs):
        rows = rows_of(p, SLOTS)
        queries += [both_heads(text_q[0, rows, first], masks), text_q[0, rows, last]]
        keys += [text_k[0, rows, first], text_k[0, rows, last]]
        values += [text_v[0, rows, first], text_v[0, rows, last]]
        probs += [text_probs[0, p, 0:256, :], text_probs[0, p, 256:384, :]]
        outer += [both_heads(text_dc[rows, first], masks), text_dc[rows, last]]
    grad_q, grad_k, grad_v = attend_back(queries, keys, values, probs, outer, SELF_HEAD**-0.5)
    size = text_g.shape[0]
    for p in range(pairs):
        rows = rows_of(p, SLOTS)
        text_d[0, rows, first] = one_tile(grad_q[2 * p], masks)
        text_d[0, rows, last] = grad_q[2 * p + 1]
        for n, grad in ((1, grad_k), (2, grad_v)):
            text_d[n, rows, first] = grad[2 * p]
            text_d[n, rows, last] = grad[2 * p + 1]

    image_dc = low(nt(image_g_low[...], side(w, 5376, 256, 4)))
    units = [(p, h) for p in range(pairs) for h in range(2)]

    def image_part(at):
        return [image_kept[0, rows_of(p, PADDED), at + h * HEAD : at + (h + 1) * HEAD] for p, h in units]

    outer = [image_dc[rows_of(p, PADDED), h * HEAD : (h + 1) * HEAD] for p, h in units]
    given = attend_back(
        image_part(0), image_part(256), image_part(512), [image_probs[0, i] for i in range(len(units))], outer, HEAD**-0.5
    )
    for n in range(3):
        for i, (p, h) in enumerate(units):
            image_d[rows_of(p, PADDED), n * 256 + h * HEAD : n * 256 + (h + 1) * HEAD] = given[n][i]

    gained = text_sum[...]
    for n in range(3):
        wide = jnp.concatenate([w[b * 576 + n * 192 : b * 576 + (n + 1) * 192, :] for b in range(3)], axis=1)
        gained = gained + nn(text_d[n], wide)
    text_sum[...] = gained
    image_sum[...] += nt(image_d[...], side(w, 2304, 1024, 3))

    slot = found.at[step]
    slot[0:size, 0:128] = text_d[0, :, first]
    slot[0:size, 128:256] = text_d[1, :, first]
    slot[size : 2 * size, 0:128] = text_d[2, :, first]
    slot[size : 2 * size, 128:256] = text_c[0, :, first]
    slot[2 * size : 3 * size, 0:128] = jnp.concatenate([text_d[0, :, last], text_d[1, :, last]], axis=1)
    slot[2 * size : 3 * size, 128:256] = jnp.concatenate([text_d[2, :, last], text_c[0, :, last]], axis=1)
    leave_blocks(slot, 3 * size, image_d[...])
    leave_blocks(slot, 3 * size + 3 * image_g.shape[0], image_kept[0, :, 768:1024])
    leave_quarter(step, found, near, keep, out_sems, [copy(n, found.at[n], near.at[n], core) for n in range(2)])

    @pl.when(step == QUARTERS - 1)
    def finish():
        leave_norm(1, text_sum, image_sum, text_pre, image_pre, text_gain, image_gain, text_n, image_n, text_vec, image_vec)


def leave_norm(norm, text_sum, image_sum, text_pre, image_pre, text_gain, image_gain, text_n, image_n, text_vec, image_vec):
    for total, pre, gain, out, vec in (
        (text_sum, text_pre, text_gain, text_n, text_vec),
        (image_sum, image_pre, image_gain, image_n, image_vec),
    ):
        unit, scale = normed(pre[...])
        out[...] = norm_back(unit, scale, gain[0, norm : norm + 1, :].astype(F32), total[...], vec)


def mlp_back(pairs, text_g, image_g, text_one, image_one, text_pre, image_pre, text_gain, image_gain, *refs):
    text_activ, text_slope, image_activ, image_slope = refs[:4]
    parts = refs[4:10]
    text_n, image_n, next_low, text_vec, image_vec, rounded, rounded_near, near, keep = refs[10:19]
    weights, found, text_sum, image_sum, text_g_low, image_g_low, text_d, sems, out_sems, send_sems, recv_sems = refs[19:]
    step = pl.program_id(0)
    fetch(step, BACKWARD, gathered(parts), weights, sems)
    size, image_size = text_g.shape[0], image_g.shape[0]
    core = partners()[0]
    copy = sender(send_sems, recv_sems)
    rounded_copy = copy(2, rounded, rounded_near, core)

    @pl.when(step == 0)
    def begin():
        text_sum[...] = text_g[...]
        image_sum[...] = image_g[...]
        text_g_low[...] = low(text_g[...])
        image_g_low[...] = low(image_g[...])
        leave_blocks(rounded, 0, text_one[...])
        leave_blocks(rounded, 3 * size, text_g_low[...])
        leave_blocks(rounded, 6 * size, image_one[...])
        leave_blocks(rounded, 6 * size + 4 * image_size, image_g_low[...])
        greet(core)
        rounded_copy.start()

    w = weights.at[step]
    slot = found.at[step]
    wide = side(w, 2304, 768, 3)
    for b in range(3):
        columns = slice(b * 256, (b + 1) * 256)
        back = nt(text_g_low[...], wide[columns])
        text_d[:, columns] = low(back * text_slope[0, :, columns].astype(F32))
    text_sum[...] += nt(text_d[...], side(w, 0, 768, 3))
    image_d = low(nt(image_g_low[...], side(w, 5632, 256, 4)) * image_slope[0].astype(F32))
    image_sum[...] += nt(image_d, w[4608:5632, :])
    leave_blocks(slot, 0, text_d[...])
    leave_blocks(slot, 3 * size, text_activ[0])
    leave_blocks(slot, 6 * size, image_d)
    leave_blocks(slot, 6 * size + image_size, image_activ[0])
    leave_quarter(step, found, near, keep, out_sems, [copy(n, found.at[n], near.at[n], core) for n in range(2)])

    @pl.when(step == QUARTERS - 1)
    def finish():
        rounded_copy.wait()
        leave_norm(0, text_sum, image_sum, text_pre, image_pre, text_gain, image_gain, text_n, image_n, text_vec, image_vec)
        leave_blocks(next_low, 0, low(text_n[...]))
        leave_blocks(next_low, 3 * size, low(image_n[...]))


def weight_grad(is_self, sizes, x_at, own, near, own_quarters, near_quarters, *refs):
    if is_self:
        to_x, own_top, to_z, text_flip, text_g_flip, image_flip, image_g_flip = refs
    else:
        to_y, own_top, to_x, own_bottom, text_flip, text_g_flip, image_flip, image_g_flip = refs
    size, image_size = sizes
    dp = own_top.shape[1]
    x = x_at[0]
    for at, source in ((0, own), (1, near)):
        rows, image_rows = rows_of(at, size), rows_of(at, image_size)
        for b in range(3):
            text_flip[rows_of(b, BLOCK), rows] = source[rows_of(b, size), :].T
            text_g_flip[rows_of(b, BLOCK), rows] = source[rows_of(3 + b, size), :].T
        for b in range(4):
            start = 6 * size
            image_flip[rows_of(b, BLOCK), image_rows] = source[start + b * image_size : start + (b + 1) * image_size, :].T
            start = 6 * size + 4 * image_size
            image_g_flip[rows_of(b, BLOCK), image_rows] = source[start + b * image_size : start + (b + 1) * image_size, :].T

    text_depth, image_depth = DT // (2 * dp), DV // (2 * dp)
    padded = -(-text_depth // 16) * 16

    def write(ref, at, row, depth, value):
        for z in range(dp):
            ref[at, z, row : row + depth, :] = low(value[z * depth : (z + 1) * depth])

    lane = lax.broadcasted_iota(jnp.int32, (1, HEAD), 1) < SELF_HEAD
    for slot in (1, 0):

        def text_block(b):
            return jnp.concatenate([q[slot, rows_of(b, size), :] for q in (own_quarters, near_quarters)], axis=0)

        def image_block(b, text_blocks):
            start = text_blocks * size + b * image_size
            return jnp.concatenate([q[slot, start : start + image_size, :] for q in (own_quarters, near_quarters)], axis=0)

        for apart in range(2):
            half = lax.bitwise_xor(x, apart)
            text_rows = pl.ds(pl.multiple_of(half * (DT // 2), 128), DT // 2)
            image_rows = pl.ds(pl.multiple_of(half * (DV // 2), 128), DV // 2)
            if is_self:
                top, top_at = (to_x, slot) if apart else (own_top, slot)
            else:
                top, top_at = (to_y, apart) if slot else (own_top, apart)
                bottom, bottom_at = (to_x, slot) if apart else (own_bottom, slot)
            text_lhs, image_lhs = text_flip[text_rows, :], image_flip[image_rows, :]
            text_g_lhs, image_g_lhs = text_g_flip[text_rows, :], image_g_flip[image_rows, :]
            if is_self:
                one, two, three = text_block(0), text_block(1), text_block(2)
                write(top, top_at, 0, text_depth, nn(text_lhs, one))
                mixed = jnp.concatenate([nn(text_lhs, two[:, :HEAD]), nn(text_g_lhs, two[:, HEAD:])], axis=1)
                write(top, top_at, padded, text_depth, mixed)
                from_x = nn(text_lhs, three)
                from_g = nn(text_g_lhs, three[:, HEAD:])
                mixed = jnp.concatenate([from_x[:, :HEAD], jnp.where(lane, from_x[:, HEAD:], from_g)], axis=1)
                write(top, top_at, 2 * padded, text_depth, mixed)
                write(top, top_at, 3 * padded, image_depth, nn(image_lhs, image_block(0, 3)))
                for b in range(3):
                    found = nn(image_g_lhs if b == 2 else image_lhs, image_block(1 + b, 3))
                    row = ((2 * slot + apart) * 3 + b) * image_depth
                    for z in range(dp):
                        to_z[z, row : row + image_depth, :] = low(found[z * image_depth : (z + 1) * image_depth])
            else:
                for b in range(3):
                    write(top, top_at, b * padded, text_depth, nn(text_lhs, text_block(b)))
                    write(bottom, bottom_at, b * padded, text_depth, nn(text_g_lhs, text_block(3 + b)))
                write(top, top_at, 3 * padded, image_depth, nn(image_lhs, image_block(0, 6)))
                write(bottom, bottom_at, 3 * padded, image_depth, nn(image_g_lhs, image_block(1, 6)))


def gathered(parts):
    own, near, far, far_rest, corner, corner_rest = parts
    cut = far.shape[0]
    return ((0, 0, own), (1, 0, near), (2, 0, far), (2, cut, far_rest), (3, 0, corner), (3, cut, corner_rest))


ANY = pl.BlockSpec(memory_space=pl.ANY)
SCALARS = pl.BlockSpec(memory_space=pltpu.SMEM)


def whole(array):
    zeros = (0,) * len(array.shape)
    return pl.BlockSpec(array.shape, lambda *s: zeros)


def quarter(array, order):
    tail = (0,) * (len(array.shape) - 1)
    if order is FORWARD:
        return pl.BlockSpec((1,) + array.shape[1:], lambda s: (s,) + tail)
    return pl.BlockSpec((1,) + array.shape[1:], lambda s: (lax.rem(2 * s + 1 - lax.div(s, 2), 4),) + tail)


def shape(*dims, of=BF):
    return jax.ShapeDtypeStruct(dims, of)


def run(kernel, order, operands, outs, scratch, us, meeting=None):
    def spec(kind, array):
        return {"s": lambda: SCALARS, "w": lambda: whole(array), "q": lambda: quarter(array, order), "a": lambda: ANY}[kind]()

    return pl.pallas_call(
        kernel,
        grid=(QUARTERS,) if order else (1,),
        in_specs=[spec(*entry) for entry in operands],
        out_specs=[spec(*entry) for entry in outs],
        out_shape=[array for unused, array in outs],
        scratch_shapes=scratch,
        compiler_params=pltpu.CompilerParams(
            dimension_semantics=("arbitrary",),
            vmem_limit_bytes=60 * 2**20,
            collective_id=meeting,
            has_side_effects=meeting is not None,
        ),
        cost_estimate=pl.CostEstimate(flops=int(us * 1.1e9), bytes_accessed=1024, transcendentals=0),
    )(*[array for unused, array in operands])


def swap(value, axis, apart):
    return lax.ppermute(value, axis, [(i, i ^ apart) for i in range(lax.axis_size(axis))])


def after(value, *earlier):
    return lax.optimization_barrier((value,) + earlier)[0]


class Line:
    def __init__(self):
        self.last = ()

    def take(self, value):
        return after(value, *self.last)

    def leave(self, *values):
        self.last = values


def spread(packed, share):
    own, first, unused = packed
    far_rest = lax.all_gather(share, ("stream", "dp"), axis=0, tiled=True)
    return own, swap(own, "tensor", 1), swap(first, "tensor", 2), far_rest


def spread_on(line, own, near, far, far_rest):
    far, far_rest = line.take((far, far_rest))
    return own, near, far, far_rest, swap(far, "tensor", 1), swap(far_rest, "tensor", 1)


def add(left, right):
    return low(left.astype(F32) + right.astype(F32))


def fold_first(to_y, own_top, to_x, own_bottom):
    return swap(to_y, "tensor", 2), swap(to_x, "stream", 1), own_top, own_bottom


def fold_second(by_y, by_x, own_top, own_bottom):
    return add(own_top[1], by_y[1]), add(own_bottom[1], by_x[1])


def fold_third(first, second):
    by_y, by_x, own_top, own_bottom = first
    then_x, then_y = second

    def three(own, one, two):
        return low(own.astype(F32) + one.astype(F32) + two.astype(F32))

    return jnp.concatenate([three(own_top[0], by_y[0], then_x), three(own_bottom[0], by_x[0], then_y)], axis=1)


def fold_last(total):
    return lax.psum_scatter(total, "dp", scatter_dimension=0, tiled=True)[0]


def s(value):
    return ("s", value)


def w(value):
    return ("w", value)


def q(value):
    return ("q", value)


def a(value):
    return ("a", value)


def local(
    text_in,
    image_in,
    lengths,
    text_cot,
    image_cot,
    text_cross_q,
    text_cross_kv,
    text_cross_out,
    text_up,
    text_down,
    text_self_qkv,
    text_self_out,
    text_gain,
    text_bias,
    image_cross_q,
    image_cross_kv,
    image_cross_out,
    image_up,
    image_down,
    image_self_qkv,
    image_self_out,
    image_gain,
    image_bias,
):
    dp = lax.axis_size("dp")
    places = 2 * dp
    x_at = lax.axis_index("stream")
    t_at = lax.axis_index("tensor")
    size = text_in.shape[0]
    pairs = size // SLOTS
    image_size = pairs * PADDED
    units = 2 * pairs
    ids = jnp.stack([x_at, x_at * dp + lax.axis_index("dp")] + [(t_at ^ j) * pairs for j in range(QUARTERS)]).astype(jnp.int32)

    def spaced(rows):
        apart = jnp.pad(rows.reshape(pairs, REGIONS, DV), ((0, 0), (0, PADDED - REGIONS), (0, 0)))
        return apart.reshape(image_size, DV)

    def leave(rows):
        return swap(rows.reshape(pairs, PADDED, DV)[:, :REGIONS].reshape(pairs * REGIONS, DV), "stream", 1).astype(F32)

    line = Line()
    mlp_packed = pack([text_up[0], text_down[0], image_up[0], image_down[0]], places, 5120, ids)
    cross_w = (
        text_cross_q[0],
        image_cross_kv[0].reshape(DT, -1),
        text_cross_kv[0].reshape(DV, -1),
        image_cross_q[0],
        text_cross_out[0],
        image_cross_out[0],
    )
    self_packed = pack(
        [
            text_self_qkv[0].transpose(1, 2, 0).reshape(-1, DT),
            text_self_out[0],
            image_self_qkv[0].reshape(DV, -1),
            image_self_out[0],
        ],
        places,
        4608,
        after(ids, mlp_packed[0]),
    )
    line.leave(self_packed[0], cross_w[1], cross_w[2])
    mlp_share = line.take(swap(mlp_packed[2], "tensor", 2))
    self_share = line.take(swap(self_packed[2], "tensor", 2))
    line.leave(mlp_share, self_share)
    mlp_w = spread(mlp_packed, mlp_share)
    self_w = spread(self_packed, after(self_share, mlp_share))
    image_cot_here = swap(spaced(image_cot), "stream", 1)

    text_wide, image_wide = shape(size, DT, of=F32), shape(image_size, DV, of=F32)
    text_f32, image_f32 = pltpu.VMEM((size, DT), F32), pltpu.VMEM((image_size, DV), F32)
    text_bf, image_bf = pltpu.VMEM((size, DT), BF), pltpu.VMEM((image_size, DV), BF)
    in_sems, out_sems = pltpu.SemaphoreType.DMA((6,)), pltpu.SemaphoreType.DMA((2,))
    text_affine = [w(text_gain), w(text_bias)]
    image_affine = [w(image_gain), w(image_bias)]
    vector_outs = [w(shape(2, DT, of=F32)), w(shape(2, DV, of=F32))]
    part_rows = 3 * size + 4 * image_size

    def buffer(weights):
        return pltpu.VMEM((QUARTERS, weights[0].shape[0], BLOCK), BF)

    in_four = [
        (QUARTERS, size, DT),
        (QUARTERS, image_size, DV),
        (QUARTERS, size, 1024),
        (QUARTERS, image_size, 1024),
        (QUARTERS, units, SLOTS, PADDED),
        (QUARTERS, units, PADDED, SLOTS),
    ]

    def links(count):
        return [pltpu.SemaphoreType.DMA((count,)), pltpu.SemaphoreType.DMA((count,))]

    text_pre1, image_pre1, image, texts, images, *cross_kept = run(
        functools.partial(cross_forward, pairs),
        None,
        [s(lengths), w(line.take(text_in)), w(spaced(image_in))] + [w(m) for m in cross_w],
        [w(text_wide), w(image_wide), w(shape(image_size, DV))] + [a(shape(*dims)) for dims in in_four],
        [pltpu.VMEM(dims, BF) for dims in in_four]
        + [pltpu.VMEM((QUARTERS, part_rows, BLOCK), BF), pltpu.VMEM((part_rows, BLOCK), BF), pltpu.VMEM((3, part_rows, BLOCK), BF)]
        + links(10)
        + [pltpu.SemaphoreType.DMA((6,))],
        70,
        1,
    )
    line.leave(text_pre1, image_cot_here)
    mlp_w = spread_on(line, *mlp_w)
    (
        text_one,
        image_one,
        text_pre2,
        image_pre2,
        text_activ,
        text_slope,
        image_activ,
        image_slope,
    ) = run(
        functools.partial(mlp_forward, pairs),
        FORWARD,
        [w(text_pre1), w(image_pre1)] + text_affine + image_affine + [a(m) for m in mlp_w],
        [
            w(shape(size, DT)),
            w(shape(image_size, DV)),
            w(text_wide),
            w(image_wide),
            q(shape(QUARTERS, size, 768)),
            q(shape(QUARTERS, size, 768)),
            q(shape(QUARTERS, image_size, 256)),
            q(shape(QUARTERS, image_size, 256)),
        ],
        [buffer(mlp_w), in_sems],
        15,
    )
    line.leave(text_pre2)
    self_w = spread_on(line, *self_w)
    (
        text_out,
        image_out,
        text_n3,
        image_n3,
        text_vec3,
        image_vec3,
        self_rounded,
        self_q,
        self_k,
        self_v,
        self_c,
        self_probs,
        self_kept,
        self_image_probs,
    ) = run(
        functools.partial(self_forward, pairs),
        FORWARD,
        [s(ids), s(lengths), w(text_pre2), w(image_pre2)]
        + text_affine
        + image_affine
        + [w(text_cot), w(image_cot_here)]
        + [a(m) for m in self_w],
        [w(text_wide), w(shape(image_size, DV)), w(text_wide), w(image_wide)]
        + vector_outs
        + [
            w(shape(2 * part_rows, BLOCK)),
            q(shape(QUARTERS, size, 192)),
            q(shape(QUARTERS, size, 192)),
            q(shape(QUARTERS, size, 192)),
            q(shape(QUARTERS, size, 192)),
            q(shape(QUARTERS, pairs, 384, SLOTS)),
            q(shape(QUARTERS, image_size, 1024)),
            q(shape(QUARTERS, units, PADDED, PADDED)),
        ],
        [buffer(self_w), text_f32, image_f32, text_bf, image_bf, in_sems],
        19,
    )
    image_out = leave(image_out)

    text_depth, image_depth = DT // places, DV // places
    padded = -(-text_depth // 16) * 16

    def back_scratch(weights, rows):
        return [
            buffer(weights),
            pltpu.VMEM((QUARTERS, rows, BLOCK), BF),
            text_f32,
            image_f32,
            text_bf,
            image_bf,
        ]

    def weight_grads(is_self, turn, rounded, rounded_near, kept, kept_near):
        top = 3 * padded + image_depth
        if is_self:
            outs = [w(shape(2, dp, top, BLOCK)), w(shape(2, dp, top, BLOCK)), w(shape(dp, 12 * image_depth, BLOCK))]
        else:
            outs = [w(shape(2, dp, top, BLOCK))] * 4
        return run(
            functools.partial(weight_grad, is_self, (size, image_size)),
            None,
            [s(turn), w(rounded), w(rounded_near), w(kept), w(kept_near)],
            outs,
            [
                pltpu.VMEM((DT, 2 * size), BF),
                pltpu.VMEM((DT, 2 * size), BF),
                pltpu.VMEM((DV, 2 * image_size), BF),
                pltpu.VMEM((DV, 2 * image_size), BF),
            ],
            12,
        )

    self_rows = 3 * size + 4 * image_size
    self_rounded_near = swap(self_rounded, "tensor", 1)
    text_n2, image_n2, text_vec2, image_vec2, self_near, self_keep = run(
        functools.partial(self_back, pairs),
        BACKWARD,
        [
            w(text_n3),
            w(image_n3),
            w(text_pre2),
            w(image_pre2),
            w(text_gain),
            w(image_gain),
            q(self_q),
            q(self_k),
            q(self_v),
            q(self_c),
            q(self_probs),
            q(self_kept),
            q(self_image_probs),
        ]
        + [a(m) for m in self_w],
        [w(text_wide), w(image_wide)] + vector_outs + [a(shape(2, self_rows, BLOCK)), a(shape(2, self_rows, BLOCK))],
        back_scratch(self_w, self_rows)
        + [pltpu.VMEM((3, size, 192), BF), pltpu.VMEM((image_size, 768), BF), in_sems, out_sems]
        + links(2),
        23,
        2,
    )
    to_x, self_top, to_z = weight_grads(True, ids, self_rounded, self_rounded_near, self_keep, self_near)
    self_by_x = swap(to_x, "stream", 1)
    self_bottom = fold_last(to_z)
    line.leave(self_top)
    mlp_rows = 6 * size + 2 * image_size
    text_n1, image_n1, grad_low, text_vec1, image_vec1, mlp_rounded, mlp_rounded_near, mlp_near, mlp_keep = run(
        functools.partial(mlp_back, pairs),
        BACKWARD,
        [
            w(text_n2),
            w(image_n2),
            w(text_one),
            w(image_one),
            w(text_pre1),
            w(image_pre1),
            w(line.take(text_gain)),
            w(image_gain),
            q(text_activ),
            q(text_slope),
            q(image_activ),
            q(image_slope),
        ]
        + [a(m) for m in mlp_w],
        [w(text_wide), w(image_wide), w(shape(part_rows, BLOCK))]
        + vector_outs
        + [
            w(shape(2 * part_rows, BLOCK)),
            a(shape(2 * part_rows, BLOCK)),
            a(shape(2, mlp_rows, BLOCK)),
            a(shape(2, mlp_rows, BLOCK)),
        ],
        back_scratch(mlp_w, mlp_rows) + [text_bf, in_sems, out_sems] + links(3),
        20,
        3,
    )
    line.leave(grad_low)
    mlp_first = fold_first(
        *weight_grads(False, line.take(ids), mlp_rounded, mlp_rounded_near, mlp_keep, mlp_near)
    )
    line.leave(mlp_first[2])
    self_top, self_by_x = line.take((self_top, self_by_x))
    self_top, to_y = add(self_top[0], self_by_x[0]), add(self_top[1], self_by_x[1])
    self_then_y = swap(to_y, "tensor", 2)
    line.leave(self_top, to_y)
    d_dims = [(QUARTERS, part_rows, BLOCK), (QUARTERS, size, 768), (QUARTERS, image_size, 768)]
    vectors = jnp.concatenate(
        [jnp.pad(v, ((0, 0), (0, DV - DT))) for v in (text_vec1, text_vec2, text_vec3)]
        + [image_vec1, image_vec2, image_vec3, jnp.zeros((4, DV), F32)],
        axis=0,
    )
    grads, text_d, image_d, own_sum, total, vectors = run(
        functools.partial(cross_back, pairs),
        None,
        [w(line.take(grad_low)), w(vectors)] + [w(k) for k in cross_kept] + [w(m) for m in cross_w],
        [a(shape(*dims)) for dims in d_dims]
        + [w(shape(part_rows, BLOCK, of=F32)), w(shape(part_rows, BLOCK)), w(shape(16, DV, of=F32))],
        [pltpu.VMEM(dims, BF) for dims in d_dims]
        + [pltpu.VMEM((QUARTERS, part_rows, BLOCK), BF), pltpu.VMEM((2, part_rows, BLOCK), BF), pltpu.VMEM((2, 16, DV), F32)]
        + links(7)
        + [pltpu.SemaphoreType.DMA((3,))],
        48,
        4,
    )
    line.leave(total)
    self_top = add(self_top, line.take(self_then_y))
    self_bottom = line.take(self_bottom).reshape(2, 2, 3 * image_depth, BLOCK)
    self_bottom_x = swap(self_bottom[:, 1], "stream", 1)
    line.leave(self_top)
    text_only, image_only = 4 * padded + 16, 4 * image_depth
    text_vector = jnp.pad(vectors[:6, :DT].reshape(6, places, text_depth), ((0, 0), (0, 0), (0, BLOCK - text_depth)))
    image_vector = jnp.pad(vectors[6:].reshape(10, places, image_depth), ((0, 0), (0, 0), (0, BLOCK - image_depth)))
    vectors = low(jnp.concatenate([text_vector, image_vector], axis=0).transpose(1, 0, 2))
    vector_keep = lax.dynamic_slice_in_dim(vectors, x_at * dp, dp, 0)
    vector_send = lax.dynamic_slice_in_dim(vectors, (1 - x_at) * dp, dp, 0)
    text_grad, image_grad, text_keep, text_send, image_keep, image_send = run(
        cross_last,
        None,
        [
            w(line.take(total)),
            w(own_sum),
            w(vector_keep),
            w(vector_send),
            w(text_n1),
            w(image_n1),
            w(texts),
            w(images),
            w(grads),
            w(cross_kept[0]),
            w(cross_kept[1]),
            w(text_d),
            w(image_d),
        ],
        [
            w(text_wide),
            w(shape(image_size, DV)),
            w(shape(dp, text_only, BLOCK)),
            w(shape(dp, text_only, BLOCK)),
            w(shape(dp, image_only, BLOCK)),
            w(shape(dp, image_only, BLOCK)),
        ],
        [
            pltpu.VMEM((part_rows, BLOCK), BF),
            pltpu.VMEM((DT, QUARTERS * size), BF),
            pltpu.VMEM((DT, QUARTERS * size), BF),
            pltpu.VMEM((DV, QUARTERS * image_size), BF),
            pltpu.VMEM((DV, QUARTERS * image_size), BF),
        ]
        + links(1),
        30,
        5,
    )
    line.leave(text_grad)
    self_top = fold_last(self_top)
    sums = fold_second(*line.take(mlp_first))
    line.leave(*sums)
    mlp_second = swap(sums[0], "stream", 1), swap(sums[1], "tensor", 2)
    self_bottom = add(self_bottom[:, 0], line.take(self_bottom_x))
    self_bottom = add(self_bottom[0], swap(self_bottom[1], "tensor", 2))
    mlp_total = fold_third(mlp_first, line.take(mlp_second))
    line.leave(mlp_total, self_bottom)
    mlp_grads = fold_last(after(mlp_total, self_top))
    cross_text = add(text_keep, line.take(swap(text_send, "stream", 1)))
    line.leave(cross_text)
    cross_text = fold_last(after(cross_text, mlp_grads))
    cross_image = add(image_keep, line.take(swap(image_send, "stream", 1)))
    line.leave(cross_image)
    cross_image = fold_last(after(cross_image, cross_text))
    self_grads = jnp.concatenate([self_top, self_bottom], axis=0)
    image_grad = leave(image_grad)

    def pick(packed, first, count, depth, stride):
        rows = [packed[first + b * stride : first + b * stride + depth] for b in range(count)]
        return jnp.concatenate(rows, axis=1).astype(F32)

    def text_pick(packed, first, count):
        return pick(packed, first, count, text_depth, padded)

    def image_pick(packed, first, count):
        return pick(packed, first, count, image_depth, image_depth)

    sums = cross_text[4 * padded :].astype(F32)
    text_vectors, image_vectors = sums[:6, :text_depth], sums[6:12, :image_depth]

    self_text = text_pick(self_grads, 0, 3)

    def heads(at):
        return jnp.concatenate([self_text[:, at * 128 : (at + 1) * 128], self_text[:, 512 + at * 64 : 576 + at * 64]], axis=1)

    below = 3 * padded
    return (
        text_out,
        image_out,
        text_grad,
        image_grad,
        text_pick(cross_text, 0, 1)[None],
        image_pick(cross_image, 0, 2).reshape(1, image_depth, 2, 256),
        text_pick(cross_text, 3 * padded, 1).T[None],
        text_pick(mlp_grads, 0, 3)[None],
        text_pick(mlp_grads, below + image_depth, 3).T[None],
        jnp.stack([heads(n) for n in range(3)], axis=1)[None],
        heads(3).T[None],
        text_vectors[0::2][None],
        text_vectors[1::2][None],
        image_pick(cross_image, 2 * image_depth, 1)[None],
        text_pick(cross_text, padded, 2).reshape(1, text_depth, 2, 256),
        image_pick(cross_image, 3 * image_depth, 1).T[None],
        image_pick(mlp_grads, below, 1)[None],
        image_pick(mlp_grads, 2 * below + image_depth, 1).T[None],
        image_pick(self_grads, below, 3).reshape(1, image_depth, 3, 256),
        image_pick(self_grads, below + 3 * image_depth, 1).T[None],
        image_vectors[0::2][None],
        image_vectors[1::2][None],
    )


def solution(mesh):
    rows = P(("stream", "dp", "tensor"), None)
    wide_in = P(None, None, "tensor")
    group_in = P(None, None, None, "tensor")
    wide_out = P(None, "tensor", None)
    grad_in = P(None, ("stream", "dp"), "tensor")
    grad_group = P(None, ("stream", "dp"), None, "tensor")
    grad_out = P(None, "tensor", ("stream", "dp"))
    vector = P(None, None, ("stream", "dp"))
    weights = (wide_in, group_in, wide_out, wide_in, wide_out, group_in, wide_out, P(), P())
    grads = (grad_in, grad_group, grad_out, grad_in, grad_out, grad_group, grad_out, vector, vector)
    return jax.shard_map(
        local,
        mesh=mesh,
        in_specs=(rows, rows, P(("stream", "dp")), rows, rows) + weights + weights,
        out_specs=(rows, rows, rows, rows) + grads + grads,
        check_vma=False,
    )
```

time: 571 us -> 535 us (0.937)
  Pallas kernels: 134 us -> 313 us
  waiting for transfers between devices: 255 us -> 128 us
  other arithmetic: 67.4 us -> 23.8 us
  local copies, waits for them, and re-layouts: 57.4 us -> 24.8 us
  blocking collectives: 6.16 us -> 0 us
    pallas_call x6 -> x11, Pallas kernels: 134 us -> 313 us  [run(): pl.pallas_call(kernel, grid=(QUARTERS,) if order else (1,), in_specs=[spe...]
    ppermute x34 -> x24, waiting for transfers between devices: 220 us -> 86.7 us  [swap(): lax.ppermute(value, axis, [(i, i ^ apart) for i in range(lax.axis_size(ax...]
    convert_element_type x18 -> x9, other arithmetic: 48.1 us -> 11.3 us  [low(): return value.astype(BF)]
    unnamed x111 -> x61, local copies, waits for them, and re-layouts: 35.2 us -> 13.9 us
    all_gather x3 -> x2, waiting for transfers between devices: 19.6 us -> 29.5 us  [spread(): far_rest = lax.all_gather(share, ('stream', 'dp'), axis=0, tiled=True)]
    slice x12 -> x8, local copies, waits for them, and re-layouts: 10.5 us -> 1.92 us  [the longest x2 1.8 us: pick(): packed[first + b * stride:first + b * stride + depth]]
    psum x1 -> x0, blocking collectives: 6.16 us -> none  [local(): lax.psum(jnp.concatenate([vec_rows, vec_image], axis=0).transpose(1, 0, 2...]
    ppermute x34 -> x24, starting transfers between devices: 29.5 us -> 24.5 us  [swap(): lax.ppermute(value, axis, [(i, i ^ apart) for i in range(lax.axis_size(ax...]
  transfers between devices with their start and end apart: 41 -> 31, of which waited for: 19 -> 15; matrix products, arithmetic and copies ran while one was open for 18% -> 8% of each run, Pallas kernels for 15% -> 52%
where the time goes in v2:
time: 535 us; the launch traced here: 530 us
  Pallas kernels  313 us (59%)
  waiting for transfers between devices  128 us (24%)
  starting transfers between devices  25 us (5%)
  local copies, waits for them, and re-layouts  24.8 us (5%)
  other arithmetic  23.8 us (4%)
  between operations  14.8 us (3%)
    pallas_call x11, Pallas kernels, run(): pl.pallas_call(kernel, grid=(QUARTERS,) if order else (1,), in_specs=[spe...  313 us
    ppermute x24, waiting for transfers between devices, swap(): lax.ppermute(value, axis, [(i, i ^ apart) for i in range(lax.axis_size(ax...  86.7 us
    all_gather x2, waiting for transfers between devices, spread(): far_rest = lax.all_gather(share, ('stream', 'dp'), axis=0, tiled=True)  29.5 us
    ppermute x24, starting transfers between devices, swap(): lax.ppermute(value, axis, [(i, i ^ apart) for i in range(lax.axis_size(ax...  24.5 us
    unnamed x61, local copies, waits for them, and re-layouts  13.9 us
    reduce_scatter x5, waiting for transfers between devices, fold_last(): return lax.psum_scatter(total, 'dp', scatter_dimension=0, tiled=True)[0]  11.8 us
    convert_element_type x9, other arithmetic, low(): return value.astype(BF)  11.3 us
  transfers between devices with their start and end apart: 31, of which 15 were waited for; matrix products, arithmetic and copies ran while one was open for 8% of the time, Pallas kernels for 52%

profile of v2, /device:TPU:0, one launch (start us, length us, event | category | flops | bytes accessed | tf_op | source)
XLA Modules:
  0.0 529.8 jit_solution(12066339912238084345)
XLA Ops:
  7.9 4.2 shard_map.390
  12.1 3.0 collective-permute-start
  15.9 1.6 copy.59.refs_2_
  17.5 4.1 shard_map.391
  21.7 1.9 collective-permute-start.3
  28.6 3.2 collective-permute-done.1
  32.6 76.3 %shard_map.392 = (f32[512,768]{1,0:T(8,128)}, f32[192,1024]{1,0:T(8,128)}, bf16[192,1024]{1,0:T(8,128)(2,1)}, bf16[4,512,768]{2,1,0:T(8,128)(2,1)}, bf16[4,192,1...) custom-call(s32[16]{0:T(128)} %lengths.3, ...), custom_call_target="tpu_custom_call" | custom-call | flops 76999999488 | bytes 1024 | tf_op jit(solution)/shard_map/pallas_call | solution.py:852
  111.6 5.0 collective-permute-done.5.refs_4_.refs_8_
  116.6 14.2 %shard_map.393 = (bf16[512,768]{1,0:T(8,128)(2,1)}, bf16[192,1024]{1,0:T(8,128)(2,1)}, f32[512,768]{1,0:T(8,128)}, f32[192,1024]{1,0:T(8,128)}, bf16[4,512,768]{...) custom-call(f32[512,768]{1,0:T(8,128)} %get-tuple-element.126.text_pre, ...), custom_call_target="tpu_custom_call" | custom-call | flops 16499999744 | bytes 1024 | tf_op jit(solution)/shard_map/pallas_call | solution.py:852
  130.8 2.2 collective-permute-done.8.refs_2_.refs_9_
  133.1 29.5 %all-gather.5.cloned.1.call-done.refs_3_.refs_10_ = bf16[4608,256]{1,0:T(8,128)(2,1)} async-done(((bf16[576,256]{1,0:T(8,128)(2,1)}), bf16[4608,256]{1,0:T(8,128)(2,1)}) %all-gather.5.cloned.1.call-update) | async-done | bytes 2359312 | tf_op jit(solution)/shard_map/all_gather | solution.py:890
  163.1 5.7 %collective-permute-done.9.refs_4_.refs_11_ = bf16[1792,256]{1,0:T(8,128)(2,1)} collective-permute-done((bf16[1792,256]{1,0:T(8,128)(2,1)}, bf16[1792,256]{1,0:T(8,128)(2,1)}, u32[]{:S(2)}, u32[]{:S(2)}) %collective-permute-start.9) | collective-permute-done | bytes 917536 | tf_op jit(solution)/shard_map/ppermute | solution.py:870
  168.8 19.8 %shard_map.394 = (f32[512,768]{1,0:T(8,128)}, bf16[192,1024]{1,0:T(8,128)(2,1)}, f32[512,768]{1,0:T(8,128)}, f32[192,1024]{1,0:T(8,128)}, f32[2,768]{1,0:T(2,128...) custom-call(s32[6]{0:T(128)} %stack.39.ids.x_at, ...), custom_call_target="tpu_custom_call" | custom-call | flops 20899999744 | bytes 1024 | tf_op jit(solution)/shard_map/pallas_call | solution.py:852
  188.8 23.3 %shard_map.395 = (f32[512,768]{1,0:T(8,128)}, f32[192,1024]{1,0:T(8,128)}, f32[2,768]{1,0:T(2,128)}, f32[2,1024]{1,0:T(2,128)}, bf16[2,2304,256]{2,1,0:T(8,128)(2,1)}, /*index=5*/bf16[2,2304,256]{2,1,0:T(8,128)(2,1)}) custom-call(f32[512,768]{1,0:T(8,128)} %get-tuple-element.139.text_g, f32[192,1024]{1,0:T(8,128)} %get-tuple-element.140.image_g, ...), custom_call_target="tpu_custom_call" | custom-call | flops 25300000768 | bytes 1024 | tf_op jit(solution)/shard_map/pallas_call | solution.py:852
  214.2 12.7 %shard_map.396 = (bf16[2,4,416,256]{3,2,1,0:T(8,128)(2,1)}, bf16[2,4,416,256]{3,2,1,0:T(8,128)(2,1)}, bf16[4,1536,256]{2,1,0:T(8,128)(2,1)}) custom-call(s32[6]{0:T(128)} %stack.39.ids.x_at, bf16[4608,256]{1,0:T(8,128)(2,1)} %get-tuple-element.152.own, bf16[4608,256]{1,0:T(8,128)(2,1)} %copy-done.20, bf16[2,2304,256]{2,1,0:T(8,128)(2,1)} %get-tuple-element.153.own_quarters, ...), custom_call_target="tpu_custom_call" | custom-call | flops 13200000000 | bytes 1024 | tf_op jit(solution)/shard_map/pallas_call | solution.py:852
  227.4 20.5 %shard_map.397 = (f32[512,768]{1,0:T(8,128)}, f32[192,1024]{1,0:T(8,128)}, bf16[2304,256]{1,0:T(8,128)(2,1)}, f32[2,768]{1,0:T(2,128)}, f32[2,1024]{1,0:T(2,128)...) custom-call(f32[512,768]{1,0:T(8,128)} %get-tuple-element.148.text_g, ...), custom_call_target="tpu_custom_call" | custom-call | flops 22000001024 | bytes 1024 | tf_op jit(solution)/shard_map/pallas_call | solution.py:852
  248.8 13.0 %shard_map.398 = (bf16[2,4,416,256]{3,2,1,0:T(8,128)(2,1)}, bf16[2,4,416,256]{3,2,1,0:T(8,128)(2,1)}, bf16[2,4,416,256]{3,2,1,0:T(8,128)(2,1)}, bf16[2,4,416,256]{3,2,1,0:T(8,128)(2,1)}) custom-call(s32[6]{0:T(128)} %stack.39.ids.x_at, bf16[4608,256]{1,0:T(8,128)(2,1)} %get-tuple-element.164.own, bf16[4608,256]{1,0:T(8,128)(2,1)} %get-tuple-element.165.near, ...), custom_call_target="tpu_custom_call" | custom-call | flops 13200000000 | bytes 1024 | tf_op jit(solution)/shard_map/pallas_call | solution.py:852
  266.5 1.8 fusion.3
  268.3 2.4 collective-permute-start.14
  270.6 86.1 %shard_map.399 = (bf16[4,2304,256]{2,1,0:T(8,128)(2,1)}, bf16[4,512,768]{2,1,0:T(8,128)(2,1)}, bf16[4,192,768]{2,1,0:T(8,128)(2,1)}, f32[2304,256]{1,0:T(8,128)}...) custom-call(bf16[2304,256]{1,0:T(8,128)(2,1)} %get-tuple-element.171.grad, f32[16,1024]{1,0:T(8,128)} %concatenate.79.vectors, ...), custom_call_target="tpu_custom_call" | custom-call | flops 52800000000 | bytes 1024 | tf_op jit(solution)/shard_map/pallas_call | solution.py:852
  359.5 39.1 %shard_map.400 = (f32[512,768]{1,0:T(8,128)}, bf16[192,1024]{1,0:T(8,128)(2,1)}, bf16[4,400,256]{2,1,0:T(8,128)(2,1)}, bf16[4,400,256]{2,1,0:T(8,128)(2,1)}, bf1...) custom-call(bf16[2304,256]{1,0:T(8,128)(2,1)} %get-tuple-element.184.total, ...), custom_call_target="tpu_custom_call" | custom-call | flops 32999999488 | bytes 1024 | tf_op jit(solution)/shard_map/pallas_call | solution.py:852
  404.6 15.6 %collective-permute-done.20 = bf16[4,416,256]{2,1,0:T(8,128)(2,1)S(1)} collective-permute-done((bf16[4,416,256]{2,1,0:T(8,128)(2,1)S(1)}, bf16[4,416,256]{2,1,0:T(8,128)(2,1)S(1)}, u32[]{:S(2)}, u32[]{:S(2)}) %collective-permute-start.20) | collective-permute-done | bytes 852000 | tf_op jit(solution)/shard_map/ppermute | solution.py:870
  420.2 2.6 collective-permute-done.19
  422.9 2.1 fusion
  429.6 10.0 %collective-permute-done.21 = bf16[2,384,256]{2,1,0:T(8,128)(2,1)S(1)} collective-permute-done((bf16[2,384,256]{2,1,0:T(8,128)(2,1)S(1)}, bf16[2,384,256]{2,1,0:T(8,128)(2,1)S(1)}, u32[]{:S(2)}, u32[]{:S(2)}) %collective-permute-start.21) | collective-permute-done | bytes 393248 | tf_op jit(solution)/shard_map/ppermute | solution.py:870
  441.4 5.1 collective-permute-done.22
  446.5 7.6 %collective-permute-done.16 = bf16[4,400,256]{2,1,0:T(8,128)(2,1)S(1)} collective-permute-done((bf16[4,400,256]{2,1,0:T(8,128)(2,1)S(1)}, bf16[4,400,256]{2,1,0:T(8,128)(2,1)S(1)}, u32[]{:S(2)}, u32[]{:S(2)}) %collective-permute-start.16) | collective-permute-done | bytes 819232 | tf_op jit(solution)/shard_map/ppermute | solution.py:870
  459.3 6.6 %collective-permute-done.11 = bf16[148,1024]{1,0:T(8,128)(2,1)S(1)} collective-permute-done((bf16[148,1024]{1,0:T(8,128)(2,1)S(1)}, bf16[148,1024]{1,0:T(8,128)(2,1)S(1)}, u32[]{:S(2)}, u32[]{:S(2)}) %collective-permute-start.11) | collective-permute-done | bytes 303136 | tf_op jit(solution)/shard_map/ppermute | solution.py:870
  466.8 5.8 %collective-permute-done.15 = bf16[148,1024]{1,0:T(8,128)(2,1)S(1)} collective-permute-done((bf16[148,1024]{1,0:T(8,128)(2,1)S(1)}, bf16[148,1024]{1,0:T(8,128)(2,1)S(1)}, u32[]{:S(2)}, u32[]{:S(2)}) %collective-permute-start.15) | collective-permute-done | bytes 303136 | tf_op jit(solution)/shard_map/ppermute | solution.py:870
  474.5 16.8 %collective-permute-done.23 = bf16[4,512,256]{2,1,0:T(8,128)(2,1)S(1)} collective-permute-done((bf16[4,512,256]{2,1,0:T(8,128)(2,1)}, bf16[4,512,256]{2,1,0:T(8,128)(2,1)S(1)}, u32[]{:S(2)}, u32[]{:S(2)}) %collective-permute-start.23) | collective-permute-done | bytes 1048608 | tf_op jit(solution)/shard_map/ppermute | solution.py:870
  506.6 11.8 %reduce-scatter.10.cloned.1.call-done = bf16[1,512,256]{2,1,0:T(8,128)(2,1)} async-done(((bf16[4,512,256]{2,1,0:T(8,128)(2,1)}), bf16[1,512,256]{2,1,0:T(8,128)(2,1)}) %reduce-scatter.10.cloned.1.call-update) | async-done | bytes 262160 | tf_op jit(solution)/shard_map/reduce_scatter | solution.py:922
  518.3 1.6 convert_bitcast_fusion.2
  (172 shorter events, 59.7 us)
Async XLA Ops:
  7.2 101.9 %all-gather.3.cloned.1.call-start = ((), (), s32[]{:S(2)}) async-start(), calls=%async_computation.5 | async-start | bytes 2949120 | tf_op jit(solution)/shard_map/all_gather | solution.py:890
  12.1 19.7 %collective-permute-start = (bf16[640,256]{1,0:T(8,128)(2,1)}, bf16[640,256]{1,0:T(8,128)(2,1)S(1)}, u32[]{:S(2)}, u32[]{:S(2)}) collective-permute-start(bf16[640,256]{1,0:T(8,128)(2,1)} %get-tuple-element.118), channel_id=1, source_target_pairs={{0,2},{1,3},{2,0},{3,1},{4,6},{5,7},{6,4},{7,5},{8,10},{9,11},{10,... | collective-permute-start | bytes 983048 | tf_op jit(solution)/shard_map/ppermute | solution.py:870
  21.6 10.1 %collective-permute-start.1 = (bf16[576,256]{1,0:T(8,128)(2,1)}, bf16[576,256]{1,0:T(8,128)(2,1)S(1)}, u32[]{:S(2)}, u32[]{:S(2)}) collective-permute-start(bf16[576,256]{1,0:T(8,128)(2,1)} %get-tuple-element.123), channel_id=1, source_target_pairs={{0,2},{1,3},{2,0},{3,1},{4,6},{5,7},{6,4},{7,5},{8,10},{9,11},{10,... | collective-permute-start | bytes 884744 | tf_op jit(solution)/shard_map/ppermute | solution.py:870
  21.7 89.9 %collective-permute-start.2 = (bf16[6656,256]{1,0:T(8,128)(2,1)}, bf16[6656,256]{1,0:T(8,128)(2,1)}, u32[]{:S(2)}, u32[]{:S(2)}) collective-permute-start(bf16[6656,256]{1,0:T(8,128)(2,1)} %get-tuple-element.119.refs_0_.refs_4_), channel_id=1, source_target_pairs={{0,1},{1,0},{2,3},{3,2},{4,5},{5,4},{6,7},{7,6},{8,9},{9,8},{10,11... | collective-permute-start | bytes 10223624 | tf_op jit(solution)/shard_map/ppermute | solution.py:870
  21.7 87.3 %collective-permute-start.3 = (bf16[1536,256]{1,0:T(8,128)(2,1)}, bf16[1536,256]{1,0:T(8,128)(2,1)}, u32[]{:S(2)}, u32[]{:S(2)}) collective-permute-start(bf16[1536,256]{1,0:T(8,128)(2,1)} %get-tuple-element.128), channel_id=1, source_target_pairs={{0,2},{1,3},{2,0},{3,1},{4,6},{5,7},{6,4},{7,5},{8,10},{9,11},{10,... | collective-permute-start | bytes 2359304 | tf_op jit(solution)/shard_map/ppermute | solution.py:870
  23.8 85.2 %collective-permute-start.4 = (bf16[192,1024]{1,0:T(8,128)(2,1)S(1)}, bf16[192,1024]{1,0:T(8,128)(2,1)S(1)}, u32[]{:S(2)}, u32[]{:S(2)}) collective-permute-start(bf16[192,1024]{1,0:T(8,128)(2,1)S(1)} %bitcast.166), channel_id=1, source_target_pairs={{0,16},{16,0},{1,17},{17,1},{2,18},{18,2},{3,19},{19,3},{4,20},{20... | collective-permute-start | bytes 1179656 | tf_op jit(solution)/shard_map/ppermute | solution.py:870
  31.8 77.2 %copy-start.12 = (bf16[576,256]{1,0:T(8,128)(2,1)}, bf16[576,256]{1,0:T(8,128)(2,1)S(1)}, u32[]{:S(2)}) copy-start(bf16[576,256]{1,0:T(8,128)(2,1)S(1)} %collective-permute-done.1) | copy-start | bytes 884740
  32.6 130.0 %all-gather.5.cloned.1.call-start = ((), (), s32[]{:S(2)}) async-start(), calls=%async_computation.6 | async-start | bytes 2654208 | tf_op jit(solution)/shard_map/all_gather | solution.py:890
  109.1 7.6 %collective-permute-start.6 = (bf16[5120,256]{1,0:T(8,128)(2,1)}, bf16[5120,256]{1,0:T(8,128)(2,1)}, u32[]{:S(2)}, u32[]{:S(2)}) collective-permute-start(bf16[5120,256]{1,0:T(8,128)(2,1)} %all-gather.3.cloned.1.call-done.refs_3_.refs_7_), channel_id=1, source_target_pairs={{0,1},{1,0},{2,3},{3,2},{4,5},{5,4},{6,7},{7,6},{8,9},{9,8},{10,11... | collective-permute-start | bytes 7864328 | tf_op jit(solution)/shard_map/ppermute | solution.py:870
  109.2 317.2 %reduce-scatter.6.cloned.1.call-start = ((), (), s32[]{:S(2)}) async-start(), calls=%async_computation.7 | async-start | bytes 3932160 | tf_op jit(solution)/shard_map/reduce_scatter | solution.py:922
  109.8 6.9 %collective-permute-start.5 = (bf16[1536,256]{1,0:T(8,128)(2,1)}, bf16[1536,256]{1,0:T(8,128)(2,1)}, u32[]{:S(2)}, u32[]{:S(2)}) collective-permute-start(bf16[1536,256]{1,0:T(8,128)(2,1)} %collective-permute-done.3.refs_2_.refs_6_), channel_id=1, source_target_pairs={{0,1},{1,0},{2,3},{3,2},{4,5},{5,4},{6,7},{7,6},{8,9},{9,8},{10,11... | collective-permute-start | bytes 2359304 | tf_op jit(solution)/shard_map/ppermute | solution.py:870
  110.0 53.1 %collective-permute-start.7 = (bf16[6400,256]{1,0:T(8,128)(2,1)}, bf16[6400,256]{1,0:T(8,128)(2,1)S(1)}, u32[]{:S(2)}, u32[]{:S(2)}) collective-permute-start(bf16[6400,256]{1,0:T(8,128)(2,1)} %get-tuple-element.121.refs_0_.refs_7_), channel_id=1, source_target_pairs={{0,1},{1,0},{2,3},{3,2},{4,5},{5,4},{6,7},{7,6},{8,9},{9,8},{10,11... | collective-permute-start | bytes 9830408 | tf_op jit(solution)/shard_map/ppermute | solution.py:870
  110.3 22.8 %collective-permute-start.8 = (bf16[1792,256]{1,0:T(8,128)(2,1)}, bf16[1792,256]{1,0:T(8,128)(2,1)}, u32[]{:S(2)}, u32[]{:S(2)}) collective-permute-start(bf16[1792,256]{1,0:T(8,128)(2,1)} %get-tuple-element.133), channel_id=1, source_target_pairs={{0,2},{1,3},{2,0},{3,1},{4,6},{5,7},{6,4},{7,5},{8,10},{9,11},{10,... | collective-permute-start | bytes 2752520 | tf_op jit(solution)/shard_map/ppermute | solution.py:870
  162.6 6.2 %collective-permute-start.10 = (bf16[4608,256]{1,0:T(8,128)(2,1)}, bf16[4608,256]{1,0:T(8,128)(2,1)}, u32[]{:S(2)}, u32[]{:S(2)}) collective-permute-start(bf16[4608,256]{1,0:T(8,128)(2,1)} %all-gather.5.cloned.1.call-done.refs_3_.refs_10_), channel_id=1, source_target_pairs={{0,1},{1,0},{2,3},{3,2},{4,5},{5,4},{6,7},{7,6},{8,9},{9,8},{10,11... | collective-permute-start | bytes 7077896 | tf_op jit(solution)/shard_map/ppermute | solution.py:870
  162.6 6.2 %collective-permute-start.9 = (bf16[1792,256]{1,0:T(8,128)(2,1)}, bf16[1792,256]{1,0:T(8,128)(2,1)}, u32[]{:S(2)}, u32[]{:S(2)}) collective-permute-start(bf16[1792,256]{1,0:T(8,128)(2,1)} %collective-permute-done.8.refs_2_.refs_9_), channel_id=1, source_target_pairs={{0,1},{1,0},{2,3},{3,2},{4,5},{5,4},{6,7},{7,6},{8,9},{9,8},{10,11... | collective-permute-start | bytes 2752520 | tf_op jit(solution)/shard_map/ppermute | solution.py:870
  188.6 24.2 %collective-permute-start.12 = (bf16[4608,256]{1,0:T(8,128)(2,1)}, bf16[4608,256]{1,0:T(8,128)(2,1)S(1)}, u32[]{:S(2)}, u32[]{:S(2)}) collective-permute-start(bf16[4608,256]{1,0:T(8,128)(2,1)} %get-tuple-element.152.own), channel_id=1, source_target_pairs={{0,1},{1,0},{2,3},{3,2},{4,5},{5,4},{6,7},{7,6},{8,9},{9,8},{10,11... | collective-permute-start | bytes 7077896 | tf_op jit(solution)/shard_map/ppermute | solution.py:870
  226.9 39.6 %collective-permute-start.13 = (bf16[2,4,416,256]{3,2,1,0:T(8,128)(2,1)}, bf16[2,4,416,256]{3,2,1,0:T(8,128)(2,1)}, u32[]{:S(2)}, u32[]{:S(2)}) collective-permute-start(bf16[2,4,416,256]{3,2,1,0:T(8,128)(2,1)} %get-tuple-element.162), channel_id=1, source_target_pairs={{0,16},{16,0},{1,17},{17,1},{2,18},{18,2},{3,19},{19,3},{4,20},{20... | collective-permute-start | bytes 5111816 | tf_op jit(solution)/shard_map/ppermute | solution.py:870
  248.7 224.8 %reduce-scatter.14.cloned.1.call-start = ((), (), s32[]{:S(2)}) async-start(), calls=%async_computation.11 | async-start | bytes 1064960 | tf_op jit(solution)/shard_map/reduce_scatter | solution.py:922
  261.8 136.8 %collective-permute-start.17 = (bf16[2,4,416,256]{3,2,1,0:T(8,128)(2,1)}, bf16[2,4,416,256]{3,2,1,0:T(8,128)(2,1)}, u32[]{:S(2)}, u32[]{:S(2)}) collective-permute-start(bf16[2,4,416,256]{3,2,1,0:T(8,128)(2,1)} %get-tuple-element.198), channel_id=1, source_target_pairs={{0,2},{1,3},{2,0},{3,1},{4,6},{5,7},{6,4},{7,5},{8,10},{9,11},{10,... | collective-permute-start | bytes 5111816 | tf_op jit(solution)/shard_map/ppermute | solution.py:870
  263.3 135.3 %collective-permute-start.18 = (bf16[2,4,416,256]{3,2,1,0:T(8,128)(2,1)}, bf16[2,4,416,256]{3,2,1,0:T(8,128)(2,1)}, u32[]{:S(2)}, u32[]{:S(2)}) collective-permute-start(bf16[2,4,416,256]{3,2,1,0:T(8,128)(2,1)} %get-tuple-element.199), channel_id=1, source_target_pairs={{0,16},{16,0},{1,17},{17,1},{2,18},{18,2},{3,19},{19,3},{4,20},{20... | collective-permute-start | bytes 5111816 | tf_op jit(solution)/shard_map/ppermute | solution.py:870
  268.3 90.1 %collective-permute-start.14 = (bf16[4,416,256]{2,1,0:T(8,128)(2,1)S(1)}, bf16[4,416,256]{2,1,0:T(8,128)(2,1)S(1)}, u32[]{:S(2)}, u32[]{:S(2)}) collective-permute-start(bf16[4,416,256]{2,1,0:T(8,128)(2,1)S(1)} %get-tuple-element.258), channel_id=1, source_target_pairs={{0,2},{1,3},{2,0},{3,1},{4,6},{5,7},{6,4},{7,5},{8,10},{9,11},{10,... | collective-permute-start | bytes 2555912 | tf_op jit(solution)/shard_map/ppermute | solution.py:870
  398.7 96.2 %reduce-scatter.12.cloned.1.call-start = ((), (), s32[]{:S(2)}) async-start(), calls=%async_computation.10 | async-start | bytes 2129920 | tf_op jit(solution)/shard_map/reduce_scatter | solution.py:922
  400.2 20.1 %collective-permute-start.20 = (bf16[4,416,256]{2,1,0:T(8,128)(2,1)S(1)}, bf16[4,416,256]{2,1,0:T(8,128)(2,1)S(1)}, u32[]{:S(2)}, u32[]{:S(2)}) collective-permute-start(bf16[4,416,256]{2,1,0:T(8,128)(2,1)S(1)} %fusion.5), channel_id=1, source_target_pairs={{0,2},{1,3},{2,0},{3,1},{4,6},{5,7},{6,4},{7,5},{8,10},{9,11},{10,... | collective-permute-start | bytes 2555912 | tf_op jit(solution)/shard_map/ppermute | solution.py:870
  403.1 19.8 %collective-permute-start.19 = (bf16[4,416,256]{2,1,0:T(8,128)(2,1)S(1)}, bf16[4,416,256]{2,1,0:T(8,128)(2,1)S(1)}, u32[]{:S(2)}, u32[]{:S(2)}) collective-permute-start(bf16[4,416,256]{2,1,0:T(8,128)(2,1)S(1)} %fusion.4), channel_id=1, source_target_pairs={{0,16},{16,0},{1,17},{17,1},{2,18},{18,2},{3,19},{19,3},{4,20},{20... | collective-permute-start | bytes 2555912 | tf_op jit(solution)/shard_map/ppermute | solution.py:870
  426.3 74.8 %reduce-scatter.8.cloned.1.call-start = ((), (), s32[]{:S(2)}) async-start(), calls=%async_computation.8 | async-start | bytes 1024000 | tf_op jit(solution)/shard_map/reduce_scatter | solution.py:922
  427.5 12.1 %collective-permute-start.21 = (bf16[2,384,256]{2,1,0:T(8,128)(2,1)S(1)}, bf16[2,384,256]{2,1,0:T(8,128)(2,1)S(1)}, u32[]{:S(2)}, u32[]{:S(2)}) collective-permute-start(bf16[2,384,256]{2,1,0:T(8,128)(2,1)S(1)} %slice_bitcast_fusion), channel_id=1, source_target_pairs={{0,16},{16,0},{1,17},{17,1},{2,18},{18,2},{3,19},{19,3},{4,20},{20... | collective-permute-start | bytes 1179656 | tf_op jit(solution)/shard_map/ppermute | solution.py:870
  429.0 25.1 %collective-permute-start.16 = (bf16[4,400,256]{2,1,0:T(8,128)(2,1)S(1)}, bf16[4,400,256]{2,1,0:T(8,128)(2,1)S(1)}, u32[]{:S(2)}, u32[]{:S(2)}) collective-permute-start(bf16[4,400,256]{2,1,0:T(8,128)(2,1)S(1)} %copy-done.21), channel_id=1, source_target_pairs={{0,16},{16,0},{1,17},{17,1},{2,18},{18,2},{3,19},{19,3},{4,20},{20... | collective-permute-start | bytes 2457608 | tf_op jit(solution)/shard_map/ppermute | solution.py:870
  440.7 5.7 %collective-permute-start.22 = (bf16[384,256]{1,0:T(8,128)(2,1)S(1)}, bf16[384,256]{1,0:T(8,128)(2,1)S(1)}, u32[]{:S(2)}, u32[]{:S(2)}) collective-permute-start(bf16[384,256]{1,0:T(8,128)(2,1)S(1)} %slice_bitcast_fusion.2), channel_id=1, source_target_pairs={{0,2},{1,3},{2,0},{3,1},{4,6},{5,7},{6,4},{7,5},{8,10},{9,11},{10,... | collective-permute-start | bytes 589832 | tf_op jit(solution)/shard_map/ppermute | solution.py:870
  455.3 63.0 %reduce-scatter.10.cloned.1.call-start = ((), (), s32[]{:S(2)}) async-start(), calls=%async_computation.9 | async-start | bytes 1310720 | tf_op jit(solution)/shard_map/reduce_scatter | solution.py:922
  455.5 10.4 %collective-permute-start.11 = (bf16[148,1024]{1,0:T(8,128)(2,1)S(1)}, bf16[148,1024]{1,0:T(8,128)(2,1)S(1)}, u32[]{:S(2)}, u32[]{:S(2)}) collective-permute-start(bf16[148,1024]{1,0:T(8,128)(2,1)S(1)} %reshape.279), channel_id=1, source_target_pairs={{0,16},{16,0},{1,17},{17,1},{2,18},{18,2},{3,19},{19,3},{4,20},{20... | collective-permute-start | bytes 909320 | tf_op jit(solution)/shard_map/ppermute | solution.py:870
  457.2 15.3 %collective-permute-start.15 = (bf16[148,1024]{1,0:T(8,128)(2,1)S(1)}, bf16[148,1024]{1,0:T(8,128)(2,1)S(1)}, u32[]{:S(2)}, u32[]{:S(2)}) collective-permute-start(bf16[148,1024]{1,0:T(8,128)(2,1)S(1)} %reshape.283), channel_id=1, source_target_pairs={{0,16},{16,0},{1,17},{17,1},{2,18},{18,2},{3,19},{19,3},{4,20},{20... | collective-permute-start | bytes 909320 | tf_op jit(solution)/shard_map/ppermute | solution.py:870
  457.8 33.4 %collective-permute-start.23 = (bf16[4,512,256]{2,1,0:T(8,128)(2,1)}, bf16[4,512,256]{2,1,0:T(8,128)(2,1)S(1)}, u32[]{:S(2)}, u32[]{:S(2)}) collective-permute-start(bf16[4,512,256]{2,1,0:T(8,128)(2,1)} %get-tuple-element.212), channel_id=1, source_target_pairs={{0,16},{16,0},{1,17},{17,1},{2,18},{18,2},{3,19},{19,3},{4,20},{20... | collective-permute-start | bytes 3145736 | tf_op jit(solution)/shard_map/ppermute | solution.py:870
  (22 other events, 262.7 us)
Sparse Core Ops, SparseCore 0:
  32.7 56.1 all-gather.2
  109.3 53.2 all-gather.4
  248.8 59.7 reduce-scatter.5
  398.8 23.5 reduce-scatter.13
  426.4 35.8 reduce-scatter.11
  464.6 22.7 reduce-scatter.7
  492.6 25.6 reduce-scatter.9

commit v3 on v2

--- a/solution.py
+++ b/solution.py
@@ -426,12 +426,13 @@
 
 
 def cross_last(total, own_sum, vector_keep, vector_send, text_n, image_n, texts, images, grads, text_kept, image_kept, text_d, image_d, *refs):
-    text_grad, image_grad, text_keep, text_send, image_keep, image_send = refs[:6]
-    got, text_flip, text_g_flip, image_flip, image_g_flip, send_sems, recv_sems = refs[6:]
-    unused_core, y, unused_x = partners()
+    text_grad, image_grad, text_keep, image_keep, image_send = refs[:5]
+    got, text_send, text_got, text_flip, text_g_flip, image_flip, image_g_flip, send_sems, recv_sems = refs[5:]
+    unused_core, y, x = partners()
     copy = sender(send_sems, recv_sems)
     far = copy(0, total, got, y)
-    greet(y)
+    text_x = copy(1, text_send, text_got, x)
+    greet(y, x)
     far.start()
     size, image_size = texts.shape[1], images.shape[1]
     below = 3 * size
@@ -464,10 +465,14 @@
                 for b in range(3):
                     out[z, b * padded : b * padded + depth, :] = low(found[taken, b * BLOCK : (b + 1) * BLOCK])
                 out[z, 3 * padded : 3 * padded + depth, :] = low(last[taken])
-    for out, vector in ((text_keep, vector_keep), (text_send, vector_send)):
-        below_all = out.shape[1] - vector.shape[1]
-        for z in range(out.shape[0]):
-            out[z, below_all:, :] = vector[z]
+        if flip is text_flip:
+            for out, vector in ((text_keep, vector_keep), (text_send, vector_send)):
+                below_all = out.shape[1] - vector.shape[1]
+                for z in range(dp):
+                    out[z, below_all:, :] = vector[z]
+            text_x.start()
+    text_x.wait()
+    text_keep[...] = add(text_keep[...], text_got[...])
     far.wait()
     text_grad[...] = text_n[...] + side(own_sum, 0, size, 3) + side(got, 0, size, 3).astype(F32)
     image_grad[...] = low(image_n[...] + side(own_sum, below, image_size, 4) + side(got, below, image_size, 4).astype(F32))
@@ -750,12 +755,9 @@
 
 
 def weight_grad(is_self, sizes, x_at, own, near, own_quarters, near_quarters, *refs):
-    if is_self:
-        to_x, own_top, to_z, text_flip, text_g_flip, image_flip, image_g_flip = refs
-    else:
-        to_y, own_top, to_x, own_bottom, text_flip, text_g_flip, image_flip, image_g_flip = refs
+    to_send, kept, to_z, text_flip, text_g_flip, image_flip, image_g_flip = refs
     size, image_size = sizes
-    dp = own_top.shape[1]
+    dp = kept.shape[1]
     x = x_at[0]
     for at, source in ((0, own), (1, near)):
         rows, image_rows = rows_of(at, size), rows_of(at, image_size)
@@ -789,34 +791,33 @@
             half = lax.bitwise_xor(x, apart)
             text_rows = pl.ds(pl.multiple_of(half * (DT // 2), 128), DT // 2)
             image_rows = pl.ds(pl.multiple_of(half * (DV // 2), 128), DV // 2)
-            if is_self:
-                top, top_at = (to_x, slot) if apart else (own_top, slot)
-            else:
-                top, top_at = (to_y, apart) if slot else (own_top, apart)
-                bottom, bottom_at = (to_x, slot) if apart else (own_bottom, slot)
             text_lhs, image_lhs = text_flip[text_rows, :], image_flip[image_rows, :]
             text_g_lhs, image_g_lhs = text_g_flip[text_rows, :], image_g_flip[image_rows, :]
+
+            def bottom(b, count, value):
+                row = ((2 * slot + apart) * count + b) * image_depth
+                for z in range(dp):
+                    to_z[z, row : row + image_depth, :] = low(value[z * image_depth : (z + 1) * image_depth])
+
             if is_self:
+                top, at = (to_send if slot else kept), apart
                 one, two, three = text_block(0), text_block(1), text_block(2)
-                write(top, top_at, 0, text_depth, nn(text_lhs, one))
+                write(top, at, 0, text_depth, nn(text_lhs, one))
                 mixed = jnp.concatenate([nn(text_lhs, two[:, :HEAD]), nn(text_g_lhs, two[:, HEAD:])], axis=1)
-                write(top, top_at, padded, text_depth, mixed)
+                write(top, at, padded, text_depth, mixed)
                 from_x = nn(text_lhs, three)
                 from_g = nn(text_g_lhs, three[:, HEAD:])
                 mixed = jnp.concatenate([from_x[:, :HEAD], jnp.where(lane, from_x[:, HEAD:], from_g)], axis=1)
-                write(top, top_at, 2 * padded, text_depth, mixed)
-                write(top, top_at, 3 * padded, image_depth, nn(image_lhs, image_block(0, 3)))
+                write(top, at, 2 * padded, text_depth, mixed)
+                write(top, at, 3 * padded, image_depth, nn(image_lhs, image_block(0, 3)))
                 for b in range(3):
-                    found = nn(image_g_lhs if b == 2 else image_lhs, image_block(1 + b, 3))
-                    row = ((2 * slot + apart) * 3 + b) * image_depth
-                    for z in range(dp):
-                        to_z[z, row : row + image_depth, :] = low(found[z * image_depth : (z + 1) * image_depth])
+                    bottom(b, 3, nn(image_g_lhs if b == 2 else image_lhs, image_block(1 + b, 3)))
             else:
-                for b in range(3):
-                    write(top, top_at, b * padded, text_depth, nn(text_lhs, text_block(b)))
-                    write(bottom, bottom_at, b * padded, text_depth, nn(text_g_lhs, text_block(3 + b)))
-                write(top, top_at, 3 * padded, image_depth, nn(image_lhs, image_block(0, 6)))
-                write(bottom, bottom_at, 3 * padded, image_depth, nn(image_g_lhs, image_block(1, 6)))
+                top, at = (to_send if apart else kept), slot
+                for b in range(6):
+                    write(top, at, b * padded, text_depth, nn(text_g_lhs if b > 2 else text_lhs, text_block(b)))
+                for b in range(2):
+                    bottom(b, 2, nn(image_g_lhs if b else image_lhs, image_block(b, 6)))
 
 
 def gathered(parts):
@@ -886,9 +887,8 @@
 
 
 def spread(packed, share):
-    own, first, unused = packed
     far_rest = lax.all_gather(share, ("stream", "dp"), axis=0, tiled=True)
-    return own, swap(own, "tensor", 1), swap(first, "tensor", 2), far_rest
+    return packed[0], swap(packed[0], "tensor", 1), swap(packed[1], "tensor", 2), far_rest
 
 
 def spread_on(line, own, near, far, far_rest):
@@ -898,24 +898,6 @@
 
 def add(left, right):
     return low(left.astype(F32) + right.astype(F32))
-
-
-def fold_first(to_y, own_top, to_x, own_bottom):
-    return swap(to_y, "tensor", 2), swap(to_x, "stream", 1), own_top, own_bottom
-
-
-def fold_second(by_y, by_x, own_top, own_bottom):
-    return add(own_top[1], by_y[1]), add(own_bottom[1], by_x[1])
-
-
-def fold_third(first, second):
-    by_y, by_x, own_top, own_bottom = first
-    then_x, then_y = second
-
-    def three(own, one, two):
-        return low(own.astype(F32) + one.astype(F32) + two.astype(F32))
-
-    return jnp.concatenate([three(own_top[0], by_y[0], then_x), three(own_bottom[0], by_x[0], then_y)], axis=1)
 
 
 def fold_last(total):
@@ -998,7 +980,7 @@
             image_self_out[0],
         ],
         places,
-        4608,
+        3584,
         after(ids, mlp_packed[0]),
     )
     line.leave(self_packed[0], cross_w[1], cross_w[2])
@@ -1047,6 +1029,7 @@
     )
     line.leave(text_pre1, image_cot_here)
     mlp_w = spread_on(line, *mlp_w)
+    self_w = (*self_w[:2], swap(line.take(self_packed[1]), "tensor", 2), self_w[3])
     (
         text_one,
         image_one,
@@ -1071,7 +1054,7 @@
             q(shape(QUARTERS, image_size, 256)),
         ],
         [buffer(mlp_w), in_sems],
-        15,
+        1,
     )
     line.leave(text_pre2)
     self_w = spread_on(line, *self_w)
@@ -1129,11 +1112,9 @@
         ]
 
     def weight_grads(is_self, turn, rounded, rounded_near, kept, kept_near):
-        top = 3 * padded + image_depth
-        if is_self:
-            outs = [w(shape(2, dp, top, BLOCK)), w(shape(2, dp, top, BLOCK)), w(shape(dp, 12 * image_depth, BLOCK))]
-        else:
-            outs = [w(shape(2, dp, top, BLOCK))] * 4
+        top = 3 * padded + image_depth if is_self else 6 * padded
+        bottom = (3 if is_self else 2) * image_depth
+        outs = [w(shape(2, dp, top, BLOCK)), w(shape(2, dp, top, BLOCK)), w(shape(dp, 4 * bottom, BLOCK))]
         return run(
             functools.partial(weight_grad, is_self, (size, image_size)),
             None,
@@ -1176,8 +1157,8 @@
         23,
         2,
     )
-    to_x, self_top, to_z = weight_grads(True, ids, self_rounded, self_rounded_near, self_keep, self_near)
-    self_by_x = swap(to_x, "stream", 1)
+    to_y, self_top, to_z = weight_grads(True, ids, self_rounded, self_rounded_near, self_keep, self_near)
+    self_by_y = swap(to_y, "tensor", 2)
     self_bottom = fold_last(to_z)
     line.leave(self_top)
     mlp_rows = 6 * size + 2 * image_size
@@ -1212,14 +1193,13 @@
         3,
     )
     line.leave(grad_low)
-    mlp_first = fold_first(
-        *weight_grads(False, line.take(ids), mlp_rounded, mlp_rounded_near, mlp_keep, mlp_near)
-    )
-    line.leave(mlp_first[2])
-    self_top, self_by_x = line.take((self_top, self_by_x))
-    self_top, to_y = add(self_top[0], self_by_x[0]), add(self_top[1], self_by_x[1])
-    self_then_y = swap(to_y, "tensor", 2)
-    line.leave(self_top, to_y)
+    to_x, mlp_top, to_z = weight_grads(False, line.take(ids), mlp_rounded, mlp_rounded_near, mlp_keep, mlp_near)
+    self_top, self_by_y, to_x, to_z = after((self_top, self_by_y, to_x, to_z), mlp_top)
+    mlp_by_x = swap(to_x, "stream", 1)
+    mlp_bottom = fold_last(to_z)
+    self_top, to_x = add(self_top[0], self_by_y[0]), add(self_top[1], self_by_y[1])
+    self_then_x = swap(to_x, "stream", 1)
+    line.leave(self_top, to_x)
     d_dims = [(QUARTERS, part_rows, BLOCK), (QUARTERS, size, 768), (QUARTERS, image_size, 768)]
     vectors = jnp.concatenate(
         [jnp.pad(v, ((0, 0), (0, DV - DT))) for v in (text_vec1, text_vec2, text_vec3)]
@@ -1240,17 +1220,13 @@
         4,
     )
     line.leave(total)
-    self_top = add(self_top, line.take(self_then_y))
-    self_bottom = line.take(self_bottom).reshape(2, 2, 3 * image_depth, BLOCK)
-    self_bottom_x = swap(self_bottom[:, 1], "stream", 1)
-    line.leave(self_top)
     text_only, image_only = 4 * padded + 16, 4 * image_depth
     text_vector = jnp.pad(vectors[:6, :DT].reshape(6, places, text_depth), ((0, 0), (0, 0), (0, BLOCK - text_depth)))
     image_vector = jnp.pad(vectors[6:].reshape(10, places, image_depth), ((0, 0), (0, 0), (0, BLOCK - image_depth)))
     vectors = low(jnp.concatenate([text_vector, image_vector], axis=0).transpose(1, 0, 2))
     vector_keep = lax.dynamic_slice_in_dim(vectors, x_at * dp, dp, 0)
     vector_send = lax.dynamic_slice_in_dim(vectors, (1 - x_at) * dp, dp, 0)
-    text_grad, image_grad, text_keep, text_send, image_keep, image_send = run(
+    text_grad, image_grad, cross_text, image_keep, image_send = run(
         cross_last,
         None,
         [
@@ -1272,37 +1248,47 @@
             w(text_wide),
             w(shape(image_size, DV)),
             w(shape(dp, text_only, BLOCK)),
-            w(shape(dp, text_only, BLOCK)),
             w(shape(dp, image_only, BLOCK)),
             w(shape(dp, image_only, BLOCK)),
         ],
         [
             pltpu.VMEM((part_rows, BLOCK), BF),
+            pltpu.VMEM((dp, text_only, BLOCK), BF),
+            pltpu.VMEM((dp, text_only, BLOCK), BF),
             pltpu.VMEM((DT, QUARTERS * size), BF),
             pltpu.VMEM((DT, QUARTERS * size), BF),
             pltpu.VMEM((DV, QUARTERS * image_size), BF),
             pltpu.VMEM((DV, QUARTERS * image_size), BF),
         ]
-        + links(1),
-        30,
+        + links(2),
+        2,
         5,
     )
     line.leave(text_grad)
-    self_top = fold_last(self_top)
-    sums = fold_second(*line.take(mlp_first))
-    line.leave(*sums)
-    mlp_second = swap(sums[0], "stream", 1), swap(sums[1], "tensor", 2)
+    self_top, self_then_x, mlp_top, mlp_by_x, self_bottom, cross_text, image_send = line.take(
+        (self_top, self_then_x, mlp_top, mlp_by_x, self_bottom, cross_text, image_send)
+    )
+    cross_text = fold_last(cross_text)
+    image_send = swap(image_send, "stream", 1)
+    mlp_top, to_y = add(mlp_top[0], mlp_by_x[0]), add(mlp_top[1], mlp_by_x[1])
+    mlp_then_y = swap(to_y, "tensor", 2)
+    self_top = fold_last(add(self_top, self_then_x))
+    line.leave(mlp_top, to_y)
+    self_bottom = line.take(self_bottom).reshape(2, 2, 3 * image_depth, BLOCK)
+    self_bottom_x = swap(self_bottom[:, 1], "stream", 1)
+    cross_image = add(image_keep, line.take(image_send))
+    line.leave(cross_image)
+    cross_image = fold_last(cross_image)
     self_bottom = add(self_bottom[:, 0], line.take(self_bottom_x))
-    self_bottom = add(self_bottom[0], swap(self_bottom[1], "tensor", 2))
-    mlp_total = fold_third(mlp_first, line.take(mlp_second))
-    line.leave(mlp_total, self_bottom)
-    mlp_grads = fold_last(after(mlp_total, self_top))
-    cross_text = add(text_keep, line.take(swap(text_send, "stream", 1)))
-    line.leave(cross_text)
-    cross_text = fold_last(after(cross_text, mlp_grads))
-    cross_image = add(image_keep, line.take(swap(image_send, "stream", 1)))
-    line.leave(cross_image)
-    cross_image = fold_last(after(cross_image, cross_text))
+    self_bottom_y = swap(self_bottom[1], "tensor", 2)
+    mlp_bottom = line.take(mlp_bottom).reshape(2, 2, 2 * image_depth, BLOCK)
+    mlp_bottom_x = swap(mlp_bottom[:, 1], "stream", 1)
+    mlp_top = add(mlp_top, line.take(mlp_then_y))
+    line.leave(mlp_top)
+    mlp_top = fold_last(mlp_top)
+    mlp_bottom = add(mlp_bottom[:, 0], line.take(mlp_bottom_x))
+    mlp_bottom = add(mlp_bottom[0], swap(mlp_bottom[1], "tensor", 2))
+    self_bottom = add(self_bottom[0], self_bottom_y)
     self_grads = jnp.concatenate([self_top, self_bottom], axis=0)
     image_grad = leave(image_grad)
 
@@ -1333,8 +1319,8 @@
         text_pick(cross_text, 0, 1)[None],
         image_pick(cross_image, 0, 2).reshape(1, image_depth, 2, 256),
         text_pick(cross_text, 3 * padded, 1).T[None],
-        text_pick(mlp_grads, 0, 3)[None],
-        text_pick(mlp_grads, below + image_depth, 3).T[None],
+        text_pick(mlp_top, 0, 3)[None],
+        text_pick(mlp_top, below, 3).T[None],
         jnp.stack([heads(n) for n in range(3)], axis=1)[None],
         heads(3).T[None],
         text_vectors[0::2][None],
@@ -1342,8 +1328,8 @@
         image_pick(cross_image, 2 * image_depth, 1)[None],
         text_pick(cross_text, padded, 2).reshape(1, text_depth, 2, 256),
         image_pick(cross_image, 3 * image_depth, 1).T[None],
-        image_pick(mlp_grads, below, 1)[None],
-        image_pick(mlp_grads, 2 * below + image_depth, 1).T[None],
+        image_pick(mlp_bottom, 0, 1)[None],
+        image_pick(mlp_bottom, image_depth, 1).T[None],
         image_pick(self_grads, below, 3).reshape(1, image_depth, 3, 256),
         image_pick(self_grads, below + 3 * image_depth, 1).T[None],
         image_vectors[0::2][None],

time: 535 us -> 470 us (0.88)
  Pallas kernels: 313 us -> 274 us
  waiting for transfers between devices: 128 us -> 89.4 us
  local copies, waits for them, and re-layouts: 24.8 us -> 37.3 us
    pallas_call x11, Pallas kernels: 313 us -> 274 us  [run(): pl.pallas_call(kernel, grid=(QUARTERS,) if order else (1,), in_specs=[spe...]
    all_gather x2, waiting for transfers between devices: 29.5 us -> 0.02 us  [spread(): far_rest = lax.all_gather(share, ('stream', 'dp'), axis=0, tiled=True)]
    ppermute x24 -> x23, waiting for transfers between devices: 86.7 us -> 60.8 us  [swap(): lax.ppermute(value, axis, [(i, i ^ apart) for i in range(lax.axis_size(ax...]
    reduce_scatter x5 -> x6, waiting for transfers between devices: 11.8 us -> 28.5 us  [fold_last(): return lax.psum_scatter(total, 'dp', scatter_dimension=0, tiled=True)[0]]
    unnamed x61 -> x53, local copies, waits for them, and re-layouts: 13.9 us -> 16.4 us
    ppermute x24 -> x23, starting transfers between devices: 24.5 us -> 23.5 us  [swap(): lax.ppermute(value, axis, [(i, i ^ apart) for i in range(lax.axis_size(ax...]
  transfers between devices with their start and end apart: 31 -> 31, of which waited for: 15 -> 12; matrix products, arithmetic and copies ran while one was open for 8% -> 12% of each run, Pallas kernels for 52% -> 51%
where the time goes in v3:
time: 470 us; the launch traced here: 466 us
  Pallas kernels  274 us (58%)
  waiting for transfers between devices  89.4 us (19%)
  local copies, waits for them, and re-layouts  37.3 us (8%)
  other arithmetic  25.7 us (5%)
  starting transfers between devices  24.3 us (5%)
  between operations  14.8 us (3%)
    pallas_call x11, Pallas kernels, run(): pl.pallas_call(kernel, grid=(QUARTERS,) if order else (1,), in_specs=[spe...  274 us
    ppermute x23, waiting for transfers between devices, swap(): lax.ppermute(value, axis, [(i, i ^ apart) for i in range(lax.axis_size(ax...  60.8 us
    reduce_scatter x6, waiting for transfers between devices, fold_last(): return lax.psum_scatter(total, 'dp', scatter_dimension=0, tiled=True)[0]  28.5 us
    ppermute x23, starting transfers between devices, swap(): lax.ppermute(value, axis, [(i, i ^ apart) for i in range(lax.axis_size(ax...  23.5 us
    unnamed x53, local copies, waits for them, and re-layouts  16.4 us
    convert_element_type x9, other arithmetic, low(): return value.astype(BF)  14.5 us
  transfers between devices with their start and end apart: 31, of which 12 were waited for; matrix products, arithmetic and copies ran while one was open for 12% of the time, Pallas kernels for 51%

profile of v3, /device:TPU:0, one launch (start us, length us, event | category | flops | bytes accessed | tf_op | source)
XLA Modules:
  0.0 465.9 jit_solution(14456443034336506088)
XLA Ops:
  7.9 4.2 shard_map.390
  12.1 3.0 collective-permute-start
  19.8 4.5 shard_map.391
  26.5 1.8 reshape.273
  28.2 1.8 pad.28
  31.5 1.8 reshape.271
  33.3 1.8 pad.27
  35.3 74.5 %shard_map.392 = (f32[512,768]{1,0:T(8,128)}, f32[192,1024]{1,0:T(8,128)}, bf16[192,1024]{1,0:T(8,128)(2,1)}, bf16[4,512,768]{2,1,0:T(8,128)(2,1)}, bf16[4,192,1...) custom-call(s32[16]{0:T(128)} %lengths.3, ...), custom_call_target="tpu_custom_call" | custom-call | flops 76999999488 | bytes 1024 | tf_op jit(solution)/shard_map/pallas_call | solution.py:853
  110.0 1.8 collective-permute-start.8
  112.3 8.7 %collective-permute-done.5.refs_4_.refs_8_ = bf16[1536,256]{1,0:T(8,128)(2,1)} collective-permute-done((bf16[1536,256]{1,0:T(8,128)(2,1)}, bf16[1536,256]{1,0:T(8,128)(2,1)}, u32[]{:S(2)}, u32[]{:S(2)}) %collective-permute-start.5) | collective-permute-done | bytes 786464 | tf_op jit(solution)/shard_map/ppermute | solution.py:871
  121.0 14.1 %shard_map.393 = (bf16[512,768]{1,0:T(8,128)(2,1)}, bf16[192,1024]{1,0:T(8,128)(2,1)}, f32[512,768]{1,0:T(8,128)}, f32[192,1024]{1,0:T(8,128)}, bf16[4,512,768]{...) custom-call(f32[512,768]{1,0:T(8,128)} %get-tuple-element.128.text_pre, ...), custom_call_target="tpu_custom_call" | custom-call | flops 1100000000 | bytes 1024 | tf_op jit(solution)/shard_map/pallas_call | solution.py:853
  135.1 9.2 %collective-permute-done.8.refs_2_.refs_9_ = bf16[2816,256]{1,0:T(8,128)(2,1)} collective-permute-done((bf16[2816,256]{1,0:T(8,128)(2,1)}, bf16[2816,256]{1,0:T(8,128)(2,1)}, u32[]{:S(2)}, u32[]{:S(2)}) %collective-permute-start.8) | collective-permute-done | bytes 1441824 | tf_op jit(solution)/shard_map/ppermute | solution.py:871
  144.8 5.5 %collective-permute-done.9.refs_4_.refs_11_ = bf16[2816,256]{1,0:T(8,128)(2,1)S(1)} collective-permute-done((bf16[2816,256]{1,0:T(8,128)(2,1)}, bf16[2816,256]{1,0:T(8,128)(2,1)S(1)}, u32[]{:S(2)}, u32[]{:S(2)}) %collective-permute-start.9) | collective-permute-done | bytes 1441824 | tf_op jit(solution)/shard_map/ppermute | solution.py:871
  152.1 19.8 %shard_map.394 = (f32[512,768]{1,0:T(8,128)}, bf16[192,1024]{1,0:T(8,128)(2,1)}, f32[512,768]{1,0:T(8,128)}, f32[192,1024]{1,0:T(8,128)}, f32[2,768]{1,0:T(2,128...) custom-call(s32[6]{0:T(128)} %stack.39.ids.x_at, ...), custom_call_target="tpu_custom_call" | custom-call | flops 20899999744 | bytes 1024 | tf_op jit(solution)/shard_map/pallas_call | solution.py:853
  172.1 23.3 %shard_map.395 = (f32[512,768]{1,0:T(8,128)}, f32[192,1024]{1,0:T(8,128)}, f32[2,768]{1,0:T(2,128)}, f32[2,1024]{1,0:T(2,128)}, bf16[2,2304,256]{2,1,0:T(8,128)(2,1)}, /*index=5*/bf16[2,2304,256]{2,1,0:T(8,128)(2,1)}) custom-call(f32[512,768]{1,0:T(8,128)} %get-tuple-element.142.text_g, f32[192,1024]{1,0:T(8,128)} %get-tuple-element.143.image_g, ...), custom_call_target="tpu_custom_call" | custom-call | flops 25300000768 | bytes 1024 | tf_op jit(solution)/shard_map/pallas_call | solution.py:853
  196.8 12.7 %shard_map.396 = (bf16[2,4,416,256]{3,2,1,0:T(8,128)(2,1)}, bf16[2,4,416,256]{3,2,1,0:T(8,128)(2,1)}, bf16[4,1536,256]{2,1,0:T(8,128)(2,1)}) custom-call(s32[6]{0:T(128)} %stack.39.ids.x_at, bf16[4608,256]{1,0:T(8,128)(2,1)} %get-tuple-element.155.own, bf16[4608,256]{1,0:T(8,128)(2,1)} %copy-done.16, bf16[2,2304,256]{2,1,0:T(8,128)(2,1)} %get-tuple-element.156.own_quarters, ...), custom_call_target="tpu_custom_call" | custom-call | flops 13200000000 | bytes 1024 | tf_op jit(solution)/shard_map/pallas_call | solution.py:853
  210.2 1.8 collective-permute-start.13
  212.0 21.0 %shard_map.397 = (f32[512,768]{1,0:T(8,128)}, f32[192,1024]{1,0:T(8,128)}, bf16[2304,256]{1,0:T(8,128)(2,1)}, f32[2,768]{1,0:T(2,128)}, f32[2,1024]{1,0:T(2,128)...) custom-call(f32[512,768]{1,0:T(8,128)} %get-tuple-element.151.text_g, ...), custom_call_target="tpu_custom_call" | custom-call | flops 22000001024 | bytes 1024 | tf_op jit(solution)/shard_map/pallas_call | solution.py:853
  233.6 2.0 concatenate.76.vectors
  235.6 13.1 %shard_map.398 = (bf16[2,4,576,256]{3,2,1,0:T(8,128)(2,1)}, bf16[2,4,576,256]{3,2,1,0:T(8,128)(2,1)}, bf16[4,1024,256]{2,1,0:T(8,128)(2,1)}) custom-call(s32[6]{0:T(128)} %stack.39.ids.x_at, bf16[4608,256]{1,0:T(8,128)(2,1)} %get-tuple-element.167.own, bf16[4608,256]{1,0:T(8,128)(2,1)} %get-tuple-element.168.near, ...), custom_call_target="tpu_custom_call" | custom-call | flops 13200000000 | bytes 1024 | tf_op jit(solution)/shard_map/pallas_call | solution.py:853
  249.8 2.7 fusion.3
  252.5 1.7 collective-permute-start.15
  254.6 44.4 %shard_map.399 = (bf16[4,2304,256]{2,1,0:T(8,128)(2,1)}, bf16[4,512,768]{2,1,0:T(8,128)(2,1)}, bf16[4,192,768]{2,1,0:T(8,128)(2,1)}, f32[2304,256]{1,0:T(8,128)}...) custom-call(bf16[2304,256]{1,0:T(8,128)(2,1)} %get-tuple-element.176.grad, f32[16,1024]{1,0:T(8,128)} %concatenate.76.vectors, ...), custom_call_target="tpu_custom_call" | custom-call | flops 52800000000 | bytes 1024 | tf_op jit(solution)/shard_map/pallas_call | solution.py:853
  300.7 42.8 %shard_map.400 = (f32[512,768]{1,0:T(8,128)}, bf16[192,1024]{1,0:T(8,128)(2,1)}, bf16[4,400,256]{2,1,0:T(8,128)(2,1)}, bf16[4,512,256]{2,1,0:T(8,128)(2,1)}, bf16[4,512,256]{2,1,0:T(8,128)(2,1)}) custom-call(bf16[2304,256]{1,0:T(8,128)(2,1)} %get-tuple-element.187.total, f32[2304,256]{1,0:T(8,128)} %get-tuple-element.188.own_sum, ...), custom_call_target="tpu_custom_call" | custom-call | flops 2200000000 | bytes 1024 | tf_op jit(solution)/shard_map/pallas_call | solution.py:853
  345.0 2.4 add_convert_fusion.4
  349.2 3.2 fusion.1
  352.4 19.1 %collective-permute-done.17 = bf16[4,512,256]{2,1,0:T(8,128)(2,1)S(1)} collective-permute-done((bf16[4,512,256]{2,1,0:T(8,128)(2,1)}, bf16[4,512,256]{2,1,0:T(8,128)(2,1)S(1)}, u32[]{:S(2)}, u32[]{:S(2)}) %collective-permute-start.17) | collective-permute-done | bytes 1048608 | tf_op jit(solution)/shard_map/ppermute | solution.py:871
  382.4 11.6 %collective-permute-done.11 = bf16[148,1024]{1,0:T(8,128)(2,1)} collective-permute-done((bf16[148,1024]{1,0:T(8,128)(2,1)}, bf16[148,1024]{1,0:T(8,128)(2,1)}, u32[]{:S(2)}, u32[]{:S(2)}) %collective-permute-start.11) | collective-permute-done | bytes 303136 | tf_op jit(solution)/shard_map/ppermute | solution.py:871
  394.0 1.9 convert_element_type.219
  402.3 2.7 add_convert_fusion
  409.6 2.9 collective-permute-done.20
  427.7 27.6 %reduce-scatter.13.cloned.1.call-done = bf16[1,576,256]{2,1,0:T(8,128)(2,1)} async-done(((bf16[4,576,256]{2,1,0:T(8,128)(2,1)}), bf16[1,576,256]{2,1,0:T(8,128)(2,1)}) %reduce-scatter.13.cloned.1.call-update) | async-done | bytes 294928 | tf_op jit(solution)/shard_map/reduce_scatter | solution.py:904
  (166 shorter events, 62.0 us)
Async XLA Ops:
  7.2 102.7 %all-gather.3.cloned.1.call-start = ((), (), s32[]{:S(2)}) async-start(), calls=%async_computation.6 | async-start | bytes 2949120 | tf_op jit(solution)/shard_map/all_gather | solution.py:890
  12.1 12.2 %collective-permute-start = (bf16[640,256]{1,0:T(8,128)(2,1)}, bf16[640,256]{1,0:T(8,128)(2,1)}, u32[]{:S(2)}, u32[]{:S(2)}) collective-permute-start(bf16[640,256]{1,0:T(8,128)(2,1)} %get-tuple-element.120), channel_id=1, source_target_pairs={{0,2},{1,3},{2,0},{3,1},{4,6},{5,7},{6,4},{7,5},{8,10},{9,11},{10,... | collective-permute-start | bytes 983048 | tf_op jit(solution)/shard_map/ppermute | solution.py:871
  24.3 120.0 %all-gather.5.cloned.1.call-start = ((), (), s32[]{:S(2)}) async-start(), calls=%async_computation.7 | async-start | bytes 2064384 | tf_op jit(solution)/shard_map/all_gather | solution.py:890
  24.4 10.7 %collective-permute-start.1 = (bf16[448,256]{1,0:T(8,128)(2,1)}, bf16[448,256]{1,0:T(8,128)(2,1)}, u32[]{:S(2)}, u32[]{:S(2)}) collective-permute-start(bf16[448,256]{1,0:T(8,128)(2,1)} %get-tuple-element.125), channel_id=1, source_target_pairs={{0,2},{1,3},{2,0},{3,1},{4,6},{5,7},{6,4},{7,5},{8,10},{9,11},{10,... | collective-permute-start | bytes 688136 | tf_op jit(solution)/shard_map/ppermute | solution.py:871
  25.0 87.3 %collective-permute-start.2 = (bf16[6656,256]{1,0:T(8,128)(2,1)S(1)}, bf16[6656,256]{1,0:T(8,128)(2,1)}, u32[]{:S(2)}, u32[]{:S(2)}) collective-permute-start(bf16[6656,256]{1,0:T(8,128)(2,1)S(1)} %copy-done), channel_id=1, source_target_pairs={{0,1},{1,0},{2,3},{3,2},{4,5},{5,4},{6,7},{7,6},{8,9},{9,8},{10,11... | collective-permute-start | bytes 10223624 | tf_op jit(solution)/shard_map/ppermute | solution.py:871
  25.0 84.9 %collective-permute-start.3 = (bf16[1536,256]{1,0:T(8,128)(2,1)}, bf16[1536,256]{1,0:T(8,128)(2,1)}, u32[]{:S(2)}, u32[]{:S(2)}) collective-permute-start(bf16[1536,256]{1,0:T(8,128)(2,1)} %get-tuple-element.130), channel_id=1, source_target_pairs={{0,2},{1,3},{2,0},{3,1},{4,6},{5,7},{6,4},{7,5},{8,10},{9,11},{10,... | collective-permute-start | bytes 2359304 | tf_op jit(solution)/shard_map/ppermute | solution.py:871
  30.0 79.9 %collective-permute-start.4 = (bf16[192,1024]{1,0:T(8,128)(2,1)}, bf16[192,1024]{1,0:T(8,128)(2,1)}, u32[]{:S(2)}, u32[]{:S(2)}) collective-permute-start(bf16[192,1024]{1,0:T(8,128)(2,1)} %bitcast.21), channel_id=1, source_target_pairs={{0,16},{16,0},{1,17},{17,1},{2,18},{18,2},{3,19},{19,3},{4,20},{20... | collective-permute-start | bytes 1179656 | tf_op jit(solution)/shard_map/ppermute | solution.py:871
  35.1 308.5 %reduce-scatter.7.cloned.1.call-start = ((), (), s32[]{:S(2)}) async-start(), calls=%async_computation.8 | async-start | bytes 3932160 | tf_op jit(solution)/shard_map/reduce_scatter | solution.py:904
  109.9 11.1 %collective-permute-start.6 = (bf16[5120,256]{1,0:T(8,128)(2,1)}, bf16[5120,256]{1,0:T(8,128)(2,1)}, u32[]{:S(2)}, u32[]{:S(2)}) collective-permute-start(bf16[5120,256]{1,0:T(8,128)(2,1)} %all-gather.3.cloned.1.call-done.refs_3_.refs_7_), channel_id=1, source_target_pairs={{0,1},{1,0},{2,3},{3,2},{4,5},{5,4},{6,7},{7,6},{8,9},{9,8},{10,11... | collective-permute-start | bytes 7864328 | tf_op jit(solution)/shard_map/ppermute | solution.py:871
  110.0 34.3 %collective-permute-start.8 = (bf16[2816,256]{1,0:T(8,128)(2,1)}, bf16[2816,256]{1,0:T(8,128)(2,1)}, u32[]{:S(2)}, u32[]{:S(2)}) collective-permute-start(bf16[2816,256]{1,0:T(8,128)(2,1)} %get-tuple-element.136), channel_id=1, source_target_pairs={{0,2},{1,3},{2,0},{3,1},{4,6},{5,7},{6,4},{7,5},{8,10},{9,11},{10,... | collective-permute-start | bytes 4325384 | tf_op jit(solution)/shard_map/ppermute | solution.py:871
  111.8 33.0 %collective-permute-start.7 = (bf16[6400,256]{1,0:T(8,128)(2,1)}, bf16[6400,256]{1,0:T(8,128)(2,1)}, u32[]{:S(2)}, u32[]{:S(2)}) collective-permute-start(bf16[6400,256]{1,0:T(8,128)(2,1)} %get-tuple-element.123.refs_0_.refs_7_), channel_id=1, source_target_pairs={{0,1},{1,0},{2,3},{3,2},{4,5},{5,4},{6,7},{7,6},{8,9},{9,8},{10,11... | collective-permute-start | bytes 9830408 | tf_op jit(solution)/shard_map/ppermute | solution.py:871
  111.9 9.1 %collective-permute-start.5 = (bf16[1536,256]{1,0:T(8,128)(2,1)}, bf16[1536,256]{1,0:T(8,128)(2,1)}, u32[]{:S(2)}, u32[]{:S(2)}) collective-permute-start(bf16[1536,256]{1,0:T(8,128)(2,1)} %collective-permute-done.3.refs_2_.refs_6_), channel_id=1, source_target_pairs={{0,1},{1,0},{2,3},{3,2},{4,5},{5,4},{6,7},{7,6},{8,9},{9,8},{10,11... | collective-permute-start | bytes 2359304 | tf_op jit(solution)/shard_map/ppermute | solution.py:871
  144.3 6.1 %collective-permute-start.10 = (bf16[3584,256]{1,0:T(8,128)(2,1)}, bf16[3584,256]{1,0:T(8,128)(2,1)S(1)}, u32[]{:S(2)}, u32[]{:S(2)}) collective-permute-start(bf16[3584,256]{1,0:T(8,128)(2,1)} %all-gather.5.cloned.1.call-done.refs_3_.refs_10_), channel_id=1, source_target_pairs={{0,1},{1,0},{2,3},{3,2},{4,5},{5,4},{6,7},{7,6},{8,9},{9,8},{10,11... | collective-permute-start | bytes 5505032 | tf_op jit(solution)/shard_map/ppermute | solution.py:871
  144.3 6.1 %collective-permute-start.9 = (bf16[2816,256]{1,0:T(8,128)(2,1)}, bf16[2816,256]{1,0:T(8,128)(2,1)S(1)}, u32[]{:S(2)}, u32[]{:S(2)}) collective-permute-start(bf16[2816,256]{1,0:T(8,128)(2,1)} %collective-permute-done.8.refs_2_.refs_9_), channel_id=1, source_target_pairs={{0,1},{1,0},{2,3},{3,2},{4,5},{5,4},{6,7},{7,6},{8,9},{9,8},{10,11... | collective-permute-start | bytes 4325384 | tf_op jit(solution)/shard_map/ppermute | solution.py:871
  171.9 23.5 %collective-permute-start.12 = (bf16[4608,256]{1,0:T(8,128)(2,1)}, bf16[4608,256]{1,0:T(8,128)(2,1)S(1)}, u32[]{:S(2)}, u32[]{:S(2)}) collective-permute-start(bf16[4608,256]{1,0:T(8,128)(2,1)} %get-tuple-element.155.own), channel_id=1, source_target_pairs={{0,1},{1,0},{2,3},{3,2},{4,5},{5,4},{6,7},{7,6},{8,9},{9,8},{10,11... | collective-permute-start | bytes 7077896 | tf_op jit(solution)/shard_map/ppermute | solution.py:871
  209.5 190.5 %reduce-scatter.17.cloned.1.call-start = ((), (), s32[]{:S(2)}) async-start(), calls=%async_computation.13 | async-start | bytes 2621440 | tf_op jit(solution)/shard_map/reduce_scatter | solution.py:904
  210.2 39.6 %collective-permute-start.13 = (bf16[2,4,416,256]{3,2,1,0:T(8,128)(2,1)}, bf16[2,4,416,256]{3,2,1,0:T(8,128)(2,1)}, u32[]{:S(2)}, u32[]{:S(2)}) collective-permute-start(bf16[2,4,416,256]{3,2,1,0:T(8,128)(2,1)} %get-tuple-element.165), channel_id=1, source_target_pairs={{0,2},{1,3},{2,0},{3,1},{4,6},{5,7},{6,4},{7,5},{8,10},{9,11},{10,... | collective-permute-start | bytes 5111816 | tf_op jit(solution)/shard_map/ppermute | solution.py:871
  252.5 91.0 %collective-permute-start.15 = (bf16[4,416,256]{2,1,0:T(8,128)(2,1)}, bf16[4,416,256]{2,1,0:T(8,128)(2,1)}, u32[]{:S(2)}, u32[]{:S(2)}) collective-permute-start(bf16[4,416,256]{2,1,0:T(8,128)(2,1)} %get-tuple-element.264), channel_id=1, source_target_pairs={{0,16},{16,0},{1,17},{17,1},{2,18},{18,2},{3,19},{19,3},{4,20},{20... | collective-permute-start | bytes 2555912 | tf_op jit(solution)/shard_map/ppermute | solution.py:871
  254.2 89.3 %collective-permute-start.16 = (bf16[2,4,576,256]{3,2,1,0:T(8,128)(2,1)}, bf16[2,4,576,256]{3,2,1,0:T(8,128)(2,1)S(1)}, u32[]{:S(2)}, u32[]{:S(2)}) collective-permute-start(bf16[2,4,576,256]{3,2,1,0:T(8,128)(2,1)} %get-tuple-element.199), channel_id=1, source_target_pairs={{0,16},{16,0},{1,17},{17,1},{2,18},{18,2},{3,19},{19,3},{4,20},{20... | collective-permute-start | bytes 7077896 | tf_op jit(solution)/shard_map/ppermute | solution.py:871
  254.5 159.4 %reduce-scatter.9.cloned.1.call-start = ((), (), s32[]{:S(2)}) async-start(), calls=%async_computation.9 | async-start | bytes 1024000 | tf_op jit(solution)/shard_map/reduce_scatter | solution.py:904
  345.0 74.4 %reduce-scatter.15.cloned.1.call-start = ((), (), s32[]{:S(2)}) async-start(), calls=%async_computation.12 | async-start | bytes 1064960 | tf_op jit(solution)/shard_map/reduce_scatter | solution.py:904
  347.5 76.9 %reduce-scatter.11.cloned.1.call-start = ((), (), s32[]{:S(2)}) async-start(), calls=%async_computation.10 | async-start | bytes 1310720 | tf_op jit(solution)/shard_map/reduce_scatter | solution.py:904
  347.6 23.9 %collective-permute-start.17 = (bf16[4,512,256]{2,1,0:T(8,128)(2,1)}, bf16[4,512,256]{2,1,0:T(8,128)(2,1)S(1)}, u32[]{:S(2)}, u32[]{:S(2)}) collective-permute-start(bf16[4,512,256]{2,1,0:T(8,128)(2,1)} %get-tuple-element.205), channel_id=1, source_target_pairs={{0,16},{16,0},{1,17},{17,1},{2,18},{18,2},{3,19},{19,3},{4,20},{20... | collective-permute-start | bytes 3145736 | tf_op jit(solution)/shard_map/ppermute | solution.py:871
  372.7 82.6 %reduce-scatter.13.cloned.1.call-start = ((), (), s32[]{:S(2)}) async-start(), calls=%async_computation.11 | async-start | bytes 1474560 | tf_op jit(solution)/shard_map/reduce_scatter | solution.py:904
  373.0 29.3 %collective-permute-start.18 = (bf16[4,576,256]{2,1,0:T(8,128)(2,1)S(1)}, bf16[4,576,256]{2,1,0:T(8,128)(2,1)}, u32[]{:S(2)}, u32[]{:S(2)}) collective-permute-start(bf16[4,576,256]{2,1,0:T(8,128)(2,1)S(1)} %copy-done.6), channel_id=1, source_target_pairs={{0,2},{1,3},{2,0},{3,1},{4,6},{5,7},{6,4},{7,5},{8,10},{9,11},{10,... | collective-permute-start | bytes 3538952 | tf_op jit(solution)/shard_map/ppermute | solution.py:871
  375.3 22.8 %collective-permute-start.21 = (bf16[2,384,256]{2,1,0:T(8,128)(2,1)}, bf16[2,384,256]{2,1,0:T(8,128)(2,1)}, u32[]{:S(2)}, u32[]{:S(2)}) collective-permute-start(bf16[2,384,256]{2,1,0:T(8,128)(2,1)} %slice_bitcast_fusion), channel_id=1, source_target_pairs={{0,16},{16,0},{1,17},{17,1},{2,18},{18,2},{3,19},{19,3},{4,20},{20... | collective-permute-start | bytes 1179656 | tf_op jit(solution)/shard_map/ppermute | solution.py:871
  378.5 15.4 %collective-permute-start.11 = (bf16[148,1024]{1,0:T(8,128)(2,1)}, bf16[148,1024]{1,0:T(8,128)(2,1)}, u32[]{:S(2)}, u32[]{:S(2)}) collective-permute-start(bf16[148,1024]{1,0:T(8,128)(2,1)} %reshape.276), channel_id=1, source_target_pairs={{0,16},{16,0},{1,17},{17,1},{2,18},{18,2},{3,19},{19,3},{4,20},{20... | collective-permute-start | bytes 909320 | tf_op jit(solution)/shard_map/ppermute | solution.py:871
  380.9 16.3 %collective-permute-start.14 = (bf16[148,1024]{1,0:T(8,128)(2,1)}, bf16[148,1024]{1,0:T(8,128)(2,1)S(1)}, u32[]{:S(2)}, u32[]{:S(2)}) collective-permute-start(bf16[148,1024]{1,0:T(8,128)(2,1)} %reshape.280), channel_id=1, source_target_pairs={{0,16},{16,0},{1,17},{17,1},{2,18},{18,2},{3,19},{19,3},{4,20},{20... | collective-permute-start | bytes 909320 | tf_op jit(solution)/shard_map/ppermute | solution.py:871
  399.2 5.8 %collective-permute-start.22 = (bf16[384,256]{1,0:T(8,128)(2,1)S(1)}, bf16[384,256]{1,0:T(8,128)(2,1)}, u32[]{:S(2)}, u32[]{:S(2)}) collective-permute-start(bf16[384,256]{1,0:T(8,128)(2,1)S(1)} %slice_bitcast_fusion.4), channel_id=1, source_target_pairs={{0,2},{1,3},{2,0},{3,1},{4,6},{5,7},{6,4},{7,5},{8,10},{9,11},{10,... | collective-permute-start | bytes 589832 | tf_op jit(solution)/shard_map/ppermute | solution.py:871
  400.9 6.4 %collective-permute-start.19 = (bf16[2,256,256]{2,1,0:T(8,128)(2,1)S(1)}, bf16[2,256,256]{2,1,0:T(8,128)(2,1)S(1)}, u32[]{:S(2)}, u32[]{:S(2)}) collective-permute-start(bf16[2,256,256]{2,1,0:T(8,128)(2,1)S(1)} %slice_bitcast_fusion.2), channel_id=1, source_target_pairs={{0,16},{16,0},{1,17},{17,1},{2,18},{18,2},{3,19},{19,3},{4,20},{20... | collective-permute-start | bytes 786440 | tf_op jit(solution)/shard_map/ppermute | solution.py:871
  407.5 5.0 %collective-permute-start.20 = (bf16[256,256]{1,0:T(8,128)(2,1)S(1)}, bf16[256,256]{1,0:T(8,128)(2,1)S(1)}, u32[]{:S(2)}, u32[]{:S(2)}) collective-permute-start(bf16[256,256]{1,0:T(8,128)(2,1)S(1)} %slice_bitcast_fusion.6), channel_id=1, source_target_pairs={{0,2},{1,3},{2,0},{3,1},{4,6},{5,7},{6,4},{7,5},{8,10},{9,11},{10,... | collective-permute-start | bytes 393224 | tf_op jit(solution)/shard_map/ppermute | solution.py:871
  423.6 34.2 %copy-start.5 = (f32[512,768]{1,0:T(8,128)S(1)}, f32[512,768]{1,0:T(8,128)}, u32[]{:S(2)}) copy-start(f32[512,768]{1,0:T(8,128)} %get-tuple-element.326) | copy-start | bytes 4718596
  (18 other events, 114.8 us)
Sparse Core Ops, SparseCore 0:
  24.4 57.8 all-gather.2
  84.4 44.8 all-gather.4
  209.6 61.6 reduce-scatter.6
  273.5 43.8 reduce-scatter.16
  345.1 24.9 reduce-scatter.8
  372.3 23.4 reduce-scatter.14
  398.1 26.2 reduce-scatter.10
  427.4 27.8 reduce-scatter.12

commit v4 on v3

--- a/solution.py
+++ b/solution.py
@@ -90,11 +90,17 @@
     return slice(pair * size, (pair + 1) * size)
 
 
-def fetch(step, order, parts, buffer, sems):
+def fetch(step, order, own, near, far, far_rest, corner, buffer, sems):
+    slots = [order.index(quarter) for quarter in range(QUARTERS)]
+    cut, rest = far.shape[0], far_rest.shape[0]
     copies = [
-        (order.index(quarter), pltpu.make_async_copy(ref, buffer.at[order.index(quarter), pl.ds(row, ref.shape[0])], sems.at[i]))
-        for i, (quarter, row, ref) in enumerate(parts)
+        (slots[0], pltpu.make_async_copy(own, buffer.at[slots[0]], sems.at[0])),
+        (slots[1], pltpu.make_async_copy(near, buffer.at[slots[1]], sems.at[1])),
+        (slots[2], pltpu.make_async_copy(far, buffer.at[slots[2], pl.ds(0, cut)], sems.at[2])),
+        (slots[2], pltpu.make_async_copy(far_rest, buffer.at[slots[2], pl.ds(cut, rest)], sems.at[3])),
     ]
+    if corner is not None:
+        copies.append((slots[3], pltpu.make_async_copy(corner, buffer.at[slots[3]], sems.at[4])))
     copies.sort(key=lambda entry: entry[0])
 
     @pl.when(step == 0)
@@ -109,6 +115,40 @@
             for slot, copy in copies:
                 if slot == at:
                     copy.wait()
+
+
+def fetch_round(step, own, near, far, far_rest, corner, buffer, sems, send_sems, recv_sems):
+    core = partners()[0]
+    copy = sender(send_sems, recv_sems)
+    cut, rest = far.shape[0], far_rest.shape[0]
+    over = copy(0, far, buffer.at[3, pl.ds(0, cut)], core), copy(1, far_rest, buffer.at[3, pl.ds(cut, rest)], core)
+    leaving = pltpu.make_async_copy(buffer.at[3], corner, sems.at[4])
+    fetch(step, FORWARD, own, near, far, far_rest, None, buffer, sems)
+
+    @pl.when(step == 0)
+    def begin():
+        greet(core)
+        for transfer in over:
+            transfer.start()
+
+    @pl.when(step == 3)
+    def last():
+        for transfer in over:
+            transfer.wait()
+        leaving.start()
+
+    return leaving
+
+
+def spacing(pairs):
+    rows, columns = pairs * PADDED, pairs * REGIONS
+    row = lax.broadcasted_iota(jnp.int32, (rows, columns), 0)
+    column = lax.broadcasted_iota(jnp.int32, (rows, columns), 1)
+    chosen = jnp.zeros((rows, columns), F32)
+    for p in range(pairs):
+        inside = (column >= p * REGIONS) & (column < (p + 1) * REGIONS)
+        chosen = jnp.where(inside & (row - p * PADDED == column - p * REGIONS), 1.0, chosen)
+    return low(chosen)
 
 
 def leave_quarter(step, buffer, near, keep, sems, copies):
@@ -223,14 +263,15 @@
 
 def cross_forward(pairs, lengths, text, image, *refs):
     matrices = refs[:6]
-    text_pre, image_pre, image_own = refs[6:9]
-    outs = refs[9:15]
-    texts, images, text_kept, image_kept, text_probs, image_probs, parts, total, got, send_sems, recv_sems, out_sems = refs[15:]
+    text_pre, image_pre = refs[6:8]
+    outs = refs[8:14]
+    texts, images, text_kept, image_kept, text_probs, image_probs, parts, total, got, image_apart = refs[14:24]
+    send_sems, recv_sems, out_sems = refs[24:]
     core, y, x = partners()
     copy = sender(send_sems, recv_sems)
     text_core = copy(0, text, texts.at[1], core)
     text_y = copy(1, text, texts.at[2], y)
-    image_x = copy(2, image, images.at[0], x)
+    image_x = copy(2, image_apart, images.at[0], x)
     image_core = copy(3, images.at[0], images.at[1], core)
     image_y = copy(4, images.at[0], images.at[2], y)
     text_corner = copy(5, texts.at[2], texts.at[3], core)
@@ -239,6 +280,7 @@
     corner_part = copy(8, parts.at[3], got.at[1], core)
     far_part = copy(9, total, got.at[2], y)
 
+    image_apart[...] = low(nn(spacing(pairs), image[...]))
     greet(core, y, x)
     image_x.start()
     text_y.start()
@@ -300,9 +342,8 @@
     total[...] = add(parts[2], got[1])
     far_part.start()
     near_part.wait()
-    size, image_size = text.shape[0], image.shape[0]
+    size, image_size = text.shape[0], image_apart.shape[0]
     below = 3 * size
-    image_own[...] = images[0]
 
     def summed(row, depth, count, start):
         for ref in (parts.at[0], got.at[0]):
@@ -425,15 +466,22 @@
         leave.wait()
 
 
-def cross_last(total, own_sum, vector_keep, vector_send, text_n, image_n, texts, images, grads, text_kept, image_kept, text_d, image_d, *refs):
-    text_grad, image_grad, text_keep, image_keep, image_send = refs[:5]
-    got, text_send, text_got, text_flip, text_g_flip, image_flip, image_g_flip, send_sems, recv_sems = refs[5:]
+def cross_last(total, own_sum, vector_keep, vector_send, self_top, self_x, text_n, image_n, texts, images, grads, text_kept, image_kept, text_d, image_d, *refs):
+    text_grad, image_grad, text_keep, image_keep, image_send, self_sum = refs[:6]
+    got, text_send, text_got, self_all, self_got, text_flip, text_g_flip, image_flip, image_g_flip, send_sems, recv_sems = refs[6:]
     unused_core, y, x = partners()
     copy = sender(send_sems, recv_sems)
     far = copy(0, total, got, y)
     text_x = copy(1, text_send, text_got, x)
-    greet(y, x)
+    dp = self_all.shape[0]
+    z_at = lax.axis_index("dp")
+    others = [lax.rem(z_at + k, dp) for k in range(1, dp)]
+    along_z = [copy(2 + k, self_all.at[other], self_got.at[k], {"dp": other}) for k, other in enumerate(others)]
+    greet(y, x, *[{"dp": other} for other in others])
     far.start()
+    self_all[...] = add(self_top[...], self_x[...])
+    for transfer in along_z:
+        transfer.start()
     size, image_size = texts.shape[1], images.shape[1]
     below = 3 * size
     for j in range(QUARTERS):
@@ -471,11 +519,17 @@
                 for z in range(dp):
                     out[z, below_all:, :] = vector[z]
             text_x.start()
+    summed = self_all[z_at].astype(F32)
+    for k, transfer in enumerate(along_z):
+        transfer.wait()
+        summed = summed + self_got[k].astype(F32)
+    self_sum[...] = low(summed)
     text_x.wait()
     text_keep[...] = add(text_keep[...], text_got[...])
     far.wait()
     text_grad[...] = text_n[...] + side(own_sum, 0, size, 3) + side(got, 0, size, 3).astype(F32)
-    image_grad[...] = low(image_n[...] + side(own_sum, below, image_size, 4) + side(got, below, image_size, 4).astype(F32))
+    image_total = low(image_n[...] + side(own_sum, below, image_size, 4) + side(got, below, image_size, 4).astype(F32))
+    image_grad[...] = low(tn(spacing(image_size // PADDED), image_total))
 
 
 def gate(hidden):
@@ -485,12 +539,12 @@
 
 
 def mlp_forward(pairs, text_pre, image_pre, text_gain, text_bias, image_gain, image_bias, *refs):
-    parts = refs[:6]
-    text_low, image_low, text_next, image_next = refs[6:10]
-    text_activ, text_slope, image_activ, image_slope = refs[10:14]
-    weights, sems = refs[14:]
+    parts = refs[:4]
+    text_low, image_low, text_next, image_next = refs[4:8]
+    text_activ, text_slope, image_activ, image_slope, corner = refs[8:13]
+    weights, sems, send_sems, recv_sems = refs[13:]
     step = pl.program_id(0)
-    fetch(step, FORWARD, gathered(parts), weights, sems)
+    leaving = fetch_round(step, *parts, corner, weights, sems, send_sems, recv_sems)
 
     @pl.when(step == 0)
     def begin():
@@ -514,6 +568,10 @@
     text_next[...] += nn(text_activ[0], side(w, 2304, 768, 3))
     image_next[...] += nn(image_activ[0], side(w, 5632, 256, 4))
 
+    @pl.when(step == QUARTERS - 1)
+    def finish():
+        leaving.wait()
+
 
 def lane_masks():
     lane = lax.broadcasted_iota(jnp.int32, (1, 2 * SELF_HEAD), 1)
@@ -530,7 +588,7 @@
 
 
 def self_forward(pairs, ids, lengths, text_pre, image_pre, text_gain, text_bias, image_gain, image_bias, text_cot, image_cot, *refs):
-    parts = refs[:6]
+    parts = refs[:4]
     (
         text_out,
         image_out,
@@ -546,10 +604,11 @@
         text_probs,
         image_kept,
         image_probs,
-    ) = refs[6:20]
-    weights, text_sum, image_sum, text_low, image_low, sems = refs[20:]
+        corner,
+    ) = refs[4:19]
+    weights, text_sum, image_sum, text_low, image_low, sems, send_sems, recv_sems = refs[19:]
     step = pl.program_id(0)
-    fetch(step, FORWARD, gathered(parts), weights, sems)
+    leaving = fetch_round(step, *parts, corner, weights, sems, send_sems, recv_sems)
     text_rows, image_rows = text_pre.shape[0], image_pre.shape[0]
 
     @pl.when(step == 0)
@@ -607,25 +666,32 @@
 
     @pl.when(step == QUARTERS - 1)
     def finish():
-        for total, gain, bias, cot, out, grad, vec, at in (
-            (text_sum, text_gain, text_bias, text_cot, text_out, text_grad, text_vec, 3 * text_rows),
-            (image_sum, image_gain, image_bias, image_cot, image_out, image_grad, image_vec, 6 * text_rows + 4 * image_rows),
+        apart = spacing(pairs)
+        image_cot_apart = nn(apart, image_cot[...])
+        for total, gain, bias, cot, grad, vec, at in (
+            (text_sum, text_gain, text_bias, text_cot[...].astype(F32), text_grad, text_vec, 3 * text_rows),
+            (image_sum, image_gain, image_bias, image_cot_apart, image_grad, image_vec, 6 * text_rows + 4 * image_rows),
         ):
             g, b = affine_row(gain, bias, 2)
             unit, scale = normed(total[...])
-            out[...] = (unit * g + b).astype(out.dtype)
-            back = norm_back(unit, scale, g, cot[...].astype(F32), vec)
+            value = unit * g + b
+            if total is text_sum:
+                text_out[...] = value
+            else:
+                image_out[...] = low(tn(apart, low(value)))
+            back = norm_back(unit, scale, g, cot, vec)
             grad[...] = back
             leave_blocks(rounded, at, low(back))
+        leaving.wait()
 
 
 def self_back(pairs, text_g, image_g, text_pre, image_pre, text_gain, image_gain, *refs):
     text_q, text_k, text_v, text_c, text_probs, image_kept, image_probs = refs[:7]
-    parts = refs[7:13]
-    text_n, image_n, text_vec, image_vec, near, keep = refs[13:19]
-    weights, found, text_sum, image_sum, text_g_low, image_g_low, text_d, image_d, sems, out_sems, send_sems, recv_sems = refs[19:]
+    parts = refs[7:12]
+    text_n, image_n, text_vec, image_vec, near, keep = refs[12:18]
+    weights, found, text_sum, image_sum, text_g_low, image_g_low, text_d, image_d, sems, out_sems, send_sems, recv_sems = refs[18:]
     step = pl.program_id(0)
-    fetch(step, BACKWARD, gathered(parts), weights, sems)
+    fetch(step, BACKWARD, *parts, weights, sems)
     core = partners()[0]
     copy = sender(send_sems, recv_sems)
 
@@ -707,11 +773,11 @@
 
 def mlp_back(pairs, text_g, image_g, text_one, image_one, text_pre, image_pre, text_gain, image_gain, *refs):
     text_activ, text_slope, image_activ, image_slope = refs[:4]
-    parts = refs[4:10]
-    text_n, image_n, next_low, text_vec, image_vec, rounded, rounded_near, near, keep = refs[10:19]
-    weights, found, text_sum, image_sum, text_g_low, image_g_low, text_d, sems, out_sems, send_sems, recv_sems = refs[19:]
+    parts = refs[4:9]
+    text_n, image_n, next_low, text_vec, image_vec, rounded, rounded_near, near, keep = refs[9:18]
+    weights, found, text_sum, image_sum, text_g_low, image_g_low, text_d, sems, out_sems, send_sems, recv_sems = refs[18:]
     step = pl.program_id(0)
-    fetch(step, BACKWARD, gathered(parts), weights, sems)
+    fetch(step, BACKWARD, *parts, weights, sems)
     size, image_size = text_g.shape[0], image_g.shape[0]
     core = partners()[0]
     copy = sender(send_sems, recv_sems)
@@ -820,12 +886,6 @@
                     bottom(b, 2, nn(image_g_lhs if b else image_lhs, image_block(b, 6)))
 
 
-def gathered(parts):
-    own, near, far, far_rest, corner, corner_rest = parts
-    cut = far.shape[0]
-    return ((0, 0, own), (1, 0, near), (2, 0, far), (2, cut, far_rest), (3, 0, corner), (3, cut, corner_rest))
-
-
 ANY = pl.BlockSpec(memory_space=pl.ANY)
 SCALARS = pl.BlockSpec(memory_space=pltpu.SMEM)
 
@@ -884,16 +944,6 @@
 
     def leave(self, *values):
         self.last = values
-
-
-def spread(packed, share):
-    far_rest = lax.all_gather(share, ("stream", "dp"), axis=0, tiled=True)
-    return packed[0], swap(packed[0], "tensor", 1), swap(packed[1], "tensor", 2), far_rest
-
-
-def spread_on(line, own, near, far, far_rest):
-    far, far_rest = line.take((far, far_rest))
-    return own, near, far, far_rest, swap(far, "tensor", 1), swap(far_rest, "tensor", 1)
 
 
 def add(left, right):
@@ -955,15 +1005,23 @@
     units = 2 * pairs
     ids = jnp.stack([x_at, x_at * dp + lax.axis_index("dp")] + [(t_at ^ j) * pairs for j in range(QUARTERS)]).astype(jnp.int32)
 
-    def spaced(rows):
-        apart = jnp.pad(rows.reshape(pairs, REGIONS, DV), ((0, 0), (0, PADDED - REGIONS), (0, 0)))
-        return apart.reshape(image_size, DV)
-
     def leave(rows):
-        return swap(rows.reshape(pairs, PADDED, DV)[:, :REGIONS].reshape(pairs * REGIONS, DV), "stream", 1).astype(F32)
+        return swap(rows, "stream", 1).astype(F32)
 
     line = Line()
-    mlp_packed = pack([text_up[0], text_down[0], image_up[0], image_down[0]], places, 5120, ids)
+    mlp_own, mlp_first, mlp_mine = pack([text_up[0], text_down[0], image_up[0], image_down[0]], places, 5120, ids)
+    mlp_share = swap(mlp_mine, "tensor", 2)
+    self_own, self_first, self_mine = pack(
+        [
+            text_self_qkv[0].transpose(1, 2, 0).reshape(-1, DT),
+            text_self_out[0],
+            image_self_qkv[0].reshape(DV, -1),
+            image_self_out[0],
+        ],
+        places,
+        4096,
+        after(ids, mlp_own),
+    )
     cross_w = (
         text_cross_q[0],
         image_cross_kv[0].reshape(DT, -1),
@@ -972,36 +1030,29 @@
         text_cross_out[0],
         image_cross_out[0],
     )
-    self_packed = pack(
-        [
-            text_self_qkv[0].transpose(1, 2, 0).reshape(-1, DT),
-            text_self_out[0],
-            image_self_qkv[0].reshape(DV, -1),
-            image_self_out[0],
-        ],
-        places,
-        3584,
-        after(ids, mlp_packed[0]),
-    )
-    line.leave(self_packed[0], cross_w[1], cross_w[2])
-    mlp_share = line.take(swap(mlp_packed[2], "tensor", 2))
-    self_share = line.take(swap(self_packed[2], "tensor", 2))
-    line.leave(mlp_share, self_share)
-    mlp_w = spread(mlp_packed, mlp_share)
-    self_w = spread(self_packed, after(self_share, mlp_share))
-    image_cot_here = swap(spaced(image_cot), "stream", 1)
+    line.leave(self_own)
+    mlp_share = line.take(mlp_share)
+    line.leave(mlp_share, cross_w[1], cross_w[2])
+    self_share = line.take(swap(self_mine, "tensor", 2))
+    line.leave(self_share)
+    mlp_rest = lax.all_gather(mlp_share, ("stream", "dp"), axis=0, tiled=True)
+    self_rest = lax.all_gather(self_share, ("stream", "dp"), axis=0, tiled=True)
+    self_near = swap(self_own, "tensor", 1)
+    mlp_near_w = swap(mlp_own, "tensor", 1)
+    image_cot_here = swap(image_cot, "stream", 1)
+    mlp_far = swap(mlp_first, "tensor", 2)
 
     text_wide, image_wide = shape(size, DT, of=F32), shape(image_size, DV, of=F32)
     text_f32, image_f32 = pltpu.VMEM((size, DT), F32), pltpu.VMEM((image_size, DV), F32)
     text_bf, image_bf = pltpu.VMEM((size, DT), BF), pltpu.VMEM((image_size, DV), BF)
-    in_sems, out_sems = pltpu.SemaphoreType.DMA((6,)), pltpu.SemaphoreType.DMA((2,))
+    in_sems, out_sems = pltpu.SemaphoreType.DMA((5,)), pltpu.SemaphoreType.DMA((2,))
     text_affine = [w(text_gain), w(text_bias)]
     image_affine = [w(image_gain), w(image_bias)]
     vector_outs = [w(shape(2, DT, of=F32)), w(shape(2, DV, of=F32))]
     part_rows = 3 * size + 4 * image_size
 
     def buffer(weights):
-        return pltpu.VMEM((QUARTERS, weights[0].shape[0], BLOCK), BF)
+        return pltpu.VMEM((QUARTERS,) + weights.shape, BF)
 
     in_four = [
         (QUARTERS, size, DT),
@@ -1015,21 +1066,22 @@
     def links(count):
         return [pltpu.SemaphoreType.DMA((count,)), pltpu.SemaphoreType.DMA((count,))]
 
-    text_pre1, image_pre1, image, texts, images, *cross_kept = run(
+    text_pre1, image_pre1, texts, images, *cross_kept = run(
         functools.partial(cross_forward, pairs),
         None,
-        [s(lengths), w(line.take(text_in)), w(spaced(image_in))] + [w(m) for m in cross_w],
-        [w(text_wide), w(image_wide), w(shape(image_size, DV))] + [a(shape(*dims)) for dims in in_four],
+        [s(lengths), w(line.take(text_in)), w(image_in)] + [w(m) for m in cross_w],
+        [w(text_wide), w(image_wide)] + [a(shape(*dims)) for dims in in_four],
         [pltpu.VMEM(dims, BF) for dims in in_four]
         + [pltpu.VMEM((QUARTERS, part_rows, BLOCK), BF), pltpu.VMEM((part_rows, BLOCK), BF), pltpu.VMEM((3, part_rows, BLOCK), BF)]
+        + [image_bf]
         + links(10)
         + [pltpu.SemaphoreType.DMA((6,))],
         70,
         1,
     )
     line.leave(text_pre1, image_cot_here)
-    mlp_w = spread_on(line, *mlp_w)
-    self_w = (*self_w[:2], swap(line.take(self_packed[1]), "tensor", 2), self_w[3])
+    mlp_far, mlp_rest = line.take((mlp_far, mlp_rest))
+    self_far = swap(after(self_first, mlp_far), "tensor", 2)
     (
         text_one,
         image_one,
@@ -1039,10 +1091,11 @@
         text_slope,
         image_activ,
         image_slope,
+        mlp_corner,
     ) = run(
         functools.partial(mlp_forward, pairs),
         FORWARD,
-        [w(text_pre1), w(image_pre1)] + text_affine + image_affine + [a(m) for m in mlp_w],
+        [w(text_pre1), w(image_pre1)] + text_affine + image_affine + [a(m) for m in (mlp_own, mlp_near_w, mlp_far, mlp_rest)],
         [
             w(shape(size, DT)),
             w(shape(image_size, DV)),
@@ -1052,12 +1105,15 @@
             q(shape(QUARTERS, size, 768)),
             q(shape(QUARTERS, image_size, 256)),
             q(shape(QUARTERS, image_size, 256)),
+            a(mlp_own),
         ],
-        [buffer(mlp_w), in_sems],
+        [buffer(mlp_own), in_sems] + links(2),
         1,
+        7,
     )
+    mlp_w = mlp_own, mlp_near_w, mlp_far, mlp_rest, mlp_corner
     line.leave(text_pre2)
-    self_w = spread_on(line, *self_w)
+    self_far, self_rest = line.take((self_far, self_rest))
     (
         text_out,
         image_out,
@@ -1073,6 +1129,7 @@
         self_probs,
         self_kept,
         self_image_probs,
+        self_corner,
     ) = run(
         functools.partial(self_forward, pairs),
         FORWARD,
@@ -1080,8 +1137,8 @@
         + text_affine
         + image_affine
         + [w(text_cot), w(image_cot_here)]
-        + [a(m) for m in self_w],
-        [w(text_wide), w(shape(image_size, DV)), w(text_wide), w(image_wide)]
+        + [a(m) for m in (self_own, self_near, self_far, self_rest)],
+        [w(text_wide), w(image_cot), w(text_wide), w(image_wide)]
         + vector_outs
         + [
             w(shape(2 * part_rows, BLOCK)),
@@ -1092,18 +1149,21 @@
             q(shape(QUARTERS, pairs, 384, SLOTS)),
             q(shape(QUARTERS, image_size, 1024)),
             q(shape(QUARTERS, units, PADDED, PADDED)),
+            a(self_own),
         ],
-        [buffer(self_w), text_f32, image_f32, text_bf, image_bf, in_sems],
+        [buffer(self_own), text_f32, image_f32, text_bf, image_bf, in_sems] + links(2),
         19,
+        8,
     )
-    image_out = leave(image_out)
+    self_w = self_own, self_near, self_far, self_rest, self_corner
+    image_out = swap(image_out, "stream", 1)
 
     text_depth, image_depth = DT // places, DV // places
     padded = -(-text_depth // 16) * 16
 
     def back_scratch(weights, rows):
         return [
-            buffer(weights),
+            buffer(weights[0]),
             pltpu.VMEM((QUARTERS, rows, BLOCK), BF),
             text_f32,
             image_f32,
@@ -1131,7 +1191,7 @@
 
     self_rows = 3 * size + 4 * image_size
     self_rounded_near = swap(self_rounded, "tensor", 1)
-    text_n2, image_n2, text_vec2, image_vec2, self_near, self_keep = run(
+    text_n2, image_n2, text_vec2, image_vec2, self_other, self_keep = run(
         functools.partial(self_back, pairs),
         BACKWARD,
         [
@@ -1157,7 +1217,7 @@
         23,
         2,
     )
-    to_y, self_top, to_z = weight_grads(True, ids, self_rounded, self_rounded_near, self_keep, self_near)
+    to_y, self_top, to_z = weight_grads(True, ids, self_rounded, self_rounded_near, self_keep, self_other)
     self_by_y = swap(to_y, "tensor", 2)
     self_bottom = fold_last(to_z)
     line.leave(self_top)
@@ -1194,7 +1254,7 @@
     )
     line.leave(grad_low)
     to_x, mlp_top, to_z = weight_grads(False, line.take(ids), mlp_rounded, mlp_rounded_near, mlp_keep, mlp_near)
-    self_top, self_by_y, to_x, to_z = after((self_top, self_by_y, to_x, to_z), mlp_top)
+    self_top, self_by_y, to_x, to_z, image_out = after((self_top, self_by_y, to_x, to_z, image_out), mlp_top)
     mlp_by_x = swap(to_x, "stream", 1)
     mlp_bottom = fold_last(to_z)
     self_top, to_x = add(self_top[0], self_by_y[0]), add(self_top[1], self_by_y[1])
@@ -1226,7 +1286,7 @@
     vectors = low(jnp.concatenate([text_vector, image_vector], axis=0).transpose(1, 0, 2))
     vector_keep = lax.dynamic_slice_in_dim(vectors, x_at * dp, dp, 0)
     vector_send = lax.dynamic_slice_in_dim(vectors, (1 - x_at) * dp, dp, 0)
-    text_grad, image_grad, cross_text, image_keep, image_send = run(
+    text_grad, image_grad, cross_text, image_keep, image_send, self_top = run(
         cross_last,
         None,
         [
@@ -1234,6 +1294,8 @@
             w(own_sum),
             w(vector_keep),
             w(vector_send),
+            w(self_top),
+            w(self_then_x),
             w(text_n1),
             w(image_n1),
             w(texts),
@@ -1246,33 +1308,35 @@
         ],
         [
             w(text_wide),
-            w(shape(image_size, DV)),
+            w(image_cot),
             w(shape(dp, text_only, BLOCK)),
             w(shape(dp, image_only, BLOCK)),
             w(shape(dp, image_only, BLOCK)),
+            w(shape(*self_top.shape[1:])),
         ],
         [
             pltpu.VMEM((part_rows, BLOCK), BF),
             pltpu.VMEM((dp, text_only, BLOCK), BF),
             pltpu.VMEM((dp, text_only, BLOCK), BF),
+            pltpu.VMEM(self_top.shape, BF),
+            pltpu.VMEM((dp - 1, *self_top.shape[1:]), BF),
             pltpu.VMEM((DT, QUARTERS * size), BF),
             pltpu.VMEM((DT, QUARTERS * size), BF),
             pltpu.VMEM((DV, QUARTERS * image_size), BF),
             pltpu.VMEM((DV, QUARTERS * image_size), BF),
         ]
-        + links(2),
+        + links(1 + dp),
         2,
         5,
     )
     line.leave(text_grad)
-    self_top, self_then_x, mlp_top, mlp_by_x, self_bottom, cross_text, image_send = line.take(
-        (self_top, self_then_x, mlp_top, mlp_by_x, self_bottom, cross_text, image_send)
+    mlp_top, mlp_by_x, self_bottom, cross_text, image_send = line.take(
+        (mlp_top, mlp_by_x, self_bottom, cross_text, image_send)
     )
     cross_text = fold_last(cross_text)
     image_send = swap(image_send, "stream", 1)
     mlp_top, to_y = add(mlp_top[0], mlp_by_x[0]), add(mlp_top[1], mlp_by_x[1])
     mlp_then_y = swap(to_y, "tensor", 2)
-    self_top = fold_last(add(self_top, self_then_x))
     line.leave(mlp_top, to_y)
     self_bottom = line.take(self_bottom).reshape(2, 2, 3 * image_depth, BLOCK)
     self_bottom_x = swap(self_bottom[:, 1], "stream", 1)
@@ -1313,7 +1377,7 @@
     below = 3 * padded
     return (
         text_out,
-        image_out,
+        image_out.astype(F32),
         text_grad,
         image_grad,
         text_pick(cross_text, 0, 1)[None],

time: 470 us -> 431 us (0.917)
  waiting for transfers between devices: 89.4 us -> 63.4 us
  local copies, waits for them, and re-layouts: 37.3 us -> 29.4 us
  starting transfers between devices: 24.3 us -> 18.7 us
    reduce_scatter x6 -> x5, waiting for transfers between devices: 28.5 us -> 12 us  [fold_last(): return lax.psum_scatter(total, 'dp', scatter_dimension=0, tiled=True)[0]]
    ppermute x23 -> x19, waiting for transfers between devices: 60.8 us -> 46.9 us  [swap(): lax.ppermute(value, axis, [(i, i ^ apart) for i in range(lax.axis_size(ax...]
    ppermute x23 -> x19, starting transfers between devices: 23.5 us -> 18 us  [swap(): lax.ppermute(value, axis, [(i, i ^ apart) for i in range(lax.axis_size(ax...]
    reshape x4 -> x0, local copies, waits for them, and re-layouts: 5.18 us -> none  [the longest x2 3.57 us: spaced(): rows.reshape(pairs, REGIONS, DV)]
    convert_element_type x9 -> x8, other arithmetic: 14.5 us -> 11 us  [low(): return value.astype(BF)]
    unnamed x53 -> x59, local copies, waits for them, and re-layouts: 16.4 us -> 17.8 us
  transfers between devices with their start and end apart: 31 -> 26, of which waited for: 12 -> 10; matrix products, arithmetic and copies ran while one was open for 12% -> 11% of each run, Pallas kernels for 51% -> 56%
where the time goes in v4:
time: 431 us; the launch traced here: 427 us
  Pallas kernels  277 us (64%)
  waiting for transfers between devices  63.4 us (15%)
  local copies, waits for them, and re-layouts  29.4 us (7%)
  other arithmetic  24.1 us (6%)
  starting transfers between devices  18.7 us (4%)
  between operations  14.8 us (3%)
    pallas_call x11, Pallas kernels, run(): pl.pallas_call(kernel, grid=(QUARTERS,) if order else (1,), in_specs=[spe...  277 us
    ppermute x19, waiting for transfers between devices, swap(): lax.ppermute(value, axis, [(i, i ^ apart) for i in range(lax.axis_size(ax...  46.9 us
    ppermute x19, starting transfers between devices, swap(): lax.ppermute(value, axis, [(i, i ^ apart) for i in range(lax.axis_size(ax...  18 us
    unnamed x59, local copies, waits for them, and re-layouts  17.8 us
    reduce_scatter x5, waiting for transfers between devices, fold_last(): return lax.psum_scatter(total, 'dp', scatter_dimension=0, tiled=True)[0]  12 us
    convert_element_type x8, other arithmetic, low(): return value.astype(BF)  11 us
  transfers between devices with their start and end apart: 26, of which 10 were waited for; matrix products, arithmetic and copies ran while one was open for 11% of the time, Pallas kernels for 56%

profile of v4, /device:TPU:0, one launch (start us, length us, event | category | flops | bytes accessed | tf_op | source)
XLA Modules:
  0.0 427.0 jit_solution(4796642009888686818)
XLA Ops:
  7.9 4.2 shard_map.390
  12.1 3.0 collective-permute-start.1
  15.9 1.6 copy.59.refs_2_
  17.5 4.3 %shard_map.391 = (bf16[6400,256]{1,0:T(8,128)(2,1)}, bf16[2304,256]{1,0:T(8,128)(2,1)}, bf16[512,256]{1,0:T(8,128)(2,1)}) custom-call(s32[6]{0:T(128)} %stack.39.ids.x_at, bf16[576,768]{1,0:T(8,128)(2,1)} %bitcast.174, bf16[192,768]{1,0:T(8,128)(2,1)} %bitcast.186, bf16[1024,768]{1,0:T(8,128)(2,1)} %copy.59.refs_2_, bf16[256,1024]{1,0:T(8,128)(2,1)} %bitcast.177), custom_call_target="tpu_custom_call" | custom-call | flops 3300000000 | bytes 1024 | tf_op jit(solution)/shard_map/pallas_call | solution.py:913
  23.2 1.8 collective-permute-start
  25.8 1.7 collective-permute-start.4
  27.5 2.4 copy.83
  31.0 1.8 collective-permute-done
  33.1 77.1 %shard_map.392 = (f32[512,768]{1,0:T(8,128)}, f32[192,1024]{1,0:T(8,128)}, bf16[4,512,768]{2,1,0:T(8,128)(2,1)}, bf16[4,192,1024]{2,1,0:T(8,128)(2,1)}, bf16[4,5...) custom-call(s32[16]{0:T(128)} %lengths.3, ...), custom_call_target="tpu_custom_call" | custom-call | flops 76999999488 | bytes 1024 | tf_op jit(solution)/shard_map/pallas_call | solution.py:913
  110.9 15.2 %shard_map.393 = (bf16[512,768]{1,0:T(8,128)(2,1)}, bf16[192,1024]{1,0:T(8,128)(2,1)}, f32[512,768]{1,0:T(8,128)}, f32[192,1024]{1,0:T(8,128)}, bf16[4,512,768]{...) custom-call(f32[512,768]{1,0:T(8,128)} %get-tuple-element.129.text_p, ...), custom_call_target="tpu_custom_call" | custom-call | flops 1100000000 | bytes 1024 | tf_op jit(solution)/shard_map/pallas_call | solution.py:913
  126.1 4.3 %all-gather.5.cloned.1.call-done.refs_3_.refs_10_ = bf16[4096,256]{1,0:T(8,128)(2,1)} async-done(((bf16[512,256]{1,0:T(8,128)(2,1)}), bf16[4096,256]{1,0:T(8,128)(2,1)}) %all-gather.5.cloned.1.call-update) | async-done | bytes 2097168 | tf_op jit(solution)/shard_map/all_gather | solution.py:1039
  130.4 7.9 %collective-permute-done.6.refs_2_.refs_9_ = bf16[2304,256]{1,0:T(8,128)(2,1)} collective-permute-done((bf16[2304,256]{1,0:T(8,128)(2,1)}, bf16[2304,256]{1,0:T(8,128)(2,1)}, u32[]{:S(2)}, u32[]{:S(2)}) %collective-permute-start.6) | collective-permute-done | bytes 1179680 | tf_op jit(solution)/shard_map/ppermute | solution.py:931
  138.3 20.0 %shard_map.394 = (f32[512,768]{1,0:T(8,128)}, bf16[148,1024]{1,0:T(8,128)(2,1)}, f32[512,768]{1,0:T(8,128)}, f32[192,1024]{1,0:T(8,128)}, f32[2,768]{1,0:T(2,128...) custom-call(s32[6]{0:T(128)} %stack.39.ids.x_at, ...), custom_call_target="tpu_custom_call" | custom-call | flops 20899999744 | bytes 1024 | tf_op jit(solution)/shard_map/pallas_call | solution.py:913
  158.8 23.0 %shard_map.395 = (f32[512,768]{1,0:T(8,128)}, f32[192,1024]{1,0:T(8,128)}, f32[2,768]{1,0:T(2,128)}, f32[2,1024]{1,0:T(2,128)}, bf16[2,2304,256]{2,1,0:T(8,128)(2,1)}, /*index=5*/bf16[2,2304,256]{2,1,0:T(8,128)(2,1)}) custom-call(f32[512,768]{1,0:T(8,128)} %get-tuple-element.142.text_g, f32[192,1024]{1,0:T(8,128)} %get-tuple-element.143.image_g, ...), custom_call_target="tpu_custom_call" | custom-call | flops 25300000768 | bytes 1024 | tf_op jit(solution)/shard_map/pallas_call | solution.py:913
  183.2 12.7 %shard_map.396 = (bf16[2,4,416,256]{3,2,1,0:T(8,128)(2,1)}, bf16[2,4,416,256]{3,2,1,0:T(8,128)(2,1)}, bf16[4,1536,256]{2,1,0:T(8,128)(2,1)}) custom-call(s32[6]{0:T(128)} %stack.39.ids.x_at, bf16[4608,256]{1,0:T(8,128)(2,1)} %get-tuple-element.141.own, bf16[4608,256]{1,0:T(8,128)(2,1)} %copy-done.20, bf16[2,2304,256]{2,1,0:T(8,128)(2,1)} %get-tuple-element.152.own_quarters, ...), custom_call_target="tpu_custom_call" | custom-call | flops 13200000000 | bytes 1024 | tf_op jit(solution)/shard_map/pallas_call | solution.py:913
  198.6 20.6 %shard_map.397 = (f32[512,768]{1,0:T(8,128)}, f32[192,1024]{1,0:T(8,128)}, bf16[2304,256]{1,0:T(8,128)(2,1)}, f32[2,768]{1,0:T(2,128)}, f32[2,1024]{1,0:T(2,128)...) custom-call(f32[512,768]{1,0:T(8,128)} %get-tuple-element.156.text_g, ...), custom_call_target="tpu_custom_call" | custom-call | flops 22000001024 | bytes 1024 | tf_op jit(solution)/shard_map/pallas_call | solution.py:913
  219.3 13.0 %shard_map.398 = (bf16[2,4,576,256]{3,2,1,0:T(8,128)(2,1)}, bf16[2,4,576,256]{3,2,1,0:T(8,128)(2,1)}, bf16[4,1024,256]{2,1,0:T(8,128)(2,1)}) custom-call(s32[6]{0:T(128)} %stack.39.ids.x_at, bf16[4608,256]{1,0:T(8,128)(2,1)} %get-tuple-element.168.own, bf16[4608,256]{1,0:T(8,128)(2,1)} %get-tuple-element.169.near, ...), custom_call_target="tpu_custom_call" | custom-call | flops 13200000000 | bytes 1024 | tf_op jit(solution)/shard_map/pallas_call | solution.py:913
  233.6 4.0 collective-permute-done.8
  237.6 1.6 fusion.3
  241.3 43.5 %shard_map.399 = (bf16[4,2304,256]{2,1,0:T(8,128)(2,1)}, bf16[4,512,768]{2,1,0:T(8,128)(2,1)}, bf16[4,192,768]{2,1,0:T(8,128)(2,1)}, f32[2304,256]{1,0:T(8,128)}...) custom-call(bf16[2304,256]{1,0:T(8,128)(2,1)} %get-tuple-element.179.grad, f32[16,1024]{1,0:T(8,128)} %concatenate.64.vectors, ...), custom_call_target="tpu_custom_call" | custom-call | flops 52800000000 | bytes 1024 | tf_op jit(solution)/shard_map/pallas_call | solution.py:913
  287.5 43.0 %shard_map.400 = (f32[512,768]{1,0:T(8,128)}, bf16[148,1024]{1,0:T(8,128)(2,1)}, bf16[4,400,256]{2,1,0:T(8,128)(2,1)}, bf16[4,512,256]{2,1,0:T(8,128)(2,1)}, bf1...) custom-call(bf16[2304,256]{1,0:T(8,128)(2,1)} %get-tuple-element.190.total, f32[2304,256]{1,0:T(8,128)} %get-tuple-element.191.own_sum, ...), custom_call_target="tpu_custom_call" | custom-call | flops 2200000000 | bytes 1024 | tf_op jit(solution)/shard_map/pallas_call | solution.py:913
  331.2 1.9 convert_element_type.209
  334.7 3.4 fusion.1
  338.1 16.4 %collective-permute-done.13 = bf16[4,512,256]{2,1,0:T(8,128)(2,1)S(1)} collective-permute-done((bf16[4,512,256]{2,1,0:T(8,128)(2,1)}, bf16[4,512,256]{2,1,0:T(8,128)(2,1)S(1)}, u32[]{:S(2)}, u32[]{:S(2)}) %collective-permute-start.13) | collective-permute-done | bytes 1048608 | tf_op jit(solution)/shard_map/ppermute | solution.py:931
  364.0 9.0 %collective-permute-done.11 = bf16[148,1024]{1,0:T(8,128)(2,1)} collective-permute-done((bf16[148,1024]{1,0:T(8,128)(2,1)}, bf16[148,1024]{1,0:T(8,128)(2,1)}, u32[]{:S(2)}, u32[]{:S(2)}) %collective-permute-start.11) | collective-permute-done | bytes 303136 | tf_op jit(solution)/shard_map/ppermute | solution.py:931
  373.1 1.9 convert_element_type.218
  378.2 1.7 slice_bitcast_fusion.2
  380.3 3.8 collective-permute-done.14
  384.2 2.6 add_convert_fusion
  390.3 2.7 collective-permute-done.16
  399.9 1.6 convert_bitcast_fusion.1
  403.2 12.0 %reduce-scatter.12.cloned.1.call-done = bf16[1,576,256]{2,1,0:T(8,128)(2,1)} async-done(((bf16[4,576,256]{2,1,0:T(8,128)(2,1)}), bf16[1,576,256]{2,1,0:T(8,128)(2,1)}) %reduce-scatter.12.cloned.1.call-update) | async-done | bytes 294928 | tf_op jit(solution)/shard_map/reduce_scatter | solution.py:954
  (153 shorter events, 48.4 us)
Async XLA Ops:
  7.2 103.0 %all-gather.3.cloned.1.call-start = ((), (), s32[]{:S(2)}) async-start(), calls=%async_computation.5 | async-start | bytes 2949120 | tf_op jit(solution)/shard_map/all_gather | solution.py:1038
  12.1 11.0 %collective-permute-start.1 = (bf16[640,256]{1,0:T(8,128)(2,1)}, bf16[640,256]{1,0:T(8,128)(2,1)}, u32[]{:S(2)}, u32[]{:S(2)}) collective-permute-start(bf16[640,256]{1,0:T(8,128)(2,1)} %get-tuple-element.124), channel_id=1, source_target_pairs={{0,2},{1,3},{2,0},{3,1},{4,6},{5,7},{6,4},{7,5},{8,10},{9,11},{10,... | collective-permute-start | bytes 983048 | tf_op jit(solution)/shard_map/ppermute | solution.py:931
  23.1 107.2 %all-gather.5.cloned.1.call-start = ((), (), s32[]{:S(2)}) async-start(), calls=%async_computation.6 | async-start | bytes 2359296 | tf_op jit(solution)/shard_map/all_gather | solution.py:1039
  23.2 9.6 %collective-permute-start = (bf16[512,256]{1,0:T(8,128)(2,1)}, bf16[512,256]{1,0:T(8,128)(2,1)}, u32[]{:S(2)}, u32[]{:S(2)}) collective-permute-start(bf16[512,256]{1,0:T(8,128)(2,1)} %get-tuple-element.123), channel_id=1, source_target_pairs={{0,2},{1,3},{2,0},{3,1},{4,6},{5,7},{6,4},{7,5},{8,10},{9,11},{10,... | collective-permute-start | bytes 786440 | tf_op jit(solution)/shard_map/ppermute | solution.py:931
  25.0 85.9 %collective-permute-start.2 = (bf16[6656,256]{1,0:T(8,128)(2,1)S(1)}, bf16[6656,256]{1,0:T(8,128)(2,1)}, u32[]{:S(2)}, u32[]{:S(2)}) collective-permute-start(bf16[6656,256]{1,0:T(8,128)(2,1)S(1)} %copy-done), channel_id=1, source_target_pairs={{0,1},{1,0},{2,3},{3,2},{4,5},{5,4},{6,7},{7,6},{8,9},{9,8},{10,11... | collective-permute-start | bytes 10223624 | tf_op jit(solution)/shard_map/ppermute | solution.py:931
  25.0 113.3 %collective-permute-start.5 = (bf16[6400,256]{1,0:T(8,128)(2,1)}, bf16[6400,256]{1,0:T(8,128)(2,1)}, u32[]{:S(2)}, u32[]{:S(2)}) collective-permute-start(bf16[6400,256]{1,0:T(8,128)(2,1)} %get-tuple-element.125.refs_0_.refs_7_), channel_id=1, source_target_pairs={{0,1},{1,0},{2,3},{3,2},{4,5},{5,4},{6,7},{7,6},{8,9},{9,8},{10,11... | collective-permute-start | bytes 9830408 | tf_op jit(solution)/shard_map/ppermute | solution.py:931
  25.5 84.7 %collective-permute-start.3 = (bf16[1536,256]{1,0:T(8,128)(2,1)}, bf16[1536,256]{1,0:T(8,128)(2,1)}, u32[]{:S(2)}, u32[]{:S(2)}) collective-permute-start(bf16[1536,256]{1,0:T(8,128)(2,1)} %get-tuple-element.131), channel_id=1, source_target_pairs={{0,2},{1,3},{2,0},{3,1},{4,6},{5,7},{6,4},{7,5},{8,10},{9,11},{10,... | collective-permute-start | bytes 2359304 | tf_op jit(solution)/shard_map/ppermute | solution.py:931
  25.8 84.4 %collective-permute-start.4 = (bf16[148,1024]{1,0:T(8,128)(2,1)}, bf16[148,1024]{1,0:T(8,128)(2,1)}, u32[]{:S(2)}, u32[]{:S(2)}) collective-permute-start(bf16[148,1024]{1,0:T(8,128)(2,1)} %param.27), channel_id=1, source_target_pairs={{0,16},{16,0},{1,17},{17,1},{2,18},{18,2},{3,19},{19,3},{4,20},{20... | collective-permute-start | bytes 909320 | tf_op jit(solution)/shard_map/ppermute | solution.py:931
  32.8 297.8 %reduce-scatter.6.cloned.1.call-start = ((), (), s32[]{:S(2)}) async-start(), calls=%async_computation.7 | async-start | bytes 3932160 | tf_op jit(solution)/shard_map/reduce_scatter | solution.py:954
  110.2 28.0 %collective-permute-start.6 = (bf16[2304,256]{1,0:T(8,128)(2,1)}, bf16[2304,256]{1,0:T(8,128)(2,1)}, u32[]{:S(2)}, u32[]{:S(2)}) collective-permute-start(bf16[2304,256]{1,0:T(8,128)(2,1)} %get-tuple-element.137), channel_id=1, source_target_pairs={{0,2},{1,3},{2,0},{3,1},{4,6},{5,7},{6,4},{7,5},{8,10},{9,11},{10,... | collective-permute-start | bytes 3538952 | tf_op jit(solution)/shard_map/ppermute | solution.py:931
  158.2 23.5 %collective-permute-start.7 = (bf16[4608,256]{1,0:T(8,128)(2,1)}, bf16[4608,256]{1,0:T(8,128)(2,1)S(1)}, u32[]{:S(2)}, u32[]{:S(2)}) collective-permute-start(bf16[4608,256]{1,0:T(8,128)(2,1)} %get-tuple-element.141.own), channel_id=1, source_target_pairs={{0,1},{1,0},{2,3},{3,2},{4,5},{5,4},{6,7},{7,6},{8,9},{9,8},{10,11... | collective-permute-start | bytes 7077896 | tf_op jit(solution)/shard_map/ppermute | solution.py:931
  195.9 182.4 %reduce-scatter.14.cloned.1.call-start = ((), (), s32[]{:S(2)}) async-start(), calls=%async_computation.11 | async-start | bytes 2621440 | tf_op jit(solution)/shard_map/reduce_scatter | solution.py:954
  196.6 37.1 %collective-permute-start.9 = (bf16[148,1024]{1,0:T(8,128)(2,1)}, bf16[148,1024]{1,0:T(8,128)(2,1)}, u32[]{:S(2)}, u32[]{:S(2)}) collective-permute-start(bf16[148,1024]{1,0:T(8,128)(2,1)} %get-tuple-element.174), channel_id=1, source_target_pairs={{0,16},{16,0},{1,17},{17,1},{2,18},{18,2},{3,19},{19,3},{4,20},{20... | collective-permute-start | bytes 909320 | tf_op jit(solution)/shard_map/ppermute | solution.py:931
  198.1 39.5 %collective-permute-start.8 = (bf16[2,4,416,256]{3,2,1,0:T(8,128)(2,1)}, bf16[2,4,416,256]{3,2,1,0:T(8,128)(2,1)S(1)}, u32[]{:S(2)}, u32[]{:S(2)}) collective-permute-start(bf16[2,4,416,256]{3,2,1,0:T(8,128)(2,1)} %get-tuple-element.155), channel_id=1, source_target_pairs={{0,2},{1,3},{2,0},{3,1},{4,6},{5,7},{6,4},{7,5},{8,10},{9,11},{10,... | collective-permute-start | bytes 5111816 | tf_op jit(solution)/shard_map/ppermute | solution.py:931
  219.2 13.1 %copy-start.14 = (f32[2,1024]{1,0:T(2,128)S(1)}, f32[2,1024]{1,0:T(2,128)}, u32[]{:S(2)}) copy-start(f32[2,1024]{1,0:T(2,128)} %get-tuple-element.185) | copy-start | bytes 24580
  219.3 13.1 %copy-start.15 = (f32[2,1024]{1,0:T(2,128)S(1)}, f32[2,1024]{1,0:T(2,128)}, u32[]{:S(2)}) copy-start(f32[2,1024]{1,0:T(2,128)} %get-tuple-element.184) | copy-start | bytes 24580
  219.3 13.1 %copy-start.16 = (f32[2,1024]{1,0:T(2,128)S(1)}, f32[2,1024]{1,0:T(2,128)}, u32[]{:S(2)}) copy-start(f32[2,1024]{1,0:T(2,128)} %get-tuple-element.183) | copy-start | bytes 24580
  219.3 18.4 %copy-start.2 = (bf16[2,4,416,256]{3,2,1,0:T(8,128)(2,1)S(1)}, bf16[2,4,416,256]{3,2,1,0:T(8,128)(2,1)}, u32[]{:S(2)}) copy-start(bf16[2,4,416,256]{3,2,1,0:T(8,128)(2,1)} %get-tuple-element.177) | copy-start | bytes 5111812
  239.2 47.4 %collective-permute-start.10 = (bf16[4,416,256]{2,1,0:T(8,128)(2,1)}, bf16[4,416,256]{2,1,0:T(8,128)(2,1)S(1)}, u32[]{:S(2)}, u32[]{:S(2)}) collective-permute-start(bf16[4,416,256]{2,1,0:T(8,128)(2,1)} %get-tuple-element.266), channel_id=1, source_target_pairs={{0,16},{16,0},{1,17},{17,1},{2,18},{18,2},{3,19},{19,3},{4,20},{20... | collective-permute-start | bytes 2555912 | tf_op jit(solution)/shard_map/ppermute | solution.py:931
  239.7 90.8 %collective-permute-start.12 = (bf16[2,4,576,256]{3,2,1,0:T(8,128)(2,1)}, bf16[2,4,576,256]{3,2,1,0:T(8,128)(2,1)}, u32[]{:S(2)}, u32[]{:S(2)}) collective-permute-start(bf16[2,4,576,256]{3,2,1,0:T(8,128)(2,1)} %get-tuple-element.202), channel_id=1, source_target_pairs={{0,16},{16,0},{1,17},{17,1},{2,18},{18,2},{3,19},{19,3},{4,20},{20... | collective-permute-start | bytes 7077896 | tf_op jit(solution)/shard_map/ppermute | solution.py:931
  241.3 153.2 %reduce-scatter.8.cloned.1.call-start = ((), (), s32[]{:S(2)}) async-start(), calls=%async_computation.8 | async-start | bytes 1024000 | tf_op jit(solution)/shard_map/reduce_scatter | solution.py:954
  330.6 69.3 %reduce-scatter.10.cloned.1.call-start = ((), (), s32[]{:S(2)}) async-start(), calls=%async_computation.9 | async-start | bytes 1310720 | tf_op jit(solution)/shard_map/reduce_scatter | solution.py:954
  330.7 23.9 %collective-permute-start.13 = (bf16[4,512,256]{2,1,0:T(8,128)(2,1)}, bf16[4,512,256]{2,1,0:T(8,128)(2,1)S(1)}, u32[]{:S(2)}, u32[]{:S(2)}) collective-permute-start(bf16[4,512,256]{2,1,0:T(8,128)(2,1)} %get-tuple-element.208), channel_id=1, source_target_pairs={{0,16},{16,0},{1,17},{17,1},{2,18},{18,2},{3,19},{19,3},{4,20},{20... | collective-permute-start | bytes 3145736 | tf_op jit(solution)/shard_map/ppermute | solution.py:931
  334.7 19.9 %copy-start.8 = (bf16[4,512,256]{2,1,0:T(8,128)(2,1)S(1)}, bf16[4,512,256]{2,1,0:T(8,128)(2,1)}, u32[]{:S(2)}) copy-start(bf16[4,512,256]{2,1,0:T(8,128)(2,1)} %get-tuple-element.207) | copy-start | bytes 3145732
  355.8 59.4 %reduce-scatter.12.cloned.1.call-start = ((), (), s32[]{:S(2)}) async-start(), calls=%async_computation.10 | async-start | bytes 1474560 | tf_op jit(solution)/shard_map/reduce_scatter | solution.py:954
  356.3 27.8 %collective-permute-start.14 = (bf16[4,576,256]{2,1,0:T(8,128)(2,1)S(1)}, bf16[4,576,256]{2,1,0:T(8,128)(2,1)}, u32[]{:S(2)}, u32[]{:S(2)}) collective-permute-start(bf16[4,576,256]{2,1,0:T(8,128)(2,1)S(1)} %copy-done.7), channel_id=1, source_target_pairs={{0,2},{1,3},{2,0},{3,1},{4,6},{5,7},{6,4},{7,5},{8,10},{9,11},{10,... | collective-permute-start | bytes 3538952 | tf_op jit(solution)/shard_map/ppermute | solution.py:931
  357.5 17.4 %collective-permute-start.17 = (bf16[2,384,256]{2,1,0:T(8,128)(2,1)}, bf16[2,384,256]{2,1,0:T(8,128)(2,1)}, u32[]{:S(2)}, u32[]{:S(2)}) collective-permute-start(bf16[2,384,256]{2,1,0:T(8,128)(2,1)} %slice_bitcast_fusion), channel_id=1, source_target_pairs={{0,16},{16,0},{1,17},{17,1},{2,18},{18,2},{3,19},{19,3},{4,20},{20... | collective-permute-start | bytes 1179656 | tf_op jit(solution)/shard_map/ppermute | solution.py:931
  360.3 12.8 %collective-permute-start.11 = (bf16[148,1024]{1,0:T(8,128)(2,1)}, bf16[148,1024]{1,0:T(8,128)(2,1)}, u32[]{:S(2)}, u32[]{:S(2)}) collective-permute-start(bf16[148,1024]{1,0:T(8,128)(2,1)} %get-tuple-element.201), channel_id=1, source_target_pairs={{0,16},{16,0},{1,17},{17,1},{2,18},{18,2},{3,19},{19,3},{4,20},{20... | collective-permute-start | bytes 909320 | tf_op jit(solution)/shard_map/ppermute | solution.py:931
  376.7 10.0 %collective-permute-start.18 = (bf16[384,256]{1,0:T(8,128)(2,1)}, bf16[384,256]{1,0:T(8,128)(2,1)}, u32[]{:S(2)}, u32[]{:S(2)}) collective-permute-start(bf16[384,256]{1,0:T(8,128)(2,1)} %slice_bitcast_fusion.4), channel_id=1, source_target_pairs={{0,2},{1,3},{2,0},{3,1},{4,6},{5,7},{6,4},{7,5},{8,10},{9,11},{10,... | collective-permute-start | bytes 589832 | tf_op jit(solution)/shard_map/ppermute | solution.py:931
  379.9 7.9 %collective-permute-start.15 = (bf16[2,256,256]{2,1,0:T(8,128)(2,1)}, bf16[2,256,256]{2,1,0:T(8,128)(2,1)S(1)}, u32[]{:S(2)}, u32[]{:S(2)}) collective-permute-start(bf16[2,256,256]{2,1,0:T(8,128)(2,1)} %slice_bitcast_fusion.2), channel_id=1, source_target_pairs={{0,16},{16,0},{1,17},{17,1},{2,18},{18,2},{3,19},{19,3},{4,20},{20... | collective-permute-start | bytes 786440 | tf_op jit(solution)/shard_map/ppermute | solution.py:931
  387.9 5.0 %collective-permute-start.16 = (bf16[256,256]{1,0:T(8,128)(2,1)S(1)}, bf16[256,256]{1,0:T(8,128)(2,1)S(1)}, u32[]{:S(2)}, u32[]{:S(2)}) collective-permute-start(bf16[256,256]{1,0:T(8,128)(2,1)S(1)} %slice_bitcast_fusion.6), channel_id=1, source_target_pairs={{0,2},{1,3},{2,0},{3,1},{4,6},{5,7},{6,4},{7,5},{8,10},{9,11},{10,... | collective-permute-start | bytes 393224 | tf_op jit(solution)/shard_map/ppermute | solution.py:931
  397.6 20.0 %copy-start.5 = (f32[512,768]{1,0:T(8,128)S(1)}, f32[512,768]{1,0:T(8,128)}, u32[]{:S(2)}) copy-start(f32[512,768]{1,0:T(8,128)} %get-tuple-element.326) | copy-start | bytes 4718596
  (15 other events, 52.5 us)
Sparse Core Ops, SparseCore 0:
  23.2 57.0 all-gather.2
  82.5 47.8 all-gather.4
  196.0 60.6 reduce-scatter.5
  258.8 43.8 reduce-scatter.13
  330.7 22.9 reduce-scatter.7
  356.5 26.4 reduce-scatter.9
  386.9 28.2 reduce-scatter.11

commit v5 on v4

--- a/solution.py
+++ b/solution.py
@@ -105,8 +105,9 @@
 
     @pl.when(step == 0)
     def begin():
-        for unused, copy in copies:
-            copy.start()
+        for slot, copy in copies:
+            if slot == 0:
+                copy.start()
 
     for at in range(QUARTERS):
 
@@ -115,6 +116,12 @@
             for slot, copy in copies:
                 if slot == at:
                     copy.wait()
+
+    @pl.when(step == 0)
+    def others():
+        for slot, copy in copies:
+            if slot > 0:
+                copy.start()
 
 
 def fetch_round(step, own, near, far, far_rest, corner, buffer, sems, send_sems, recv_sems):
@@ -151,18 +158,12 @@
     return low(chosen)
 
 
-def leave_quarter(step, buffer, near, keep, sems, copies):
-    kept = [pltpu.make_async_copy(buffer.at[at], keep.at[at - 2], sems.at[at - 2]) for at in (2, 3)]
-    for at in range(QUARTERS):
+def send_quarter(step, copies):
+    for at, copy in enumerate(copies):
 
         @pl.when(step == at)
         def leave():
-            (copies[at] if at < 2 else kept[at - 2]).start()
-
-    @pl.when(step == QUARTERS - 1)
-    def finish():
-        for copy in list(copies) + kept:
-            copy.wait()
+            copy.start()
 
 
 def affine_row(gain, bias, norm):
@@ -396,9 +397,18 @@
 def cross_back(pairs, grad, vectors, text_kept, image_kept, text_probs, image_probs, *refs):
     matrices = refs[:6]
     grads_out, text_d_out, image_d_out, own_sum, total, vector_sum = refs[6:12]
-    grads, text_d, image_d, parts, got, got_vectors, send_sems, recv_sems, out_sems = refs[12:]
+    grads, text_d, image_d, parts, got, got_vectors, *kept = refs[12:-4]
+    send_sems, recv_sems, out_sems, in_sems = refs[-4:]
     core, y, unused_x = partners()
     copy = sender(send_sems, recv_sems)
+    loads = [
+        [
+            pltpu.make_async_copy(source.at[j], ref.at[j], in_sems.at[j, n])
+            for n, (source, ref) in enumerate(zip((text_kept, image_kept, text_probs, image_probs), kept))
+        ]
+        for j in range(QUARTERS)
+    ]
+    text_kept, image_kept, text_probs, image_probs = kept
     to_core = copy(0, grad, grads.at[1], core)
     to_y = copy(1, grad, grads.at[2], y)
     corner = copy(2, grads.at[2], grads.at[3], core)
@@ -406,10 +416,14 @@
     corner_part = copy(4, parts.at[3], got.at[1], core)
     vectors_core = copy(5, vectors, got_vectors.at[0], core)
     vectors_y = copy(6, vector_sum, got_vectors.at[1], y)
+    for load in loads[0]:
+        load.start()
     greet(core, y)
     vectors_core.start()
     to_y.start()
     to_core.start()
+    for load in sum(loads[1:], []):
+        load.start()
     grads[0] = grad[...]
     vectors_core.wait()
     vector_sum[...] = vectors[...] + got_vectors[0]
@@ -428,6 +442,13 @@
         @pl.when(j == 3)
         def last():
             corner.wait()
+
+        for at in range(QUARTERS):
+
+            @pl.when(j == at)
+            def loaded():
+                for load in loads[at]:
+                    load.wait()
 
         cross_block_back(
             pairs,
@@ -466,9 +487,25 @@
         leave.wait()
 
 
-def cross_last(total, own_sum, vector_keep, vector_send, self_top, self_x, text_n, image_n, texts, images, grads, text_kept, image_kept, text_d, image_d, *refs):
-    text_grad, image_grad, text_keep, image_keep, image_send, self_sum = refs[:6]
-    got, text_send, text_got, self_all, self_got, text_flip, text_g_flip, image_flip, image_g_flip, send_sems, recv_sems = refs[6:]
+def halves(flip, values, x):
+    half = flip.shape[0] // 2
+    starts = [pl.multiple_of(lax.bitwise_xor(x, apart) * half, HEAD) for apart in range(2)]
+    return [nn(flip[pl.ds(start, half), :], values) for start in starts]
+
+
+def cross_last(total, vector_keep, vector_send, *refs):
+    sources, loaded = refs[:12], refs[18:30]
+    text_grad, image_grad, text_keep, image_keep_out, image_send_out, self_sum = refs[12:18]
+    got, image_keep, image_send, text_send, text_got, self_got, text_flip, text_g_flip, image_flip, image_g_flip = refs[30:40]
+    send_sems, recv_sems, in_sems, out_sems = refs[40:]
+    self_all, self_x, texts, grads, text_d, text_c, images, image_d, image_c, own_sum, text_n, image_n = loaded
+    loads = []
+    for n, (source, ref) in enumerate(zip(sources, loaded)):
+        if source.shape != ref.shape:
+            source = source.at[:, :, pl.ds(768, BLOCK)]
+        loads.append(pltpu.make_async_copy(source, ref, in_sems.at[n]))
+    for load in loads:
+        load.start()
     unused_core, y, x = partners()
     copy = sender(send_sems, recv_sems)
     far = copy(0, total, got, y)
@@ -479,57 +516,67 @@
     along_z = [copy(2 + k, self_all.at[other], self_got.at[k], {"dp": other}) for k, other in enumerate(others)]
     greet(y, x, *[{"dp": other} for other in others])
     far.start()
-    self_all[...] = add(self_top[...], self_x[...])
+    loads[0].wait()
+    loads[1].wait()
+    self_all[...] = add(self_all[...], self_x[...])
     for transfer in along_z:
         transfer.start()
     size, image_size = texts.shape[1], images.shape[1]
     below = 3 * size
-    for j in range(QUARTERS):
-        text_flip[:, rows_of(j, size)] = texts[j].T
-        image_flip[:, rows_of(j, image_size)] = images[j].T
-        for b in range(3):
-            text_g_flip[rows_of(b, BLOCK), rows_of(j, size)] = grads[j, rows_of(b, size), :].T
-        for b in range(4):
-            start = below + b * image_size
-            image_g_flip[rows_of(b, BLOCK), rows_of(j, image_size)] = grads[j, start : start + image_size, :].T
     at = lax.axis_index("stream")
-    for flip, g_flip, d, kept, keep, send in (
-        (text_flip, text_g_flip, text_d, text_kept, text_keep, text_send),
-        (image_flip, image_g_flip, image_d, image_kept, image_keep, image_send),
+    leaving = []
+    for first, rows, count, flip, g_flip, keep, send, number in (
+        (0, size, 3, text_flip, text_g_flip, text_keep, text_send, (2, 3, 4, 5)),
+        (below, image_size, 4, image_flip, image_g_flip, image_keep, image_send, (6, 3, 7, 8)),
     ):
-        dp = keep.shape[0]
-        half = flip.shape[0] // 2
-        depth = half // dp
+        values, unused, outer, context = (loaded[n] for n in number)
+        for n in number[:1] if count == 4 else number[:2]:
+            loads[n].wait()
+        for j in range(QUARTERS):
+            columns = rows_of(j, rows)
+            for b in range(count):
+                flip[rows_of(b, BLOCK), columns] = values[j, :, b * BLOCK : (b + 1) * BLOCK].T
+                g_flip[rows_of(b, BLOCK), columns] = grads[j, first + b * rows : first + (b + 1) * rows, :].T
+        loads[number[2]].wait()
+        loads[number[3]].wait()
+        depth = flip.shape[0] // (2 * dp)
         padded = -(-depth // 16) * 16
-        rows = flip.shape[1]
-        outer = d[...].reshape(rows, 768)
-        context = kept[:, :, 768:1024].reshape(rows, 256)
-        for out, apart in ((send, 1), (keep, 0)):
-            start = pl.multiple_of(lax.bitwise_xor(at, apart) * half, 128)
-            found = nn(flip[pl.ds(start, half), :], outer)
-            last = nn(g_flip[pl.ds(start, half), :], context)
+        found_halves = halves(flip, outer[...].reshape(QUARTERS * rows, 768), at)
+        last_halves = halves(g_flip, context[...].reshape(QUARTERS * rows, BLOCK), at)
+        for out, found, last in zip((keep, send), found_halves, last_halves):
             for z in range(dp):
                 taken = slice(z * depth, (z + 1) * depth)
                 for b in range(3):
                     out[z, b * padded : b * padded + depth, :] = low(found[taken, b * BLOCK : (b + 1) * BLOCK])
                 out[z, 3 * padded : 3 * padded + depth, :] = low(last[taken])
-        if flip is text_flip:
+        if count == 3:
             for out, vector in ((text_keep, vector_keep), (text_send, vector_send)):
                 below_all = out.shape[1] - vector.shape[1]
                 for z in range(dp):
                     out[z, below_all:, :] = vector[z]
             text_x.start()
+        else:
+            leaving = [
+                pltpu.make_async_copy(image_keep, image_keep_out, out_sems.at[0]),
+                pltpu.make_async_copy(image_send, image_send_out, out_sems.at[1]),
+            ]
+            for leave in leaving:
+                leave.start()
     summed = self_all[z_at].astype(F32)
     for k, transfer in enumerate(along_z):
         transfer.wait()
         summed = summed + self_got[k].astype(F32)
     self_sum[...] = low(summed)
-    text_x.wait()
-    text_keep[...] = add(text_keep[...], text_got[...])
+    for load in loads[9:]:
+        load.wait()
     far.wait()
     text_grad[...] = text_n[...] + side(own_sum, 0, size, 3) + side(got, 0, size, 3).astype(F32)
     image_total = low(image_n[...] + side(own_sum, below, image_size, 4) + side(got, below, image_size, 4).astype(F32))
     image_grad[...] = low(tn(spacing(image_size // PADDED), image_total))
+    text_x.wait()
+    text_keep[...] = add(text_keep[...], text_got[...])
+    for leave in leaving:
+        leave.wait()
 
 
 def gate(hidden):
@@ -685,19 +732,24 @@
         leaving.wait()
 
 
-def self_back(pairs, text_g, image_g, text_pre, image_pre, text_gain, image_gain, *refs):
+def self_back(pairs, dp, text_g, image_g, text_pre, image_pre, text_gain, image_gain, rounded, *refs):
     text_q, text_k, text_v, text_c, text_probs, image_kept, image_probs = refs[:7]
     parts = refs[7:12]
-    text_n, image_n, text_vec, image_vec, near, keep = refs[12:18]
-    weights, found, text_sum, image_sum, text_g_low, image_g_low, text_d, image_d, sems, out_sems, send_sems, recv_sems = refs[18:]
+    text_n, image_n, text_vec, image_vec = refs[12:16]
+    outs = refs[16:19]
+    weights, found, text_sum, image_sum, text_g_low, image_g_low, near, rounded_near = refs[19:27]
+    flips, (text_d, image_d, sems, out_sems, send_sems, recv_sems) = refs[27:31], refs[31:]
     step = pl.program_id(0)
     fetch(step, BACKWARD, *parts, weights, sems)
     core = partners()[0]
     copy = sender(send_sems, recv_sems)
+    copies = [copy(n, found.at[n], near.at[n], core) for n in range(2)]
+    rounded_copy = copy(2, rounded, rounded_near, core)
 
     @pl.when(step == 0)
     def begin():
         greet(core)
+        rounded_copy.start()
         text_sum[...] = text_g[...]
         image_sum[...] = image_g[...]
         text_g_low[...] = low(text_g[...])
@@ -755,11 +807,15 @@
     slot[2 * size : 3 * size, 128:256] = jnp.concatenate([text_d[2, :, last], text_c[0, :, last]], axis=1)
     leave_blocks(slot, 3 * size, image_d[...])
     leave_blocks(slot, 3 * size + 3 * image_g.shape[0], image_kept[0, :, 768:1024])
-    leave_quarter(step, found, near, keep, out_sems, [copy(n, found.at[n], near.at[n], core) for n in range(2)])
+    send_quarter(step, copies)
 
     @pl.when(step == QUARTERS - 1)
     def finish():
         leave_norm(1, text_sum, image_sum, text_pre, image_pre, text_gain, image_gain, text_n, image_n, text_vec, image_vec)
+        rounded_copy.wait()
+        for transfer in copies:
+            transfer.wait()
+        weight_grad(True, dp, (size, image_g.shape[0]), (rounded, rounded_near), found, near, weights, outs, flips, out_sems)
 
 
 def leave_norm(norm, text_sum, image_sum, text_pre, image_pre, text_gain, image_gain, text_n, image_n, text_vec, image_vec):
@@ -771,17 +827,20 @@
         out[...] = norm_back(unit, scale, gain[0, norm : norm + 1, :].astype(F32), total[...], vec)
 
 
-def mlp_back(pairs, text_g, image_g, text_one, image_one, text_pre, image_pre, text_gain, image_gain, *refs):
+def mlp_back(pairs, dp, text_g, image_g, text_one, image_one, text_pre, image_pre, text_gain, image_gain, *refs):
     text_activ, text_slope, image_activ, image_slope = refs[:4]
     parts = refs[4:9]
-    text_n, image_n, next_low, text_vec, image_vec, rounded, rounded_near, near, keep = refs[9:18]
-    weights, found, text_sum, image_sum, text_g_low, image_g_low, text_d, sems, out_sems, send_sems, recv_sems = refs[18:]
+    text_n, image_n, next_low, text_vec, image_vec = refs[9:14]
+    outs = refs[14:17]
+    weights, found, text_sum, image_sum, text_g_low, image_g_low, near, rounded_near = refs[17:25]
+    flips, (rounded, text_d, sems, out_sems, send_sems, recv_sems) = refs[25:29], refs[29:]
     step = pl.program_id(0)
     fetch(step, BACKWARD, *parts, weights, sems)
     size, image_size = text_g.shape[0], image_g.shape[0]
     core = partners()[0]
     copy = sender(send_sems, recv_sems)
     rounded_copy = copy(2, rounded, rounded_near, core)
+    copies = [copy(n, found.at[n], near.at[n], core) for n in range(2)]
 
     @pl.when(step == 0)
     def begin():
@@ -810,89 +869,101 @@
     leave_blocks(slot, 3 * size, text_activ[0])
     leave_blocks(slot, 6 * size, image_d)
     leave_blocks(slot, 6 * size + image_size, image_activ[0])
-    leave_quarter(step, found, near, keep, out_sems, [copy(n, found.at[n], near.at[n], core) for n in range(2)])
+    send_quarter(step, copies)
 
     @pl.when(step == QUARTERS - 1)
     def finish():
-        rounded_copy.wait()
         leave_norm(0, text_sum, image_sum, text_pre, image_pre, text_gain, image_gain, text_n, image_n, text_vec, image_vec)
         leave_blocks(next_low, 0, low(text_n[...]))
         leave_blocks(next_low, 3 * size, low(image_n[...]))
-
-
-def weight_grad(is_self, sizes, x_at, own, near, own_quarters, near_quarters, *refs):
-    to_send, kept, to_z, text_flip, text_g_flip, image_flip, image_g_flip = refs
+        rounded_copy.wait()
+        for transfer in copies:
+            transfer.wait()
+        weight_grad(False, dp, (size, image_size), (rounded, rounded_near), found, near, weights, outs, flips, out_sems)
+
+
+def weight_grad(is_self, dp, sizes, rounded, found, near, spare, outs, flips, out_sems):
+    text_flip, text_g_flip, image_flip, image_g_flip = flips
+    to_send, kept, to_z = (spare.at[n] for n in range(3))
     size, image_size = sizes
-    dp = kept.shape[1]
-    x = x_at[0]
-    for at, source in ((0, own), (1, near)):
-        rows, image_rows = rows_of(at, size), rows_of(at, image_size)
+    x = lax.axis_index("stream")
+    for at in range(2):
         for b in range(3):
-            text_flip[rows_of(b, BLOCK), rows] = source[rows_of(b, size), :].T
-            text_g_flip[rows_of(b, BLOCK), rows] = source[rows_of(3 + b, size), :].T
-        for b in range(4):
-            start = 6 * size
-            image_flip[rows_of(b, BLOCK), image_rows] = source[start + b * image_size : start + (b + 1) * image_size, :].T
-            start = 6 * size + 4 * image_size
-            image_g_flip[rows_of(b, BLOCK), image_rows] = source[start + b * image_size : start + (b + 1) * image_size, :].T
+            text_flip[rows_of(b, BLOCK), rows_of(at, size)] = rounded[at][rows_of(b, size), :].T
+            text_g_flip[rows_of(b, BLOCK), rows_of(at, size)] = rounded[at][rows_of(3 + b, size), :].T
+        for b in range(8):
+            start = 6 * size + b * image_size
+            flip = image_g_flip if b > 3 else image_flip
+            flip[rows_of(b % 4, BLOCK), rows_of(at, image_size)] = rounded[at][start : start + image_size, :].T
 
     text_depth, image_depth = DT // (2 * dp), DV // (2 * dp)
     padded = -(-text_depth // 16) * 16
-
-    def write(ref, at, row, depth, value):
-        for z in range(dp):
-            ref[at, z, row : row + depth, :] = low(value[z * depth : (z + 1) * depth])
-
     lane = lax.broadcasted_iota(jnp.int32, (1, HEAD), 1) < SELF_HEAD
+    top = 3 * padded + image_depth if is_self else 6 * padded
+    count = 3 if is_self else 2
+    leaving = []
+
+    def leave(source, target):
+        leaving.append(pltpu.make_async_copy(source.at[pl.ds(0, target.shape[0])], target, out_sems.at[len(leaving)]))
+        leaving[-1].start()
+
     for slot in (1, 0):
 
+        def block(start, rows):
+            return jnp.concatenate([found[2 + slot, start : start + rows, :], near[slot, start : start + rows, :]], axis=0)
+
         def text_block(b):
-            return jnp.concatenate([q[slot, rows_of(b, size), :] for q in (own_quarters, near_quarters)], axis=0)
+            return block(b * size, size)
 
         def image_block(b, text_blocks):
-            start = text_blocks * size + b * image_size
-            return jnp.concatenate([q[slot, start : start + image_size, :] for q in (own_quarters, near_quarters)], axis=0)
-
-        for apart in range(2):
-            half = lax.bitwise_xor(x, apart)
-            text_rows = pl.ds(pl.multiple_of(half * (DT // 2), 128), DT // 2)
-            image_rows = pl.ds(pl.multiple_of(half * (DV // 2), 128), DV // 2)
-            text_lhs, image_lhs = text_flip[text_rows, :], image_flip[image_rows, :]
-            text_g_lhs, image_g_lhs = text_g_flip[text_rows, :], image_g_flip[image_rows, :]
-
-            def bottom(b, count, value):
-                row = ((2 * slot + apart) * count + b) * image_depth
+            return block(text_blocks * size + b * image_size, image_size)
+
+        def write(row, depth, value):
+            for apart in range(2):
+                ref, at = ((to_send if slot else kept), apart) if is_self else ((to_send if apart else kept), slot)
                 for z in range(dp):
-                    to_z[z, row : row + image_depth, :] = low(value[z * image_depth : (z + 1) * image_depth])
-
-            if is_self:
-                top, at = (to_send if slot else kept), apart
-                one, two, three = text_block(0), text_block(1), text_block(2)
-                write(top, at, 0, text_depth, nn(text_lhs, one))
-                mixed = jnp.concatenate([nn(text_lhs, two[:, :HEAD]), nn(text_g_lhs, two[:, HEAD:])], axis=1)
-                write(top, at, padded, text_depth, mixed)
-                from_x = nn(text_lhs, three)
-                from_g = nn(text_g_lhs, three[:, HEAD:])
-                mixed = jnp.concatenate([from_x[:, :HEAD], jnp.where(lane, from_x[:, HEAD:], from_g)], axis=1)
-                write(top, at, 2 * padded, text_depth, mixed)
-                write(top, at, 3 * padded, image_depth, nn(image_lhs, image_block(0, 3)))
-                for b in range(3):
-                    bottom(b, 3, nn(image_g_lhs if b == 2 else image_lhs, image_block(1 + b, 3)))
-            else:
-                top, at = (to_send if apart else kept), slot
-                for b in range(6):
-                    write(top, at, b * padded, text_depth, nn(text_g_lhs if b > 2 else text_lhs, text_block(b)))
-                for b in range(2):
-                    bottom(b, 2, nn(image_g_lhs if b else image_lhs, image_block(b, 6)))
+                    to = (at * dp + z) * top + row
+                    ref[to : to + depth, :] = low(value[apart][z * depth : (z + 1) * depth])
+
+        def bottom(b, value):
+            for apart in range(2):
+                for z in range(dp):
+                    to = ((z * 4 + 2 * slot + apart) * count + b) * image_depth
+                    to_z[to : to + image_depth, :] = low(value[apart][z * image_depth : (z + 1) * image_depth])
+
+        if is_self:
+            one, two, three = text_block(0), text_block(1), text_block(2)
+            write(0, text_depth, halves(text_flip, one, x))
+            pairs = zip(halves(text_flip, two[:, :HEAD], x), halves(text_g_flip, two[:, HEAD:], x))
+            write(padded, text_depth, [jnp.concatenate(pair, axis=1) for pair in pairs])
+            pairs = zip(halves(text_flip, three, x), halves(text_g_flip, three[:, HEAD:], x))
+            mixed = [jnp.concatenate([a[:, :HEAD], jnp.where(lane, a[:, HEAD:], b)], axis=1) for a, b in pairs]
+            write(2 * padded, text_depth, mixed)
+            write(3 * padded, image_depth, halves(image_flip, image_block(0, 3), x))
+            leave(*((to_send, outs[0]) if slot else (kept, outs[1])))
+            for b in range(3):
+                bottom(b, halves(image_g_flip if b == 2 else image_flip, image_block(1 + b, 3), x))
+        else:
+            for b in range(6):
+                write(b * padded, text_depth, halves(text_g_flip if b > 2 else text_flip, text_block(b), x))
+            for b in range(2):
+                bottom(b, halves(image_g_flip if b else image_flip, image_block(b, 6), x))
+    if not is_self:
+        leave(to_send, outs[0])
+        leave(kept, outs[1])
+    leave(to_z, outs[2])
+    for copy in leaving:
+        copy.wait()
 
 
 ANY = pl.BlockSpec(memory_space=pl.ANY)
 SCALARS = pl.BlockSpec(memory_space=pltpu.SMEM)
 
 
-def whole(array):
+def whole(array, buffers=None):
     zeros = (0,) * len(array.shape)
-    return pl.BlockSpec(array.shape, lambda *s: zeros)
+    mode = {} if buffers is None else {"pipeline_mode": pl.Buffered(buffers)}
+    return pl.BlockSpec(array.shape, lambda *s: zeros, **mode)
 
 
 def quarter(array, order):
@@ -907,13 +978,15 @@
 
 
 def run(kernel, order, operands, outs, scratch, us, meeting=None):
-    def spec(kind, array):
+    def spec(kind, array, given=False):
+        if kind == "w" and given and order:
+            return whole(array, 1)
         return {"s": lambda: SCALARS, "w": lambda: whole(array), "q": lambda: quarter(array, order), "a": lambda: ANY}[kind]()
 
     return pl.pallas_call(
         kernel,
         grid=(QUARTERS,) if order else (1,),
-        in_specs=[spec(*entry) for entry in operands],
+        in_specs=[spec(*entry, given=True) for entry in operands],
         out_specs=[spec(*entry) for entry in outs],
         out_shape=[array for unused, array in outs],
         scratch_shapes=scratch,
@@ -1045,7 +1118,7 @@
     text_wide, image_wide = shape(size, DT, of=F32), shape(image_size, DV, of=F32)
     text_f32, image_f32 = pltpu.VMEM((size, DT), F32), pltpu.VMEM((image_size, DV), F32)
     text_bf, image_bf = pltpu.VMEM((size, DT), BF), pltpu.VMEM((image_size, DV), BF)
-    in_sems, out_sems = pltpu.SemaphoreType.DMA((5,)), pltpu.SemaphoreType.DMA((2,))
+    in_sems, out_sems = pltpu.SemaphoreType.DMA((5,)), pltpu.SemaphoreType.DMA((3,))
     text_affine = [w(text_gain), w(text_bias)]
     image_affine = [w(image_gain), w(image_bias)]
     vector_outs = [w(shape(2, DT, of=F32)), w(shape(2, DV, of=F32))]
@@ -1169,30 +1242,30 @@
             image_f32,
             text_bf,
             image_bf,
+            pltpu.VMEM((2, rows, BLOCK), BF),
+            pltpu.VMEM((2 * part_rows, BLOCK), BF),
+            pltpu.VMEM((DT, 2 * size), BF),
+            pltpu.VMEM((DT, 2 * size), BF),
+            pltpu.VMEM((DV, 2 * image_size), BF),
+            pltpu.VMEM((DV, 2 * image_size), BF),
         ]
 
-    def weight_grads(is_self, turn, rounded, rounded_near, kept, kept_near):
+    def grad_shapes(is_self):
         top = 3 * padded + image_depth if is_self else 6 * padded
         bottom = (3 if is_self else 2) * image_depth
-        outs = [w(shape(2, dp, top, BLOCK)), w(shape(2, dp, top, BLOCK)), w(shape(dp, 4 * bottom, BLOCK))]
-        return run(
-            functools.partial(weight_grad, is_self, (size, image_size)),
-            None,
-            [s(turn), w(rounded), w(rounded_near), w(kept), w(kept_near)],
-            outs,
-            [
-                pltpu.VMEM((DT, 2 * size), BF),
-                pltpu.VMEM((DT, 2 * size), BF),
-                pltpu.VMEM((DV, 2 * image_size), BF),
-                pltpu.VMEM((DV, 2 * image_size), BF),
-            ],
-            12,
-        )
+        return (2, dp, top, BLOCK), (dp, 4 * bottom, BLOCK)
+
+    def grad_outs(is_self):
+        first, last = grad_shapes(is_self)
+        return [a(shape(2 * dp * first[2], BLOCK))] * 2 + [a(shape(dp * last[1], BLOCK))]
+
+    def grad_arrays(is_self, to_send, kept, to_z):
+        first, last = grad_shapes(is_self)
+        return to_send.reshape(first), kept.reshape(first), to_z.reshape(last)
 
     self_rows = 3 * size + 4 * image_size
-    self_rounded_near = swap(self_rounded, "tensor", 1)
-    text_n2, image_n2, text_vec2, image_vec2, self_other, self_keep = run(
-        functools.partial(self_back, pairs),
+    text_n2, image_n2, text_vec2, image_vec2, *self_found = run(
+        functools.partial(self_back, pairs, dp),
         BACKWARD,
         [
             w(text_n3),
@@ -1201,6 +1274,7 @@
             w(image_pre2),
             w(text_gain),
             w(image_gain),
+            w(self_rounded),
             q(self_q),
             q(self_k),
             q(self_v),
@@ -1210,20 +1284,20 @@
             q(self_image_probs),
         ]
         + [a(m) for m in self_w],
-        [w(text_wide), w(image_wide)] + vector_outs + [a(shape(2, self_rows, BLOCK)), a(shape(2, self_rows, BLOCK))],
+        [w(text_wide), w(image_wide)] + vector_outs + grad_outs(True),
         back_scratch(self_w, self_rows)
         + [pltpu.VMEM((3, size, 192), BF), pltpu.VMEM((image_size, 768), BF), in_sems, out_sems]
-        + links(2),
-        23,
+        + links(3),
+        32,
         2,
     )
-    to_y, self_top, to_z = weight_grads(True, ids, self_rounded, self_rounded_near, self_keep, self_other)
+    to_y, self_top, to_z = grad_arrays(True, *self_found)
     self_by_y = swap(to_y, "tensor", 2)
     self_bottom = fold_last(to_z)
     line.leave(self_top)
     mlp_rows = 6 * size + 2 * image_size
-    text_n1, image_n1, grad_low, text_vec1, image_vec1, mlp_rounded, mlp_rounded_near, mlp_near, mlp_keep = run(
-        functools.partial(mlp_back, pairs),
+    text_n1, image_n1, grad_low, text_vec1, image_vec1, *mlp_found = run(
+        functools.partial(mlp_back, pairs, dp),
         BACKWARD,
         [
             w(text_n2),
@@ -1242,18 +1316,15 @@
         + [a(m) for m in mlp_w],
         [w(text_wide), w(image_wide), w(shape(part_rows, BLOCK))]
         + vector_outs
-        + [
-            w(shape(2 * part_rows, BLOCK)),
-            a(shape(2 * part_rows, BLOCK)),
-            a(shape(2, mlp_rows, BLOCK)),
-            a(shape(2, mlp_rows, BLOCK)),
-        ],
-        back_scratch(mlp_w, mlp_rows) + [text_bf, in_sems, out_sems] + links(3),
-        20,
+        + grad_outs(False),
+        back_scratch(mlp_w, mlp_rows)
+        + [pltpu.VMEM((2 * part_rows, BLOCK), BF), text_bf, in_sems, out_sems]
+        + links(3),
+        28,
         3,
     )
     line.leave(grad_low)
-    to_x, mlp_top, to_z = weight_grads(False, line.take(ids), mlp_rounded, mlp_rounded_near, mlp_keep, mlp_near)
+    to_x, mlp_top, to_z = grad_arrays(False, *mlp_found)
     self_top, self_by_y, to_x, to_z, image_out = after((self_top, self_by_y, to_x, to_z, image_out), mlp_top)
     mlp_by_x = swap(to_x, "stream", 1)
     mlp_bottom = fold_last(to_z)
@@ -1269,13 +1340,14 @@
     grads, text_d, image_d, own_sum, total, vectors = run(
         functools.partial(cross_back, pairs),
         None,
-        [w(line.take(grad_low)), w(vectors)] + [w(k) for k in cross_kept] + [w(m) for m in cross_w],
+        [w(line.take(grad_low)), w(vectors)] + [a(k) for k in cross_kept] + [w(m) for m in cross_w],
         [a(shape(*dims)) for dims in d_dims]
         + [w(shape(part_rows, BLOCK, of=F32)), w(shape(part_rows, BLOCK)), w(shape(16, DV, of=F32))],
         [pltpu.VMEM(dims, BF) for dims in d_dims]
         + [pltpu.VMEM((QUARTERS, part_rows, BLOCK), BF), pltpu.VMEM((2, part_rows, BLOCK), BF), pltpu.VMEM((2, 16, DV), F32)]
+        + [pltpu.VMEM(k.shape, BF) for k in cross_kept]
         + links(7)
-        + [pltpu.SemaphoreType.DMA((3,))],
+        + [pltpu.SemaphoreType.DMA((3,)), pltpu.SemaphoreType.DMA((QUARTERS, 4))],
         48,
         4,
     )
@@ -1286,46 +1358,49 @@
     vectors = low(jnp.concatenate([text_vector, image_vector], axis=0).transpose(1, 0, 2))
     vector_keep = lax.dynamic_slice_in_dim(vectors, x_at * dp, dp, 0)
     vector_send = lax.dynamic_slice_in_dim(vectors, (1 - x_at) * dp, dp, 0)
+    last_inputs = [
+        self_top,
+        self_then_x,
+        texts,
+        grads,
+        text_d,
+        cross_kept[0],
+        images,
+        image_d,
+        cross_kept[1],
+        own_sum,
+        text_n1,
+        image_n1,
+    ]
+    last_scratch = [pltpu.VMEM(m.shape, m.dtype) for m in last_inputs]
+    last_scratch[5], last_scratch[8] = pltpu.VMEM((QUARTERS, size, BLOCK), BF), pltpu.VMEM((QUARTERS, image_size, BLOCK), BF)
     text_grad, image_grad, cross_text, image_keep, image_send, self_top = run(
         cross_last,
         None,
-        [
-            w(line.take(total)),
-            w(own_sum),
-            w(vector_keep),
-            w(vector_send),
-            w(self_top),
-            w(self_then_x),
-            w(text_n1),
-            w(image_n1),
-            w(texts),
-            w(images),
-            w(grads),
-            w(cross_kept[0]),
-            w(cross_kept[1]),
-            w(text_d),
-            w(image_d),
-        ],
+        [w(line.take(total)), w(vector_keep), w(vector_send)] + [a(m) for m in last_inputs],
         [
             w(text_wide),
             w(image_cot),
             w(shape(dp, text_only, BLOCK)),
-            w(shape(dp, image_only, BLOCK)),
-            w(shape(dp, image_only, BLOCK)),
+            a(shape(dp, image_only, BLOCK)),
+            a(shape(dp, image_only, BLOCK)),
             w(shape(*self_top.shape[1:])),
         ],
-        [
+        last_scratch
+        + [
             pltpu.VMEM((part_rows, BLOCK), BF),
+            pltpu.VMEM((dp, image_only, BLOCK), BF),
+            pltpu.VMEM((dp, image_only, BLOCK), BF),
             pltpu.VMEM((dp, text_only, BLOCK), BF),
             pltpu.VMEM((dp, text_only, BLOCK), BF),
-            pltpu.VMEM(self_top.shape, BF),
             pltpu.VMEM((dp - 1, *self_top.shape[1:]), BF),
             pltpu.VMEM((DT, QUARTERS * size), BF),
             pltpu.VMEM((DT, QUARTERS * size), BF),
             pltpu.VMEM((DV, QUARTERS * image_size), BF),
             pltpu.VMEM((DV, QUARTERS * image_size), BF),
         ]
-        + links(1 + dp),
+        + links(1 + dp)
+        + [pltpu.SemaphoreType.DMA((12,)), pltpu.SemaphoreType.DMA((2,))],
         2,
         5,
     )

time: 431 us -> 423 us (0.981)
  Pallas kernels: 277 us -> 267 us
    pallas_call x11 -> x9, Pallas kernels: 277 us -> 267 us  [run(): pl.pallas_call(kernel, grid=(QUARTERS,) if order else (1,), in_specs=[spe...]
    unnamed x59 -> x53, local copies, waits for them, and re-layouts: 17.8 us -> 15.7 us
    ppermute x19 -> x18, starting transfers between devices: 18 us -> 19.8 us  [swap(): lax.ppermute(value, axis, [(i, i ^ apart) for i in range(lax.axis_size(ax...]
    ppermute x19 -> x18, waiting for transfers between devices: 46.9 us -> 46.6 us  [swap(): lax.ppermute(value, axis, [(i, i ^ apart) for i in range(lax.axis_size(ax...]
  transfers between devices with their start and end apart: 26 -> 25, of which waited for: 10 -> 10; matrix products, arithmetic and copies ran while one was open for 11% -> 11% of each run, Pallas kernels for 56% -> 50%
where the time goes in v5:
time: 423 us; the launch traced here: 419 us
  Pallas kernels  267 us (63%)
  waiting for transfers between devices  64.3 us (15%)
  local copies, waits for them, and re-layouts  28.7 us (7%)
  other arithmetic  24 us (6%)
  starting transfers between devices  20.6 us (5%)
  between operations  14.8 us (3%)
    pallas_call x9, Pallas kernels, run(): pl.pallas_call(kernel, grid=(QUARTERS,) if order else (1,), in_specs=[spe...  267 us
    ppermute x18, waiting for transfers between devices, swap(): lax.ppermute(value, axis, [(i, i ^ apart) for i in range(lax.axis_size(ax...  46.6 us
    ppermute x18, starting transfers between devices, swap(): lax.ppermute(value, axis, [(i, i ^ apart) for i in range(lax.axis_size(ax...  19.8 us
    unnamed x53, local copies, waits for them, and re-layouts  15.7 us
    reduce_scatter x5, waiting for transfers between devices, fold_last(): return lax.psum_scatter(total, 'dp', scatter_dimension=0, tiled=True)[0]  13.2 us
    convert_element_type x8, other arithmetic, low(): return value.astype(BF)  11 us
  transfers between devices with their start and end apart: 25, of which 10 were waited for; matrix products, arithmetic and copies ran while one was open for 11% of the time, Pallas kernels for 50%

profile of v5, /device:TPU:0, one launch (start us, length us, event | category | flops | bytes accessed | tf_op | source)
XLA Modules:
  0.0 419.2 jit_solution(11178766589163252073)
XLA Ops:
  7.9 4.2 %shard_map.390 = (bf16[6656,256]{1,0:T(8,128)(2,1)}, bf16[1536,256]{1,0:T(8,128)(2,1)}, bf16[640,256]{1,0:T(8,128)(2,1)}) custom-call(s32[6]{0:T(128)} %stack.39.ids, bf16[768,768]{1,0:T(8,128)(2,1)} %bitcast.180, bf16[768,768]{1,0:T(8,128)(2,1)} %bitcast.181, bf16[1024,256]{1,0:T(8,128)(2,1)} %bitcast.183, bf16[256,1024]{1,0:T(8,128)(2,1)} %bitcast.184), custom_call_target="tpu_custom_call" | custom-call | flops 3300000000 | bytes 1024 | tf_op jit(solution)/shard_map/pallas_call | solution.py:986
  12.1 3.0 collective-permute-start.1
  15.9 1.6 copy.57.refs_2_
  17.5 4.3 %shard_map.391 = (bf16[6400,256]{1,0:T(8,128)(2,1)}, bf16[2304,256]{1,0:T(8,128)(2,1)}, bf16[512,256]{1,0:T(8,128)(2,1)}) custom-call(s32[6]{0:T(128)} %stack.39.ids, bf16[576,768]{1,0:T(8,128)(2,1)} %bitcast.182, bf16[192,768]{1,0:T(8,128)(2,1)} %bitcast.194, bf16[1024,768]{1,0:T(8,128)(2,1)} %copy.57.refs_2_, bf16[256,1024]{1,0:T(8,128)(2,1)} %bitcast.185), custom_call_target="tpu_custom_call" | custom-call | flops 3300000000 | bytes 1024 | tf_op jit(solution)/shard_map/pallas_call | solution.py:986
  23.2 1.8 collective-permute-start
  25.8 1.7 collective-permute-start.4
  27.5 2.4 copy.79
  31.0 1.8 collective-permute-done
  33.2 76.9 %shard_map.392 = (f32[512,768]{1,0:T(8,128)}, f32[192,1024]{1,0:T(8,128)}, bf16[4,512,768]{2,1,0:T(8,128)(2,1)}, bf16[4,192,1024]{2,1,0:T(8,128)(2,1)}, bf16[4,5...) custom-call(s32[16]{0:T(128)} %lengths.3, ...), custom_call_target="tpu_custom_call" | custom-call | flops 76999999488 | bytes 1024 | tf_op jit(solution)/shard_map/pallas_call | solution.py:986
  110.8 15.1 %shard_map.393 = (bf16[512,768]{1,0:T(8,128)(2,1)}, bf16[192,1024]{1,0:T(8,128)(2,1)}, f32[512,768]{1,0:T(8,128)}, f32[192,1024]{1,0:T(8,128)}, bf16[4,512,768]{...) custom-call(f32[512,768]{1,0:T(8,128)} %get-tuple-element.122.text_p, ...), custom_call_target="tpu_custom_call" | custom-call | flops 1100000000 | bytes 1024 | tf_op jit(solution)/shard_map/pallas_call | solution.py:986
  126.0 4.4 %all-gather.5.cloned.1.call-done.refs_3_.refs_10_ = bf16[4096,256]{1,0:T(8,128)(2,1)} async-done(((bf16[512,256]{1,0:T(8,128)(2,1)}), bf16[4096,256]{1,0:T(8,128)(2,1)}) %all-gather.5.cloned.1.call-update) | async-done | bytes 2097168 | tf_op jit(solution)/shard_map/all_gather | solution.py:1112
  130.3 7.9 %collective-permute-done.6.refs_2_.refs_9_ = bf16[2304,256]{1,0:T(8,128)(2,1)} collective-permute-done((bf16[2304,256]{1,0:T(8,128)(2,1)}, bf16[2304,256]{1,0:T(8,128)(2,1)}, u32[]{:S(2)}, u32[]{:S(2)}) %collective-permute-start.6) | collective-permute-done | bytes 1179680 | tf_op jit(solution)/shard_map/ppermute | solution.py:1004
  138.2 20.0 %shard_map.394 = (f32[512,768]{1,0:T(8,128)}, bf16[148,1024]{1,0:T(8,128)(2,1)}, f32[512,768]{1,0:T(8,128)}, f32[192,1024]{1,0:T(8,128)}, f32[2,768]{1,0:T(2,128...) custom-call(s32[6]{0:T(128)} %stack.39.ids, ...), custom_call_target="tpu_custom_call" | custom-call | flops 20899999744 | bytes 1024 | tf_op jit(solution)/shard_map/pallas_call | solution.py:986
  158.3 32.2 %shard_map.395 = (f32[512,768]{1,0:T(8,128)}, f32[192,1024]{1,0:T(8,128)}, f32[2,768]{1,0:T(2,128)}, f32[2,1024]{1,0:T(2,128)}, bf16[3328,256]{1,0:T(8,128)(2,1)...) custom-call(f32[512,768]{1,0:T(8,128)} %get-tuple-element.134.text_g, f32[192,1024]{1,0:T(8,128)} %get-tuple-element.135.image_g, ...), custom_call_target="tpu_custom_call" | custom-call | flops 35200000000 | bytes 1024 | tf_op jit(solution)/shard_map/pallas_call | solution.py:986
  192.7 28.1 %shard_map.396 = (f32[512,768]{1,0:T(8,128)}, f32[192,1024]{1,0:T(8,128)}, bf16[2304,256]{1,0:T(8,128)(2,1)}, f32[2,768]{1,0:T(2,128)}, f32[2,1024]{1,0:T(2,128)...) custom-call(f32[512,768]{1,0:T(8,128)} %get-tuple-element.147.text_g, ...), custom_call_target="tpu_custom_call" | custom-call | flops 30799998976 | bytes 1024 | tf_op jit(solution)/shard_map/pallas_call | solution.py:986
  221.5 2.0 concatenate.64.vectors
  223.5 6.5 %collective-permute-done.7 = bf16[2,4,416,256]{3,2,1,0:T(8,128)(2,1)S(1)} collective-permute-done((bf16[2,4,416,256]{3,2,1,0:T(8,128)(2,1)}, bf16[2,4,416,256]{3,2,1,0:T(8,128)(2,1)S(1)}, u32[]{:S(2)}, u32[]{:S(2)}) %collective-permute-start.7) | collective-permute-done | bytes 1703968 | tf_op jit(solution)/shard_map/ppermute | solution.py:1004
  230.0 1.6 fusion.3
  233.7 41.7 %shard_map.397 = (bf16[4,2304,256]{2,1,0:T(8,128)(2,1)}, bf16[4,512,768]{2,1,0:T(8,128)(2,1)}, bf16[4,192,768]{2,1,0:T(8,128)(2,1)}, f32[2304,256]{1,0:T(8,128)}...) custom-call(bf16[2304,256]{1,0:T(8,128)(2,1)} %get-tuple-element.165.grad, f32[16,1024]{1,0:T(8,128)} %concatenate.64.vectors, ...), custom_call_target="tpu_custom_call" | custom-call | flops 52800000000 | bytes 1024 | tf_op jit(solution)/shard_map/pallas_call | solution.py:986
  278.0 44.0 %shard_map.398 = (f32[512,768]{1,0:T(8,128)}, bf16[148,1024]{1,0:T(8,128)(2,1)}, bf16[4,400,256]{2,1,0:T(8,128)(2,1)}, bf16[4,512,256]{2,1,0:T(8,128)(2,1)}, bf1...) custom-call(bf16[2304,256]{1,0:T(8,128)(2,1)} %get-tuple-element.176.total, ...), custom_call_target="tpu_custom_call" | custom-call | flops 2200000000 | bytes 1024 | tf_op jit(solution)/shard_map/pallas_call | solution.py:986
  323.7 1.9 convert_element_type.209
  327.2 3.4 fusion.1
  330.6 15.3 %collective-permute-done.12 = bf16[4,512,256]{2,1,0:T(8,128)(2,1)S(1)} collective-permute-done((bf16[4,512,256]{2,1,0:T(8,128)(2,1)}, bf16[4,512,256]{2,1,0:T(8,128)(2,1)S(1)}, u32[]{:S(2)}, u32[]{:S(2)}) %collective-permute-start.12) | collective-permute-done | bytes 1048608 | tf_op jit(solution)/shard_map/ppermute | solution.py:1004
  355.5 8.7 %collective-permute-done.10 = bf16[148,1024]{1,0:T(8,128)(2,1)} collective-permute-done((bf16[148,1024]{1,0:T(8,128)(2,1)}, bf16[148,1024]{1,0:T(8,128)(2,1)}, u32[]{:S(2)}, u32[]{:S(2)}) %collective-permute-start.10) | collective-permute-done | bytes 303136 | tf_op jit(solution)/shard_map/ppermute | solution.py:1004
  364.2 1.9 convert_element_type.218
  369.3 1.7 slice_bitcast_fusion.2
  372.4 2.7 collective-permute-done.13
  375.2 2.6 add_convert_fusion
  381.5 2.5 collective-permute-done.15
  386.3 1.6 slice_bitcast_fusion.13
  390.9 1.6 convert_bitcast_fusion.1
  394.2 13.2 %reduce-scatter.12.cloned.1.call-done = bf16[1,576,256]{2,1,0:T(8,128)(2,1)} async-done(((bf16[4,576,256]{2,1,0:T(8,128)(2,1)}), bf16[1,576,256]{2,1,0:T(8,128)(2,1)}) %reduce-scatter.12.cloned.1.call-update) | async-done | bytes 294928 | tf_op jit(solution)/shard_map/reduce_scatter | solution.py:1027
  (143 shorter events, 46.2 us)
Async XLA Ops:
  7.2 103.0 %all-gather.3.cloned.1.call-start = ((), (), s32[]{:S(2)}) async-start(), calls=%async_computation.5 | async-start | bytes 2949120 | tf_op jit(solution)/shard_map/all_gather | solution.py:1111
  12.1 11.0 %collective-permute-start.1 = (bf16[640,256]{1,0:T(8,128)(2,1)}, bf16[640,256]{1,0:T(8,128)(2,1)}, u32[]{:S(2)}, u32[]{:S(2)}) collective-permute-start(bf16[640,256]{1,0:T(8,128)(2,1)} %get-tuple-element.117), channel_id=1, source_target_pairs={{0,2},{1,3},{2,0},{3,1},{4,6},{5,7},{6,4},{7,5},{8,10},{9,11},{10,... | collective-permute-start | bytes 983048 | tf_op jit(solution)/shard_map/ppermute | solution.py:1004
  23.1 107.2 %all-gather.5.cloned.1.call-start = ((), (), s32[]{:S(2)}) async-start(), calls=%async_computation.6 | async-start | bytes 2359296 | tf_op jit(solution)/shard_map/all_gather | solution.py:1112
  23.2 9.6 %collective-permute-start = (bf16[512,256]{1,0:T(8,128)(2,1)}, bf16[512,256]{1,0:T(8,128)(2,1)}, u32[]{:S(2)}, u32[]{:S(2)}) collective-permute-start(bf16[512,256]{1,0:T(8,128)(2,1)} %get-tuple-element.116), channel_id=1, source_target_pairs={{0,2},{1,3},{2,0},{3,1},{4,6},{5,7},{6,4},{7,5},{8,10},{9,11},{10,... | collective-permute-start | bytes 786440 | tf_op jit(solution)/shard_map/ppermute | solution.py:1004
  25.0 85.9 %collective-permute-start.2 = (bf16[6656,256]{1,0:T(8,128)(2,1)S(1)}, bf16[6656,256]{1,0:T(8,128)(2,1)}, u32[]{:S(2)}, u32[]{:S(2)}) collective-permute-start(bf16[6656,256]{1,0:T(8,128)(2,1)S(1)} %copy-done), channel_id=1, source_target_pairs={{0,1},{1,0},{2,3},{3,2},{4,5},{5,4},{6,7},{7,6},{8,9},{9,8},{10,11... | collective-permute-start | bytes 10223624 | tf_op jit(solution)/shard_map/ppermute | solution.py:1004
  25.0 113.2 %collective-permute-start.5 = (bf16[6400,256]{1,0:T(8,128)(2,1)}, bf16[6400,256]{1,0:T(8,128)(2,1)}, u32[]{:S(2)}, u32[]{:S(2)}) collective-permute-start(bf16[6400,256]{1,0:T(8,128)(2,1)} %get-tuple-element.118.refs_0_.refs_7_), channel_id=1, source_target_pairs={{0,1},{1,0},{2,3},{3,2},{4,5},{5,4},{6,7},{7,6},{8,9},{9,8},{10,11... | collective-permute-start | bytes 9830408 | tf_op jit(solution)/shard_map/ppermute | solution.py:1004
  25.5 84.6 %collective-permute-start.3 = (bf16[1536,256]{1,0:T(8,128)(2,1)}, bf16[1536,256]{1,0:T(8,128)(2,1)}, u32[]{:S(2)}, u32[]{:S(2)}) collective-permute-start(bf16[1536,256]{1,0:T(8,128)(2,1)} %get-tuple-element.124), channel_id=1, source_target_pairs={{0,2},{1,3},{2,0},{3,1},{4,6},{5,7},{6,4},{7,5},{8,10},{9,11},{10,... | collective-permute-start | bytes 2359304 | tf_op jit(solution)/shard_map/ppermute | solution.py:1004
  25.8 84.3 %collective-permute-start.4 = (bf16[148,1024]{1,0:T(8,128)(2,1)}, bf16[148,1024]{1,0:T(8,128)(2,1)}, u32[]{:S(2)}, u32[]{:S(2)}) collective-permute-start(bf16[148,1024]{1,0:T(8,128)(2,1)} %param.27), channel_id=1, source_target_pairs={{0,16},{16,0},{1,17},{17,1},{2,18},{18,2},{3,19},{19,3},{4,20},{20... | collective-permute-start | bytes 909320 | tf_op jit(solution)/shard_map/ppermute | solution.py:1004
  32.8 289.2 %reduce-scatter.6.cloned.1.call-start = ((), (), s32[]{:S(2)}) async-start(), calls=%async_computation.7 | async-start | bytes 3932160 | tf_op jit(solution)/shard_map/reduce_scatter | solution.py:1027
  110.2 28.0 %collective-permute-start.6 = (bf16[2304,256]{1,0:T(8,128)(2,1)}, bf16[2304,256]{1,0:T(8,128)(2,1)}, u32[]{:S(2)}, u32[]{:S(2)}) collective-permute-start(bf16[2304,256]{1,0:T(8,128)(2,1)} %get-tuple-element.130), channel_id=1, source_target_pairs={{0,2},{1,3},{2,0},{3,1},{4,6},{5,7},{6,4},{7,5},{8,10},{9,11},{10,... | collective-permute-start | bytes 3538952 | tf_op jit(solution)/shard_map/ppermute | solution.py:1004
  190.5 178.7 %reduce-scatter.14.cloned.1.call-start = ((), (), s32[]{:S(2)}) async-start(), calls=%async_computation.11 | async-start | bytes 2621440 | tf_op jit(solution)/shard_map/reduce_scatter | solution.py:1027
  190.6 39.4 %collective-permute-start.7 = (bf16[2,4,416,256]{3,2,1,0:T(8,128)(2,1)}, bf16[2,4,416,256]{3,2,1,0:T(8,128)(2,1)S(1)}, u32[]{:S(2)}, u32[]{:S(2)}) collective-permute-start(bf16[2,4,416,256]{3,2,1,0:T(8,128)(2,1)} %bitcast.21), channel_id=1, source_target_pairs={{0,2},{1,3},{2,0},{3,1},{4,6},{5,7},{6,4},{7,5},{8,10},{9,11},{10,... | collective-permute-start | bytes 5111816 | tf_op jit(solution)/shard_map/ppermute | solution.py:1004
  191.3 32.2 %collective-permute-start.8 = (bf16[148,1024]{1,0:T(8,128)(2,1)}, bf16[148,1024]{1,0:T(8,128)(2,1)}, u32[]{:S(2)}, u32[]{:S(2)}) collective-permute-start(bf16[148,1024]{1,0:T(8,128)(2,1)} %get-tuple-element.159), channel_id=1, source_target_pairs={{0,16},{16,0},{1,17},{17,1},{2,18},{18,2},{3,19},{19,3},{4,20},{20... | collective-permute-start | bytes 909320 | tf_op jit(solution)/shard_map/ppermute | solution.py:1004
  192.7 28.8 %copy-start.17 = (f32[2,768]{1,0:T(2,128)S(1)}, f32[2,768]{1,0:T(2,128)}, u32[]{:S(2)}) copy-start(f32[2,768]{1,0:T(2,128)} %get-tuple-element.167) | copy-start | bytes 18436
  192.7 28.8 %copy-start.16 = (f32[2,768]{1,0:T(2,128)S(1)}, f32[2,768]{1,0:T(2,128)}, u32[]{:S(2)}) copy-start(f32[2,768]{1,0:T(2,128)} %get-tuple-element.168) | copy-start | bytes 18436
  192.7 28.8 %copy-start.14 = (f32[2,1024]{1,0:T(2,128)S(1)}, f32[2,1024]{1,0:T(2,128)}, u32[]{:S(2)}) copy-start(f32[2,1024]{1,0:T(2,128)} %get-tuple-element.171) | copy-start | bytes 24580
  192.7 28.9 %copy-start.15 = (f32[2,1024]{1,0:T(2,128)S(1)}, f32[2,1024]{1,0:T(2,128)}, u32[]{:S(2)}) copy-start(f32[2,1024]{1,0:T(2,128)} %get-tuple-element.170) | copy-start | bytes 24580
  192.7 37.3 %copy-start.2 = (bf16[3328,256]{1,0:T(8,128)(2,1)S(1)}, bf16[3328,256]{1,0:T(8,128)(2,1)}, u32[]{:S(2)}) copy-start(bf16[3328,256]{1,0:T(8,128)(2,1)} %get-tuple-element.145) | copy-start | bytes 5111812
  231.6 45.5 %collective-permute-start.9 = (bf16[4,416,256]{2,1,0:T(8,128)(2,1)}, bf16[4,416,256]{2,1,0:T(8,128)(2,1)S(1)}, u32[]{:S(2)}, u32[]{:S(2)}) collective-permute-start(bf16[4,416,256]{2,1,0:T(8,128)(2,1)} %get-tuple-element.252), channel_id=1, source_target_pairs={{0,16},{16,0},{1,17},{17,1},{2,18},{18,2},{3,19},{19,3},{4,20},{20... | collective-permute-start | bytes 2555912 | tf_op jit(solution)/shard_map/ppermute | solution.py:1004
  233.1 89.0 %collective-permute-start.11 = (bf16[2,4,576,256]{3,2,1,0:T(8,128)(2,1)}, bf16[2,4,576,256]{3,2,1,0:T(8,128)(2,1)}, u32[]{:S(2)}, u32[]{:S(2)}) collective-permute-start(bf16[2,4,576,256]{3,2,1,0:T(8,128)(2,1)} %bitcast.22), channel_id=1, source_target_pairs={{0,16},{16,0},{1,17},{17,1},{2,18},{18,2},{3,19},{19,3},{4,20},{20... | collective-permute-start | bytes 7077896 | tf_op jit(solution)/shard_map/ppermute | solution.py:1004
  233.6 151.9 %reduce-scatter.8.cloned.1.call-start = ((), (), s32[]{:S(2)}) async-start(), calls=%async_computation.8 | async-start | bytes 1024000 | tf_op jit(solution)/shard_map/reduce_scatter | solution.py:1027
  322.1 68.8 %reduce-scatter.10.cloned.1.call-start = ((), (), s32[]{:S(2)}) async-start(), calls=%async_computation.9 | async-start | bytes 1310720 | tf_op jit(solution)/shard_map/reduce_scatter | solution.py:1027
  322.1 23.7 %collective-permute-start.12 = (bf16[4,512,256]{2,1,0:T(8,128)(2,1)}, bf16[4,512,256]{2,1,0:T(8,128)(2,1)S(1)}, u32[]{:S(2)}, u32[]{:S(2)}) collective-permute-start(bf16[4,512,256]{2,1,0:T(8,128)(2,1)} %get-tuple-element.194), channel_id=1, source_target_pairs={{0,16},{16,0},{1,17},{17,1},{2,18},{18,2},{3,19},{19,3},{4,20},{20... | collective-permute-start | bytes 3145736 | tf_op jit(solution)/shard_map/ppermute | solution.py:1004
  327.2 18.7 %copy-start.8 = (bf16[4,512,256]{2,1,0:T(8,128)(2,1)S(1)}, bf16[4,512,256]{2,1,0:T(8,128)(2,1)}, u32[]{:S(2)}) copy-start(bf16[4,512,256]{2,1,0:T(8,128)(2,1)} %get-tuple-element.193) | copy-start | bytes 3145732
  347.1 60.3 %reduce-scatter.12.cloned.1.call-start = ((), (), s32[]{:S(2)}) async-start(), calls=%async_computation.10 | async-start | bytes 1474560 | tf_op jit(solution)/shard_map/reduce_scatter | solution.py:1027
  347.6 27.6 %collective-permute-start.13 = (bf16[4,576,256]{2,1,0:T(8,128)(2,1)S(1)}, bf16[4,576,256]{2,1,0:T(8,128)(2,1)}, u32[]{:S(2)}, u32[]{:S(2)}) collective-permute-start(bf16[4,576,256]{2,1,0:T(8,128)(2,1)S(1)} %copy-done.7), channel_id=1, source_target_pairs={{0,2},{1,3},{2,0},{3,1},{4,6},{5,7},{6,4},{7,5},{8,10},{9,11},{10,... | collective-permute-start | bytes 3538952 | tf_op jit(solution)/shard_map/ppermute | solution.py:1004
  349.0 17.1 %collective-permute-start.16 = (bf16[2,384,256]{2,1,0:T(8,128)(2,1)}, bf16[2,384,256]{2,1,0:T(8,128)(2,1)}, u32[]{:S(2)}, u32[]{:S(2)}) collective-permute-start(bf16[2,384,256]{2,1,0:T(8,128)(2,1)} %slice_bitcast_fusion), channel_id=1, source_target_pairs={{0,16},{16,0},{1,17},{17,1},{2,18},{18,2},{3,19},{19,3},{4,20},{20... | collective-permute-start | bytes 1179656 | tf_op jit(solution)/shard_map/ppermute | solution.py:1004
  352.5 11.6 %collective-permute-start.10 = (bf16[148,1024]{1,0:T(8,128)(2,1)}, bf16[148,1024]{1,0:T(8,128)(2,1)}, u32[]{:S(2)}, u32[]{:S(2)}) collective-permute-start(bf16[148,1024]{1,0:T(8,128)(2,1)} %get-tuple-element.187), channel_id=1, source_target_pairs={{0,16},{16,0},{1,17},{17,1},{2,18},{18,2},{3,19},{19,3},{4,20},{20... | collective-permute-start | bytes 909320 | tf_op jit(solution)/shard_map/ppermute | solution.py:1004
  367.8 10.0 %collective-permute-start.17 = (bf16[384,256]{1,0:T(8,128)(2,1)}, bf16[384,256]{1,0:T(8,128)(2,1)}, u32[]{:S(2)}, u32[]{:S(2)}) collective-permute-start(bf16[384,256]{1,0:T(8,128)(2,1)} %slice_bitcast_fusion.4), channel_id=1, source_target_pairs={{0,2},{1,3},{2,0},{3,1},{4,6},{5,7},{6,4},{7,5},{8,10},{9,11},{10,... | collective-permute-start | bytes 589832 | tf_op jit(solution)/shard_map/ppermute | solution.py:1004
  371.0 7.9 %collective-permute-start.14 = (bf16[2,256,256]{2,1,0:T(8,128)(2,1)}, bf16[2,256,256]{2,1,0:T(8,128)(2,1)S(1)}, u32[]{:S(2)}, u32[]{:S(2)}) collective-permute-start(bf16[2,256,256]{2,1,0:T(8,128)(2,1)} %slice_bitcast_fusion.2), channel_id=1, source_target_pairs={{0,16},{16,0},{1,17},{17,1},{2,18},{18,2},{3,19},{19,3},{4,20},{20... | collective-permute-start | bytes 786440 | tf_op jit(solution)/shard_map/ppermute | solution.py:1004
  379.0 5.0 %collective-permute-start.15 = (bf16[256,256]{1,0:T(8,128)(2,1)S(1)}, bf16[256,256]{1,0:T(8,128)(2,1)S(1)}, u32[]{:S(2)}, u32[]{:S(2)}) collective-permute-start(bf16[256,256]{1,0:T(8,128)(2,1)S(1)} %slice_bitcast_fusion.6), channel_id=1, source_target_pairs={{0,2},{1,3},{2,0},{3,1},{4,6},{5,7},{6,4},{7,5},{8,10},{9,11},{10,... | collective-permute-start | bytes 393224 | tf_op jit(solution)/shard_map/ppermute | solution.py:1004
  388.7 21.1 %copy-start.5 = (f32[512,768]{1,0:T(8,128)S(1)}, f32[512,768]{1,0:T(8,128)}, u32[]{:S(2)}) copy-start(f32[512,768]{1,0:T(8,128)} %get-tuple-element.312) | copy-start | bytes 4718596
  (11 other events, 38.0 us)
Sparse Core Ops, SparseCore 0:
  23.2 57.0 all-gather.2
  82.4 47.8 all-gather.4
  190.7 60.5 reduce-scatter.5
  253.4 56.4 reduce-scatter.13
  322.2 23.9 reduce-scatter.7
  349.0 26.4 reduce-scatter.9
  378.4 28.9 reduce-scatter.11

commit v6 on v5

--- a/solution.py
+++ b/solution.py
@@ -1,4 +1,5 @@
 import functools
+import math
 
 import jax
 import jax.numpy as jnp
@@ -394,10 +395,10 @@
     leave_blocks(part, 3 * text_rows, low(image_dx))
 
 
-def cross_back(pairs, grad, vectors, text_kept, image_kept, text_probs, image_probs, *refs):
-    matrices = refs[:6]
-    grads_out, text_d_out, image_d_out, own_sum, total, vector_sum = refs[6:12]
-    grads, text_d, image_d, parts, got, got_vectors, *kept = refs[12:-4]
+def cross_back(pairs, grad, *refs):
+    given, (text_kept, image_kept, text_probs, image_probs), matrices = refs[:6], refs[6:10], refs[10:16]
+    grads_out, text_d_out, image_d_out, own_sum, total, vector_sum = refs[16:22]
+    grads, text_d, image_d, parts, got, got_vectors, vectors, *kept = refs[22:-4]
     send_sems, recv_sems, out_sems, in_sems = refs[-4:]
     core, y, unused_x = partners()
     copy = sender(send_sems, recv_sems)
@@ -418,6 +419,9 @@
     vectors_y = copy(6, vector_sum, got_vectors.at[1], y)
     for load in loads[0]:
         load.start()
+    vectors[...] = jnp.zeros_like(vectors)
+    for n, vector in enumerate(given):
+        vectors[2 * n : 2 * n + 2, 0 : vector.shape[1]] = vector[...]
     greet(core, y)
     vectors_core.start()
     to_y.start()
@@ -493,18 +497,30 @@
     return [nn(flip[pl.ds(start, half), :], values) for start in starts]
 
 
-def cross_last(total, vector_keep, vector_send, *refs):
-    sources, loaded = refs[:12], refs[18:30]
-    text_grad, image_grad, text_keep, image_keep_out, image_send_out, self_sum = refs[12:18]
-    got, image_keep, image_send, text_send, text_got, self_got, text_flip, text_g_flip, image_flip, image_g_flip = refs[30:40]
-    send_sems, recv_sems, in_sems, out_sems = refs[40:]
-    self_all, self_x, texts, grads, text_d, text_c, images, image_d, image_c, own_sum, text_n, image_n = loaded
-    loads = []
-    for n, (source, ref) in enumerate(zip(sources, loaded)):
+def pick_columns(values, start, depth):
+    row = lax.broadcasted_iota(jnp.int32, (values.shape[1], BLOCK), 0)
+    column = lax.broadcasted_iota(jnp.int32, (values.shape[1], BLOCK), 1)
+    chosen = (row == column + start) & (column < depth)
+    return nn(values, low(jnp.where(chosen, 1.0, 0.0)))
+
+
+def cross_last(total, vectors, *refs):
+    sources, loaded = refs[:14], refs[21:33]
+    grad_left, grad_right, image_grad, text_keep, image_keep_out, image_send_out, self_sum = refs[14:21]
+    got, image_keep, image_send, text_send, text_got, self_got, text_flip, text_g_flip, image_flip, image_g_flip = refs[33:43]
+    send_sems, recv_sems, in_sems, out_sems = refs[43:]
+    self_all, self_more, texts, grads, text_d, text_c, images, image_d, image_c, own_sum, text_n, image_n = loaded
+    self_loads = []
+    for n, (target, first) in enumerate(((self_all, 0), (self_all, 1), (self_more, 0), (self_more, 1))):
+        depth = sources[n].shape[1]
+        target = target.at[:, pl.ds(first * sources[n - 1].shape[1], depth)]
+        self_loads.append(pltpu.make_async_copy(sources[n], target, in_sems.at[n]))
+    loads = [None, None]
+    for n, (source, ref) in enumerate(zip(sources[4:], loaded[2:])):
         if source.shape != ref.shape:
             source = source.at[:, :, pl.ds(768, BLOCK)]
-        loads.append(pltpu.make_async_copy(source, ref, in_sems.at[n]))
-    for load in loads:
+        loads.append(pltpu.make_async_copy(source, ref, in_sems.at[4 + n]))
+    for load in self_loads + loads[2:]:
         load.start()
     unused_core, y, x = partners()
     copy = sender(send_sems, recv_sems)
@@ -516,9 +532,9 @@
     along_z = [copy(2 + k, self_all.at[other], self_got.at[k], {"dp": other}) for k, other in enumerate(others)]
     greet(y, x, *[{"dp": other} for other in others])
     far.start()
-    loads[0].wait()
-    loads[1].wait()
-    self_all[...] = add(self_all[...], self_x[...])
+    for load in self_loads:
+        load.wait()
+    self_all[...] = add(self_all[...], self_more[...])
     for transfer in along_z:
         transfer.start()
     size, image_size = texts.shape[1], images.shape[1]
@@ -550,10 +566,15 @@
                     out[z, b * padded : b * padded + depth, :] = low(found[taken, b * BLOCK : (b + 1) * BLOCK])
                 out[z, 3 * padded : 3 * padded + depth, :] = low(last[taken])
         if count == 3:
-            for out, vector in ((text_keep, vector_keep), (text_send, vector_send)):
-                below_all = out.shape[1] - vector.shape[1]
+            rounded = low(vectors[...])
+            is_text = lax.broadcasted_iota(jnp.int32, (rounded.shape[0], BLOCK), 0) < 6
+            for apart, out in enumerate((text_keep, text_send)):
                 for z in range(dp):
-                    out[z, below_all:, :] = vector[z]
+                    place = lax.bitwise_xor(at, apart) * dp + z
+                    text_part = pick_columns(rounded[:, :DT], place * depth, depth)
+                    image_depth = DV // (2 * dp)
+                    image_part = pick_columns(rounded, place * image_depth, image_depth)
+                    out[z, 4 * padded :, :] = low(jnp.where(is_text, text_part, image_part))
             text_x.start()
         else:
             leaving = [
@@ -570,7 +591,9 @@
     for load in loads[9:]:
         load.wait()
     far.wait()
-    text_grad[...] = text_n[...] + side(own_sum, 0, size, 3) + side(got, 0, size, 3).astype(F32)
+    text_total = text_n[...] + side(own_sum, 0, size, 3) + side(got, 0, size, 3).astype(F32)
+    grad_left[...] = text_total[:, : DT // 2]
+    grad_right[...] = text_total[:, DT // 2 :]
     image_total = low(image_n[...] + side(own_sum, below, image_size, 4) + side(got, below, image_size, 4).astype(F32))
     image_grad[...] = low(tn(spacing(image_size // PADDED), image_total))
     text_x.wait()
@@ -637,7 +660,8 @@
 def self_forward(pairs, ids, lengths, text_pre, image_pre, text_gain, text_bias, image_gain, image_bias, text_cot, image_cot, *refs):
     parts = refs[:4]
     (
-        text_out,
+        text_left,
+        text_right,
         image_out,
         text_grad,
         image_grad,
@@ -652,8 +676,8 @@
         image_kept,
         image_probs,
         corner,
-    ) = refs[4:19]
-    weights, text_sum, image_sum, text_low, image_low, sems, send_sems, recv_sems = refs[19:]
+    ) = refs[4:20]
+    weights, text_sum, image_sum, text_low, image_low, sems, send_sems, recv_sems = refs[20:]
     step = pl.program_id(0)
     leaving = fetch_round(step, *parts, corner, weights, sems, send_sems, recv_sems)
     text_rows, image_rows = text_pre.shape[0], image_pre.shape[0]
@@ -723,7 +747,8 @@
             unit, scale = normed(total[...])
             value = unit * g + b
             if total is text_sum:
-                text_out[...] = value
+                text_left[...] = value[:, : DT // 2]
+                text_right[...] = value[:, DT // 2 :]
             else:
                 image_out[...] = low(tn(apart, low(value)))
             back = norm_back(unit, scale, g, cot, vec)
@@ -736,9 +761,9 @@
     text_q, text_k, text_v, text_c, text_probs, image_kept, image_probs = refs[:7]
     parts = refs[7:12]
     text_n, image_n, text_vec, image_vec = refs[12:16]
-    outs = refs[16:19]
-    weights, found, text_sum, image_sum, text_g_low, image_g_low, near, rounded_near = refs[19:27]
-    flips, (text_d, image_d, sems, out_sems, send_sems, recv_sems) = refs[27:31], refs[31:]
+    outs = refs[16:21]
+    weights, found, text_sum, image_sum, text_g_low, image_g_low, near, rounded_near = refs[21:29]
+    flips, (text_d, image_d, sems, out_sems, send_sems, recv_sems) = refs[29:33], refs[33:]
     step = pl.program_id(0)
     fetch(step, BACKWARD, *parts, weights, sems)
     core = partners()[0]
@@ -884,7 +909,7 @@
 
 def weight_grad(is_self, dp, sizes, rounded, found, near, spare, outs, flips, out_sems):
     text_flip, text_g_flip, image_flip, image_g_flip = flips
-    to_send, kept, to_z = (spare.at[n] for n in range(3))
+    to_send, kept, to_z, by_image = (spare.at[n] for n in range(QUARTERS))
     size, image_size = sizes
     x = lax.axis_index("stream")
     for at in range(2):
@@ -899,12 +924,12 @@
     text_depth, image_depth = DT // (2 * dp), DV // (2 * dp)
     padded = -(-text_depth // 16) * 16
     lane = lax.broadcasted_iota(jnp.int32, (1, HEAD), 1) < SELF_HEAD
-    top = 3 * padded + image_depth if is_self else 6 * padded
-    count = 3 if is_self else 2
+    top = 3 * padded if is_self else 5 * padded
+    below = 2 * image_depth if is_self else 2 * image_depth + padded
     leaving = []
 
-    def leave(source, target):
-        leaving.append(pltpu.make_async_copy(source.at[pl.ds(0, target.shape[0])], target, out_sems.at[len(leaving)]))
+    def leave(source, target, first=0):
+        leaving.append(pltpu.make_async_copy(source.at[pl.ds(first, target.shape[0])], target, out_sems.at[len(leaving)]))
         leaving[-1].start()
 
     for slot in (1, 0):
@@ -925,11 +950,11 @@
                     to = (at * dp + z) * top + row
                     ref[to : to + depth, :] = low(value[apart][z * depth : (z + 1) * depth])
 
-        def bottom(b, value):
+        def bottom(row, depth, value):
             for apart in range(2):
                 for z in range(dp):
-                    to = ((z * 4 + 2 * slot + apart) * count + b) * image_depth
-                    to_z[to : to + image_depth, :] = low(value[apart][z * image_depth : (z + 1) * image_depth])
+                    to = (z * 4 + 2 * slot + apart) * below + row
+                    to_z[to : to + depth, :] = low(value[apart][z * depth : (z + 1) * depth])
 
         if is_self:
             one, two, three = text_block(0), text_block(1), text_block(2)
@@ -939,19 +964,26 @@
             pairs = zip(halves(text_flip, three, x), halves(text_g_flip, three[:, HEAD:], x))
             mixed = [jnp.concatenate([a[:, :HEAD], jnp.where(lane, a[:, HEAD:], b)], axis=1) for a, b in pairs]
             write(2 * padded, text_depth, mixed)
-            write(3 * padded, image_depth, halves(image_flip, image_block(0, 3), x))
+            for b in range(2):
+                for apart, value in enumerate(halves(image_flip, image_block(b, 3), x)):
+                    for z in range(dp):
+                        to = (((2 * (1 - apart) + slot) * dp + z) * 2 + b) * image_depth
+                        by_image[to : to + image_depth, :] = low(value[z * image_depth : (z + 1) * image_depth])
             leave(*((to_send, outs[0]) if slot else (kept, outs[1])))
-            for b in range(3):
-                bottom(b, halves(image_g_flip if b == 2 else image_flip, image_block(1 + b, 3), x))
+            for b, flip in enumerate((image_flip, image_g_flip)):
+                bottom(b * image_depth, image_depth, halves(flip, image_block(2 + b, 3), x))
         else:
-            for b in range(6):
+            for b in range(5):
                 write(b * padded, text_depth, halves(text_g_flip if b > 2 else text_flip, text_block(b), x))
-            for b in range(2):
-                bottom(b, halves(image_g_flip if b else image_flip, image_block(b, 6), x))
+            bottom(2 * image_depth, text_depth, halves(text_g_flip, text_block(5), x))
+            for b, flip in enumerate((image_flip, image_g_flip)):
+                bottom(b * image_depth, image_depth, halves(flip, image_block(b, 6), x))
     if not is_self:
         leave(to_send, outs[0])
         leave(kept, outs[1])
     leave(to_z, outs[2])
+    for number, out in enumerate(outs[3:]):
+        leave(by_image, out, number * out.shape[0])
     for copy in leaving:
         copy.wait()
 
@@ -1116,9 +1148,10 @@
     mlp_far = swap(mlp_first, "tensor", 2)
 
     text_wide, image_wide = shape(size, DT, of=F32), shape(image_size, DV, of=F32)
+    text_half = shape(size, DT // 2, of=F32)
     text_f32, image_f32 = pltpu.VMEM((size, DT), F32), pltpu.VMEM((image_size, DV), F32)
     text_bf, image_bf = pltpu.VMEM((size, DT), BF), pltpu.VMEM((image_size, DV), BF)
-    in_sems, out_sems = pltpu.SemaphoreType.DMA((5,)), pltpu.SemaphoreType.DMA((3,))
+    in_sems, out_sems = pltpu.SemaphoreType.DMA((5,)), pltpu.SemaphoreType.DMA((5,))
     text_affine = [w(text_gain), w(text_bias)]
     image_affine = [w(image_gain), w(image_bias)]
     vector_outs = [w(shape(2, DT, of=F32)), w(shape(2, DV, of=F32))]
@@ -1188,7 +1221,8 @@
     line.leave(text_pre2)
     self_far, self_rest = line.take((self_far, self_rest))
     (
-        text_out,
+        text_left,
+        text_right,
         image_out,
         text_n3,
         image_n3,
@@ -1211,7 +1245,7 @@
         + image_affine
         + [w(text_cot), w(image_cot_here)]
         + [a(m) for m in (self_own, self_near, self_far, self_rest)],
-        [w(text_wide), w(image_cot), w(text_wide), w(image_wide)]
+        [w(text_half), w(text_half), w(image_cot), w(text_wide), w(image_wide)]
         + vector_outs
         + [
             w(shape(2 * part_rows, BLOCK)),
@@ -1251,17 +1285,15 @@
         ]
 
     def grad_shapes(is_self):
-        top = 3 * padded + image_depth if is_self else 6 * padded
-        bottom = (3 if is_self else 2) * image_depth
-        return (2, dp, top, BLOCK), (dp, 4 * bottom, BLOCK)
+        first = (2, dp, (3 if is_self else 5) * padded, BLOCK)
+        last = (dp, 4 * (2 * image_depth + (0 if is_self else padded)), BLOCK)
+        return [first, first, last] + [(2, dp, 2 * image_depth, BLOCK)] * (2 if is_self else 0)
 
     def grad_outs(is_self):
-        first, last = grad_shapes(is_self)
-        return [a(shape(2 * dp * first[2], BLOCK))] * 2 + [a(shape(dp * last[1], BLOCK))]
-
-    def grad_arrays(is_self, to_send, kept, to_z):
-        first, last = grad_shapes(is_self)
-        return to_send.reshape(first), kept.reshape(first), to_z.reshape(last)
+        return [a(shape(math.prod(dims[:-1]), BLOCK)) for dims in grad_shapes(is_self)]
+
+    def grad_arrays(is_self, *found):
+        return [out.reshape(dims) for out, dims in zip(found, grad_shapes(is_self))]
 
     self_rows = 3 * size + 4 * image_size
     text_n2, image_n2, text_vec2, image_vec2, *self_found = run(
@@ -1291,8 +1323,9 @@
         32,
         2,
     )
-    to_y, self_top, to_z = grad_arrays(True, *self_found)
+    to_y, self_top, to_z, to_x, self_side = grad_arrays(True, *self_found)
     self_by_y = swap(to_y, "tensor", 2)
+    self_by_x = swap(to_x, "stream", 1)
     self_bottom = fold_last(to_z)
     line.leave(self_top)
     mlp_rows = 6 * size + 2 * image_size
@@ -1325,26 +1358,28 @@
     )
     line.leave(grad_low)
     to_x, mlp_top, to_z = grad_arrays(False, *mlp_found)
-    self_top, self_by_y, to_x, to_z, image_out = after((self_top, self_by_y, to_x, to_z, image_out), mlp_top)
+    self_top, self_by_y, self_side, self_by_x, to_x, to_z, image_out = after(
+        (self_top, self_by_y, self_side, self_by_x, to_x, to_z, image_out), mlp_top
+    )
     mlp_by_x = swap(to_x, "stream", 1)
     mlp_bottom = fold_last(to_z)
     self_top, to_x = add(self_top[0], self_by_y[0]), add(self_top[1], self_by_y[1])
     self_then_x = swap(to_x, "stream", 1)
-    line.leave(self_top, to_x)
+    self_side, to_y = add(self_side[0], self_by_x[0]), add(self_side[1], self_by_x[1])
+    self_then_y = swap(to_y, "tensor", 2)
+    line.leave(self_top, to_x, self_side, to_y)
     d_dims = [(QUARTERS, part_rows, BLOCK), (QUARTERS, size, 768), (QUARTERS, image_size, 768)]
-    vectors = jnp.concatenate(
-        [jnp.pad(v, ((0, 0), (0, DV - DT))) for v in (text_vec1, text_vec2, text_vec3)]
-        + [image_vec1, image_vec2, image_vec3, jnp.zeros((4, DV), F32)],
-        axis=0,
-    )
     grads, text_d, image_d, own_sum, total, vectors = run(
         functools.partial(cross_back, pairs),
         None,
-        [w(line.take(grad_low)), w(vectors)] + [a(k) for k in cross_kept] + [w(m) for m in cross_w],
+        [w(line.take(grad_low))]
+        + [w(v) for v in (text_vec1, text_vec2, text_vec3, image_vec1, image_vec2, image_vec3)]
+        + [a(k) for k in cross_kept] + [w(m) for m in cross_w],
         [a(shape(*dims)) for dims in d_dims]
         + [w(shape(part_rows, BLOCK, of=F32)), w(shape(part_rows, BLOCK)), w(shape(16, DV, of=F32))],
         [pltpu.VMEM(dims, BF) for dims in d_dims]
         + [pltpu.VMEM((QUARTERS, part_rows, BLOCK), BF), pltpu.VMEM((2, part_rows, BLOCK), BF), pltpu.VMEM((2, 16, DV), F32)]
+        + [pltpu.VMEM((16, DV), F32)]
         + [pltpu.VMEM(k.shape, BF) for k in cross_kept]
         + links(7)
         + [pltpu.SemaphoreType.DMA((3,)), pltpu.SemaphoreType.DMA((QUARTERS, 4))],
@@ -1353,14 +1388,11 @@
     )
     line.leave(total)
     text_only, image_only = 4 * padded + 16, 4 * image_depth
-    text_vector = jnp.pad(vectors[:6, :DT].reshape(6, places, text_depth), ((0, 0), (0, 0), (0, BLOCK - text_depth)))
-    image_vector = jnp.pad(vectors[6:].reshape(10, places, image_depth), ((0, 0), (0, 0), (0, BLOCK - image_depth)))
-    vectors = low(jnp.concatenate([text_vector, image_vector], axis=0).transpose(1, 0, 2))
-    vector_keep = lax.dynamic_slice_in_dim(vectors, x_at * dp, dp, 0)
-    vector_send = lax.dynamic_slice_in_dim(vectors, (1 - x_at) * dp, dp, 0)
     last_inputs = [
         self_top,
+        self_side,
         self_then_x,
+        self_then_y,
         texts,
         grads,
         text_d,
@@ -1372,19 +1404,21 @@
         text_n1,
         image_n1,
     ]
-    last_scratch = [pltpu.VMEM(m.shape, m.dtype) for m in last_inputs]
+    self_all = (dp, 3 * padded + 2 * image_depth, BLOCK)
+    last_scratch = [pltpu.VMEM(self_all, BF)] * 2 + [pltpu.VMEM(m.shape, m.dtype) for m in last_inputs[4:]]
     last_scratch[5], last_scratch[8] = pltpu.VMEM((QUARTERS, size, BLOCK), BF), pltpu.VMEM((QUARTERS, image_size, BLOCK), BF)
-    text_grad, image_grad, cross_text, image_keep, image_send, self_top = run(
+    grad_left, grad_right, image_grad, cross_text, image_keep, image_send, self_top = run(
         cross_last,
         None,
-        [w(line.take(total)), w(vector_keep), w(vector_send)] + [a(m) for m in last_inputs],
+        [w(line.take(total)), w(vectors)] + [a(m) for m in last_inputs],
         [
-            w(text_wide),
+            w(text_half),
+            w(text_half),
             w(image_cot),
             w(shape(dp, text_only, BLOCK)),
             a(shape(dp, image_only, BLOCK)),
             a(shape(dp, image_only, BLOCK)),
-            w(shape(*self_top.shape[1:])),
+            w(shape(*self_all[1:])),
         ],
         last_scratch
         + [
@@ -1393,34 +1427,34 @@
             pltpu.VMEM((dp, image_only, BLOCK), BF),
             pltpu.VMEM((dp, text_only, BLOCK), BF),
             pltpu.VMEM((dp, text_only, BLOCK), BF),
-            pltpu.VMEM((dp - 1, *self_top.shape[1:]), BF),
+            pltpu.VMEM((dp - 1, *self_all[1:]), BF),
             pltpu.VMEM((DT, QUARTERS * size), BF),
             pltpu.VMEM((DT, QUARTERS * size), BF),
             pltpu.VMEM((DV, QUARTERS * image_size), BF),
             pltpu.VMEM((DV, QUARTERS * image_size), BF),
         ]
         + links(1 + dp)
-        + [pltpu.SemaphoreType.DMA((12,)), pltpu.SemaphoreType.DMA((2,))],
+        + [pltpu.SemaphoreType.DMA((14,)), pltpu.SemaphoreType.DMA((2,))],
         2,
         5,
     )
-    line.leave(text_grad)
-    mlp_top, mlp_by_x, self_bottom, cross_text, image_send = line.take(
-        (mlp_top, mlp_by_x, self_bottom, cross_text, image_send)
+    line.leave(grad_left)
+    mlp_top, mlp_by_x, self_bottom, mlp_bottom, cross_text, image_send = line.take(
+        (mlp_top, mlp_by_x, self_bottom, mlp_bottom, cross_text, image_send)
     )
     cross_text = fold_last(cross_text)
     image_send = swap(image_send, "stream", 1)
     mlp_top, to_y = add(mlp_top[0], mlp_by_x[0]), add(mlp_top[1], mlp_by_x[1])
     mlp_then_y = swap(to_y, "tensor", 2)
     line.leave(mlp_top, to_y)
-    self_bottom = line.take(self_bottom).reshape(2, 2, 3 * image_depth, BLOCK)
+    self_bottom = line.take(self_bottom).reshape(2, 2, 2 * image_depth, BLOCK)
     self_bottom_x = swap(self_bottom[:, 1], "stream", 1)
     cross_image = add(image_keep, line.take(image_send))
     line.leave(cross_image)
     cross_image = fold_last(cross_image)
     self_bottom = add(self_bottom[:, 0], line.take(self_bottom_x))
     self_bottom_y = swap(self_bottom[1], "tensor", 2)
-    mlp_bottom = line.take(mlp_bottom).reshape(2, 2, 2 * image_depth, BLOCK)
+    mlp_bottom = line.take(mlp_bottom).reshape(2, 2, 2 * image_depth + padded, BLOCK)
     mlp_bottom_x = swap(mlp_bottom[:, 1], "stream", 1)
     mlp_top = add(mlp_top, line.take(mlp_then_y))
     line.leave(mlp_top)
@@ -1451,15 +1485,15 @@
 
     below = 3 * padded
     return (
-        text_out,
+        jnp.concatenate([text_left, text_right], axis=1),
         image_out.astype(F32),
-        text_grad,
+        jnp.concatenate([grad_left, grad_right], axis=1),
         image_grad,
         text_pick(cross_text, 0, 1)[None],
         image_pick(cross_image, 0, 2).reshape(1, image_depth, 2, 256),
         text_pick(cross_text, 3 * padded, 1).T[None],
         text_pick(mlp_top, 0, 3)[None],
-        text_pick(mlp_top, below, 3).T[None],
+        jnp.concatenate([text_pick(mlp_top, below, 2), text_pick(mlp_bottom, 2 * image_depth, 1)], axis=1).T[None],
         jnp.stack([heads(n) for n in range(3)], axis=1)[None],
         heads(3).T[None],
         text_vectors[0::2][None],

time: 423 us -> 416 us (0.983)
  local copies, waits for them, and re-layouts: 28.7 us -> 18.5 us
  waiting for transfers between devices: 64.3 us -> 71.6 us
    reduce_scatter x5, waiting for transfers between devices: 13.2 us -> 27.5 us  [fold_last(): return lax.psum_scatter(total, 'dp', scatter_dimension=0, tiled=True)[0]]
    ppermute x18 -> x20, waiting for transfers between devices: 46.6 us -> 40.4 us  [swap(): lax.ppermute(value, axis, [(i, i ^ apart) for i in range(lax.axis_size(ax...]
    ppermute x18 -> x20, starting transfers between devices: 19.8 us -> 22.1 us  [swap(): lax.ppermute(value, axis, [(i, i ^ apart) for i in range(lax.axis_size(ax...]
    unnamed x53 -> x52, local copies, waits for them, and re-layouts: 15.7 us -> 14.9 us
    convert_element_type x8 -> x9, other arithmetic: 11 us -> 10.7 us  [low(): return value.astype(BF)]
  transfers between devices with their start and end apart: 25 -> 27, of which waited for: 10 -> 11; matrix products, arithmetic and copies ran while one was open for 11% -> 8% of each run, Pallas kernels for 50% -> 50%
where the time goes in v6:
time: 416 us; the launch traced here: 413 us
  Pallas kernels  263 us (63%)
  waiting for transfers between devices  71.6 us (17%)
  starting transfers between devices  23 us (6%)
  other arithmetic  21.8 us (5%)
  local copies, waits for them, and re-layouts  18.5 us (4%)
  between operations  14.8 us (4%)
    pallas_call x9, Pallas kernels, run(): pl.pallas_call(kernel, grid=(QUARTERS,) if order else (1,), in_specs=[spe...  263 us
    ppermute x20, waiting for transfers between devices, swap(): lax.ppermute(value, axis, [(i, i ^ apart) for i in range(lax.axis_size(ax...  40.4 us
    reduce_scatter x5, waiting for transfers between devices, fold_last(): return lax.psum_scatter(total, 'dp', scatter_dimension=0, tiled=True)[0]  27.5 us
    ppermute x20, starting transfers between devices, swap(): lax.ppermute(value, axis, [(i, i ^ apart) for i in range(lax.axis_size(ax...  22.1 us
    unnamed x52, local copies, waits for them, and re-layouts  14.9 us
    convert_element_type x9, other arithmetic, low(): return value.astype(BF)  10.7 us
  transfers between devices with their start and end apart: 27, of which 11 were waited for; matrix products, arithmetic and copies ran while one was open for 8% of the time, Pallas kernels for 50%

profile of v6, /device:TPU:0, one launch (start us, length us, event | category | flops | bytes accessed | tf_op | source)
XLA Modules:
  0.0 412.7 jit_solution(8454374662355450216)
XLA Ops:
  7.9 4.2 %shard_map.390 = (bf16[6656,256]{1,0:T(8,128)(2,1)}, bf16[1536,256]{1,0:T(8,128)(2,1)}, bf16[640,256]{1,0:T(8,128)(2,1)}) custom-call(s32[6]{0:T(128)} %stack.39.ids, bf16[768,768]{1,0:T(8,128)(2,1)} %bitcast.176, bf16[768,768]{1,0:T(8,128)(2,1)} %bitcast.177, bf16[1024,256]{1,0:T(8,128)(2,1)} %bitcast.180, bf16[256,1024]{1,0:T(8,128)(2,1)} %bitcast.181), custom_call_target="tpu_custom_call" | custom-call | flops 3300000000 | bytes 1024 | tf_op jit(solution)/shard_map/pallas_call | solution.py:1018
  12.1 3.0 collective-permute-start.1
  15.9 1.6 copy.61.refs_2_
  17.5 4.3 %shard_map.391 = (bf16[6400,256]{1,0:T(8,128)(2,1)}, bf16[2304,256]{1,0:T(8,128)(2,1)}, bf16[512,256]{1,0:T(8,128)(2,1)}) custom-call(s32[6]{0:T(128)} %stack.39.ids, bf16[576,768]{1,0:T(8,128)(2,1)} %bitcast.179, bf16[192,768]{1,0:T(8,128)(2,1)} %bitcast.191, bf16[1024,768]{1,0:T(8,128)(2,1)} %copy.61.refs_2_, bf16[256,1024]{1,0:T(8,128)(2,1)} %bitcast.182), custom_call_target="tpu_custom_call" | custom-call | flops 3300000000 | bytes 1024 | tf_op jit(solution)/shard_map/pallas_call | solution.py:1018
  23.2 1.8 collective-permute-start
  27.5 2.2 copy.80
  32.8 77.3 %shard_map.392 = (f32[512,768]{1,0:T(8,128)}, f32[192,1024]{1,0:T(8,128)}, bf16[4,512,768]{2,1,0:T(8,128)(2,1)}, bf16[4,192,1024]{2,1,0:T(8,128)(2,1)}, bf16[4,5...) custom-call(s32[16]{0:T(128)} %lengths.3, ...), custom_call_target="tpu_custom_call" | custom-call | flops 76999999488 | bytes 1024 | tf_op jit(solution)/shard_map/pallas_call | solution.py:1018
  110.8 15.0 %shard_map.393 = (bf16[512,768]{1,0:T(8,128)(2,1)}, bf16[192,1024]{1,0:T(8,128)(2,1)}, f32[512,768]{1,0:T(8,128)}, f32[192,1024]{1,0:T(8,128)}, bf16[4,512,768]{...) custom-call(f32[512,768]{1,0:T(8,128)} %get-tuple-element.129.text_p, ...), custom_call_target="tpu_custom_call" | custom-call | flops 1100000000 | bytes 1024 | tf_op jit(solution)/shard_map/pallas_call | solution.py:1018
  125.8 3.7 all-gather.5.cloned.1.call-done.refs_3_.refs_10_
  129.5 8.7 %collective-permute-done.6.refs_2_.refs_9_ = bf16[2304,256]{1,0:T(8,128)(2,1)} collective-permute-done((bf16[2304,256]{1,0:T(8,128)(2,1)}, bf16[2304,256]{1,0:T(8,128)(2,1)}, u32[]{:S(2)}, u32[]{:S(2)}) %collective-permute-start.6) | collective-permute-done | bytes 1179680 | tf_op jit(solution)/shard_map/ppermute | solution.py:1036
  138.2 19.9 %shard_map.394 = (f32[512,384]{1,0:T(8,128)}, f32[512,384]{1,0:T(8,128)}, bf16[148,1024]{1,0:T(8,128)(2,1)}, f32[512,768]{1,0:T(8,128)}, f32[192,1024]{1,0:T(8,1...) custom-call(s32[6]{0:T(128)} %stack.39.ids, ...), custom_call_target="tpu_custom_call" | custom-call | flops 20899999744 | bytes 1024 | tf_op jit(solution)/shard_map/pallas_call | solution.py:1018
  158.2 32.6 %shard_map.395 = (f32[512,768]{1,0:T(8,128)}, f32[192,1024]{1,0:T(8,128)}, f32[2,768]{1,0:T(2,128)}, f32[2,1024]{1,0:T(2,128)}, bf16[2304,256]{1,0:T(8,128)(2,1)...) custom-call(f32[512,768]{1,0:T(8,128)} %get-tuple-element.142.text_g, ...), custom_call_target="tpu_custom_call" | custom-call | flops 35200000000 | bytes 1024 | tf_op jit(solution)/shard_map/pallas_call | solution.py:1018
  190.8 1.6 collective-permute-start.9
  193.5 27.7 %shard_map.396 = (f32[512,768]{1,0:T(8,128)}, f32[192,1024]{1,0:T(8,128)}, bf16[2304,256]{1,0:T(8,128)(2,1)}, f32[2,768]{1,0:T(2,128)}, f32[2,1024]{1,0:T(2,128)...) custom-call(f32[512,768]{1,0:T(8,128)} %get-tuple-element.157.text_g, ...), custom_call_target="tpu_custom_call" | custom-call | flops 30799998976 | bytes 1024 | tf_op jit(solution)/shard_map/pallas_call | solution.py:1018
  221.3 1.6 collective-permute-done.8
  223.9 2.5 fusion.6
  230.2 46.9 %shard_map.397 = (bf16[4,2304,256]{2,1,0:T(8,128)(2,1)}, bf16[4,512,768]{2,1,0:T(8,128)(2,1)}, bf16[4,192,768]{2,1,0:T(8,128)(2,1)}, f32[2304,256]{1,0:T(8,128)}...) custom-call(bf16[2304,256]{1,0:T(8,128)(2,1)} %get-tuple-element.177.grad, f32[2,768]{1,0:T(2,128)} %get-tuple-element.178.refs_0_, ...), custom_call_target="tpu_custom_call" | custom-call | flops 52800000000 | bytes 1024 | tf_op jit(solution)/shard_map/pallas_call | solution.py:1018
  277.9 35.0 %shard_map.398 = (f32[512,384]{1,0:T(8,128)}, f32[512,384]{1,0:T(8,128)}, bf16[148,1024]{1,0:T(8,128)(2,1)}, bf16[4,400,256]{2,1,0:T(8,128)(2,1)}, bf16[4,512,25...) custom-call(bf16[2304,256]{1,0:T(8,128)(2,1)} %get-tuple-element.188.total, ...), custom_call_target="tpu_custom_call" | custom-call | flops 2200000000 | bytes 1024 | tf_op jit(solution)/shard_map/pallas_call | solution.py:1018
  313.0 1.6 collective-permute-start.14
  314.9 3.1 fusion.1
  323.5 15.9 %collective-permute-done.14 = bf16[4,512,256]{2,1,0:T(8,128)(2,1)} collective-permute-done((bf16[4,512,256]{2,1,0:T(8,128)(2,1)}, bf16[4,512,256]{2,1,0:T(8,128)(2,1)}, u32[]{:S(2)}, u32[]{:S(2)}) %collective-permute-start.14) | collective-permute-done | bytes 1048608 | tf_op jit(solution)/shard_map/ppermute | solution.py:1036
  339.4 2.5 add_convert_fusion
  344.2 1.6 collective-permute-start.18
  345.8 4.8 %collective-permute-done.18 = bf16[2,256,256]{2,1,0:T(8,128)(2,1)S(1)} collective-permute-done((bf16[2,256,256]{2,1,0:T(8,128)(2,1)S(1)}, bf16[2,256,256]{2,1,0:T(8,128)(2,1)S(1)}, u32[]{:S(2)}, u32[]{:S(2)}) %collective-permute-start.18) | collective-permute-done | bytes 262176 | tf_op jit(solution)/shard_map/ppermute | solution.py:1036
  350.7 1.6 collective-permute-start.19
  352.4 1.6 collective-permute-start.16
  356.4 3.5 collective-permute-done.16
  362.4 3.1 collective-permute-done.17
  370.1 1.6 slice_bitcast_fusion.13
  372.5 1.7 reduce-scatter.14.cloned.1.call-done
  376.6 25.7 %reduce-scatter.12.cloned.1.call-done = bf16[1,512,256]{2,1,0:T(8,128)(2,1)} async-done(((bf16[4,512,256]{2,1,0:T(8,128)(2,1)}), bf16[1,512,256]{2,1,0:T(8,128)(2,1)}) %reduce-scatter.12.cloned.1.call-update) | async-done | bytes 262160 | tf_op jit(solution)/shard_map/reduce_scatter | solution.py:1059
  402.3 1.6 convert_bitcast_fusion.1
  (136 shorter events, 38.5 us)
Async XLA Ops:
  7.2 103.0 %all-gather.3.cloned.1.call-start = ((), (), s32[]{:S(2)}) async-start(), calls=%async_computation.5 | async-start | bytes 2949120 | tf_op jit(solution)/shard_map/all_gather | solution.py:1143
  7.8 7.2 %copy-start.2 = (bf16[1,1024,3,256]{3,1,2,0:T(8,128)(2,1)S(1)}, bf16[1,1024,3,256]{3,1,2,0:T(8,128)(2,1)}, u32[]{:S(2)}) copy-start(bf16[1,1024,3,256]{3,1,2,0:T(8,128)(2,1)} %param.42) | copy-start | bytes 4718596
  12.1 11.0 %collective-permute-start.1 = (bf16[640,256]{1,0:T(8,128)(2,1)}, bf16[640,256]{1,0:T(8,128)(2,1)}, u32[]{:S(2)}, u32[]{:S(2)}) collective-permute-start(bf16[640,256]{1,0:T(8,128)(2,1)} %get-tuple-element.124), channel_id=1, source_target_pairs={{0,2},{1,3},{2,0},{3,1},{4,6},{5,7},{6,4},{7,5},{8,10},{9,11},{10,... | collective-permute-start | bytes 983048 | tf_op jit(solution)/shard_map/ppermute | solution.py:1036
  17.5 7.5 %copy-start = (bf16[6656,256]{1,0:T(8,128)(2,1)S(1)}, bf16[6656,256]{1,0:T(8,128)(2,1)}, u32[]{:S(2)}) copy-start(bf16[6656,256]{1,0:T(8,128)(2,1)} %get-tuple-element.121.refs_0_.refs_4_) | copy-start | bytes 10223620
  23.1 106.4 %all-gather.5.cloned.1.call-start = ((), (), s32[]{:S(2)}) async-start(), calls=%async_computation.6 | async-start | bytes 2359296 | tf_op jit(solution)/shard_map/all_gather | solution.py:1144
  23.2 9.2 %collective-permute-start = (bf16[512,256]{1,0:T(8,128)(2,1)}, bf16[512,256]{1,0:T(8,128)(2,1)}, u32[]{:S(2)}, u32[]{:S(2)}) collective-permute-start(bf16[512,256]{1,0:T(8,128)(2,1)} %get-tuple-element.123), channel_id=1, source_target_pairs={{0,2},{1,3},{2,0},{3,1},{4,6},{5,7},{6,4},{7,5},{8,10},{9,11},{10,... | collective-permute-start | bytes 786440 | tf_op jit(solution)/shard_map/ppermute | solution.py:1036
  25.0 113.2 %collective-permute-start.5 = (bf16[6400,256]{1,0:T(8,128)(2,1)}, bf16[6400,256]{1,0:T(8,128)(2,1)}, u32[]{:S(2)}, u32[]{:S(2)}) collective-permute-start(bf16[6400,256]{1,0:T(8,128)(2,1)} %get-tuple-element.125.refs_0_.refs_7_), channel_id=1, source_target_pairs={{0,1},{1,0},{2,3},{3,2},{4,5},{5,4},{6,7},{7,6},{8,9},{9,8},{10,11... | collective-permute-start | bytes 9830408 | tf_op jit(solution)/shard_map/ppermute | solution.py:1036
  25.0 85.9 %collective-permute-start.2 = (bf16[6656,256]{1,0:T(8,128)(2,1)S(1)}, bf16[6656,256]{1,0:T(8,128)(2,1)}, u32[]{:S(2)}, u32[]{:S(2)}) collective-permute-start(bf16[6656,256]{1,0:T(8,128)(2,1)S(1)} %copy-done), channel_id=1, source_target_pairs={{0,1},{1,0},{2,3},{3,2},{4,5},{5,4},{6,7},{7,6},{8,9},{9,8},{10,11... | collective-permute-start | bytes 10223624 | tf_op jit(solution)/shard_map/ppermute | solution.py:1036
  25.5 84.6 %collective-permute-start.4 = (bf16[148,1024]{1,0:T(8,128)(2,1)}, bf16[148,1024]{1,0:T(8,128)(2,1)}, u32[]{:S(2)}, u32[]{:S(2)}) collective-permute-start(bf16[148,1024]{1,0:T(8,128)(2,1)} %param.27), channel_id=1, source_target_pairs={{0,16},{16,0},{1,17},{17,1},{2,18},{18,2},{3,19},{19,3},{4,20},{20... | collective-permute-start | bytes 909320 | tf_op jit(solution)/shard_map/ppermute | solution.py:1036
  27.0 83.2 %collective-permute-start.3 = (bf16[1536,256]{1,0:T(8,128)(2,1)}, bf16[1536,256]{1,0:T(8,128)(2,1)}, u32[]{:S(2)}, u32[]{:S(2)}) collective-permute-start(bf16[1536,256]{1,0:T(8,128)(2,1)} %get-tuple-element.131), channel_id=1, source_target_pairs={{0,2},{1,3},{2,0},{3,1},{4,6},{5,7},{6,4},{7,5},{8,10},{9,11},{10,... | collective-permute-start | bytes 2359304 | tf_op jit(solution)/shard_map/ppermute | solution.py:1036
  32.4 280.5 %reduce-scatter.6.cloned.1.call-start = ((), (), s32[]{:S(2)}) async-start(), calls=%async_computation.7 | async-start | bytes 2621440 | tf_op jit(solution)/shard_map/reduce_scatter | solution.py:1059
  110.2 28.0 %collective-permute-start.6 = (bf16[2304,256]{1,0:T(8,128)(2,1)}, bf16[2304,256]{1,0:T(8,128)(2,1)}, u32[]{:S(2)}, u32[]{:S(2)}) collective-permute-start(bf16[2304,256]{1,0:T(8,128)(2,1)} %get-tuple-element.137), channel_id=1, source_target_pairs={{0,2},{1,3},{2,0},{3,1},{4,6},{5,7},{6,4},{7,5},{8,10},{9,11},{10,... | collective-permute-start | bytes 3538952 | tf_op jit(solution)/shard_map/ppermute | solution.py:1036
  190.8 122.2 %reduce-scatter.8.cloned.1.call-start = ((), (), s32[]{:S(2)}) async-start(), calls=%async_computation.8 | async-start | bytes 3604480 | tf_op jit(solution)/shard_map/reduce_scatter | solution.py:1059
  190.8 30.4 %collective-permute-start.9 = (bf16[148,1024]{1,0:T(8,128)(2,1)}, bf16[148,1024]{1,0:T(8,128)(2,1)S(1)}, u32[]{:S(2)}, u32[]{:S(2)}) collective-permute-start(bf16[148,1024]{1,0:T(8,128)(2,1)} %get-tuple-element.169), channel_id=1, source_target_pairs={{0,16},{16,0},{1,17},{17,1},{2,18},{18,2},{3,19},{19,3},{4,20},{20... | collective-permute-start | bytes 909320 | tf_op jit(solution)/shard_map/ppermute | solution.py:1036
  192.4 30.5 %collective-permute-start.8 = (bf16[2,4,256,256]{3,2,1,0:T(8,128)(2,1)}, bf16[2,4,256,256]{3,2,1,0:T(8,128)(2,1)S(1)}, u32[]{:S(2)}, u32[]{:S(2)}) collective-permute-start(bf16[2,4,256,256]{3,2,1,0:T(8,128)(2,1)} %bitcast.23), channel_id=1, source_target_pairs={{0,16},{16,0},{1,17},{17,1},{2,18},{18,2},{3,19},{19,3},{4,20},{20... | collective-permute-start | bytes 3145736 | tf_op jit(solution)/shard_map/ppermute | solution.py:1036
  192.9 29.9 %collective-permute-start.7 = (bf16[2,4,288,256]{3,2,1,0:T(8,128)(2,1)}, bf16[2,4,288,256]{3,2,1,0:T(8,128)(2,1)S(1)}, u32[]{:S(2)}, u32[]{:S(2)}) collective-permute-start(bf16[2,4,288,256]{3,2,1,0:T(8,128)(2,1)} %bitcast.178), channel_id=1, source_target_pairs={{0,2},{1,3},{2,0},{3,1},{4,6},{5,7},{6,4},{7,5},{8,10},{9,11},{10,... | collective-permute-start | bytes 3538952 | tf_op jit(solution)/shard_map/ppermute | solution.py:1036
  223.9 143.2 %reduce-scatter.10.cloned.1.call-start = ((), (), s32[]{:S(2)}) async-start(), calls=%async_computation.9 | async-start | bytes 1024000 | tf_op jit(solution)/shard_map/reduce_scatter | solution.py:1059
  226.4 50.7 %collective-permute-start.11 = (bf16[4,256,256]{2,1,0:T(8,128)(2,1)}, bf16[4,256,256]{2,1,0:T(8,128)(2,1)}, u32[]{:S(2)}, u32[]{:S(2)}) collective-permute-start(bf16[4,256,256]{2,1,0:T(8,128)(2,1)} %get-tuple-element.268), channel_id=1, source_target_pairs={{0,2},{1,3},{2,0},{3,1},{4,6},{5,7},{6,4},{7,5},{8,10},{9,11},{10,... | collective-permute-start | bytes 1572872 | tf_op jit(solution)/shard_map/ppermute | solution.py:1036
  228.1 49.0 %collective-permute-start.10 = (bf16[4,288,256]{2,1,0:T(8,128)(2,1)S(1)}, bf16[4,288,256]{2,1,0:T(8,128)(2,1)S(1)}, u32[]{:S(2)}, u32[]{:S(2)}) collective-permute-start(bf16[4,288,256]{2,1,0:T(8,128)(2,1)S(1)} %get-tuple-element.266), channel_id=1, source_target_pairs={{0,16},{16,0},{1,17},{17,1},{2,18},{18,2},{3,19},{19,3},{4,20},{20... | collective-permute-start | bytes 1769480 | tf_op jit(solution)/shard_map/ppermute | solution.py:1036
  229.5 83.4 %collective-permute-start.13 = (bf16[2,4,480,256]{3,2,1,0:T(8,128)(2,1)}, bf16[2,4,480,256]{3,2,1,0:T(8,128)(2,1)}, u32[]{:S(2)}, u32[]{:S(2)}) collective-permute-start(bf16[2,4,480,256]{3,2,1,0:T(8,128)(2,1)} %bitcast.24), channel_id=1, source_target_pairs={{0,16},{16,0},{1,17},{17,1},{2,18},{18,2},{3,19},{19,3},{4,20},{20... | collective-permute-start | bytes 5898248 | tf_op jit(solution)/shard_map/ppermute | solution.py:1036
  277.9 36.9 %copy-start.1 = (bf16[3840,256]{1,0:T(8,128)(2,1)S(1)}, bf16[3840,256]{1,0:T(8,128)(2,1)}, u32[]{:S(2)}) copy-start(bf16[3840,256]{1,0:T(8,128)(2,1)} %get-tuple-element.170) | copy-start | bytes 5898244
  313.0 26.4 %collective-permute-start.14 = (bf16[4,512,256]{2,1,0:T(8,128)(2,1)}, bf16[4,512,256]{2,1,0:T(8,128)(2,1)}, u32[]{:S(2)}, u32[]{:S(2)}) collective-permute-start(bf16[4,512,256]{2,1,0:T(8,128)(2,1)} %get-tuple-element.208), channel_id=1, source_target_pairs={{0,16},{16,0},{1,17},{17,1},{2,18},{18,2},{3,19},{19,3},{4,20},{20... | collective-permute-start | bytes 3145736 | tf_op jit(solution)/shard_map/ppermute | solution.py:1036
  314.5 59.7 %reduce-scatter.14.cloned.1.call-start = ((), (), s32[]{:S(2)}) async-start(), calls=%async_computation.11 | async-start | bytes 1228800 | tf_op jit(solution)/shard_map/reduce_scatter | solution.py:1059
  317.9 24.0 %collective-permute-start.15 = (bf16[4,480,256]{2,1,0:T(8,128)(2,1)}, bf16[4,480,256]{2,1,0:T(8,128)(2,1)S(1)}, u32[]{:S(2)}, u32[]{:S(2)}) collective-permute-start(bf16[4,480,256]{2,1,0:T(8,128)(2,1)} %get-tuple-element.264), channel_id=1, source_target_pairs={{0,2},{1,3},{2,0},{3,1},{4,6},{5,7},{6,4},{7,5},{8,10},{9,11},{10,... | collective-permute-start | bytes 2949128 | tf_op jit(solution)/shard_map/ppermute | solution.py:1036
  321.6 33.9 %collective-permute-start.12 = (bf16[148,1024]{1,0:T(8,128)(2,1)S(1)}, bf16[148,1024]{1,0:T(8,128)(2,1)S(1)}, u32[]{:S(2)}, u32[]{:S(2)}) collective-permute-start(bf16[148,1024]{1,0:T(8,128)(2,1)S(1)} %copy-done.18), channel_id=1, source_target_pairs={{0,16},{16,0},{1,17},{17,1},{2,18},{18,2},{3,19},{19,3},{4,20},{20... | collective-permute-start | bytes 909320 | tf_op jit(solution)/shard_map/ppermute | solution.py:1036
  322.3 17.1 %copy-start.5 = (bf16[4,512,256]{2,1,0:T(8,128)(2,1)S(1)}, bf16[4,512,256]{2,1,0:T(8,128)(2,1)}, u32[]{:S(2)}) copy-start(bf16[4,512,256]{2,1,0:T(8,128)(2,1)} %get-tuple-element.207) | copy-start | bytes 3145732
  343.2 9.2 %copy-start.12 = (bf16[1,1408,256]{2,1,0:T(8,128)(2,1)S(1)}, bf16[1,1408,256]{2,1,0:T(8,128)(2,1)}, u32[]{:S(2)}) copy-start(bf16[1,1408,256]{2,1,0:T(8,128)(2,1)} %reduce-scatter.8.cloned.1.call-done) | copy-start | bytes 2162692
  343.2 59.1 %reduce-scatter.12.cloned.1.call-start = ((), (), s32[]{:S(2)}) async-start(), calls=%async_computation.10 | async-start | bytes 1310720 | tf_op jit(solution)/shard_map/reduce_scatter | solution.py:1059
  344.2 6.4 %collective-permute-start.18 = (bf16[2,256,256]{2,1,0:T(8,128)(2,1)S(1)}, bf16[2,256,256]{2,1,0:T(8,128)(2,1)S(1)}, u32[]{:S(2)}, u32[]{:S(2)}) collective-permute-start(bf16[2,256,256]{2,1,0:T(8,128)(2,1)S(1)} %slice_bitcast_fusion.2), channel_id=1, source_target_pairs={{0,16},{16,0},{1,17},{17,1},{2,18},{18,2},{3,19},{19,3},{4,20},{20... | collective-permute-start | bytes 786440 | tf_op jit(solution)/shard_map/ppermute | solution.py:1036
  350.7 5.6 %collective-permute-start.19 = (bf16[256,256]{1,0:T(8,128)(2,1)S(1)}, bf16[256,256]{1,0:T(8,128)(2,1)S(1)}, u32[]{:S(2)}, u32[]{:S(2)}) collective-permute-start(bf16[256,256]{1,0:T(8,128)(2,1)S(1)} %slice_bitcast_fusion.6), channel_id=1, source_target_pairs={{0,2},{1,3},{2,0},{3,1},{4,6},{5,7},{6,4},{7,5},{8,10},{9,11},{10,... | collective-permute-start | bytes 393224 | tf_op jit(solution)/shard_map/ppermute | solution.py:1036
  352.4 7.5 %collective-permute-start.16 = (bf16[2,352,256]{2,1,0:T(8,128)(2,1)S(1)}, bf16[2,352,256]{2,1,0:T(8,128)(2,1)S(1)}, u32[]{:S(2)}, u32[]{:S(2)}) collective-permute-start(bf16[2,352,256]{2,1,0:T(8,128)(2,1)S(1)} %slice_bitcast_fusion), channel_id=1, source_target_pairs={{0,16},{16,0},{1,17},{17,1},{2,18},{18,2},{3,19},{19,3},{4,20},{20... | collective-permute-start | bytes 1081352 | tf_op jit(solution)/shard_map/ppermute | solution.py:1036
  360.0 5.6 %collective-permute-start.17 = (bf16[352,256]{1,0:T(8,128)(2,1)S(1)}, bf16[352,256]{1,0:T(8,128)(2,1)S(1)}, u32[]{:S(2)}, u32[]{:S(2)}) collective-permute-start(bf16[352,256]{1,0:T(8,128)(2,1)S(1)} %slice_bitcast_fusion.4), channel_id=1, source_target_pairs={{0,2},{1,3},{2,0},{3,1},{4,6},{5,7},{6,4},{7,5},{8,10},{9,11},{10,... | collective-permute-start | bytes 540680 | tf_op jit(solution)/shard_map/ppermute | solution.py:1036
  (14 other events, 35.2 us)
Sparse Core Ops, SparseCore 0:
  23.2 56.1 all-gather.2
  81.6 47.8 all-gather.4
  190.9 44.1 reduce-scatter.5
  237.4 65.7 reduce-scatter.7
  314.7 27.4 reduce-scatter.9
  344.5 29.6 reduce-scatter.13
  376.5 25.7 reduce-scatter.11

commit v7 on v6

--- a/solution.py
+++ b/solution.py
@@ -1124,7 +1124,7 @@
             image_self_out[0],
         ],
         places,
-        4096,
+        4608,
         after(ids, mlp_own),
     )
     cross_w = (

time: 416 us -> 411 us (0.988)
  waiting for transfers between devices: 71.6 us -> 67.2 us
    ppermute x20, waiting for transfers between devices: 40.4 us -> 34 us  [swap(): lax.ppermute(value, axis, [(i, i ^ apart) for i in range(lax.axis_size(ax...]
where the time goes in v7:
time: 411 us; the launch traced here: 408 us
  Pallas kernels  263 us (64%)
  waiting for transfers between devices  67.2 us (16%)
  starting transfers between devices  23 us (6%)
  other arithmetic  21.8 us (5%)
  local copies, waits for them, and re-layouts  18.5 us (5%)
  between operations  14.8 us (4%)
    pallas_call x9, Pallas kernels, run(): pl.pallas_call(kernel, grid=(QUARTERS,) if order else (1,), in_specs=[spe...  263 us
    ppermute x20, waiting for transfers between devices, swap(): lax.ppermute(value, axis, [(i, i ^ apart) for i in range(lax.axis_size(ax...  34 us
    reduce_scatter x5, waiting for transfers between devices, fold_last(): return lax.psum_scatter(total, 'dp', scatter_dimension=0, tiled=True)[0]  27.4 us
    ppermute x20, starting transfers between devices, swap(): lax.ppermute(value, axis, [(i, i ^ apart) for i in range(lax.axis_size(ax...  22.1 us
    unnamed x52, local copies, waits for them, and re-layouts  14.9 us
    convert_element_type x9, other arithmetic, low(): return value.astype(BF)  10.6 us
  transfers between devices with their start and end apart: 27, of which 11 were waited for; matrix products, arithmetic and copies ran while one was open for 8% of the time, Pallas kernels for 50%

profile of v7, /device:TPU:0, one launch (start us, length us, event | category | flops | bytes accessed | tf_op | source)
XLA Modules:
  0.0 407.7 jit_solution(3984566930635764662)
XLA Ops:
  7.9 4.2 %shard_map.390 = (bf16[6656,256]{1,0:T(8,128)(2,1)}, bf16[1536,256]{1,0:T(8,128)(2,1)}, bf16[640,256]{1,0:T(8,128)(2,1)}) custom-call(s32[6]{0:T(128)} %stack.39.ids, bf16[768,768]{1,0:T(8,128)(2,1)} %bitcast.176, bf16[768,768]{1,0:T(8,128)(2,1)} %bitcast.177, bf16[1024,256]{1,0:T(8,128)(2,1)} %bitcast.180, bf16[256,1024]{1,0:T(8,128)(2,1)} %bitcast.181), custom_call_target="tpu_custom_call" | custom-call | flops 3300000000 | bytes 1024 | tf_op jit(solution)/shard_map/pallas_call | solution.py:1018
  12.1 3.0 collective-permute-start.1
  15.9 1.6 copy.61.refs_2_
  17.5 4.2 %shard_map.391 = (bf16[6400,256]{1,0:T(8,128)(2,1)}, bf16[1792,256]{1,0:T(8,128)(2,1)}, bf16[576,256]{1,0:T(8,128)(2,1)}) custom-call(s32[6]{0:T(128)} %stack.39.ids, bf16[576,768]{1,0:T(8,128)(2,1)} %bitcast.179, bf16[192,768]{1,0:T(8,128)(2,1)} %bitcast.191, bf16[1024,768]{1,0:T(8,128)(2,1)} %copy.61.refs_2_, bf16[256,1024]{1,0:T(8,128)(2,1)} %bitcast.182), custom_call_target="tpu_custom_call" | custom-call | flops 3300000000 | bytes 1024 | tf_op jit(solution)/shard_map/pallas_call | solution.py:1018
  23.2 1.8 collective-permute-start
  27.5 2.2 copy.80
  30.9 2.6 collective-permute-done
  33.9 77.0 %shard_map.392 = (f32[512,768]{1,0:T(8,128)}, f32[192,1024]{1,0:T(8,128)}, bf16[4,512,768]{2,1,0:T(8,128)(2,1)}, bf16[4,192,1024]{2,1,0:T(8,128)(2,1)}, bf16[4,5...) custom-call(s32[16]{0:T(128)} %lengths.3, ...), custom_call_target="tpu_custom_call" | custom-call | flops 76999999488 | bytes 1024 | tf_op jit(solution)/shard_map/pallas_call | solution.py:1018
  111.6 15.1 %shard_map.393 = (bf16[512,768]{1,0:T(8,128)(2,1)}, bf16[192,1024]{1,0:T(8,128)(2,1)}, f32[512,768]{1,0:T(8,128)}, f32[192,1024]{1,0:T(8,128)}, bf16[4,512,768]{...) custom-call(f32[512,768]{1,0:T(8,128)} %get-tuple-element.129.text_p, ...), custom_call_target="tpu_custom_call" | custom-call | flops 1100000000 | bytes 1024 | tf_op jit(solution)/shard_map/pallas_call | solution.py:1018
  126.6 5.6 %all-gather.5.cloned.1.call-done.refs_3_.refs_10_ = bf16[4608,256]{1,0:T(8,128)(2,1)} async-done(((bf16[576,256]{1,0:T(8,128)(2,1)}), bf16[4608,256]{1,0:T(8,128)(2,1)}) %all-gather.5.cloned.1.call-update) | async-done | bytes 2359312 | tf_op jit(solution)/shard_map/all_gather | solution.py:1144
  133.3 19.9 %shard_map.394 = (f32[512,384]{1,0:T(8,128)}, f32[512,384]{1,0:T(8,128)}, bf16[148,1024]{1,0:T(8,128)(2,1)}, f32[512,768]{1,0:T(8,128)}, f32[192,1024]{1,0:T(8,1...) custom-call(s32[6]{0:T(128)} %stack.39.ids, ...), custom_call_target="tpu_custom_call" | custom-call | flops 20899999744 | bytes 1024 | tf_op jit(solution)/shard_map/pallas_call | solution.py:1018
  153.2 32.6 %shard_map.395 = (f32[512,768]{1,0:T(8,128)}, f32[192,1024]{1,0:T(8,128)}, f32[2,768]{1,0:T(2,128)}, f32[2,1024]{1,0:T(2,128)}, bf16[2304,256]{1,0:T(8,128)(2,1)...) custom-call(f32[512,768]{1,0:T(8,128)} %get-tuple-element.142.text_g, ...), custom_call_target="tpu_custom_call" | custom-call | flops 35200000000 | bytes 1024 | tf_op jit(solution)/shard_map/pallas_call | solution.py:1018
  185.9 1.6 collective-permute-start.9
  188.6 27.7 %shard_map.396 = (f32[512,768]{1,0:T(8,128)}, f32[192,1024]{1,0:T(8,128)}, bf16[2304,256]{1,0:T(8,128)(2,1)}, f32[2,768]{1,0:T(2,128)}, f32[2,1024]{1,0:T(2,128)...) custom-call(f32[512,768]{1,0:T(8,128)} %get-tuple-element.157.text_g, ...), custom_call_target="tpu_custom_call" | custom-call | flops 30799998976 | bytes 1024 | tf_op jit(solution)/shard_map/pallas_call | solution.py:1018
  216.3 1.6 collective-permute-done.8
  219.0 2.5 fusion.6
  225.2 46.9 %shard_map.397 = (bf16[4,2304,256]{2,1,0:T(8,128)(2,1)}, bf16[4,512,768]{2,1,0:T(8,128)(2,1)}, bf16[4,192,768]{2,1,0:T(8,128)(2,1)}, f32[2304,256]{1,0:T(8,128)}...) custom-call(bf16[2304,256]{1,0:T(8,128)(2,1)} %get-tuple-element.177.grad, f32[2,768]{1,0:T(2,128)} %get-tuple-element.178.refs_0_, ...), custom_call_target="tpu_custom_call" | custom-call | flops 52800000000 | bytes 1024 | tf_op jit(solution)/shard_map/pallas_call | solution.py:1018
  272.9 35.0 %shard_map.398 = (f32[512,384]{1,0:T(8,128)}, f32[512,384]{1,0:T(8,128)}, bf16[148,1024]{1,0:T(8,128)(2,1)}, bf16[4,400,256]{2,1,0:T(8,128)(2,1)}, bf16[4,512,25...) custom-call(bf16[2304,256]{1,0:T(8,128)(2,1)} %get-tuple-element.188.total, ...), custom_call_target="tpu_custom_call" | custom-call | flops 2200000000 | bytes 1024 | tf_op jit(solution)/shard_map/pallas_call | solution.py:1018
  308.0 1.6 collective-permute-start.14
  309.9 3.1 fusion.1
  318.6 15.9 %collective-permute-done.14 = bf16[4,512,256]{2,1,0:T(8,128)(2,1)} collective-permute-done((bf16[4,512,256]{2,1,0:T(8,128)(2,1)}, bf16[4,512,256]{2,1,0:T(8,128)(2,1)}, u32[]{:S(2)}, u32[]{:S(2)}) %collective-permute-start.14) | collective-permute-done | bytes 1048608 | tf_op jit(solution)/shard_map/ppermute | solution.py:1036
  334.5 2.5 add_convert_fusion
  339.3 1.6 collective-permute-start.18
  340.9 4.8 %collective-permute-done.18 = bf16[2,256,256]{2,1,0:T(8,128)(2,1)S(1)} collective-permute-done((bf16[2,256,256]{2,1,0:T(8,128)(2,1)S(1)}, bf16[2,256,256]{2,1,0:T(8,128)(2,1)S(1)}, u32[]{:S(2)}, u32[]{:S(2)}) %collective-permute-start.18) | collective-permute-done | bytes 262176 | tf_op jit(solution)/shard_map/ppermute | solution.py:1036
  345.8 1.6 collective-permute-start.19
  347.4 1.6 collective-permute-start.16
  351.5 3.5 collective-permute-done.16
  357.5 3.1 collective-permute-done.17
  365.1 1.6 slice_bitcast_fusion.13
  367.6 1.7 reduce-scatter.14.cloned.1.call-done
  371.7 25.7 %reduce-scatter.12.cloned.1.call-done = bf16[1,512,256]{2,1,0:T(8,128)(2,1)} async-done(((bf16[4,512,256]{2,1,0:T(8,128)(2,1)}), bf16[1,512,256]{2,1,0:T(8,128)(2,1)}) %reduce-scatter.12.cloned.1.call-update) | async-done | bytes 262160 | tf_op jit(solution)/shard_map/reduce_scatter | solution.py:1059
  397.3 1.6 convert_bitcast_fusion.1
  (136 shorter events, 38.2 us)
Async XLA Ops:
  7.2 103.7 %all-gather.3.cloned.1.call-start = ((), (), s32[]{:S(2)}) async-start(), calls=%async_computation.5 | async-start | bytes 2949120 | tf_op jit(solution)/shard_map/all_gather | solution.py:1143
  7.8 7.2 %copy-start.2 = (bf16[1,1024,3,256]{3,1,2,0:T(8,128)(2,1)S(1)}, bf16[1,1024,3,256]{3,1,2,0:T(8,128)(2,1)}, u32[]{:S(2)}) copy-start(bf16[1,1024,3,256]{3,1,2,0:T(8,128)(2,1)} %param.42) | copy-start | bytes 4718596
  12.1 11.0 %collective-permute-start.1 = (bf16[640,256]{1,0:T(8,128)(2,1)}, bf16[640,256]{1,0:T(8,128)(2,1)}, u32[]{:S(2)}, u32[]{:S(2)}) collective-permute-start(bf16[640,256]{1,0:T(8,128)(2,1)} %get-tuple-element.124), channel_id=1, source_target_pairs={{0,2},{1,3},{2,0},{3,1},{4,6},{5,7},{6,4},{7,5},{8,10},{9,11},{10,... | collective-permute-start | bytes 983048 | tf_op jit(solution)/shard_map/ppermute | solution.py:1036
  17.5 7.5 %copy-start = (bf16[6656,256]{1,0:T(8,128)(2,1)S(1)}, bf16[6656,256]{1,0:T(8,128)(2,1)}, u32[]{:S(2)}) copy-start(bf16[6656,256]{1,0:T(8,128)(2,1)} %get-tuple-element.121.refs_0_.refs_4_) | copy-start | bytes 10223620
  23.1 109.1 %all-gather.5.cloned.1.call-start = ((), (), s32[]{:S(2)}) async-start(), calls=%async_computation.6 | async-start | bytes 2654208 | tf_op jit(solution)/shard_map/all_gather | solution.py:1144
  23.2 10.3 %collective-permute-start = (bf16[576,256]{1,0:T(8,128)(2,1)}, bf16[576,256]{1,0:T(8,128)(2,1)}, u32[]{:S(2)}, u32[]{:S(2)}) collective-permute-start(bf16[576,256]{1,0:T(8,128)(2,1)} %get-tuple-element.123), channel_id=1, source_target_pairs={{0,2},{1,3},{2,0},{3,1},{4,6},{5,7},{6,4},{7,5},{8,10},{9,11},{10,... | collective-permute-start | bytes 884744 | tf_op jit(solution)/shard_map/ppermute | solution.py:1036
  25.0 108.3 %collective-permute-start.5 = (bf16[6400,256]{1,0:T(8,128)(2,1)}, bf16[6400,256]{1,0:T(8,128)(2,1)}, u32[]{:S(2)}, u32[]{:S(2)}) collective-permute-start(bf16[6400,256]{1,0:T(8,128)(2,1)} %get-tuple-element.125.refs_0_.refs_7_), channel_id=1, source_target_pairs={{0,1},{1,0},{2,3},{3,2},{4,5},{5,4},{6,7},{7,6},{8,9},{9,8},{10,11... | collective-permute-start | bytes 9830408 | tf_op jit(solution)/shard_map/ppermute | solution.py:1036
  25.0 86.6 %collective-permute-start.2 = (bf16[6656,256]{1,0:T(8,128)(2,1)S(1)}, bf16[6656,256]{1,0:T(8,128)(2,1)}, u32[]{:S(2)}, u32[]{:S(2)}) collective-permute-start(bf16[6656,256]{1,0:T(8,128)(2,1)S(1)} %copy-done), channel_id=1, source_target_pairs={{0,1},{1,0},{2,3},{3,2},{4,5},{5,4},{6,7},{7,6},{8,9},{9,8},{10,11... | collective-permute-start | bytes 10223624 | tf_op jit(solution)/shard_map/ppermute | solution.py:1036
  25.5 85.4 %collective-permute-start.4 = (bf16[148,1024]{1,0:T(8,128)(2,1)}, bf16[148,1024]{1,0:T(8,128)(2,1)}, u32[]{:S(2)}, u32[]{:S(2)}) collective-permute-start(bf16[148,1024]{1,0:T(8,128)(2,1)} %param.27), channel_id=1, source_target_pairs={{0,16},{16,0},{1,17},{17,1},{2,18},{18,2},{3,19},{19,3},{4,20},{20... | collective-permute-start | bytes 909320 | tf_op jit(solution)/shard_map/ppermute | solution.py:1036
  27.0 83.9 %collective-permute-start.3 = (bf16[1536,256]{1,0:T(8,128)(2,1)}, bf16[1536,256]{1,0:T(8,128)(2,1)}, u32[]{:S(2)}, u32[]{:S(2)}) collective-permute-start(bf16[1536,256]{1,0:T(8,128)(2,1)} %get-tuple-element.131), channel_id=1, source_target_pairs={{0,2},{1,3},{2,0},{3,1},{4,6},{5,7},{6,4},{7,5},{8,10},{9,11},{10,... | collective-permute-start | bytes 2359304 | tf_op jit(solution)/shard_map/ppermute | solution.py:1036
  33.5 274.5 %reduce-scatter.6.cloned.1.call-start = ((), (), s32[]{:S(2)}) async-start(), calls=%async_computation.7 | async-start | bytes 2621440 | tf_op jit(solution)/shard_map/reduce_scatter | solution.py:1059
  110.9 22.4 %collective-permute-start.6 = (bf16[1792,256]{1,0:T(8,128)(2,1)}, bf16[1792,256]{1,0:T(8,128)(2,1)}, u32[]{:S(2)}, u32[]{:S(2)}) collective-permute-start(bf16[1792,256]{1,0:T(8,128)(2,1)} %get-tuple-element.137), channel_id=1, source_target_pairs={{0,2},{1,3},{2,0},{3,1},{4,6},{5,7},{6,4},{7,5},{8,10},{9,11},{10,... | collective-permute-start | bytes 2752520 | tf_op jit(solution)/shard_map/ppermute | solution.py:1036
  185.8 122.2 %reduce-scatter.8.cloned.1.call-start = ((), (), s32[]{:S(2)}) async-start(), calls=%async_computation.8 | async-start | bytes 3604480 | tf_op jit(solution)/shard_map/reduce_scatter | solution.py:1059
  185.9 30.4 %collective-permute-start.9 = (bf16[148,1024]{1,0:T(8,128)(2,1)}, bf16[148,1024]{1,0:T(8,128)(2,1)S(1)}, u32[]{:S(2)}, u32[]{:S(2)}) collective-permute-start(bf16[148,1024]{1,0:T(8,128)(2,1)} %get-tuple-element.169), channel_id=1, source_target_pairs={{0,16},{16,0},{1,17},{17,1},{2,18},{18,2},{3,19},{19,3},{4,20},{20... | collective-permute-start | bytes 909320 | tf_op jit(solution)/shard_map/ppermute | solution.py:1036
  187.4 30.5 %collective-permute-start.8 = (bf16[2,4,256,256]{3,2,1,0:T(8,128)(2,1)}, bf16[2,4,256,256]{3,2,1,0:T(8,128)(2,1)S(1)}, u32[]{:S(2)}, u32[]{:S(2)}) collective-permute-start(bf16[2,4,256,256]{3,2,1,0:T(8,128)(2,1)} %bitcast.23), channel_id=1, source_target_pairs={{0,16},{16,0},{1,17},{17,1},{2,18},{18,2},{3,19},{19,3},{4,20},{20... | collective-permute-start | bytes 3145736 | tf_op jit(solution)/shard_map/ppermute | solution.py:1036
  188.0 29.9 %collective-permute-start.7 = (bf16[2,4,288,256]{3,2,1,0:T(8,128)(2,1)}, bf16[2,4,288,256]{3,2,1,0:T(8,128)(2,1)S(1)}, u32[]{:S(2)}, u32[]{:S(2)}) collective-permute-start(bf16[2,4,288,256]{3,2,1,0:T(8,128)(2,1)} %bitcast.178), channel_id=1, source_target_pairs={{0,2},{1,3},{2,0},{3,1},{4,6},{5,7},{6,4},{7,5},{8,10},{9,11},{10,... | collective-permute-start | bytes 3538952 | tf_op jit(solution)/shard_map/ppermute | solution.py:1036
  218.9 143.2 %reduce-scatter.10.cloned.1.call-start = ((), (), s32[]{:S(2)}) async-start(), calls=%async_computation.9 | async-start | bytes 1024000 | tf_op jit(solution)/shard_map/reduce_scatter | solution.py:1059
  221.5 50.6 %collective-permute-start.11 = (bf16[4,256,256]{2,1,0:T(8,128)(2,1)}, bf16[4,256,256]{2,1,0:T(8,128)(2,1)}, u32[]{:S(2)}, u32[]{:S(2)}) collective-permute-start(bf16[4,256,256]{2,1,0:T(8,128)(2,1)} %get-tuple-element.268), channel_id=1, source_target_pairs={{0,2},{1,3},{2,0},{3,1},{4,6},{5,7},{6,4},{7,5},{8,10},{9,11},{10,... | collective-permute-start | bytes 1572872 | tf_op jit(solution)/shard_map/ppermute | solution.py:1036
  223.2 48.9 %collective-permute-start.10 = (bf16[4,288,256]{2,1,0:T(8,128)(2,1)S(1)}, bf16[4,288,256]{2,1,0:T(8,128)(2,1)S(1)}, u32[]{:S(2)}, u32[]{:S(2)}) collective-permute-start(bf16[4,288,256]{2,1,0:T(8,128)(2,1)S(1)} %get-tuple-element.266), channel_id=1, source_target_pairs={{0,16},{16,0},{1,17},{17,1},{2,18},{18,2},{3,19},{19,3},{4,20},{20... | collective-permute-start | bytes 1769480 | tf_op jit(solution)/shard_map/ppermute | solution.py:1036
  224.6 83.4 %collective-permute-start.13 = (bf16[2,4,480,256]{3,2,1,0:T(8,128)(2,1)}, bf16[2,4,480,256]{3,2,1,0:T(8,128)(2,1)}, u32[]{:S(2)}, u32[]{:S(2)}) collective-permute-start(bf16[2,4,480,256]{3,2,1,0:T(8,128)(2,1)} %bitcast.24), channel_id=1, source_target_pairs={{0,16},{16,0},{1,17},{17,1},{2,18},{18,2},{3,19},{19,3},{4,20},{20... | collective-permute-start | bytes 5898248 | tf_op jit(solution)/shard_map/ppermute | solution.py:1036
  272.9 36.9 %copy-start.1 = (bf16[3840,256]{1,0:T(8,128)(2,1)S(1)}, bf16[3840,256]{1,0:T(8,128)(2,1)}, u32[]{:S(2)}) copy-start(bf16[3840,256]{1,0:T(8,128)(2,1)} %get-tuple-element.170) | copy-start | bytes 5898244
  308.0 26.4 %collective-permute-start.14 = (bf16[4,512,256]{2,1,0:T(8,128)(2,1)}, bf16[4,512,256]{2,1,0:T(8,128)(2,1)}, u32[]{:S(2)}, u32[]{:S(2)}) collective-permute-start(bf16[4,512,256]{2,1,0:T(8,128)(2,1)} %get-tuple-element.208), channel_id=1, source_target_pairs={{0,16},{16,0},{1,17},{17,1},{2,18},{18,2},{3,19},{19,3},{4,20},{20... | collective-permute-start | bytes 3145736 | tf_op jit(solution)/shard_map/ppermute | solution.py:1036
  309.6 59.7 %reduce-scatter.14.cloned.1.call-start = ((), (), s32[]{:S(2)}) async-start(), calls=%async_computation.11 | async-start | bytes 1228800 | tf_op jit(solution)/shard_map/reduce_scatter | solution.py:1059
  313.0 24.0 %collective-permute-start.15 = (bf16[4,480,256]{2,1,0:T(8,128)(2,1)}, bf16[4,480,256]{2,1,0:T(8,128)(2,1)S(1)}, u32[]{:S(2)}, u32[]{:S(2)}) collective-permute-start(bf16[4,480,256]{2,1,0:T(8,128)(2,1)} %get-tuple-element.264), channel_id=1, source_target_pairs={{0,2},{1,3},{2,0},{3,1},{4,6},{5,7},{6,4},{7,5},{8,10},{9,11},{10,... | collective-permute-start | bytes 2949128 | tf_op jit(solution)/shard_map/ppermute | solution.py:1036
  316.6 33.9 %collective-permute-start.12 = (bf16[148,1024]{1,0:T(8,128)(2,1)S(1)}, bf16[148,1024]{1,0:T(8,128)(2,1)S(1)}, u32[]{:S(2)}, u32[]{:S(2)}) collective-permute-start(bf16[148,1024]{1,0:T(8,128)(2,1)S(1)} %copy-done.18), channel_id=1, source_target_pairs={{0,16},{16,0},{1,17},{17,1},{2,18},{18,2},{3,19},{19,3},{4,20},{20... | collective-permute-start | bytes 909320 | tf_op jit(solution)/shard_map/ppermute | solution.py:1036
  317.3 17.1 %copy-start.5 = (bf16[4,512,256]{2,1,0:T(8,128)(2,1)S(1)}, bf16[4,512,256]{2,1,0:T(8,128)(2,1)}, u32[]{:S(2)}) copy-start(bf16[4,512,256]{2,1,0:T(8,128)(2,1)} %get-tuple-element.207) | copy-start | bytes 3145732
  338.2 9.2 %copy-start.12 = (bf16[1,1408,256]{2,1,0:T(8,128)(2,1)S(1)}, bf16[1,1408,256]{2,1,0:T(8,128)(2,1)}, u32[]{:S(2)}) copy-start(bf16[1,1408,256]{2,1,0:T(8,128)(2,1)} %reduce-scatter.8.cloned.1.call-done) | copy-start | bytes 2162692
  338.2 59.1 %reduce-scatter.12.cloned.1.call-start = ((), (), s32[]{:S(2)}) async-start(), calls=%async_computation.10 | async-start | bytes 1310720 | tf_op jit(solution)/shard_map/reduce_scatter | solution.py:1059
  339.3 6.4 %collective-permute-start.18 = (bf16[2,256,256]{2,1,0:T(8,128)(2,1)S(1)}, bf16[2,256,256]{2,1,0:T(8,128)(2,1)S(1)}, u32[]{:S(2)}, u32[]{:S(2)}) collective-permute-start(bf16[2,256,256]{2,1,0:T(8,128)(2,1)S(1)} %slice_bitcast_fusion.2), channel_id=1, source_target_pairs={{0,16},{16,0},{1,17},{17,1},{2,18},{18,2},{3,19},{19,3},{4,20},{20... | collective-permute-start | bytes 786440 | tf_op jit(solution)/shard_map/ppermute | solution.py:1036
  345.8 5.7 %collective-permute-start.19 = (bf16[256,256]{1,0:T(8,128)(2,1)S(1)}, bf16[256,256]{1,0:T(8,128)(2,1)S(1)}, u32[]{:S(2)}, u32[]{:S(2)}) collective-permute-start(bf16[256,256]{1,0:T(8,128)(2,1)S(1)} %slice_bitcast_fusion.6), channel_id=1, source_target_pairs={{0,2},{1,3},{2,0},{3,1},{4,6},{5,7},{6,4},{7,5},{8,10},{9,11},{10,... | collective-permute-start | bytes 393224 | tf_op jit(solution)/shard_map/ppermute | solution.py:1036
  347.4 7.5 %collective-permute-start.16 = (bf16[2,352,256]{2,1,0:T(8,128)(2,1)S(1)}, bf16[2,352,256]{2,1,0:T(8,128)(2,1)S(1)}, u32[]{:S(2)}, u32[]{:S(2)}) collective-permute-start(bf16[2,352,256]{2,1,0:T(8,128)(2,1)S(1)} %slice_bitcast_fusion), channel_id=1, source_target_pairs={{0,16},{16,0},{1,17},{17,1},{2,18},{18,2},{3,19},{19,3},{4,20},{20... | collective-permute-start | bytes 1081352 | tf_op jit(solution)/shard_map/ppermute | solution.py:1036
  355.1 5.6 %collective-permute-start.17 = (bf16[352,256]{1,0:T(8,128)(2,1)S(1)}, bf16[352,256]{1,0:T(8,128)(2,1)S(1)}, u32[]{:S(2)}, u32[]{:S(2)}) collective-permute-start(bf16[352,256]{1,0:T(8,128)(2,1)S(1)} %slice_bitcast_fusion.4), channel_id=1, source_target_pairs={{0,2},{1,3},{2,0},{3,1},{4,6},{5,7},{6,4},{7,5},{8,10},{9,11},{10,... | collective-permute-start | bytes 540680 | tf_op jit(solution)/shard_map/ppermute | solution.py:1036
  (14 other events, 35.3 us)
Sparse Core Ops, SparseCore 0:
  23.2 56.1 all-gather.2
  81.5 50.6 all-gather.4
  185.9 44.1 reduce-scatter.5
  232.4 65.6 reduce-scatter.7
  309.7 27.4 reduce-scatter.9
  339.5 29.6 reduce-scatter.13
  371.6 25.7 reduce-scatter.11

commit v8 on v7

--- a/solution.py
+++ b/solution.py
@@ -62,7 +62,7 @@
     tops = [jnp.max(s, axis=-1, keepdims=True) for s in scores]
     powers = [jnp.exp(s - t) for s, t in zip(scores, tops)]
     sums = [jnp.sum(e, axis=-1, keepdims=True) for e in powers]
-    return [low(e / total) for e, total in zip(powers, sums)]
+    return [low(e * (1.0 / total)) for e, total in zip(powers, sums)]
 
 
 def attend(queries, keys, values, scale, masks):

time: 411 us -> 411 us (level)
  no operation moved by 1% of the time
where the time goes in v8:
time: 411 us; the launch traced here: 408 us
  Pallas kernels  263 us (64%)
  waiting for transfers between devices  67.2 us (16%)
  starting transfers between devices  23 us (6%)
  other arithmetic  21.8 us (5%)
  local copies, waits for them, and re-layouts  18.5 us (5%)
  between operations  14.8 us (4%)
    pallas_call x9, Pallas kernels, run(): pl.pallas_call(kernel, grid=(QUARTERS,) if order else (1,), in_specs=[spe...  263 us
    ppermute x20, waiting for transfers between devices, swap(): lax.ppermute(value, axis, [(i, i ^ apart) for i in range(lax.axis_size(ax...  34 us
    reduce_scatter x5, waiting for transfers between devices, fold_last(): return lax.psum_scatter(total, 'dp', scatter_dimension=0, tiled=True)[0]  27.4 us
    ppermute x20, starting transfers between devices, swap(): lax.ppermute(value, axis, [(i, i ^ apart) for i in range(lax.axis_size(ax...  22.1 us
    unnamed x52, local copies, waits for them, and re-layouts  14.9 us
    convert_element_type x9, other arithmetic, low(): return value.astype(BF)  10.6 us
  transfers between devices with their start and end apart: 27, of which 11 were waited for; matrix products, arithmetic and copies ran while one was open for 8% of the time, Pallas kernels for 50%

profile of v8, /device:TPU:0, one launch (start us, length us, event | category | flops | bytes accessed | tf_op | source)
XLA Modules:
  0.0 407.7 jit_solution(3984566930635764662)
XLA Ops:
  7.9 4.2 %shard_map.390 = (bf16[6656,256]{1,0:T(8,128)(2,1)}, bf16[1536,256]{1,0:T(8,128)(2,1)}, bf16[640,256]{1,0:T(8,128)(2,1)}) custom-call(s32[6]{0:T(128)} %stack.39.ids, bf16[768,768]{1,0:T(8,128)(2,1)} %bitcast.176, bf16[768,768]{1,0:T(8,128)(2,1)} %bitcast.177, bf16[1024,256]{1,0:T(8,128)(2,1)} %bitcast.180, bf16[256,1024]{1,0:T(8,128)(2,1)} %bitcast.181), custom_call_target="tpu_custom_call" | custom-call | flops 3300000000 | bytes 1024 | tf_op jit(solution)/shard_map/pallas_call | solution.py:1018
  12.1 3.0 collective-permute-start.1
  15.9 1.6 copy.61.refs_2_
  17.5 4.2 %shard_map.391 = (bf16[6400,256]{1,0:T(8,128)(2,1)}, bf16[1792,256]{1,0:T(8,128)(2,1)}, bf16[576,256]{1,0:T(8,128)(2,1)}) custom-call(s32[6]{0:T(128)} %stack.39.ids, bf16[576,768]{1,0:T(8,128)(2,1)} %bitcast.179, bf16[192,768]{1,0:T(8,128)(2,1)} %bitcast.191, bf16[1024,768]{1,0:T(8,128)(2,1)} %copy.61.refs_2_, bf16[256,1024]{1,0:T(8,128)(2,1)} %bitcast.182), custom_call_target="tpu_custom_call" | custom-call | flops 3300000000 | bytes 1024 | tf_op jit(solution)/shard_map/pallas_call | solution.py:1018
  23.2 1.8 collective-permute-start
  27.5 2.2 copy.80
  30.9 2.6 collective-permute-done
  33.9 77.0 %shard_map.392 = (f32[512,768]{1,0:T(8,128)}, f32[192,1024]{1,0:T(8,128)}, bf16[4,512,768]{2,1,0:T(8,128)(2,1)}, bf16[4,192,1024]{2,1,0:T(8,128)(2,1)}, bf16[4,5...) custom-call(s32[16]{0:T(128)} %lengths.3, ...), custom_call_target="tpu_custom_call" | custom-call | flops 76999999488 | bytes 1024 | tf_op jit(solution)/shard_map/pallas_call | solution.py:1018
  111.6 15.1 %shard_map.393 = (bf16[512,768]{1,0:T(8,128)(2,1)}, bf16[192,1024]{1,0:T(8,128)(2,1)}, f32[512,768]{1,0:T(8,128)}, f32[192,1024]{1,0:T(8,128)}, bf16[4,512,768]{...) custom-call(f32[512,768]{1,0:T(8,128)} %get-tuple-element.129.text_p, ...), custom_call_target="tpu_custom_call" | custom-call | flops 1100000000 | bytes 1024 | tf_op jit(solution)/shard_map/pallas_call | solution.py:1018
  126.6 5.6 %all-gather.5.cloned.1.call-done.refs_3_.refs_10_ = bf16[4608,256]{1,0:T(8,128)(2,1)} async-done(((bf16[576,256]{1,0:T(8,128)(2,1)}), bf16[4608,256]{1,0:T(8,128)(2,1)}) %all-gather.5.cloned.1.call-update) | async-done | bytes 2359312 | tf_op jit(solution)/shard_map/all_gather | solution.py:1144
  133.3 19.9 %shard_map.394 = (f32[512,384]{1,0:T(8,128)}, f32[512,384]{1,0:T(8,128)}, bf16[148,1024]{1,0:T(8,128)(2,1)}, f32[512,768]{1,0:T(8,128)}, f32[192,1024]{1,0:T(8,1...) custom-call(s32[6]{0:T(128)} %stack.39.ids, ...), custom_call_target="tpu_custom_call" | custom-call | flops 20899999744 | bytes 1024 | tf_op jit(solution)/shard_map/pallas_call | solution.py:1018
  153.2 32.6 %shard_map.395 = (f32[512,768]{1,0:T(8,128)}, f32[192,1024]{1,0:T(8,128)}, f32[2,768]{1,0:T(2,128)}, f32[2,1024]{1,0:T(2,128)}, bf16[2304,256]{1,0:T(8,128)(2,1)...) custom-call(f32[512,768]{1,0:T(8,128)} %get-tuple-element.142.text_g, ...), custom_call_target="tpu_custom_call" | custom-call | flops 35200000000 | bytes 1024 | tf_op jit(solution)/shard_map/pallas_call | solution.py:1018
  185.9 1.6 collective-permute-start.9
  188.6 27.7 %shard_map.396 = (f32[512,768]{1,0:T(8,128)}, f32[192,1024]{1,0:T(8,128)}, bf16[2304,256]{1,0:T(8,128)(2,1)}, f32[2,768]{1,0:T(2,128)}, f32[2,1024]{1,0:T(2,128)...) custom-call(f32[512,768]{1,0:T(8,128)} %get-tuple-element.157.text_g, ...), custom_call_target="tpu_custom_call" | custom-call | flops 30799998976 | bytes 1024 | tf_op jit(solution)/shard_map/pallas_call | solution.py:1018
  216.3 1.6 collective-permute-done.8
  219.0 2.5 fusion.6
  225.2 46.9 %shard_map.397 = (bf16[4,2304,256]{2,1,0:T(8,128)(2,1)}, bf16[4,512,768]{2,1,0:T(8,128)(2,1)}, bf16[4,192,768]{2,1,0:T(8,128)(2,1)}, f32[2304,256]{1,0:T(8,128)}...) custom-call(bf16[2304,256]{1,0:T(8,128)(2,1)} %get-tuple-element.177.grad, f32[2,768]{1,0:T(2,128)} %get-tuple-element.178.refs_0_, ...), custom_call_target="tpu_custom_call" | custom-call | flops 52800000000 | bytes 1024 | tf_op jit(solution)/shard_map/pallas_call | solution.py:1018
  272.9 35.0 %shard_map.398 = (f32[512,384]{1,0:T(8,128)}, f32[512,384]{1,0:T(8,128)}, bf16[148,1024]{1,0:T(8,128)(2,1)}, bf16[4,400,256]{2,1,0:T(8,128)(2,1)}, bf16[4,512,25...) custom-call(bf16[2304,256]{1,0:T(8,128)(2,1)} %get-tuple-element.188.total, ...), custom_call_target="tpu_custom_call" | custom-call | flops 2200000000 | bytes 1024 | tf_op jit(solution)/shard_map/pallas_call | solution.py:1018
  308.0 1.6 collective-permute-start.14
  309.9 3.1 fusion.1
  318.6 15.9 %collective-permute-done.14 = bf16[4,512,256]{2,1,0:T(8,128)(2,1)} collective-permute-done((bf16[4,512,256]{2,1,0:T(8,128)(2,1)}, bf16[4,512,256]{2,1,0:T(8,128)(2,1)}, u32[]{:S(2)}, u32[]{:S(2)}) %collective-permute-start.14) | collective-permute-done | bytes 1048608 | tf_op jit(solution)/shard_map/ppermute | solution.py:1036
  334.5 2.5 add_convert_fusion
  339.3 1.6 collective-permute-start.18
  340.9 4.8 %collective-permute-done.18 = bf16[2,256,256]{2,1,0:T(8,128)(2,1)S(1)} collective-permute-done((bf16[2,256,256]{2,1,0:T(8,128)(2,1)S(1)}, bf16[2,256,256]{2,1,0:T(8,128)(2,1)S(1)}, u32[]{:S(2)}, u32[]{:S(2)}) %collective-permute-start.18) | collective-permute-done | bytes 262176 | tf_op jit(solution)/shard_map/ppermute | solution.py:1036
  345.8 1.6 collective-permute-start.19
  347.4 1.6 collective-permute-start.16
  351.5 3.5 collective-permute-done.16
  357.5 3.1 collective-permute-done.17
  365.1 1.6 slice_bitcast_fusion.13
  367.6 1.7 reduce-scatter.14.cloned.1.call-done
  371.7 25.7 %reduce-scatter.12.cloned.1.call-done = bf16[1,512,256]{2,1,0:T(8,128)(2,1)} async-done(((bf16[4,512,256]{2,1,0:T(8,128)(2,1)}), bf16[1,512,256]{2,1,0:T(8,128)(2,1)}) %reduce-scatter.12.cloned.1.call-update) | async-done | bytes 262160 | tf_op jit(solution)/shard_map/reduce_scatter | solution.py:1059
  397.3 1.6 convert_bitcast_fusion.1
  (136 shorter events, 38.2 us)
Async XLA Ops:
  7.2 103.7 %all-gather.3.cloned.1.call-start = ((), (), s32[]{:S(2)}) async-start(), calls=%async_computation.5 | async-start | bytes 2949120 | tf_op jit(solution)/shard_map/all_gather | solution.py:1143
  7.8 7.2 %copy-start.2 = (bf16[1,1024,3,256]{3,1,2,0:T(8,128)(2,1)S(1)}, bf16[1,1024,3,256]{3,1,2,0:T(8,128)(2,1)}, u32[]{:S(2)}) copy-start(bf16[1,1024,3,256]{3,1,2,0:T(8,128)(2,1)} %param.42) | copy-start | bytes 4718596
  12.1 11.0 %collective-permute-start.1 = (bf16[640,256]{1,0:T(8,128)(2,1)}, bf16[640,256]{1,0:T(8,128)(2,1)}, u32[]{:S(2)}, u32[]{:S(2)}) collective-permute-start(bf16[640,256]{1,0:T(8,128)(2,1)} %get-tuple-element.124), channel_id=1, source_target_pairs={{0,2},{1,3},{2,0},{3,1},{4,6},{5,7},{6,4},{7,5},{8,10},{9,11},{10,... | collective-permute-start | bytes 983048 | tf_op jit(solution)/shard_map/ppermute | solution.py:1036
  17.5 7.5 %copy-start = (bf16[6656,256]{1,0:T(8,128)(2,1)S(1)}, bf16[6656,256]{1,0:T(8,128)(2,1)}, u32[]{:S(2)}) copy-start(bf16[6656,256]{1,0:T(8,128)(2,1)} %get-tuple-element.121.refs_0_.refs_4_) | copy-start | bytes 10223620
  23.1 109.1 %all-gather.5.cloned.1.call-start = ((), (), s32[]{:S(2)}) async-start(), calls=%async_computation.6 | async-start | bytes 2654208 | tf_op jit(solution)/shard_map/all_gather | solution.py:1144
  23.2 10.3 %collective-permute-start = (bf16[576,256]{1,0:T(8,128)(2,1)}, bf16[576,256]{1,0:T(8,128)(2,1)}, u32[]{:S(2)}, u32[]{:S(2)}) collective-permute-start(bf16[576,256]{1,0:T(8,128)(2,1)} %get-tuple-element.123), channel_id=1, source_target_pairs={{0,2},{1,3},{2,0},{3,1},{4,6},{5,7},{6,4},{7,5},{8,10},{9,11},{10,... | collective-permute-start | bytes 884744 | tf_op jit(solution)/shard_map/ppermute | solution.py:1036
  25.0 108.3 %collective-permute-start.5 = (bf16[6400,256]{1,0:T(8,128)(2,1)}, bf16[6400,256]{1,0:T(8,128)(2,1)}, u32[]{:S(2)}, u32[]{:S(2)}) collective-permute-start(bf16[6400,256]{1,0:T(8,128)(2,1)} %get-tuple-element.125.refs_0_.refs_7_), channel_id=1, source_target_pairs={{0,1},{1,0},{2,3},{3,2},{4,5},{5,4},{6,7},{7,6},{8,9},{9,8},{10,11... | collective-permute-start | bytes 9830408 | tf_op jit(solution)/shard_map/ppermute | solution.py:1036
  25.0 86.6 %collective-permute-start.2 = (bf16[6656,256]{1,0:T(8,128)(2,1)S(1)}, bf16[6656,256]{1,0:T(8,128)(2,1)}, u32[]{:S(2)}, u32[]{:S(2)}) collective-permute-start(bf16[6656,256]{1,0:T(8,128)(2,1)S(1)} %copy-done), channel_id=1, source_target_pairs={{0,1},{1,0},{2,3},{3,2},{4,5},{5,4},{6,7},{7,6},{8,9},{9,8},{10,11... | collective-permute-start | bytes 10223624 | tf_op jit(solution)/shard_map/ppermute | solution.py:1036
  25.5 85.4 %collective-permute-start.4 = (bf16[148,1024]{1,0:T(8,128)(2,1)}, bf16[148,1024]{1,0:T(8,128)(2,1)}, u32[]{:S(2)}, u32[]{:S(2)}) collective-permute-start(bf16[148,1024]{1,0:T(8,128)(2,1)} %param.27), channel_id=1, source_target_pairs={{0,16},{16,0},{1,17},{17,1},{2,18},{18,2},{3,19},{19,3},{4,20},{20... | collective-permute-start | bytes 909320 | tf_op jit(solution)/shard_map/ppermute | solution.py:1036
  27.0 83.9 %collective-permute-start.3 = (bf16[1536,256]{1,0:T(8,128)(2,1)}, bf16[1536,256]{1,0:T(8,128)(2,1)}, u32[]{:S(2)}, u32[]{:S(2)}) collective-permute-start(bf16[1536,256]{1,0:T(8,128)(2,1)} %get-tuple-element.131), channel_id=1, source_target_pairs={{0,2},{1,3},{2,0},{3,1},{4,6},{5,7},{6,4},{7,5},{8,10},{9,11},{10,... | collective-permute-start | bytes 2359304 | tf_op jit(solution)/shard_map/ppermute | solution.py:1036
  33.5 274.5 %reduce-scatter.6.cloned.1.call-start = ((), (), s32[]{:S(2)}) async-start(), calls=%async_computation.7 | async-start | bytes 2621440 | tf_op jit(solution)/shard_map/reduce_scatter | solution.py:1059
  110.9 22.4 %collective-permute-start.6 = (bf16[1792,256]{1,0:T(8,128)(2,1)}, bf16[1792,256]{1,0:T(8,128)(2,1)}, u32[]{:S(2)}, u32[]{:S(2)}) collective-permute-start(bf16[1792,256]{1,0:T(8,128)(2,1)} %get-tuple-element.137), channel_id=1, source_target_pairs={{0,2},{1,3},{2,0},{3,1},{4,6},{5,7},{6,4},{7,5},{8,10},{9,11},{10,... | collective-permute-start | bytes 2752520 | tf_op jit(solution)/shard_map/ppermute | solution.py:1036
  185.8 122.2 %reduce-scatter.8.cloned.1.call-start = ((), (), s32[]{:S(2)}) async-start(), calls=%async_computation.8 | async-start | bytes 3604480 | tf_op jit(solution)/shard_map/reduce_scatter | solution.py:1059
  185.9 30.4 %collective-permute-start.9 = (bf16[148,1024]{1,0:T(8,128)(2,1)}, bf16[148,1024]{1,0:T(8,128)(2,1)S(1)}, u32[]{:S(2)}, u32[]{:S(2)}) collective-permute-start(bf16[148,1024]{1,0:T(8,128)(2,1)} %get-tuple-element.169), channel_id=1, source_target_pairs={{0,16},{16,0},{1,17},{17,1},{2,18},{18,2},{3,19},{19,3},{4,20},{20... | collective-permute-start | bytes 909320 | tf_op jit(solution)/shard_map/ppermute | solution.py:1036
  187.4 30.5 %collective-permute-start.8 = (bf16[2,4,256,256]{3,2,1,0:T(8,128)(2,1)}, bf16[2,4,256,256]{3,2,1,0:T(8,128)(2,1)S(1)}, u32[]{:S(2)}, u32[]{:S(2)}) collective-permute-start(bf16[2,4,256,256]{3,2,1,0:T(8,128)(2,1)} %bitcast.23), channel_id=1, source_target_pairs={{0,16},{16,0},{1,17},{17,1},{2,18},{18,2},{3,19},{19,3},{4,20},{20... | collective-permute-start | bytes 3145736 | tf_op jit(solution)/shard_map/ppermute | solution.py:1036
  188.0 29.9 %collective-permute-start.7 = (bf16[2,4,288,256]{3,2,1,0:T(8,128)(2,1)}, bf16[2,4,288,256]{3,2,1,0:T(8,128)(2,1)S(1)}, u32[]{:S(2)}, u32[]{:S(2)}) collective-permute-start(bf16[2,4,288,256]{3,2,1,0:T(8,128)(2,1)} %bitcast.178), channel_id=1, source_target_pairs={{0,2},{1,3},{2,0},{3,1},{4,6},{5,7},{6,4},{7,5},{8,10},{9,11},{10,... | collective-permute-start | bytes 3538952 | tf_op jit(solution)/shard_map/ppermute | solution.py:1036
  218.9 143.2 %reduce-scatter.10.cloned.1.call-start = ((), (), s32[]{:S(2)}) async-start(), calls=%async_computation.9 | async-start | bytes 1024000 | tf_op jit(solution)/shard_map/reduce_scatter | solution.py:1059
  221.5 50.6 %collective-permute-start.11 = (bf16[4,256,256]{2,1,0:T(8,128)(2,1)}, bf16[4,256,256]{2,1,0:T(8,128)(2,1)}, u32[]{:S(2)}, u32[]{:S(2)}) collective-permute-start(bf16[4,256,256]{2,1,0:T(8,128)(2,1)} %get-tuple-element.268), channel_id=1, source_target_pairs={{0,2},{1,3},{2,0},{3,1},{4,6},{5,7},{6,4},{7,5},{8,10},{9,11},{10,... | collective-permute-start | bytes 1572872 | tf_op jit(solution)/shard_map/ppermute | solution.py:1036
  223.2 48.9 %collective-permute-start.10 = (bf16[4,288,256]{2,1,0:T(8,128)(2,1)S(1)}, bf16[4,288,256]{2,1,0:T(8,128)(2,1)S(1)}, u32[]{:S(2)}, u32[]{:S(2)}) collective-permute-start(bf16[4,288,256]{2,1,0:T(8,128)(2,1)S(1)} %get-tuple-element.266), channel_id=1, source_target_pairs={{0,16},{16,0},{1,17},{17,1},{2,18},{18,2},{3,19},{19,3},{4,20},{20... | collective-permute-start | bytes 1769480 | tf_op jit(solution)/shard_map/ppermute | solution.py:1036
  224.6 83.4 %collective-permute-start.13 = (bf16[2,4,480,256]{3,2,1,0:T(8,128)(2,1)}, bf16[2,4,480,256]{3,2,1,0:T(8,128)(2,1)}, u32[]{:S(2)}, u32[]{:S(2)}) collective-permute-start(bf16[2,4,480,256]{3,2,1,0:T(8,128)(2,1)} %bitcast.24), channel_id=1, source_target_pairs={{0,16},{16,0},{1,17},{17,1},{2,18},{18,2},{3,19},{19,3},{4,20},{20... | collective-permute-start | bytes 5898248 | tf_op jit(solution)/shard_map/ppermute | solution.py:1036
  272.9 36.9 %copy-start.1 = (bf16[3840,256]{1,0:T(8,128)(2,1)S(1)}, bf16[3840,256]{1,0:T(8,128)(2,1)}, u32[]{:S(2)}) copy-start(bf16[3840,256]{1,0:T(8,128)(2,1)} %get-tuple-element.170) | copy-start | bytes 5898244
  308.0 26.4 %collective-permute-start.14 = (bf16[4,512,256]{2,1,0:T(8,128)(2,1)}, bf16[4,512,256]{2,1,0:T(8,128)(2,1)}, u32[]{:S(2)}, u32[]{:S(2)}) collective-permute-start(bf16[4,512,256]{2,1,0:T(8,128)(2,1)} %get-tuple-element.208), channel_id=1, source_target_pairs={{0,16},{16,0},{1,17},{17,1},{2,18},{18,2},{3,19},{19,3},{4,20},{20... | collective-permute-start | bytes 3145736 | tf_op jit(solution)/shard_map/ppermute | solution.py:1036
  309.6 59.7 %reduce-scatter.14.cloned.1.call-start = ((), (), s32[]{:S(2)}) async-start(), calls=%async_computation.11 | async-start | bytes 1228800 | tf_op jit(solution)/shard_map/reduce_scatter | solution.py:1059
  313.0 24.0 %collective-permute-start.15 = (bf16[4,480,256]{2,1,0:T(8,128)(2,1)}, bf16[4,480,256]{2,1,0:T(8,128)(2,1)S(1)}, u32[]{:S(2)}, u32[]{:S(2)}) collective-permute-start(bf16[4,480,256]{2,1,0:T(8,128)(2,1)} %get-tuple-element.264), channel_id=1, source_target_pairs={{0,2},{1,3},{2,0},{3,1},{4,6},{5,7},{6,4},{7,5},{8,10},{9,11},{10,... | collective-permute-start | bytes 2949128 | tf_op jit(solution)/shard_map/ppermute | solution.py:1036
  316.6 33.9 %collective-permute-start.12 = (bf16[148,1024]{1,0:T(8,128)(2,1)S(1)}, bf16[148,1024]{1,0:T(8,128)(2,1)S(1)}, u32[]{:S(2)}, u32[]{:S(2)}) collective-permute-start(bf16[148,1024]{1,0:T(8,128)(2,1)S(1)} %copy-done.18), channel_id=1, source_target_pairs={{0,16},{16,0},{1,17},{17,1},{2,18},{18,2},{3,19},{19,3},{4,20},{20... | collective-permute-start | bytes 909320 | tf_op jit(solution)/shard_map/ppermute | solution.py:1036
  317.3 17.1 %copy-start.5 = (bf16[4,512,256]{2,1,0:T(8,128)(2,1)S(1)}, bf16[4,512,256]{2,1,0:T(8,128)(2,1)}, u32[]{:S(2)}) copy-start(bf16[4,512,256]{2,1,0:T(8,128)(2,1)} %get-tuple-element.207) | copy-start | bytes 3145732
  338.2 9.2 %copy-start.12 = (bf16[1,1408,256]{2,1,0:T(8,128)(2,1)S(1)}, bf16[1,1408,256]{2,1,0:T(8,128)(2,1)}, u32[]{:S(2)}) copy-start(bf16[1,1408,256]{2,1,0:T(8,128)(2,1)} %reduce-scatter.8.cloned.1.call-done) | copy-start | bytes 2162692
  338.2 59.1 %reduce-scatter.12.cloned.1.call-start = ((), (), s32[]{:S(2)}) async-start(), calls=%async_computation.10 | async-start | bytes 1310720 | tf_op jit(solution)/shard_map/reduce_scatter | solution.py:1059
  339.3 6.4 %collective-permute-start.18 = (bf16[2,256,256]{2,1,0:T(8,128)(2,1)S(1)}, bf16[2,256,256]{2,1,0:T(8,128)(2,1)S(1)}, u32[]{:S(2)}, u32[]{:S(2)}) collective-permute-start(bf16[2,256,256]{2,1,0:T(8,128)(2,1)S(1)} %slice_bitcast_fusion.2), channel_id=1, source_target_pairs={{0,16},{16,0},{1,17},{17,1},{2,18},{18,2},{3,19},{19,3},{4,20},{20... | collective-permute-start | bytes 786440 | tf_op jit(solution)/shard_map/ppermute | solution.py:1036
  345.8 5.7 %collective-permute-start.19 = (bf16[256,256]{1,0:T(8,128)(2,1)S(1)}, bf16[256,256]{1,0:T(8,128)(2,1)S(1)}, u32[]{:S(2)}, u32[]{:S(2)}) collective-permute-start(bf16[256,256]{1,0:T(8,128)(2,1)S(1)} %slice_bitcast_fusion.6), channel_id=1, source_target_pairs={{0,2},{1,3},{2,0},{3,1},{4,6},{5,7},{6,4},{7,5},{8,10},{9,11},{10,... | collective-permute-start | bytes 393224 | tf_op jit(solution)/shard_map/ppermute | solution.py:1036
  347.4 7.5 %collective-permute-start.16 = (bf16[2,352,256]{2,1,0:T(8,128)(2,1)S(1)}, bf16[2,352,256]{2,1,0:T(8,128)(2,1)S(1)}, u32[]{:S(2)}, u32[]{:S(2)}) collective-permute-start(bf16[2,352,256]{2,1,0:T(8,128)(2,1)S(1)} %slice_bitcast_fusion), channel_id=1, source_target_pairs={{0,16},{16,0},{1,17},{17,1},{2,18},{18,2},{3,19},{19,3},{4,20},{20... | collective-permute-start | bytes 1081352 | tf_op jit(solution)/shard_map/ppermute | solution.py:1036
  355.1 5.6 %collective-permute-start.17 = (bf16[352,256]{1,0:T(8,128)(2,1)S(1)}, bf16[352,256]{1,0:T(8,128)(2,1)S(1)}, u32[]{:S(2)}, u32[]{:S(2)}) collective-permute-start(bf16[352,256]{1,0:T(8,128)(2,1)S(1)} %slice_bitcast_fusion.4), channel_id=1, source_target_pairs={{0,2},{1,3},{2,0},{3,1},{4,6},{5,7},{6,4},{7,5},{8,10},{9,11},{10,... | collective-permute-start | bytes 540680 | tf_op jit(solution)/shard_map/ppermute | solution.py:1036
  (14 other events, 35.3 us)
Sparse Core Ops, SparseCore 0:
  23.2 56.1 all-gather.2
  81.5 50.6 all-gather.4
  185.9 44.1 reduce-scatter.5
  232.4 65.6 reduce-scatter.7
  309.7 27.4 reduce-scatter.9
  339.5 29.6 reduce-scatter.13
  371.6 25.7 reduce-scatter.11
